TPU v7x, 256 devices: a whole 4x4x8 slice. The times are simulated.
256 devices in a mesh: seq: 32 (over x, z), exp: 8 (over y, core).
Axes of the slice: x: 4, y: 4, z: 8, core: 2. Of those that a mesh axis runs over, the one named last changes fastest.
Arguments:
- x_att: bfloat16 [16384, 2048], P('seq'), may hold values from -200 to 200
- w_qk: bfloat16 [2048, 2048], P(None, 'exp'), may hold values from -1.5 to 1.5
- w_val: bfloat16 [2048, 2048], P(None, 'exp'), may hold values from -0.125 to 0.125
- w_out: bfloat16 [2048, 2048], P('exp'), may hold values from -0.125 to 0.125
- perms: int32 [2, 16384], replicated, may hold values from 0 to 16383, as said below
- tokens_b: bfloat16 [16384, 2048], P('seq'), may hold values from -6 to 6
- expert_ids: int32 [16384, 1], P('seq'), may hold values from 0 to 63; in each aligned block of 512 rows (0 to 511, 512 to 1023, ...) at most 16 rows name the same one
- w_gate: bfloat16 [64, 2048, 2048], P('seq', None, 'exp'), may hold values from -0.125 to 0.125
- w_up: bfloat16 [64, 2048, 2048], P('seq', None, 'exp'), may hold values from -0.125 to 0.125
- w_down: bfloat16 [64, 2048, 2048], P('seq', 'exp'), may hold values from -0.125 to 0.125
Outputs:
- attended: bfloat16 [16384, 2048], P('seq', 'exp')
- mixed: bfloat16 [16384, 2048], P('seq', 'exp')
Inputs may be any that keep to these rules, and one draw needn't show every extreme that they name: `perms`: each row is a permutation of the token indices; the 512 sorted positions of every aligned block of 512 hold exactly 16 tokens of every aligned block of 512 token indices. `expert_ids`: in the 512 rows of one index of seq no expert is named by more than 16 rows; in every draw some expert is named by exactly 16 of them.
All inputs are finite; a program needn't handle non-finite values.
Results may differ from a plain program's by a relative error of at most 0.035.
Values may be sent and summed in bfloat16 or wider, within the bound.
No kernel may reach another device: no remote copies, remote signals or barrier semaphores. Data moves between devices by JAX's collectives and lax.ppermute only.
A program may use at most 128 MiB of HBM per device.

v0:
```python
import math

import jax
import jax.numpy as jnp
from jax import lax
from jax.sharding import PartitionSpec as P

HEAD_DIM = 128
BLOCK_LEN = 64
EXP_DEV = 2


def shifted(shard, axis, by):
    count = lax.axis_size(axis)
    return lax.ppermute(shard, axis, [(i, (i + by) % count) for i in range(count)])


def normalize(queries):
    return (
        queries
        * lax.rsqrt(jnp.sum(queries * queries, axis=-1, keepdims=True) + 1e-06)
        / math.sqrt(HEAD_DIM)
    )


def attend(sorted_rows, positions, last_rows, last_positions, head_count):
    span = head_count * HEAD_DIM
    blocks = sorted_rows.shape[0] // BLOCK_LEN
    earlier = jnp.concatenate([last_rows, sorted_rows[:-BLOCK_LEN]], axis=0)
    earlier_pos = jnp.concatenate([last_positions, positions[:-BLOCK_LEN]], axis=0)
    block_shape = (blocks, BLOCK_LEN, head_count, HEAD_DIM)
    queries = sorted_rows[:, :span].astype(jnp.float32).reshape(block_shape)
    all_keys = jnp.concatenate(
        [normalize(earlier[:, :span].astype(jnp.float32).reshape(block_shape)), normalize(queries)],
        axis=1,
    )
    values = jnp.concatenate(
        [earlier[:, span:].reshape(block_shape), sorted_rows[:, span:].reshape(block_shape)], axis=1
    )
    pos_query = positions.reshape(blocks, BLOCK_LEN)
    pos_key = jnp.concatenate([earlier_pos.reshape(blocks, BLOCK_LEN), pos_query], axis=1)
    scores = jnp.einsum("bqhd,bkhd->bhqk", queries, all_keys)
    later = pos_key[:, None, None, :] > pos_query[:, None, :, None]
    itself = pos_key[:, None, None, :] == pos_query[:, None, :, None]
    scores = jnp.where(itself, scores - 10000.0, scores)
    scores = jnp.where(later, -1e30, scores)
    row_max = jnp.max(scores, axis=-1, keepdims=True)
    exponent = jnp.exp(scores - row_max)
    row_total = jnp.sum(exponent, axis=-1, keepdims=True)
    weights = (exponent / row_total).astype(jnp.bfloat16)
    outcome = jnp.einsum("bhqk,bkhd->bqhd", weights, values, preferred_element_type=jnp.float32)
    log_total = jnp.transpose((row_max + jnp.log(row_total))[..., 0], (0, 2, 1)).reshape(
        blocks * BLOCK_LEN, head_count
    )
    return (outcome.reshape(blocks * BLOCK_LEN, span), log_total)


def combine(round_outs, round_lses):
    round_count, length, head_count = round_lses.shape
    peak = jnp.max(round_lses, axis=0, keepdims=True)
    whole = peak + jnp.log(jnp.sum(jnp.exp(round_lses - peak), axis=0, keepdims=True))
    shares = jnp.exp(round_lses - whole)
    weighted = round_outs.reshape(round_count, length, head_count, HEAD_DIM) * shares[..., None]
    return jnp.sum(weighted, axis=0).reshape(length, head_count * HEAD_DIM).astype(jnp.bfloat16)


def body(x_att, w_qk, w_val, w_out, perms, tokens_b, expert_ids, w_gate, w_up, w_down):
    seq_count = lax.axis_size("seq")
    seq_index = lax.axis_index("seq")
    tok_count = x_att.shape[0]
    seq_total = perms.shape[1]
    round_count = perms.shape[0]
    per_peer = tok_count // seq_count
    head_span = w_qk.shape[1]
    head_count = head_span // HEAD_DIM
    query_part = jnp.dot(x_att, w_qk, preferred_element_type=jnp.float32).astype(jnp.bfloat16)
    value_part = jnp.dot(x_att, w_val, preferred_element_type=jnp.float32).astype(jnp.bfloat16)
    projected = jnp.concatenate([query_part, value_part], axis=1)
    my_orders = lax.dynamic_slice_in_dim(perms, seq_index * tok_count, tok_count, 1)
    source = my_orders // tok_count
    peer_ids = jnp.arange(seq_count, dtype=jnp.int32)
    one_hot = (source[:, :, None] == peer_ids[None, None, :]).astype(jnp.int32)
    peer_rank = jnp.sum((jnp.cumsum(one_hot, axis=1) - one_hot) * one_hot, axis=2)
    grid_shape = (round_count, seq_count, tok_count)
    picked = (perms // tok_count == seq_index).reshape(grid_shape)
    slot_place = jnp.where(picked, jnp.cumsum(picked.astype(jnp.int32), axis=2) - 1, per_peer)
    round_ids = jnp.broadcast_to(
        jnp.arange(round_count, dtype=jnp.int32)[:, None, None], grid_shape
    )
    dest_ids = jnp.broadcast_to(peer_ids[None, :, None], grid_shape)
    send_index = (
        jnp.zeros((seq_count, round_count, per_peer), jnp.int32)
        .at[dest_ids, round_ids, slot_place]
        .set((perms % tok_count).reshape(grid_shape), mode="drop")
    )
    outgoing = projected[send_index].reshape(seq_count, round_count * per_peer, 2 * head_span)
    expert_count = EXP_DEV * seq_count
    tokb_count = tokens_b.shape[0]
    capacity = 2 * tokb_count // expert_count
    expert_no = expert_ids[:, 0]
    expert_hot = (expert_no[:, None] == jnp.arange(expert_count, dtype=jnp.int32)[None, :]).astype(
        jnp.int32
    )
    expert_rank = jnp.sum((jnp.cumsum(expert_hot, axis=0) - expert_hot) * expert_hot, axis=1)
    slot_of = expert_no * capacity + expert_rank
    slot_table = (
        jnp.full((expert_count * capacity,), tokb_count, jnp.int32)
        .at[slot_of]
        .set(jnp.arange(tokb_count, dtype=jnp.int32))
    )
    padded = jnp.concatenate([tokens_b, jnp.zeros((1, tokens_b.shape[1]), tokens_b.dtype)], axis=0)
    dispatch = padded[slot_table].reshape(seq_count, EXP_DEV, capacity, tokens_b.shape[1])
    arrived, received = (
        lax.all_to_all(outgoing, "seq", split_axis=0, concat_axis=0, tiled=True),
        lax.all_to_all(dispatch, "seq", split_axis=0, concat_axis=0, tiled=True),
    )
    gate = jnp.einsum("secd,edf->secf", received, w_gate, preferred_element_type=jnp.float32)
    up_val = jnp.einsum("secd,edf->secf", received, w_up, preferred_element_type=jnp.float32)
    hidden = (jax.nn.silu(gate) * up_val).astype(jnp.bfloat16)
    expert_part = jnp.einsum("secf,efd->secd", hidden, w_down, preferred_element_type=jnp.float32)
    arrived = arrived.reshape(seq_count, round_count, per_peer, 2 * head_span)
    round_grid = jnp.broadcast_to(
        jnp.arange(round_count, dtype=jnp.int32)[:, None], (round_count, tok_count)
    )
    sorted_rows = arrived[source, round_grid, peer_rank]
    last_rows = shifted(sorted_rows[:, tok_count - BLOCK_LEN :], "seq", 1)
    last_start = (seq_index * tok_count + seq_total - BLOCK_LEN) % seq_total
    last_orders = lax.dynamic_slice_in_dim(perms, last_start, BLOCK_LEN, 1)
    outcomes = [
        attend(
            sorted_rows[round_no],
            my_orders[round_no],
            last_rows[round_no],
            last_orders[round_no],
            head_count,
        )
        for round_no in range(round_count)
    ]
    round_outs = jnp.stack([pair[0] for pair in outcomes])
    round_lses = jnp.stack([pair[1] for pair in outcomes])
    cube_shape = (seq_count, round_count, per_peer)
    round_cube = jnp.broadcast_to(
        jnp.arange(round_count, dtype=jnp.int32)[None, :, None], cube_shape
    )
    back_index = (
        jnp.zeros(cube_shape, jnp.int32)
        .at[source, round_grid, peer_rank]
        .set(
            jnp.broadcast_to(
                jnp.arange(tok_count, dtype=jnp.int32)[None, :], (round_count, tok_count)
            )
        )
    )
    send_out = round_outs[round_cube, back_index]
    send_lse = round_lses[round_cube, back_index]
    got_out, got_lse = (
        lax.all_to_all(send_out, "seq", split_axis=0, concat_axis=0, tiled=True),
        lax.all_to_all(send_lse, "seq", split_axis=0, concat_axis=0, tiled=True),
    )
    flat_spot = jnp.broadcast_to(
        peer_ids[:, None, None] * per_peer + jnp.arange(per_peer, dtype=jnp.int32)[None, None, :],
        cube_shape,
    )
    inverse = (
        jnp.zeros((round_count, tok_count), jnp.int32).at[round_cube, send_index].set(flat_spot)
    )
    home_out = got_out[inverse // per_peer, round_grid, inverse % per_peer]
    home_lse = got_lse[inverse // per_peer, round_grid, inverse % per_peer]
    mixed_heads = combine(home_out, home_lse)
    attn_part = jnp.dot(mixed_heads, w_out, preferred_element_type=jnp.float32)
    attended_sum, expert_sum = (
        lax.psum_scatter(attn_part, "exp", scatter_dimension=1, tiled=True),
        lax.psum_scatter(expert_part, "exp", scatter_dimension=3, tiled=True),
    )
    expert_back = lax.all_to_all(
        expert_sum.astype(jnp.bfloat16), "seq", split_axis=0, concat_axis=0, tiled=True
    )
    mixed = expert_back.reshape(expert_count * capacity, expert_back.shape[3])[slot_of]
    return (attended_sum.astype(jnp.bfloat16), mixed)


def solution(mesh):
    in_specs = (
        P("seq", None),
        P(None, "exp"),
        P(None, "exp"),
        P("exp", None),
        P(),
        P("seq", None),
        P("seq", None),
        P("seq", None, "exp"),
        P("seq", None, "exp"),
        P("seq", "exp", None),
    )
    out_specs = (P("seq", "exp"), P("seq", "exp"))
    return jax.shard_map(body, mesh=mesh, in_specs=in_specs, out_specs=out_specs, check_vma=False)
```

profile of v0, /device:TPU:32, one launch (start us, length us, event | category | flops | bytes accessed | tf_op | source)
XLA Modules:
  0.0 469.6 jit_solution(17173008346858267445)
XLA Ops:
  7.2 0.8 fusion.88
  8.0 1.2 reduce-window.26
  9.5 0.8 fusion.83
  10.3 0.7 compare_select_fusion.7
  11.0 2.4 scatter_custom_fusion
  13.5 3.2 concatenate.70
  16.7 10.7 %gather_fusion.6 = bf16[1024,2048]{1,0:T(8,128)(2,1)} fusion(bf16[513,2048]{1,0:T(8,128)(2,1)} %concatenate.70, s32[1024]{0:T(1024)S(1)} %fusion.96), kind=kCustom, calls=%fused_computation.6 | custom fusion | bytes 8392704 | tf_op jit(solution)/shard_map/gather | solution.py:112
  27.4 11.2 %all-to-all-start.3 = ((bf16[32,2,16,2048]{3,2,1,0:T(8,128)(2,1)}), bf16[32,2,16,2048]{3,2,1,0:T(8,128)(2,1)}, u32[]{:S(2)}, u32[]{:S(2)}) async-start(bf16[32,2,16,2048]{3,2,1,0:T(8,128)(2,1)} %bitcast.185), calls=%async_computation.4 | async-start | bytes 8388608 | tf_op jit(solution)/shard_map/all_to_all | solution.py:115
  38.7 95.5 %all-to-all-done.3 = bf16[32,2,16,2048]{3,2,1,0:T(8,128)(2,1)} async-done(((bf16[32,2,16,2048]{3,2,1,0:T(8,128)(2,1)}), bf16[32,2,16,2048]{3,2,1,0:T(8,128)(2,1)}, u32[]{:S(2)}, u32[]{:S(2)}) %all-to-all-start.3) | async-done | bytes 4194336 | tf_op jit(solution)/shard_map/all_to_all | solution.py:115
  134.1 4.1 fusion.7
  138.2 8.5 %convolution_bitcast_fusion = f32[32,2,16,2048]{3,2,0,1:T(8,128)} fusion(bf16[2,256,2048]{2,1,0:T(8,128)(2,1)S(1)} %copy-done, bf16[2,2048,256]{2,1,0:T(8,128)(2,1)} %param.18, bf16[32,2,16,2048]{3,2,1,0:T(8,128)(2,1)} %all-to-all-done.3, f32[32,2,16,256]{3,2,0,1:T(8,128)S(1)} %fusion.7), kind=kOutput, calls=%fused_computation.12 | convolution fusion | flops 2149056512 | bytes 17825792 | tf_op jit(solution)/shard_map/secf,efd->secd/dot_general | solution.py:120
  146.8 0.9 copy-done.4
  147.7 0.4 fusion.118
  148.2 2.3 reduce-window.20
  151.8 120.0 %scatter_custom_fusion.1 = s32[1024]{0:T(1024)S(1)} fusion(s32[32768]{0:T(1024)S(1)} %bitcast.195, s32[32768]{0:T(1024)S(1)} %bitcast.196, s32[]{:T(128)} %constant.124.clone.1), kind=kCustom, calls=%fused_computation.199 | custom fusion | bytes 4100
  272.1 2.4 convolution_convert_fusion
  274.5 2.6 convolution_convert_fusion.1
  277.4 5.1 %gather_fusion = bf16[1024,512]{1,0:T(8,128)(2,1)} fusion(bf16[512,512]{1,0:T(8,128)(2,1)S(1)} %copy.127, s32[1024]{0:T(1024)S(1)} %broadcast_clamp_fusion), kind=kCustom, calls=%fused_computation | custom fusion | bytes 2101248 | tf_op jit(solution)/shard_map/gather | solution.py:96
  282.4 6.7 %all-to-all-start = ((bf16[32,32,512]{2,1,0:T(8,128)(2,1)}), bf16[32,32,512]{2,1,0:T(8,128)(2,1)S(1)}, u32[]{:S(2)}, u32[]{:S(2)}) async-start(bf16[32,32,512]{2,1,0:T(8,128)(2,1)} %bitcast.1), calls=%async_computation | async-start | bytes 2097152 | tf_op jit(solution)/shard_map/all_to_all | solution.py:114
  289.2 2.3 reduce-window.24
  292.9 4.3 scatter_custom_fusion.2
  297.7 0.8 broadcast_compare_fusion.3
  298.5 0.8 broadcast_compare_fusion.1
  299.3 18.3 %all-to-all-done = bf16[32,32,512]{2,1,0:T(8,128)(2,1)S(1)} async-done(((bf16[32,32,512]{2,1,0:T(8,128)(2,1)}), bf16[32,32,512]{2,1,0:T(8,128)(2,1)S(1)}, u32[]{:S(2)}, u32[]{:S(2)}) %all-to-all-start) | async-done | bytes 1048608 | tf_op jit(solution)/shard_map/all_to_all | solution.py:114
  317.5 8.5 %gather_fusion.1 = bf16[1024,512]{1,0:T(8,128)(2,1)S(1)} fusion(bf16[32,2,16,512]{3,2,1,0:T(8,128)(2,1)S(1)} %bitcast.183, s32[1024]{0:T(1024)S(1)} %bitcast.184), kind=kCustom, calls=%fused_computation.1 | custom fusion | bytes 2109440 | tf_op jit(solution)/shard_map/gather | solution.py:125
  326.1 0.7 slice.158
  327.5 0.8 copy.130
  328.4 0.9 fusion.53
  329.4 0.9 fusion.55
  330.3 1.6 collective-permute-done
  332.3 0.6 multiply_reduce_fusion.2
  333.3 1.5 fusion.122
  334.9 0.4 fusion.65
  336.0 0.6 multiply_reduce_fusion.1
  337.0 0.6 fusion.121
  337.6 0.4 fusion.66
  338.1 0.3 copy-done.7
  338.7 6.8 %gather_fusion.4 = f32[1024,2]{1,0:T(8,128)S(1)} fusion(f32[2,512,2]{2,1,0:T(8,128)S(1)} %copy.153, s32[1024]{0:T(1024)S(1)} %reshape.336), kind=kCustom, calls=%fused_computation.4 | custom fusion | bytes 24576 | tf_op jit(solution)/shard_map/gather | solution.py:155
  345.5 1.1 copy.154
  346.6 7.2 %all-to-all-start.2 = ((f32[32,2,16,2]{2,3,1,0:T(2,128)}), f32[32,2,16,2]{2,3,1,0:T(2,128)S(1)}, u32[]{:S(2)}, u32[]{:S(2)}) async-start(f32[32,2,16,2]{2,3,1,0:T(2,128)} %copy.154), calls=%async_computation.2 | async-start | bytes 131072 | tf_op jit(solution)/shard_map/all_to_all | solution.py:158
  354.0 0.7 convolution_bitcast_fusion.2
  354.7 0.4 copy.138
  355.1 0.4 stack_reshape.12
  355.7 0.7 convolution_bitcast_fusion.1
  356.3 0.4 copy.148
  356.8 0.4 stack_reshape.13
  357.3 12.2 %gather_fusion.2 = f32[1024,256]{1,0:T(8,128)} fusion(f32[2,512,256]{2,1,0:T(8,128)S(1)} %pad_maximum_fusion, s32[1024]{0:T(1024)S(1)} %reshape.336), kind=kCustom, calls=%fused_computation.2 | custom fusion | bytes 2105344 | tf_op jit(solution)/shard_map/gather | solution.py:154
  369.4 10.0 %all-to-all-start.1 = ((f32[32,2,16,256]{3,2,1,0:T(8,128)}), f32[32,2,16,256]{3,2,1,0:T(8,128)S(1)}, u32[]{:S(2)}, u32[]{:S(2)}) async-start(f32[32,2,16,256]{3,2,1,0:T(8,128)} %bitcast.19), calls=%async_computation.1 | async-start | bytes 2097152 | tf_op jit(solution)/shard_map/all_to_all | solution.py:157
  380.1 4.3 scatter_custom_fusion.3
  384.5 0.4 copy.155
  384.9 8.4 %gather_fusion.5 = f32[1024,2]{1,0:T(8,128)S(1)} fusion(f32[32,2,16,2]{3,2,1,0:T(8,128)S(1)} %copy.155, s32[1024]{0:T(1024)S(1)} %bitcast.181), kind=kCustom, calls=%fused_computation.5 | custom fusion | bytes 28672 | tf_op jit(solution)/shard_map/gather | solution.py:168
  393.6 0.9 subtract_exponential_fusion
  394.4 10.7 %all-to-all-done.1 = f32[32,2,16,256]{3,2,1,0:T(8,128)S(1)} async-done(((f32[32,2,16,256]{3,2,1,0:T(8,128)}), f32[32,2,16,256]{3,2,1,0:T(8,128)S(1)}, u32[]{:S(2)}, u32[]{:S(2)}) %all-to-all-start.1) | async-done | bytes 1048608 | tf_op jit(solution)/shard_map/all_to_all | solution.py:157
  405.1 9.0 %gather_fusion.3 = f32[1024,256]{1,0:T(8,128)S(1)} fusion(f32[32,2,16,256]{3,2,1,0:T(8,128)S(1)} %all-to-all-done.1, s32[1024]{0:T(1024)S(1)} %bitcast.182), kind=kCustom, calls=%fused_computation.3 | custom fusion | bytes 2109440 | tf_op jit(solution)/shard_map/gather | solution.py:167
  414.1 0.5 gather.30
  414.6 0.5 copy-done.2
  415.1 3.1 multiply_reduce_fusion
  418.3 2.7 fusion.71
  421.0 1.3 convert_element_type.66
  422.3 0.9 copy.159
  423.2 5.1 %all-to-all-start.4 = ((bf16[32,2,16,256]{3,2,1,0:T(8,128)(2,1)}), bf16[32,2,16,256]{3,2,1,0:T(8,128)(2,1)S(1)}, u32[]{:S(2)}, u32[]{:S(2)}) async-start(bf16[32,2,16,256]{3,2,1,0:T(8,128)(2,1)} %copy.159), calls=%async_computation.6 | async-start | bytes 1048576 | tf_op jit(solution)/shard_map/all_to_all | solution.py:175
  428.4 30.0 %reduce-scatter.3.cloned.1.call-done = f32[512,256]{1,0:T(8,128)} async-done(((f32[512,2048]{1,0:T(8,128)}), f32[512,256]{1,0:T(8,128)}) %reduce-scatter.3.cloned.1.call-update) | async-done | bytes 524304 | tf_op jit(solution)/shard_map/reduce_scatter | solution.py:172
  458.4 1.8 convert_element_type.62
  460.1 2.6 gather_fusion.7
  (160 shorter events, 8.2 us)
Async XLA Ops:
  7.2 131.1 %copy-start = (bf16[2,256,2048]{2,1,0:T(8,128)(2,1)S(1)}, bf16[2,256,2048]{2,1,0:T(8,128)(2,1)}, u32[]{:S(2)}) copy-start(bf16[2,256,2048]{2,1,0:T(8,128)(2,1)} %param.19) | copy-start | bytes 6291460
  27.4 106.8 %all-to-all-start.3 = ((bf16[32,2,16,2048]{3,2,1,0:T(8,128)(2,1)}), bf16[32,2,16,2048]{3,2,1,0:T(8,128)(2,1)}, u32[]{:S(2)}, u32[]{:S(2)}) async-start(bf16[32,2,16,2048]{3,2,1,0:T(8,128)(2,1)} %bitcast.185), calls=%async_computation.4 | async-start | bytes 8388608 | tf_op jit(solution)/shard_map/all_to_all | solution.py:115
  38.6 382.4 %reduce-scatter.5.cloned.1.call-start = ((), (), s32[]{:S(2)}) async-start(), calls=%async_computation.8 | async-start | bytes 9437184 | tf_op jit(solution)/shard_map/reduce_scatter | solution.py:173
  146.8 0.9 copy-start.4
  147.7 3.6 copy-start.15
  147.7 3.7 copy-start.16
  148.2 123.9 %copy-start.19 = (bf16[2048,256]{1,0:T(8,128)(2,1)S(1)}, bf16[2048,256]{1,0:T(8,128)(2,1)}, u32[]{:S(2)}) copy-start(bf16[2048,256]{1,0:T(8,128)(2,1)} %param.12) | copy-start | bytes 3145732
  282.4 35.1 %all-to-all-start = ((bf16[32,32,512]{2,1,0:T(8,128)(2,1)}), bf16[32,32,512]{2,1,0:T(8,128)(2,1)S(1)}, u32[]{:S(2)}, u32[]{:S(2)}) async-start(bf16[32,32,512]{2,1,0:T(8,128)(2,1)} %bitcast.1), calls=%async_computation | async-start | bytes 2097152 | tf_op jit(solution)/shard_map/all_to_all | solution.py:114
  326.7 5.2 %collective-permute-start = (bf16[2,64,512]{2,1,0:T(8,128)(2,1)}, bf16[2,64,512]{2,1,0:T(8,128)(2,1)S(1)}, u32[]{:S(2)}, u32[]{:S(2)}) collective-permute-start(bf16[2,64,512]{2,1,0:T(8,128)(2,1)} %slice.158), channel_id=1, source_target_pairs={{0,8},{8,16},{16,24},{24,32},{32,40},{40,48},{48,56},{56,64},{64,7... | collective-permute-start | bytes 393224 | tf_op jit(solution)/shard_map/ppermute | solution.py:15
  332.0 1.3 copy-start.13
  332.0 1.3 copy-start.14
  334.9 0.8 copy-start.5
  334.9 2.1 copy-start.10
  334.9 2.1 copy-start.11
  334.9 2.1 copy-start.12
  337.6 0.9 copy-start.7
  338.7 15.3 %copy-start.6 = (f32[8,2,64,128]{3,2,1,0:T(8,128)S(1)}, f32[8,2,64,128]{3,2,1,0:T(8,128)}, u32[]{:S(2)}) copy-start(f32[8,2,64,128]{3,2,1,0:T(8,128)} %copy-done.5) | copy-start | bytes 1572868
  338.7 15.3 %copy-start.9 = (bf16[8,64,2,128]{3,1,2,0:T(8,128)(2,1)S(1)}, bf16[8,64,2,128]{3,1,2,0:T(8,128)(2,1)}, u32[]{:S(2)}) copy-start(bf16[8,64,2,128]{3,1,2,0:T(8,128)(2,1)} %copy.130) | copy-start | bytes 786436
  346.6 22.9 %all-to-all-start.2 = ((f32[32,2,16,2]{2,3,1,0:T(2,128)}), f32[32,2,16,2]{2,3,1,0:T(2,128)S(1)}, u32[]{:S(2)}, u32[]{:S(2)}) async-start(f32[32,2,16,2]{2,3,1,0:T(2,128)} %copy.154), calls=%async_computation.2 | async-start | bytes 131072 | tf_op jit(solution)/shard_map/all_to_all | solution.py:158
  354.6 1.0 copy-start.8
  369.4 10.1 %copy-start.18 = (s32[2]{0:T(128)S(1)}, s32[2]{0:T(128)}, u32[]{:S(2)}) copy-start(s32[2]{0:T(128)} %constant.166) | copy-start | bytes 28
  369.4 10.2 %copy-start.17 = (s32[2]{0:T(128)S(1)}, s32[2]{0:T(128)}, u32[]{:S(2)}) copy-start(s32[2]{0:T(128)} %constant.169) | copy-start | bytes 28
  369.4 35.7 %all-to-all-start.1 = ((f32[32,2,16,256]{3,2,1,0:T(8,128)}), f32[32,2,16,256]{3,2,1,0:T(8,128)S(1)}, u32[]{:S(2)}, u32[]{:S(2)}) async-start(f32[32,2,16,256]{3,2,1,0:T(8,128)} %bitcast.19), calls=%async_computation.1 | async-start | bytes 2097152 | tf_op jit(solution)/shard_map/all_to_all | solution.py:157
  379.5 78.9 %reduce-scatter.3.cloned.1.call-start = ((), (), s32[]{:S(2)}) async-start(), calls=%async_computation.7 | async-start | bytes 4718592 | tf_op jit(solution)/shard_map/reduce_scatter | solution.py:172
  414.1 1.0 copy-start.2
  415.1 3.1 copy-start.3
  422.3 40.4 %copy-start.1 = (bf16[2,256,2048]{2,1,0:T(8,128)(2,1)S(1)}, bf16[2,256,2048]{2,1,0:T(8,128)(2,1)}, u32[]{:S(2)}) copy-start(bf16[2,256,2048]{2,1,0:T(8,128)(2,1)} %param.19) | copy-start | bytes 6291460
  423.2 36.9 %all-to-all-start.4 = ((bf16[32,2,16,256]{3,2,1,0:T(8,128)(2,1)}), bf16[32,2,16,256]{3,2,1,0:T(8,128)(2,1)S(1)}, u32[]{:S(2)}, u32[]{:S(2)}) async-start(bf16[32,2,16,256]{3,2,1,0:T(8,128)(2,1)} %copy.159), calls=%async_computation.6 | async-start | bytes 1048576 | tf_op jit(solution)/shard_map/all_to_all | solution.py:175
Sparse Core Ops, SparseCore 0:
  146.9 53.1 reduce-scatter.4
  421.1 37.2 reduce-scatter.2
where the time goes:
time: 471 us; the launch traced here: 470 us
  local copies, waits for them, and re-layouts  210 us (45%)
  waiting for transfers between devices  156 us (33%)
  starting transfers between devices  40.4 us (9%)
  other arithmetic  24 us (5%)
  matrix products  23.7 us (5%)
  between operations  15 us (3%)
    unnamed x54, local copies, waits for them, and re-layouts  131 us
    all_to_all x1, waiting for transfers between devices, body(): lax.all_to_all(dispatch, 'seq', split_axis=0, concat_axis=0, tiled=True)  95.5 us
    reduce_scatter x1, waiting for transfers between devices, body(): lax.psum_scatter(attn_part, 'exp', scatter_dimension=1, tiled=True)  30 us
    all_to_all x1, waiting for transfers between devices, body(): lax.all_to_all(outgoing, 'seq', split_axis=0, concat_axis=0, tiled=True)  18.3 us
    gather x1, local copies, waits for them, and re-layouts, body(): send_out = round_outs[round_cube, back_index]  12.2 us
    all_to_all x1, starting transfers between devices, body(): lax.all_to_all(dispatch, 'seq', split_axis=0, concat_axis=0, tiled=True)  11.2 us
    gather x1, local copies, waits for them, and re-layouts, body(): padded[slot_table].reshape(seq_count, EXP_DEV, capacity, tokens_b.shape[1])  10.7 us
    all_to_all x1, waiting for transfers between devices, body(): lax.all_to_all(send_out, 'seq', split_axis=0, concat_axis=0, tiled=True)  10.7 us
  transfers between devices with their start and end apart: 8, of which 5 were waited for; matrix products, arithmetic and copies ran while one was open for 47% of the time, Pallas kernels for 0%

commit v1 on v0

v1 whole, which is shorter than its diff:
```python
import functools
import math

import jax
import jax.numpy as jnp
from jax import lax
from jax.experimental import pallas as pl
from jax.experimental.pallas import tpu as pltpu
from jax.sharding import PartitionSpec as P

HEAD_DIM = 128
BLOCK_LEN = 64
EXP_DEV = 2
LANES = 128
F32, BF16, I32 = jnp.float32, jnp.bfloat16, jnp.int32
BIG = pltpu.CompilerParams(vmem_limit_bytes=48 * 1024 * 1024)


def dot(a, b):
    return jnp.dot(a, b, preferred_element_type=F32)


def dot_t(a, b):
    return lax.dot_general(a, b, (((1,), (1,)), ((), ())), preferred_element_type=F32)


def to_col(row):
    return jnp.broadcast_to(row, (LANES, row.shape[1])).T[:, :1]


def to_row(col):
    return jnp.broadcast_to(col, (col.shape[0], LANES)).T[:1, :]


def iota(shape, dim):
    return lax.broadcasted_iota(I32, shape, dim)


def flag(mask, kind=BF16):
    return jnp.where(mask, 1.0, 0.0).astype(kind)


def upper(count):
    return flag(iota((count, count), 0) <= iota((count, count), 1))


def pack_rows_kernel(me_ref, perms_ref, x_ref, qk_ref, val_ref, out_ref, token_ref, scratch):
    length, span = x_ref.shape[0], qk_ref.shape[1]
    rounds, total = perms_ref.shape
    peers = total // length
    per_peer = length // peers
    for peer in range(peers):
        scratch[peer * rounds : (peer + 1) * rounds, :] = perms_ref[
            :, peer * length : (peer + 1) * length
        ]
    perms = scratch[...]
    token = perms & (length - 1)
    mine = (perms >> (length.bit_length() - 1)) == me_ref[0]
    rank = dot(flag(mine), upper(length)).astype(I32) - 1
    slot = jnp.where(mine, rank, -1)
    groups = peers * rounds
    chosen = slot[:, None, :] == iota((groups, per_peer, length), 1)
    token_3d = jnp.where(chosen, token.astype(F32)[:, None, :], 0.0)
    column = jnp.sum(token_3d, axis=-1, keepdims=True).reshape(groups * per_peer, 1)
    token_ref[...] = jnp.broadcast_to(to_row(column), token_ref.shape).astype(I32)
    pick = flag(column.astype(I32) == iota((groups * per_peer, length), 1))
    for part, weight in enumerate((qk_ref, val_ref)):
        rows = dot(x_ref[...], weight[...]).astype(BF16)
        out_ref[:, part * span : (part + 1) * span] = dot(pick, rows).astype(BF16)


def pack_rows(me, perms, x_att, w_qk, w_val):
    length, width = x_att.shape
    rounds, total = perms.shape
    span = w_qk.shape[1]
    groups = rounds * (total // length)
    slots = rounds * length

    def whole(shape):
        return pl.BlockSpec(shape, lambda i, me_ref: (0, 0))

    return pl.pallas_call(
        pack_rows_kernel,
        grid_spec=pltpu.PrefetchScalarGridSpec(
            num_scalar_prefetch=1,
            grid=(1,),
            in_specs=[
                whole((rounds, total)),
                whole((length, width)),
                whole((width, span)),
                whole((width, span)),
            ],
            out_specs=[whole((slots, 2 * span)), whole((8, slots))],
            scratch_shapes=[pltpu.VMEM((groups, length), I32)],
        ),
        out_shape=[
            jax.ShapeDtypeStruct((slots, 2 * span), BF16),
            jax.ShapeDtypeStruct((8, slots), I32),
        ],
        compiler_params=BIG,
        name="pack_rows",
    )(me, perms, x_att, w_qk, w_val)


def pack_tokens_kernel(my_exp_ref, ids_ref, tokens_ref, out_ref, slot_ref):
    length = tokens_ref.shape[0]
    slots = out_ref.shape[0]
    experts = slot_ref.shape[0]
    capacity = slots // experts
    hot = ids_ref[...] == iota((experts, length), 0)
    counts = dot(flag(hot), upper(length))
    rank = jnp.sum(jnp.where(hot, counts, 0.0), axis=0, keepdims=True) - 1.0
    slot = ids_ref[...] * capacity + rank.astype(I32)
    slot_ref[...] = jnp.broadcast_to(slot, slot_ref.shape)
    pick = flag(iota((slots, length), 0) == slot)
    out_ref[...] = dot(pick, tokens_ref[...]).astype(BF16)


def pack_tokens(my_exp, ids, tokens, experts, capacity, part):
    length = tokens.shape[0]
    slots = experts * capacity
    return pl.pallas_call(
        pack_tokens_kernel,
        grid_spec=pltpu.PrefetchScalarGridSpec(
            num_scalar_prefetch=1,
            grid=(1,),
            in_specs=[
                pl.BlockSpec((1, length), lambda i, e: (0, 0)),
                pl.BlockSpec((length, part), lambda i, e: (0, e[0])),
            ],
            out_specs=[
                pl.BlockSpec((slots, part), lambda i, e: (0, 0)),
                pl.BlockSpec((experts, length), lambda i, e: (0, 0)),
            ],
        ),
        out_shape=[
            jax.ShapeDtypeStruct((slots, part), BF16),
            jax.ShapeDtypeStruct((experts, length), I32),
        ],
        compiler_params=BIG,
        name="pack_tokens",
    )(my_exp, ids, tokens)


def experts_kernel(x_ref, gate_ref, up_ref, down_ref, out_ref):
    parts, peers, _, capacity, part = x_ref.shape
    rows = peers * capacity
    gate = jnp.zeros((rows, gate_ref.shape[2]), F32)
    up_val = jnp.zeros((rows, gate_ref.shape[2]), F32)
    for index in range(parts):
        x = x_ref[index, :, 0].reshape(rows, part)
        gate = gate + dot(x, gate_ref[0, index * part : (index + 1) * part, :])
        up_val = up_val + dot(x, up_ref[0, index * part : (index + 1) * part, :])
    hidden = (gate / (1.0 + jnp.exp(-gate)) * up_val).astype(BF16)
    for index in range(parts):
        piece = dot(hidden, down_ref[0, :, index * part : (index + 1) * part])
        out_ref[index, :, 0] = piece.reshape(peers, capacity, part).astype(out_ref.dtype)


def run_experts(x, w_gate, w_up, w_down, kind):
    parts, peers, own, capacity, part = x.shape
    width, hidden = w_gate.shape[1:]
    return pl.pallas_call(
        experts_kernel,
        grid=(own,),
        in_specs=[
            pl.BlockSpec((parts, peers, 1, capacity, part), lambda e: (0, 0, e, 0, 0)),
            pl.BlockSpec((1, width, hidden), lambda e: (e, 0, 0)),
            pl.BlockSpec((1, width, hidden), lambda e: (e, 0, 0)),
            pl.BlockSpec((1, hidden, width), lambda e: (e, 0, 0)),
        ],
        out_specs=pl.BlockSpec((parts, peers, 1, capacity, part), lambda e: (0, 0, e, 0, 0)),
        out_shape=jax.ShapeDtypeStruct((parts, peers, own, capacity, part), kind),
        compiler_params=BIG,
        name="experts",
    )(x, w_gate, w_up, w_down)


def unpack_tokens_kernel(back_ref, slot_ref, out_ref):
    length = out_ref.shape[0]
    column = to_col(slot_ref[:1, :].astype(F32)).astype(I32)
    pick = flag(column == iota((length, back_ref.shape[0]), 1))
    out_ref[...] = dot(pick, back_ref[...]).astype(BF16)


def unpack_tokens(back, slot):
    return pl.pallas_call(
        unpack_tokens_kernel,
        out_shape=jax.ShapeDtypeStruct((slot.shape[1], back.shape[1]), BF16),
        compiler_params=BIG,
        name="unpack_tokens",
    )(back, slot)


def sort_rows_kernel(peers, me_ref, perms_ref, arrived_ref, rows_ref, last_ref, slot_ref):
    rounds, length = perms_ref.shape
    per_peer = length // peers
    for turn in range(rounds):
        source = perms_ref[turn : turn + 1, :] >> (length.bit_length() - 1)
        hot = source == iota((peers, length), 0)
        counts = dot(flag(hot), upper(length))
        rank = jnp.sum(jnp.where(hot, counts, 0.0), axis=0, keepdims=True) - 1.0
        slot = source * per_peer + rank.astype(I32)
        slot_ref[turn] = jnp.broadcast_to(slot, slot_ref.shape[1:])
        pick = flag(to_col(slot.astype(F32)).astype(I32) == iota((length, length), 1))
        have = arrived_ref[:, turn * per_peer : (turn + 1) * per_peer, :]
        rows = dot(pick, have.reshape(length, have.shape[2])).astype(BF16)
        rows_ref[turn] = rows
        last_ref[turn] = rows[length - BLOCK_LEN :]


def sort_rows(me, perms, arrived, length):
    rounds = perms.shape[0]
    peers, _, width = arrived.shape
    return pl.pallas_call(
        functools.partial(sort_rows_kernel, peers),
        grid_spec=pltpu.PrefetchScalarGridSpec(
            num_scalar_prefetch=1,
            grid=(1,),
            in_specs=[
                pl.BlockSpec((rounds, length), lambda i, s: (0, s[0])),
                pl.BlockSpec(arrived.shape, lambda i, s: (0, 0, 0)),
            ],
            out_specs=[
                pl.BlockSpec((rounds, length, width), lambda i, s: (0, 0, 0)),
                pl.BlockSpec((rounds, BLOCK_LEN, width), lambda i, s: (0, 0, 0)),
                pl.BlockSpec((rounds, 8, length), lambda i, s: (0, 0, 0)),
            ],
        ),
        out_shape=[
            jax.ShapeDtypeStruct((rounds, length, width), BF16),
            jax.ShapeDtypeStruct((rounds, BLOCK_LEN, width), BF16),
            jax.ShapeDtypeStruct((rounds, 8, length), I32),
        ],
        compiler_params=BIG,
        name="sort_rows",
    )(me, perms, arrived)


def attend_kernel(
    peers, me_ref, perms_ref, earlier_ref, rows_ref, last_ref, slot_ref, out_ref, lse_ref
):
    rounds, length = perms_ref.shape
    per_peer = length // peers
    span = rows_ref.shape[2] // 2
    tile, window = 2 * BLOCK_LEN, 4 * BLOCK_LEN
    block_q = iota((tile, window), 0) // BLOCK_LEN
    block_k = iota((tile, window), 1) // BLOCK_LEN
    met = (block_k == block_q + 1) | (block_k == block_q + 2)
    for turn in range(rounds):
        position = perms_ref[turn : turn + 1, :].astype(F32)
        position_col = to_col(position)
        positions = jnp.concatenate([earlier_ref[turn : turn + 1, :].astype(F32), position], axis=1)
        back = flag(iota((length, length), 0) == slot_ref[turn, :1, :])
        totals = []
        for head in range(span // HEAD_DIM):
            at = head * HEAD_DIM
            empty = jnp.zeros((BLOCK_LEN, HEAD_DIM), BF16)
            own = rows_ref[turn, :, at : at + HEAD_DIM]
            keys = jnp.concatenate([empty, last_ref[turn, :, at : at + HEAD_DIM], own], axis=0)
            at = span + at
            values = jnp.concatenate(
                [
                    empty,
                    last_ref[turn, :, at : at + HEAD_DIM],
                    rows_ref[turn, :, at : at + HEAD_DIM],
                ],
                axis=0,
            )
            wide = keys.astype(F32)
            squares = jnp.sum(wide * wide, axis=-1, keepdims=True)
            scale = to_row(lax.rsqrt(squares + 1e-06) / math.sqrt(HEAD_DIM))
            outs, lses = [], []
            for first in range(0, length, tile):
                query = own[first : first + tile]
                scores = dot_t(query, keys[first : first + window])
                scores = scores * scale[:, first : first + window]
                pos_q = position_col[first : first + tile]
                pos_k = positions[:, first : first + window]
                scores = jnp.where(pos_k == pos_q, scores - 10000.0, scores)
                scores = jnp.where(met & (pos_k <= pos_q), scores, -1e30)
                peak = jnp.max(scores, axis=-1, keepdims=True)
                exponent = jnp.exp(scores - peak)
                total = jnp.sum(exponent, axis=-1, keepdims=True)
                weights = (exponent / total).astype(BF16)
                outs.append(dot(weights, values[first : first + window]).astype(BF16))
                lses.append(peak + jnp.log(total))
            out = dot(back, jnp.concatenate(outs, axis=0)).astype(BF16)
            at = head * HEAD_DIM
            out_ref[:, turn * per_peer : (turn + 1) * per_peer, at : at + HEAD_DIM] = out.reshape(
                peers, per_peer, HEAD_DIM
            )
            totals.append(jnp.concatenate(lses, axis=0))
        lane = iota((length, LANES), 1)
        logs = jnp.zeros((length, LANES), F32)
        for head, total in enumerate(totals):
            logs = jnp.where(lane == head, total, logs)
        moved = jnp.zeros((length, LANES), F32)
        for _ in range(3):
            piece = logs.astype(BF16)
            moved = moved + dot(back, piece)
            logs = logs - piece.astype(F32)
        lse_ref[:, turn * per_peer : (turn + 1) * per_peer, :] = moved[:, : len(totals)].reshape(
            peers, per_peer, len(totals)
        )


def attend(me, perms, rows, last, slot, peers):
    rounds, length, width = rows.shape
    span = width // 2
    per_peer = length // peers
    lane_blocks = length // LANES
    fixed = lambda shape: pl.BlockSpec(shape, lambda i, s: (0, 0, 0))
    out = (peers, rounds * per_peer, span)
    lse = (peers, rounds * per_peer, span // HEAD_DIM)
    return pl.pallas_call(
        functools.partial(attend_kernel, peers),
        grid_spec=pltpu.PrefetchScalarGridSpec(
            num_scalar_prefetch=1,
            grid=(1,),
            in_specs=[
                pl.BlockSpec((rounds, length), lambda i, s: (0, s[0])),
                pl.BlockSpec(
                    (rounds, LANES),
                    lambda i, s: (
                        0,
                        jnp.where(s[0] == 0, peers * lane_blocks - 1, s[0] * lane_blocks - 1),
                    ),
                ),
                fixed(rows.shape),
                fixed(last.shape),
                fixed(slot.shape),
            ],
            out_specs=[fixed(out), fixed(lse)],
        ),
        out_shape=[jax.ShapeDtypeStruct(out, BF16), jax.ShapeDtypeStruct(lse, F32)],
        compiler_params=BIG,
        name="attend",
    )(me, perms, perms, rows, last, slot)


def combine_kernel(out_ref, lse_ref, token_ref, mixed_ref):
    peers, both, span = out_ref.shape
    length = mixed_ref.shape[0]
    rounds = both * peers // length
    per_peer = both // rounds
    heads = span // HEAD_DIM
    column = iota((length, peers * both), 0)
    pick_all = flag(token_ref[:1, :] == column)
    slot_round = (iota((1, peers * both), 1) // per_peer) % rounds
    outs, lses = [], []
    for turn in range(rounds):
        pick = jnp.where(slot_round == turn, pick_all, jnp.zeros_like(pick_all))
        outs.append(dot(pick, out_ref[...].reshape(peers * both, span)))
        logs = lse_ref[...].reshape(peers * both, heads)
        moved = jnp.zeros((length, heads), F32)
        for _ in range(3):
            piece = logs.astype(BF16)
            moved = moved + dot(pick, piece)
            logs = logs - piece.astype(F32)
        lses.append(moved)
    peak = functools.reduce(jnp.maximum, lses)
    whole = peak + jnp.log(functools.reduce(jnp.add, [jnp.exp(lse - peak) for lse in lses]))
    shares = [jnp.exp(lse - whole) for lse in lses]
    for head in range(heads):
        at = head * HEAD_DIM
        mixed = jnp.zeros((length, HEAD_DIM), F32)
        for out, share in zip(outs, shares):
            mixed = mixed + out[:, at : at + HEAD_DIM] * share[:, head : head + 1]
        mixed_ref[:, at : at + HEAD_DIM] = mixed.astype(BF16)


def combine(out, lse, token, length):
    return pl.pallas_call(
        combine_kernel,
        out_shape=jax.ShapeDtypeStruct((length, out.shape[2]), BF16),
        compiler_params=BIG,
        name="combine",
    )(out, lse, token)


def exchange(x, axis):
    return lax.all_to_all(x, axis, split_axis=0, concat_axis=0, tiled=True)


def body(x_att, w_qk, w_val, w_out, perms, tokens_b, expert_ids, w_gate, w_up, w_down):
    peers, parts = lax.axis_size("seq"), lax.axis_size("exp")
    me = lax.axis_index("seq").astype(I32).reshape(1)
    my_exp = lax.axis_index("exp").astype(I32).reshape(1)
    length, width = x_att.shape
    rounds = perms.shape[0]
    per_peer = length // peers
    experts = EXP_DEV * peers
    tokb = tokens_b.shape[0]
    capacity = 2 * tokb // experts
    part = width // parts
    dispatch, token_slot = pack_tokens(
        my_exp, expert_ids.reshape(1, tokb), tokens_b, experts, capacity, part
    )
    outgoing, slot_token = pack_rows(me, perms, x_att, w_qk, w_val)
    received = exchange(dispatch.reshape(peers, EXP_DEV, capacity, part), "seq")
    arrived = exchange(outgoing.reshape(peers, rounds * per_peer, outgoing.shape[1]), "seq")
    gathered = lax.all_gather(received, "exp", axis=0, tiled=False)
    rows, last, row_slot = sort_rows(me, perms, arrived, length)
    last = lax.ppermute(last, "seq", [(i, (i + 1) % peers) for i in range(peers)])
    outs, lses = attend(me, perms, rows, last, row_slot, peers)
    got_out = exchange(outs, "seq")
    got_lse = exchange(lses, "seq")
    expert_part = run_experts(gathered, w_gate, w_up, w_down, BF16)
    expert_rows = lax.psum_scatter(expert_part, "exp", scatter_dimension=0, tiled=False)
    expert_back = exchange(expert_rows, "seq")
    mixed = unpack_tokens(expert_back.reshape(experts * capacity, part), token_slot)
    mixed_heads = combine(got_out, got_lse, slot_token, length)
    attn_part = dot(mixed_heads, w_out).astype(BF16)
    attended = lax.psum_scatter(attn_part, "exp", scatter_dimension=1, tiled=True)
    return (attended, mixed)


def solution(mesh):
    in_specs = (
        P("seq", None),
        P(None, "exp"),
        P(None, "exp"),
        P("exp", None),
        P(),
        P("seq", None),
        P("seq", None),
        P("seq", None, "exp"),
        P("seq", None, "exp"),
        P("seq", "exp", None),
    )
    out_specs = (P("seq", "exp"), P("seq", "exp"))
    return jax.shard_map(body, mesh=mesh, in_specs=in_specs, out_specs=out_specs, check_vma=False)
```

time: 471 us -> 218 us (0.46)
  local copies, waits for them, and re-layouts: 210 us -> 8.56 us
  blocking collectives: 0 us -> 103 us
  waiting for transfers between devices: 156 us -> 61.1 us
  starting transfers between devices: 40.4 us -> 5.19 us
  Pallas kernels: 0 us -> 24.1 us
  other arithmetic: 24 us -> 0 us
  matrix products: 23.7 us -> 2.07 us
    unnamed x54 -> x18, local copies, waits for them, and re-layouts: 131 us -> 8.03 us
    all_to_all x5 -> x1, waiting for transfers between devices: 124 us -> 15.3 us  [exchange(): return lax.all_to_all(x, axis, split_axis=0, concat_axis=0, tiled=True)]
    all_to_all x0 -> x4, blocking collectives: none -> 103 us  [exchange(): return lax.all_to_all(x, axis, split_axis=0, concat_axis=0, tiled=True)]
    gather x10 -> x0, local copies, waits for them, and re-layouts: 64.8 us -> none  [the longest x1 12.2 us: body(): send_out = round_outs[round_cube, back_index]]
    all_to_all x5 -> x1, starting transfers between devices: 40.3 us -> 4.81 us  [exchange(): return lax.all_to_all(x, axis, split_axis=0, concat_axis=0, tiled=True)]
    all_gather x0 -> x1, waiting for transfers between devices: none -> 31.1 us  [body(): gathered = lax.all_gather(received, 'exp', axis=0, tiled=False)]
    pallas_call x0 -> x7, Pallas kernels: none -> 24.1 us  [the longest x1 6.97 us: attend(): pl.pallas_call(functools.partial(attend_kernel, peers), grid_spec=pltpu.P...]
    dot_general x9 -> x1, matrix products: 23.7 us -> 2.07 us  [dot(): return jnp.dot(a, b, preferred_element_type=F32)]
  transfers between devices with their start and end apart: 8 -> 5, of which waited for: 5 -> 4; matrix products, arithmetic and copies ran while one was open for 47% -> 1% of each run, Pallas kernels for 0% -> 8%
where the time goes in v1:
time: 218 us
  blocking collectives  103 us (47%)
  waiting for transfers between devices  61.1 us (28%)
  Pallas kernels  24.1 us (11%)
  between operations  13.8 us (6%)
  local copies, waits for them, and re-layouts  8.56 us (4%)
  starting transfers between devices  5.19 us (2%)
    all_to_all x4, blocking collectives, exchange(): return lax.all_to_all(x, axis, split_axis=0, concat_axis=0, tiled=True)  103 us
    all_gather x1, waiting for transfers between devices, body(): gathered = lax.all_gather(received, 'exp', axis=0, tiled=False)  31.1 us
    all_to_all x1, waiting for transfers between devices, exchange(): return lax.all_to_all(x, axis, split_axis=0, concat_axis=0, tiled=True)  15.3 us
    reduce_scatter x1, waiting for transfers between devices, body(): lax.psum_scatter(attn_part, 'exp', scatter_dimension=1, tiled=True)  9.75 us
    unnamed x18, local copies, waits for them, and re-layouts  8.03 us
    pallas_call x1, Pallas kernels, attend(): pl.pallas_call(functools.partial(attend_kernel, peers), grid_spec=pltpu.P...  6.97 us
    pallas_call x1, Pallas kernels, run_experts(): pl.pallas_call(experts_kernel, grid=(own,), in_specs=[pl.BlockSpec((parts...  6.9 us
    ppermute x1, waiting for transfers between devices, body(): lax.ppermute(last, 'seq', [(i, (i + 1) % peers) for i in range(peers)])  4.95 us
  transfers between devices with their start and end apart: 5, of which 4 were waited for; matrix products, arithmetic and copies ran while one was open for 1% of the time, Pallas kernels for 8%

profile of v1, /device:TPU:32, one launch (start us, length us, event | category | flops | bytes accessed | tf_op | source)
XLA Modules:
  0.0 217.5 jit_solution(6392681572775771680)
XLA Ops:
  7.2 0.0 copy-start
  7.2 0.0 copy-start.1
  7.2 0.0 all-gather.3.cloned.1.call-start
  7.2 0.0 copy-start.3
  7.2 1.7 copy-done.3
  9.0 0.0 copy-start.8
  9.0 0.7 copy-done.8
  9.7 0.6 pack_tokens.1
  10.3 28.7 %all_to_all.25 = bf16[32,2,16,256]{3,2,1,0:T(8,128)(2,1)} all-to-all(bf16[32,2,16,256]{3,2,1,0:T(8,128)(2,1)S(1)} %bitcast.12), channel_id=1, replica_groups=mesh['seq'=32,'exp'=8] {'seq'}, dimensions={0} | all-to-all | bytes 1048576 | tf_op jit(solution)/shard_map/all_to_all | solution.py:383
  39.0 0.0 all-gather.3.cloned.1.call-update
  39.1 0.0 reduce-scatter.5.cloned.1.call-start
  39.1 31.1 %all-gather.3.cloned.1.call-done = bf16[256,2,16,256]{3,2,1,0:T(8,128)(2,1)} async-done(((bf16[32,2,16,256]{3,2,1,0:T(8,128)(2,1)}), bf16[256,2,16,256]{3,2,1,0:T(8,128)(2,1)}) %all-gather.3.cloned.1.call-update) | async-done | bytes 4194320 | tf_op jit(solution)/shard_map/all_gather | solution.py:403
  70.2 0.0 copy-done.1
  70.2 0.0 copy-start.2
  70.2 1.6 copy-done.2
  71.8 6.9 %experts.1 = bf16[8,32,2,16,256]{4,3,2,1,0:T(8,128)(2,1)} custom-call(bf16[8,32,2,16,256]{4,3,2,1,0:T(8,128)(2,1)} %bitcast.14, bf16[2,2048,256]{2,1,0:T(8,128)(2,1)S(1)} %copy-done.1, bf16[2,2048,256]{2,1,0:T(8,128)(2,1)S(1)} %copy-done.2, bf16[2,256,2048]{2,1,0:T(8,128)(2,1)} %down_ref.1), custom_call_target="tpu_custom_call" | custom-call | tf_op jit(solution)/shard_map/experts/pallas_call | solution.py:163
  78.7 0.0 copy-start.4
  78.7 0.0 copy-start.5
  78.7 0.0 reduce-scatter.5.cloned.1.call-update
  78.7 1.6 copy-done.4
  80.3 0.0 copy-done.5
  80.3 0.0 copy-start.6
  80.3 1.2 copy-done.6
  81.5 0.0 copy-start.7
  81.5 1.2 copy-done.7
  82.7 3.8 %pack_rows.1 = (bf16[1024,512]{1,0:T(8,128)(2,1)S(1)}, s32[8,1024]{1,0:T(8,128)S(1)}) custom-call(s32[1]{0:T(128)} %bitcast.me_ref, s32[2,16384]{1,0:T(2,128)S(1)} %copy-done.5, bf16[512,2048]{1,0:T(8,128)(2,1)S(1)} %copy-done.4, bf16[2048,256]{1,0:T(8,128)(2,1)S(1)} %copy-done.6, bf16[2048,256]{1,0:T(8,128)(2,1)S(1)} %copy-done.7), custom_call_target="tpu_custom_call" | custom-call | tf_op jit(solution)/shard_map/pack_rows/pallas_call | solution.py:82
  86.5 38.6 %all_to_all.26.arrived_ref = bf16[32,32,512]{2,1,0:T(8,128)(2,1)S(1)} all-to-all(bf16[32,32,512]{2,1,0:T(8,128)(2,1)S(1)} %bitcast.11), channel_id=1, replica_groups=mesh['seq'=32,'exp'=8] {'seq'}, dimensions={0} | all-to-all | bytes 2097152 | tf_op jit(solution)/shard_map/all_to_all | solution.py:383
  125.1 1.7 sort_rows.1
  126.8 0.3 collective-permute-start
  127.1 5.0 %collective-permute-done.last_ref = bf16[2,64,512]{2,1,0:T(8,128)(2,1)S(1)} collective-permute-done((bf16[2,64,512]{2,1,0:T(8,128)(2,1)S(1)}, bf16[2,64,512]{2,1,0:T(8,128)(2,1)S(1)}, u32[]{:S(2)}, u32[]{:S(2)}) %collective-permute-start) | collective-permute-done | bytes 131104 | tf_op jit(solution)/shard_map/ppermute | solution.py:405
  132.1 7.0 %attend.1 = (bf16[32,32,256]{2,1,0:T(8,128)(2,1)}, f32[32,32,2]{2,1,0:T(8,128)S(1)}) custom-call(s32[1]{0:T(128)} %bitcast.me_ref, s32[2,16384]{1,0:T(2,128)S(1)} %copy-done.5, s32[2,16384]{1,0:T(2,128)S(1)} %copy-done.5, bf16[2,512,512]{2,1,0:T(8,128)(2,1)S(1)} %get-tuple-element.12.rows_ref, bf16[2,64,512]{2,1,0:T(8,128)(2,1)S(1)} %collective-permute-done.last_ref, ...), custom_call_target="tpu_custom_call" | custom-call | tf_op jit(solution)/shard_map/attend/pallas_call | solution.py:316
  139.0 0.3 copy.12
  139.3 15.4 %all_to_all.27 = f32[32,32,2]{1,2,0:T(2,128)S(1)} all-to-all(f32[32,32,2]{1,2,0:T(2,128)S(1)} %copy.12), channel_id=1, replica_groups=mesh['seq'=32,'exp'=8] {'seq'}, dimensions={0} | all-to-all | bytes 16384 | tf_op jit(solution)/shard_map/all_to_all | solution.py:383
  154.7 4.8 %all-to-all-start.1 = ((bf16[32,32,256]{2,1,0:T(8,128)(2,1)}), bf16[32,32,256]{2,1,0:T(8,128)(2,1)S(1)}, u32[]{:S(2)}, u32[]{:S(2)}) async-start(bf16[32,32,256]{2,1,0:T(8,128)(2,1)} %get-tuple-element.15), calls=%async_computation.1 | async-start | bytes 1048576 | tf_op jit(solution)/shard_map/all_to_all | solution.py:383
  159.5 0.0 reduce-scatter.3.cloned.1.call-start
  159.6 0.3 copy.13.lse_ref
  159.8 15.3 %all-to-all-done.1.out_ref = bf16[32,32,256]{2,1,0:T(8,128)(2,1)S(1)} async-done(((bf16[32,32,256]{2,1,0:T(8,128)(2,1)}), bf16[32,32,256]{2,1,0:T(8,128)(2,1)S(1)}, u32[]{:S(2)}, u32[]{:S(2)}) %all-to-all-start.1) | async-done | bytes 524320 | tf_op jit(solution)/shard_map/all_to_all | solution.py:383
  175.1 2.6 %combine.1 = bf16[512,256]{1,0:T(8,128)(2,1)S(1)} custom-call(bf16[32,32,256]{2,1,0:T(8,128)(2,1)S(1)} %all-to-all-done.1.out_ref, f32[32,32,2]{2,1,0:T(8,128)S(1)} %copy.13.lse_ref, s32[8,1024]{1,0:T(8,128)S(1)} %get-tuple-element.17.token_ref), custom_call_target="tpu_custom_call" | custom-call | tf_op jit(solution)/shard_map/combine/pallas_call | solution.py:374
  177.7 0.0 copy-done
  177.7 2.1 convolution_convert_fusion
  179.8 0.0 reduce-scatter.3.cloned.1.call-update
  179.8 0.0 reduce-scatter.5.cloned.1.call-done
  179.8 20.0 %all_to_all.28 = bf16[32,2,16,256]{3,2,1,0:T(8,128)(2,1)S(1)} all-to-all(bf16[32,2,16,256]{3,2,1,0:T(8,128)(2,1)} %bitcast.15), channel_id=1, replica_groups=mesh['seq'=32,'exp'=8] {'seq'}, dimensions={0} | all-to-all | bytes 1048576 | tf_op jit(solution)/shard_map/all_to_all | solution.py:383
  199.8 1.4 unpack_tokens.1
  201.3 9.8 %reduce-scatter.3.cloned.1.call-done = bf16[512,256]{1,0:T(8,128)(2,1)} async-done(((bf16[512,2048]{1,0:T(8,128)(2,1)}), bf16[512,256]{1,0:T(8,128)(2,1)}) %reduce-scatter.3.cloned.1.call-update) | async-done | bytes 262160 | tf_op jit(solution)/shard_map/reduce_scatter | solution.py:415
Async XLA Ops:
  7.2 170.5 %copy-start = (bf16[256,2048]{1,0:T(8,128)(2,1)S(1)}, bf16[256,2048]{1,0:T(8,128)(2,1)}, u32[]{:S(2)}) copy-start(bf16[256,2048]{1,0:T(8,128)(2,1)} %param.13) | copy-start | bytes 3145732
  7.2 63.0 %copy-start.1 = (bf16[2,2048,256]{2,1,0:T(8,128)(2,1)S(1)}, bf16[2,2048,256]{2,1,0:T(8,128)(2,1)}, u32[]{:S(2)}) copy-start(bf16[2,2048,256]{2,1,0:T(8,128)(2,1)} %gate_ref.1) | copy-start | bytes 6291460
  7.2 63.0 %all-gather.3.cloned.1.call-start = ((), (), s32[]{:S(2)}) async-start(), calls=%async_computation.9 | async-start | bytes 4718592 | tf_op jit(solution)/shard_map/all_gather | solution.py:403
  7.2 1.7 copy-start.3
  9.0 0.7 copy-start.8
  39.1 140.8 %reduce-scatter.5.cloned.1.call-start = ((), (), s32[]{:S(2)}) async-start(), calls=%async_computation.8 | async-start | bytes 4718592 | tf_op jit(solution)/shard_map/reduce_scatter | solution.py:410
  70.2 1.6 copy-start.2
  78.7 1.6 copy-start.4
  78.7 1.6 copy-start.5
  80.3 1.2 copy-start.6
  81.5 1.2 copy-start.7
  126.8 5.2 %collective-permute-start = (bf16[2,64,512]{2,1,0:T(8,128)(2,1)S(1)}, bf16[2,64,512]{2,1,0:T(8,128)(2,1)S(1)}, u32[]{:S(2)}, u32[]{:S(2)}) collective-permute-start(bf16[2,64,512]{2,1,0:T(8,128)(2,1)S(1)} %get-tuple-element.13), channel_id=1, source_target_pairs={{0,8},{8,16},{16,24},{24,32},{32,40},{40,48},{48,56},{56,64},{64,7... | collective-permute-start | bytes 393224 | tf_op jit(solution)/shard_map/ppermute | solution.py:405
  154.7 20.4 %all-to-all-start.1 = ((bf16[32,32,256]{2,1,0:T(8,128)(2,1)}), bf16[32,32,256]{2,1,0:T(8,128)(2,1)S(1)}, u32[]{:S(2)}, u32[]{:S(2)}) async-start(bf16[32,32,256]{2,1,0:T(8,128)(2,1)} %get-tuple-element.15), calls=%async_computation.1 | async-start | bytes 1048576 | tf_op jit(solution)/shard_map/all_to_all | solution.py:383
  159.5 51.5 %reduce-scatter.3.cloned.1.call-start = ((), (), s32[]{:S(2)}) async-start(), calls=%async_computation.7 | async-start | bytes 2359296 | tf_op jit(solution)/shard_map/reduce_scatter | solution.py:415
Sparse Core Ops, SparseCore 0:
  39.2 30.9 all-gather.2
  78.8 40.7 reduce-scatter.4
  179.9 31.0 reduce-scatter.2

commit v2 on v1

v2 whole, which is shorter than its diff:
```python
import functools
import math

import jax
import jax.numpy as jnp
from jax import lax
from jax.experimental import pallas as pl
from jax.experimental.pallas import tpu as pltpu
from jax.sharding import PartitionSpec as P

HEAD_DIM = 128
BLOCK_LEN = 64
EXP_DEV = 2
LANES = 128
F32, BF16, I32 = jnp.float32, jnp.bfloat16, jnp.int32
BIG = pltpu.CompilerParams(vmem_limit_bytes=48 * 1024 * 1024)


def dot(a, b):
    return jnp.dot(a, b, preferred_element_type=F32)


def dot_t(a, b):
    return lax.dot_general(a, b, (((1,), (1,)), ((), ())), preferred_element_type=F32)


def to_col(row):
    return jnp.broadcast_to(row, (LANES, row.shape[1])).T[:, :1]


def to_row(col):
    return jnp.broadcast_to(col, (col.shape[0], LANES)).T[:1, :]


def iota(shape, dim):
    return lax.broadcasted_iota(I32, shape, dim)


def flag(mask, kind=BF16):
    return jnp.where(mask, 1.0, 0.0).astype(kind)


def cost(flops, size):
    return pl.CostEstimate(flops=flops, bytes_accessed=size, transcendentals=0)


def upper(count):
    return flag(iota((count, count), 0) <= iota((count, count), 1))


def pack_rows_kernel(me_ref, perms_ref, x_ref, qk_ref, val_ref, out_ref, token_ref, scratch):
    length, span = x_ref.shape[0], qk_ref.shape[1]
    rounds, total = perms_ref.shape
    peers = total // length
    per_peer = length // peers
    for peer in range(peers):
        scratch[peer * rounds : (peer + 1) * rounds, :] = perms_ref[
            :, peer * length : (peer + 1) * length
        ]
    perms = scratch[...]
    token = perms & (length - 1)
    mine = (perms >> (length.bit_length() - 1)) == me_ref[0]
    rank = dot(flag(mine), upper(length)).astype(I32) - 1
    slot = jnp.where(mine, rank, -1)
    groups = peers * rounds
    chosen = slot[:, None, :] == iota((groups, per_peer, length), 1)
    token_3d = jnp.where(chosen, token.astype(F32)[:, None, :], 0.0)
    column = jnp.sum(token_3d, axis=-1, keepdims=True).reshape(groups * per_peer, 1)
    by_round = column.reshape(peers, rounds, per_peer, 1)
    for turn in range(rounds):
        row = to_row(by_round[:, turn].reshape(peers * per_peer, 1)).astype(I32)
        token_ref[turn] = jnp.broadcast_to(row, token_ref.shape[1:])
    pick = flag(column.astype(I32) == iota((groups * per_peer, length), 1))
    for part, weight in enumerate((qk_ref, val_ref)):
        rows = dot(x_ref[...], weight[...]).astype(BF16)
        out_ref[:, part * span : (part + 1) * span] = dot(pick, rows).astype(BF16)


def pack_rows(me, perms, x_att, w_qk, w_val):
    length, width = x_att.shape
    rounds, total = perms.shape
    span = w_qk.shape[1]
    groups = rounds * (total // length)
    slots = rounds * length

    def whole(shape):
        return pl.BlockSpec(shape, lambda i, me_ref: (0, 0))

    return pl.pallas_call(
        pack_rows_kernel,
        grid_spec=pltpu.PrefetchScalarGridSpec(
            num_scalar_prefetch=1,
            grid=(1,),
            in_specs=[
                whole((rounds, total)),
                whole((length, width)),
                whole((width, span)),
                whole((width, span)),
            ],
            out_specs=[
                whole((slots, 2 * span)),
                pl.BlockSpec((rounds, 8, length), lambda i, me_ref: (0, 0, 0)),
            ],
            scratch_shapes=[pltpu.VMEM((groups, length), I32)],
        ),
        out_shape=[
            jax.ShapeDtypeStruct((slots, 2 * span), BF16),
            jax.ShapeDtypeStruct((rounds, 8, length), I32),
        ],
        cost_estimate=cost(4 * length * width * span + 4 * slots * length * span, 6 << 20),
        compiler_params=BIG,
        name="pack_rows",
    )(me, perms, x_att, w_qk, w_val)


def pack_tokens_kernel(peers, where_ref, ids_ref, tokens_ref, out_ref, slot_ref):
    length = tokens_ref.shape[0]
    slots = out_ref.shape[0]
    capacity = slots // peers
    experts = EXP_DEV * peers
    ids = ids_ref[...]
    hot = ids == iota((experts, length), 0)
    counts = dot(flag(hot), upper(length))
    rank = jnp.sum(jnp.where(hot, counts, 0.0), axis=0, keepdims=True).astype(I32) - 1
    core = where_ref[1]
    turn = (ids % EXP_DEV + core) % EXP_DEV
    peer = ids // EXP_DEV
    slot_ref[...] = jnp.broadcast_to(
        (peer * EXP_DEV + turn) * capacity + rank, slot_ref.shape
    )
    slot = jnp.where(turn == 0, peer * capacity + rank, -1)
    pick = flag(iota((slots, length), 0) == slot)
    out_ref[...] = dot(pick, tokens_ref[...]).astype(BF16)


def pack_tokens(where, ids, tokens, peers, capacity, part):
    length = tokens.shape[0]
    slots = peers * capacity
    return pl.pallas_call(
        functools.partial(pack_tokens_kernel, peers),
        grid_spec=pltpu.PrefetchScalarGridSpec(
            num_scalar_prefetch=1,
            grid=(1,),
            in_specs=[
                pl.BlockSpec((1, length), lambda i, e: (0, 0)),
                pl.BlockSpec((length, part), lambda i, e: (0, e[0])),
            ],
            out_specs=[
                pl.BlockSpec((slots, part), lambda i, e: (0, 0)),
                pl.BlockSpec((8, length), lambda i, e: (0, 0)),
            ],
        ),
        out_shape=[
            jax.ShapeDtypeStruct((slots, part), BF16),
            jax.ShapeDtypeStruct((8, length), I32),
        ],
        cost_estimate=cost(2 * slots * length * part, 2 << 20),
        compiler_params=BIG,
        name="pack_tokens",
    )(where, ids, tokens)


def experts_kernel(where_ref, x_ref, *refs):
    weights, out_ref = refs[:-1], refs[-1]
    parts, peers, capacity, part = x_ref.shape
    rows = peers * capacity
    hiddens = []
    for gate_ref, up_ref in (weights[0:2], weights[3:5]):
        gate = jnp.zeros((rows, gate_ref.shape[2]), F32)
        up_val = jnp.zeros((rows, gate_ref.shape[2]), F32)
        for index in range(parts):
            x = x_ref[index].reshape(rows, part)
            gate = gate + dot(x, gate_ref[0, index * part : (index + 1) * part, :])
            up_val = up_val + dot(x, up_ref[0, index * part : (index + 1) * part, :])
        hiddens.append((gate / (1.0 + jnp.exp(-gate)) * up_val).astype(BF16))
    half = part // EXP_DEV
    for index in range(parts):
        at = index * part
        piece = dot(hiddens[0], weights[2][0, :, at : at + part])
        piece = (piece + dot(hiddens[1], weights[5][0, :, at : at + part])).astype(BF16)
        for side in range(EXP_DEV):
            columns = piece[:, side * half : (side + 1) * half]
            out_ref[index, side] = columns.reshape(peers, capacity, half)


def run_experts(where, x, own, sibling):
    parts, peers, capacity, part = x.shape
    width, hidden = own[0].shape[1:]
    out = (parts, EXP_DEV, peers, capacity, part // EXP_DEV)
    rows = peers * capacity

    def mine(i, e):
        return (e[1], 0, 0)

    def first(i, e):
        return (0, 0, 0)

    up_block, down_block = (1, width, hidden), (1, hidden, width)
    blocks = (up_block, up_block, down_block)
    return pl.pallas_call(
        experts_kernel,
        grid_spec=pltpu.PrefetchScalarGridSpec(
            num_scalar_prefetch=1,
            grid=(1,),
            in_specs=[pl.BlockSpec(x.shape, lambda i, e: (0, 0, 0, 0))]
            + [pl.BlockSpec(block, mine) for block in blocks]
            + [pl.BlockSpec(block, first) for block in blocks],
            out_specs=pl.BlockSpec(out, lambda i, e: (0, 0, 0, 0, 0)),
        ),
        out_shape=jax.ShapeDtypeStruct(out, BF16),
        cost_estimate=cost(12 * rows * width * hidden, 10 << 20),
        compiler_params=BIG,
        name="experts",
    )(where, x, *own, *sibling)


def unpack_tokens_kernel(back_ref, slot_ref, out_ref):
    length = out_ref.shape[0]
    column = to_col(slot_ref[:1, :].astype(F32)).astype(I32)
    pick = flag(column == iota((length, back_ref.shape[0]), 1))
    out_ref[...] = dot(pick, back_ref[...]).astype(BF16)


def unpack_tokens(back, slot):
    length, width = slot.shape[1], back.shape[1]
    return pl.pallas_call(
        unpack_tokens_kernel,
        out_shape=jax.ShapeDtypeStruct((length, width), BF16),
        cost_estimate=cost(2 * length * back.shape[0] * width, 1 << 20),
        compiler_params=BIG,
        name="unpack_tokens",
    )(back, slot)


def sort_rows_kernel(peers, me_ref, perms_ref, arrived_ref, rows_ref, last_ref, slot_ref):
    rounds, length = perms_ref.shape
    per_peer = length // peers
    for turn in range(rounds):
        source = perms_ref[turn : turn + 1, :] >> (length.bit_length() - 1)
        hot = source == iota((peers, length), 0)
        counts = dot(flag(hot), upper(length))
        rank = jnp.sum(jnp.where(hot, counts, 0.0), axis=0, keepdims=True) - 1.0
        slot = source * per_peer + rank.astype(I32)
        slot_ref[turn] = jnp.broadcast_to(slot, slot_ref.shape[1:])
        pick = flag(to_col(slot.astype(F32)).astype(I32) == iota((length, length), 1))
        have = arrived_ref[:, turn * per_peer : (turn + 1) * per_peer, :]
        rows = dot(pick, have.reshape(length, have.shape[2])).astype(BF16)
        rows_ref[turn] = rows
        last_ref[turn] = rows[length - BLOCK_LEN :]


def sort_rows(me, perms, arrived, length):
    rounds = perms.shape[0]
    peers, _, width = arrived.shape
    return pl.pallas_call(
        functools.partial(sort_rows_kernel, peers),
        grid_spec=pltpu.PrefetchScalarGridSpec(
            num_scalar_prefetch=1,
            grid=(1,),
            in_specs=[
                pl.BlockSpec((rounds, length), lambda i, s: (0, s[0])),
                pl.BlockSpec(arrived.shape, lambda i, s: (0, 0, 0)),
            ],
            out_specs=[
                pl.BlockSpec((rounds, length, width), lambda i, s: (0, 0, 0)),
                pl.BlockSpec((rounds, BLOCK_LEN, width), lambda i, s: (0, 0, 0)),
                pl.BlockSpec((rounds, 8, length), lambda i, s: (0, 0, 0)),
            ],
        ),
        out_shape=[
            jax.ShapeDtypeStruct((rounds, length, width), BF16),
            jax.ShapeDtypeStruct((rounds, BLOCK_LEN, width), BF16),
            jax.ShapeDtypeStruct((rounds, 8, length), I32),
        ],
        cost_estimate=cost(2 * rounds * length * length * width, 4 << 20),
        compiler_params=BIG,
        name="sort_rows",
    )(me, perms, arrived)


def window_scale(keys):
    wide = keys.astype(F32)
    squares = jnp.sum(wide * wide, axis=-1, keepdims=True)
    return to_row(lax.rsqrt(squares + 1e-06) / math.sqrt(HEAD_DIM))


def attend_tile(query, keys, values, scale, pos_q, pos_k):
    tile, window = query.shape[0], keys.shape[0]
    block_q = iota((tile, window), 0) // BLOCK_LEN
    block_k = iota((tile, window), 1) // BLOCK_LEN
    met = (block_k == block_q + 1) | (block_k == block_q + 2)
    scores = dot_t(query, keys) * scale
    scores = jnp.where(pos_k == pos_q, scores - 10000.0, scores)
    scores = jnp.where(met & (pos_k <= pos_q), scores, -1e30)
    peak = jnp.max(scores, axis=-1, keepdims=True)
    exponent = jnp.exp(scores - peak)
    total = jnp.sum(exponent, axis=-1, keepdims=True)
    weights = (exponent / total).astype(BF16)
    return dot(weights, values).astype(BF16), peak + jnp.log(total)


TILE, WINDOW, PIECES, GROUP = 2 * BLOCK_LEN, 4 * BLOCK_LEN, 3, 8


def put_logs(totals):
    lane = iota((totals[0].shape[0], LANES), 1) % GROUP
    logs = jnp.zeros(lane.shape, F32)
    for head, total in enumerate(totals):
        rest = total
        for piece in range(PIECES):
            part = rest.astype(BF16).astype(F32)
            logs = jnp.where(lane == head * PIECES + piece, part, logs)
            rest = rest - part
    return logs.astype(BF16)


def attend_later_kernel(me_ref, perms_ref, rows_ref, out_ref):
    rounds, length = perms_ref.shape
    span = rows_ref.shape[2] // 2
    for turn in range(rounds):
        position = perms_ref[turn : turn + 1, :].astype(F32)
        position_col = to_col(position)
        scales = []
        for head in range(span // HEAD_DIM):
            at = head * HEAD_DIM
            scales.append(window_scale(rows_ref[turn, :, at : at + HEAD_DIM]))
        for first in range(TILE, length, TILE):
            totals = []
            window = slice(first + TILE - WINDOW, first + TILE)
            queries = slice(first, first + TILE)
            for head in range(span // HEAD_DIM):
                at = head * HEAD_DIM
                out, total = attend_tile(
                    rows_ref[turn, queries, at : at + HEAD_DIM],
                    rows_ref[turn, window, at : at + HEAD_DIM],
                    rows_ref[turn, window, span + at : span + at + HEAD_DIM],
                    scales[head][:, window],
                    position_col[queries],
                    position[:, window],
                )
                out_ref[turn, first - TILE : first, at : at + HEAD_DIM] = out
                totals.append(total)
            out_ref[turn, first - TILE : first, span:] = put_logs(totals)


def attend_first_kernel(
    peers,
    me_ref,
    perms_ref,
    earlier_ref,
    rows_ref,
    last_ref,
    slot_ref,
    later_ref,
    out_ref,
):
    rounds, length = slot_ref.shape[0], slot_ref.shape[2]
    per_peer = length // peers
    span = rows_ref.shape[2] // 2
    lane_group = iota((peers, per_peer, LANES), 2) // GROUP
    own_group = lane_group == iota((peers, per_peer, LANES), 1)
    empty = jnp.zeros((BLOCK_LEN, HEAD_DIM), BF16)
    for turn in range(rounds):
        position = perms_ref[turn : turn + 1, :].astype(F32)
        positions = jnp.concatenate([earlier_ref[turn : turn + 1, :].astype(F32), position], axis=1)
        position_col = to_col(position)
        totals, outs = [], []
        for head in range(span // HEAD_DIM):
            at = head * HEAD_DIM
            own = rows_ref[turn, :, at : at + HEAD_DIM]
            keys = jnp.concatenate([empty, last_ref[turn, :, at : at + HEAD_DIM], own], axis=0)
            at = span + at
            values = jnp.concatenate(
                [
                    empty,
                    last_ref[turn, :, at : at + HEAD_DIM],
                    rows_ref[turn, :, at : at + HEAD_DIM],
                ],
                axis=0,
            )
            out, total = attend_tile(
                own, keys, values, window_scale(keys), position_col, positions
            )
            outs.append(out)
            totals.append(total)
        top = jnp.concatenate(outs + [put_logs(totals)], axis=1)
        whole = jnp.concatenate([top, later_ref[turn]], axis=0) if length > TILE else top
        back = flag(iota((length, length), 0) == slot_ref[turn, :1, :])
        moved = dot(back, whole)
        at = turn * per_peer
        out_ref[:, at : at + per_peer, :] = (
            moved[:, :span].astype(BF16).reshape(peers, per_peer, span)
        )
        logs = moved[:, span:].reshape(peers, per_peer, LANES)
        logs = jnp.sum(jnp.where(own_group, logs, 0.0), axis=1, keepdims=True)
        at = rounds * per_peer
        out_ref[:, at : at + GROUP, turn * LANES : (turn + 1) * LANES] = jnp.broadcast_to(
            logs, (peers, GROUP, LANES)
        ).astype(BF16)


def attend_later(me, perms, rows):
    rounds, length, width = rows.shape
    span = width // 2
    out = (rounds, length - TILE, span + LANES)
    return pl.pallas_call(
        attend_later_kernel,
        grid_spec=pltpu.PrefetchScalarGridSpec(
            num_scalar_prefetch=1,
            grid=(1,),
            in_specs=[
                pl.BlockSpec((rounds, length), lambda i, s: (0, s[0])),
                pl.BlockSpec(rows.shape, lambda i, s: (0, 0, 0)),
            ],
            out_specs=pl.BlockSpec(out, lambda i, s: (0, 0, 0)),
        ),
        out_shape=jax.ShapeDtypeStruct(out, BF16),
        cost_estimate=cost(2 << 30, 4 << 20),
        compiler_params=BIG,
        name="attend_later",
    )(me, perms, rows)


def attend_first(me, perms, rows, last, slot, later, peers):
    rounds, length, width = rows.shape
    span = width // 2
    per_peer = length // peers
    lane_blocks = length // LANES

    def fixed(shape):
        return pl.BlockSpec(shape, lambda i, s: (0, 0, 0))

    out = (peers, rounds * per_peer + GROUP, span)
    return pl.pallas_call(
        functools.partial(attend_first_kernel, peers),
        grid_spec=pltpu.PrefetchScalarGridSpec(
            num_scalar_prefetch=1,
            grid=(1,),
            in_specs=[
                pl.BlockSpec((rounds, TILE), lambda i, s: (0, s[0] * lane_blocks)),
                pl.BlockSpec(
                    (rounds, LANES),
                    lambda i, s: (
                        0,
                        jnp.where(s[0] == 0, peers * lane_blocks - 1, s[0] * lane_blocks - 1),
                    ),
                ),
                fixed((rounds, TILE, width)),
                fixed(last.shape),
                fixed(slot.shape),
                fixed(later.shape),
            ],
            out_specs=fixed(out),
        ),
        out_shape=jax.ShapeDtypeStruct(out, BF16),
        cost_estimate=cost(2 << 30, 4 << 20),
        compiler_params=BIG,
        name="attend_first",
    )(me, perms, perms, rows, last, slot, later)


def combine_kernel(got_ref, token_ref, mixed_ref):
    peers, _, span = got_ref.shape
    rounds, _, length = token_ref.shape
    per_peer = length // peers
    heads = span // HEAD_DIM
    lane_group = iota((peers, per_peer, LANES), 2) // GROUP
    own_group = lane_group == iota((peers, per_peer, LANES), 1)
    lane = iota((length, LANES), 1) % GROUP // PIECES
    column = iota((length, length), 0)
    outs, lses = [], []
    for turn in range(rounds):
        pick = flag(token_ref[turn, :1, :] == column)
        at = turn * per_peer
        rows = got_ref[:, at : at + per_peer, :].reshape(length, span)
        logs = got_ref[
            :, rounds * per_peer : rounds * per_peer + GROUP, turn * LANES : (turn + 1) * LANES
        ]
        logs = jnp.concatenate([logs] * (per_peer // GROUP), axis=1)
        logs = jnp.where(own_group, logs, jnp.zeros_like(logs)).reshape(length, LANES)
        outs.append(dot(pick, rows))
        moved = dot(pick, logs)
        lses.append(
            [
                jnp.sum(jnp.where(lane == head, moved, 0.0), axis=1, keepdims=True)
                for head in range(heads)
            ]
        )
    for head in range(heads):
        logs = [lse[head] for lse in lses]
        peak = functools.reduce(jnp.maximum, logs)
        whole = peak + jnp.log(functools.reduce(jnp.add, [jnp.exp(lse - peak) for lse in logs]))
        at = head * HEAD_DIM
        mixed = jnp.zeros((length, HEAD_DIM), F32)
        for out, lse in zip(outs, logs):
            mixed = mixed + out[:, at : at + HEAD_DIM] * jnp.exp(lse - whole)
        mixed_ref[:, at : at + HEAD_DIM] = mixed.astype(BF16)


def combine(got, token):
    rounds, _, length = token.shape
    return pl.pallas_call(
        combine_kernel,
        out_shape=jax.ShapeDtypeStruct((length, got.shape[2]), BF16),
        cost_estimate=cost(2 * rounds * length * length * (got.shape[2] + LANES), 1 << 20),
        compiler_params=BIG,
        name="combine",
    )(got, token)


def project_kernel(heads_ref, weight_ref, out_ref):
    span = heads_ref.shape[2]
    total = jnp.zeros(out_ref.shape, F32)
    for index in range(heads_ref.shape[0]):
        total = total + dot(heads_ref[index], weight_ref[index * span : (index + 1) * span, :])
    out_ref[...] = total.astype(BF16)


def project(heads, weight):
    parts, length, span = heads.shape
    return pl.pallas_call(
        project_kernel,
        out_shape=jax.ShapeDtypeStruct((length, weight.shape[1]), BF16),
        cost_estimate=cost(2 * length * parts * span * weight.shape[1], 3 << 20),
        compiler_params=BIG,
        name="project",
    )(heads, weight)


def exchange(x, axis):
    return lax.all_to_all(x, axis, split_axis=0, concat_axis=0, tiled=True)


def after(x, *done):
    return lax.optimization_barrier((x, *done))[0]


def body(x_att, w_qk, w_val, w_out, perms, tokens_b, expert_ids, w_gate, w_up, w_down):
    peers, parts = lax.axis_size("seq"), lax.axis_size("exp")
    chips = parts // EXP_DEV
    me = lax.axis_index("seq").astype(I32).reshape(1)
    my_exp = lax.axis_index("exp").astype(I32)
    core = my_exp % EXP_DEV
    where = jnp.stack([my_exp // EXP_DEV, core])
    length, width = x_att.shape
    rounds = perms.shape[0]
    per_peer = length // peers
    tokb = tokens_b.shape[0]
    capacity = tokb // peers
    part = width // chips
    lines = [[chip * EXP_DEV + side for chip in range(chips)] for side in range(EXP_DEV)]
    siblings = [(i, i ^ 1) for i in range(parts)]

    dispatch, token_slot = pack_tokens(
        where, expert_ids.reshape(1, tokb), tokens_b, peers, capacity, part
    )
    received = exchange(dispatch.reshape(peers, capacity, part), "seq")
    outgoing, slot_token = pack_rows(me, perms, x_att, w_qk, w_val)
    outgoing = after(outgoing, received)
    gathered = lax.all_gather(received, "exp", axis=0, tiled=False, axis_index_groups=lines)
    arrived = exchange(outgoing.reshape(peers, rounds * per_peer, outgoing.shape[1]), "seq")
    own = (w_gate, w_up, w_down)
    sibling = [
        lax.ppermute(
            lax.dynamic_slice_in_dim(after(weight, received), 1 - core, 1, 0), "exp", siblings
        )
        for weight in own
    ]
    w_columns = lax.all_to_all(
        after(w_out, received), "exp", split_axis=1, concat_axis=0, tiled=True
    )
    expert_part = run_experts(where, gathered, own, sibling)
    arrived = after(arrived, expert_part, w_columns)
    expert_rows = lax.psum_scatter(
        expert_part, "exp", scatter_dimension=0, tiled=False, axis_index_groups=lines
    )
    rows, last, row_slot = sort_rows(me, perms, arrived, length)
    last = lax.ppermute(last, "seq", [(i, (i + 1) % peers) for i in range(peers)])
    later = attend_later(me, perms, rows)
    last = after(last, later)
    packed = attend_first(me, perms, rows, last, row_slot, later, peers)
    got = exchange(packed, "seq")
    expert_rows = after(expert_rows, packed)
    kept = lax.dynamic_index_in_dim(expert_rows, core, 0, keepdims=False)
    given = lax.dynamic_index_in_dim(expert_rows, 1 - core, 0, keepdims=False)
    taken = lax.ppermute(given, "exp", siblings)
    expert_rows = jnp.stack([kept, taken], axis=1)
    mixed_heads = combine(got, slot_token)
    expert_rows = after(expert_rows, mixed_heads)
    all_heads = lax.all_gather(mixed_heads, "exp", axis=0, tiled=False)
    expert_back = exchange(expert_rows, "seq")
    mixed = unpack_tokens(
        expert_back.reshape(peers * EXP_DEV * capacity, width // parts), token_slot
    )
    attended = project(after(all_heads, mixed), w_columns)
    return (attended, mixed)


def solution(mesh):
    in_specs = (
        P("seq", None),
        P(None, "exp"),
        P(None, "exp"),
        P("exp", None),
        P(),
        P("seq", None),
        P("seq", None),
        P("seq", None, "exp"),
        P("seq", None, "exp"),
        P("seq", "exp", None),
    )
    out_specs = (P("seq", "exp"), P("seq", "exp"))
    return jax.shard_map(body, mesh=mesh, in_specs=in_specs, out_specs=out_specs, check_vma=False)
```

time: 218 us -> 205 us (0.940)
  waiting for transfers between devices: 61.1 us -> 34.4 us
  blocking collectives: 103 us -> 112 us
  local copies, waits for them, and re-layouts: 8.56 us -> 14 us
    all_to_all x1, waiting for transfers between devices: 15.3 us -> 0.01 us  [body(): lax.all_to_all(after(w_out, received), 'exp', split_axis=1, concat_axis=0...]
    reduce_scatter x2 -> x1, waiting for transfers between devices: 9.77 us -> 0.02 us  [body(): lax.psum_scatter(expert_part, 'exp', scatter_dimension=0, tiled=False, ax...]
    all_to_all x4, blocking collectives: 103 us -> 112 us  [exchange(): return lax.all_to_all(x, axis, split_axis=0, concat_axis=0, tiled=True)]
    dynamic_slice x0 -> x3, local copies, waits for them, and re-layouts: none -> 3.13 us  [body(): lax.dynamic_slice_in_dim(after(weight, received), 1 - core, 1, 0)]
    ppermute x1, waiting for transfers between devices: 4.95 us -> 1.96 us  [body(): lax.ppermute(last, 'seq', [(i, (i + 1) % peers) for i in range(peers)])]
    unnamed x18 -> x22, local copies, waits for them, and re-layouts: 8.03 us -> 8.72 us
    pallas_call x5 -> x7, Pallas kernels: 18.5 us -> 19.1 us  [the longest x1 8.08 us: run_experts(): pl.pallas_call(experts_kernel, grid_spec=pltpu.PrefetchScalarGridSpec(num...]
    all_gather x1 -> x2, waiting for transfers between devices: 31.1 us -> 30.9 us  [the longest x1 30.9 us: body(): lax.all_gather(received, 'exp', axis=0, tiled=False, axis_index_groups=li...]
  transfers between devices with their start and end apart: 5 -> 9, of which waited for: 4 -> 3; matrix products, arithmetic and copies ran while one was open for 1% -> 3% of each run, Pallas kernels for 8% -> 11%
where the time goes in v2:
time: 205 us
  blocking collectives  112 us (55%)
  waiting for transfers between devices  34.4 us (17%)
  Pallas kernels  24.6 us (12%)
  local copies, waits for them, and re-layouts  14 us (7%)
  between operations  13.9 us (7%)
  starting transfers between devices  5.45 us (3%)
    all_to_all x4, blocking collectives, exchange(): return lax.all_to_all(x, axis, split_axis=0, concat_axis=0, tiled=True)  112 us
    all_gather x1, waiting for transfers between devices, body(): lax.all_gather(received, 'exp', axis=0, tiled=False, axis_index_groups=li...  30.9 us
    unnamed x22, local copies, waits for them, and re-layouts  8.72 us
    pallas_call x1, Pallas kernels, run_experts(): pl.pallas_call(experts_kernel, grid_spec=pltpu.PrefetchScalarGridSpec(num...  8.08 us
    all_to_all x1, starting transfers between devices, body(): lax.all_to_all(after(w_out, received), 'exp', split_axis=1, concat_axis=0...  4.47 us
  transfers between devices with their start and end apart: 9, of which 3 were waited for; matrix products, arithmetic and copies ran while one was open for 3% of the time, Pallas kernels for 11%

profile of v2, /device:TPU:32, one launch (start us, length us, event | category | flops | bytes accessed | tf_op | source)
XLA Modules:
  0.0 204.7 jit_solution(11129374219896894540)
XLA Ops:
  7.2 0.0 all-gather.5.cloned.1.call-start
  7.2 0.1 pad_add_fusion.where_ref
  7.3 0.0 copy-start
  7.3 1.6 copy-done
  8.9 0.0 copy-start.2
  8.9 0.7 copy-done.2
  9.6 0.0 copy-start.7
  9.6 1.2 pack_tokens.1
  10.8 28.7 %all_to_all.39 = bf16[32,16,512]{2,1,0:T(8,128)(2,1)} all-to-all(bf16[32,16,512]{2,1,0:T(8,128)(2,1)S(1)} %bitcast.26), channel_id=1, replica_groups=mesh['seq'=32,'exp'=8] {'seq'}, dimensions={0} | all-to-all | bytes 1048576 | tf_op jit(solution)/shard_map/all_to_all | solution.py:531
  39.5 0.0 all-gather.5.cloned.1.call-update
  39.5 0.0 copy-done.7
  39.5 0.0 copy-start.8
  39.5 0.0 copy-start.9
  39.5 1.1 constant_dynamic-slice_fusion.2
  40.6 0.0 copy-start.10
  40.6 0.0 collective-permute-start
  40.6 0.9 copy-done.8
  41.5 1.0 constant_dynamic-slice_fusion.1
  42.5 0.0 collective-permute-start.1
  42.5 0.0 copy-done.9
  42.5 1.0 constant_dynamic-slice_fusion
  43.6 0.5 collective-permute-start.2
  44.1 0.0 copy-done.10
  44.1 1.1 copy.16
  45.2 4.5 %all-to-all-start.2 = ((bf16[256,8,256]{2,0,1:T(8,128)(2,1)}), bf16[256,8,256]{2,0,1:T(8,128)(2,1)S(1)}, u32[]{:S(2)}, u32[]{:S(2)}) async-start(bf16[256,8,256]{2,0,1:T(8,128)(2,1)} %bitcast.28), calls=%async_computation.2 | async-start | bytes 2097152 | tf_op jit(solution)/shard_map/all_to_all | solution.py:569
  49.6 0.0 reduce-scatter.2.cloned.1.call-start
  49.7 0.0 collective-permute-done.refs_3_
  49.7 0.0 collective-permute-done.1.refs_4_
  49.7 0.0 collective-permute-done.2.refs_5_
  49.7 30.9 %all-gather.5.cloned.1.call-done = bf16[128,16,512]{2,1,0:T(8,128)(2,1)} async-done(((bf16[32,16,512]{2,1,0:T(8,128)(2,1)}), bf16[128,16,512]{2,1,0:T(8,128)(2,1)}) %all-gather.5.cloned.1.call-update) | async-done | bytes 2097168 | tf_op jit(solution)/shard_map/all_gather | solution.py:560
  80.6 8.1 %experts.1 = bf16[4,2,32,16,256]{4,3,2,1,0:T(8,128)(2,1)} custom-call(s32[2]{0:T(128)S(1)} %pad_add_fusion.where_ref, bf16[4,32,16,512]{3,2,1,0:T(8,128)(2,1)} %bitcast.29, bf16[2,2048,256]{2,1,0:T(8,128)(2,1)} %refs_0_.1, bf16[2,2048,256]{2,1,0:T(8,128)(2,1)} %refs_1_.1, bf16[2,256,2048]{2,1,0:T(8,128)(2,1)} %refs_2_.1, ...), custom_call_target="tpu_custom_call" | custom-call | flops 3221225472 | bytes 10485760 | tf_op jit(solution)/shard_map/experts/pallas_call | solution.py:200
  88.7 0.0 copy-start.4
  88.7 0.0 copy-start.6
  88.7 0.0 reduce-scatter.2.cloned.1.call-update
  88.7 0.0 all-gather.7.cloned.1.call-start
  88.8 1.1 copy-done.4
  89.9 0.0 copy-done.6
  89.9 0.0 copy-start.3
  89.9 1.6 copy-done.3
  91.5 0.0 copy-start.5
  91.5 1.2 copy-done.5
  92.7 3.8 %pack_rows.1 = (bf16[1024,512]{1,0:T(8,128)(2,1)S(1)}, s32[2,8,512]{2,1,0:T(8,128)S(1)}) custom-call(s32[1]{0:T(128)} %bitcast.me_ref, s32[2,16384]{1,0:T(2,128)S(1)} %copy-done.6, bf16[512,2048]{1,0:T(8,128)(2,1)S(1)} %copy-done.3, bf16[2048,256]{1,0:T(8,128)(2,1)S(1)} %copy-done.4, bf16[2048,256]{1,0:T(8,128)(2,1)S(1)} %copy-done.5), custom_call_target="tpu_custom_call" | custom-call | flops 1610612736 | bytes 6291456 | tf_op jit(solution)/shard_map/pack_rows/pallas_call | solution.py:89
  96.5 0.0 all-to-all-done.2
  96.6 35.4 %all_to_all.40.arrived_ref = bf16[32,32,512]{2,1,0:T(8,128)(2,1)S(1)} all-to-all(bf16[32,32,512]{2,1,0:T(8,128)(2,1)S(1)} %bitcast.24), channel_id=1, replica_groups=mesh['seq'=32,'exp'=8] {'seq'}, dimensions={0} | all-to-all | bytes 2097152 | tf_op jit(solution)/shard_map/all_to_all | solution.py:531
  131.9 1.7 sort_rows.1
  133.6 0.3 collective-permute-start.3
  133.9 3.0 %attend_later.1.later_ref = bf16[2,384,384]{2,1,0:T(8,128)(2,1)S(1)} custom-call(s32[1]{0:T(128)} %bitcast.me_ref, s32[2,16384]{1,0:T(2,128)S(1)} %copy-done.6, bf16[2,512,512]{2,1,0:T(8,128)(2,1)S(1)} %get-tuple-element.27.rows_ref), custom_call_target="tpu_custom_call" | custom-call | flops 2147483648 | bytes 4194304 | tf_op jit(solution)/shard_map/attend_later/pallas_call | solution.py:406
  136.9 2.0 collective-permute-done.3.last_ref
  138.9 2.2 %attend_first.1 = bf16[32,40,256]{2,1,0:T(8,128)(2,1)S(1)} custom-call(s32[1]{0:T(128)} %bitcast.me_ref, s32[2,16384]{1,0:T(2,128)S(1)} %copy-done.6, s32[2,16384]{1,0:T(2,128)S(1)} %copy-done.6, bf16[2,512,512]{2,1,0:T(8,128)(2,1)S(1)} %get-tuple-element.27.rows_ref, bf16[2,64,512]{2,1,0:T(8,128)(2,1)S(1)} %collective-permute-done.3.last_ref, ...), custom_call_target="tpu_custom_call" | custom-call | flops 2147483648 | bytes 4194304 | tf_op jit(solution)/shard_map/attend_first/pallas_call | solution.py:434
  141.1 25.5 %all_to_all.41.got_ref = bf16[32,40,256]{2,1,0:T(8,128)(2,1)S(1)} all-to-all(bf16[32,40,256]{2,1,0:T(8,128)(2,1)S(1)} %attend_first.1), channel_id=1, replica_groups=mesh['seq'=32,'exp'=8] {'seq'}, dimensions={0} | all-to-all | bytes 1310720 | tf_op jit(solution)/shard_map/all_to_all | solution.py:531
  166.6 1.8 combine.1
  168.4 0.0 all-gather.7.cloned.1.call-update
  168.4 0.0 reduce-scatter.2.cloned.1.call-done
  168.5 1.1 dynamic-slice_bitcast_fusion.1
  169.5 0.1 collective-permute-start.4
  169.6 1.5 collective-permute-done.4
  171.2 22.5 %all_to_all.42 = bf16[32,2,16,256]{3,2,1,0:T(8,128)(2,1)S(1)} all-to-all(bf16[32,2,16,256]{3,2,1,0:T(8,128)(2,1)S(1)} %pad_maximum_fusion), channel_id=1, replica_groups=mesh['seq'=32,'exp'=8] {'seq'}, dimensions={0} | all-to-all | bytes 1048576 | tf_op jit(solution)/shard_map/all_to_all | solution.py:531
  193.7 1.4 unpack_tokens.1
  195.2 0.0 all-gather.7.cloned.1.call-done
  195.2 0.0 copy-start.1
  195.2 1.6 copy-done.1
  196.8 1.4 project.1
  (1 shorter events, 0.0 us)
Async XLA Ops:
  7.2 73.4 %all-gather.5.cloned.1.call-start = ((), (), s32[]{:S(2)}) async-start(), calls=%async_computation.7 | async-start | bytes 2621440 | tf_op jit(solution)/shard_map/all_gather | solution.py:560
  7.3 1.6 copy-start
  8.9 0.7 copy-start.2
  9.6 29.9 %copy-start.7 = (bf16[2,2048,256]{2,1,0:T(8,128)(2,1)S(1)}, bf16[2,2048,256]{2,1,0:T(8,128)(2,1)}, u32[]{:S(2)}) copy-start(bf16[2,2048,256]{2,1,0:T(8,128)(2,1)} %refs_0_.1) | copy-start | bytes 6291460
  39.5 2.0 copy-start.8
  39.5 3.0 %copy-start.9 = (bf16[2,256,2048]{2,1,0:T(8,128)(2,1)S(1)}, bf16[2,256,2048]{2,1,0:T(8,128)(2,1)}, u32[]{:S(2)}) copy-start(bf16[2,256,2048]{2,1,0:T(8,128)(2,1)} %refs_2_.1) | copy-start | bytes 6291460
  40.6 3.5 %copy-start.10 = (bf16[256,2048]{1,0:T(8,128)(2,1)S(1)}, bf16[256,2048]{1,0:T(8,128)(2,1)}, u32[]{:S(2)}) copy-start(bf16[256,2048]{1,0:T(8,128)(2,1)} %param.13) | copy-start | bytes 3145732
  40.6 9.1 %collective-permute-start = (bf16[1,2048,256]{2,1,0:T(8,128)(2,1)}, bf16[1,2048,256]{2,1,0:T(8,128)(2,1)S(1)}, u32[]{:S(2)}, u32[]{:S(2)}) collective-permute-start(bf16[1,2048,256]{2,1,0:T(8,128)(2,1)} %constant_dynamic-slice_fusion.2), channel_id=1, source_target_pairs={{0,1},{1,0},{2,3},{3,2},{4,5},{5,4},{6,7},{7,6},{8,9},{9,8},{10,11... | collective-permute-start | bytes 3145736 | tf_op jit(solution)/shard_map/ppermute | solution.py:564
  42.5 7.2 %collective-permute-start.1 = (bf16[1,2048,256]{2,1,0:T(8,128)(2,1)}, bf16[1,2048,256]{2,1,0:T(8,128)(2,1)S(1)}, u32[]{:S(2)}, u32[]{:S(2)}) collective-permute-start(bf16[1,2048,256]{2,1,0:T(8,128)(2,1)} %constant_dynamic-slice_fusion.1), channel_id=1, source_target_pairs={{0,1},{1,0},{2,3},{3,2},{4,5},{5,4},{6,7},{7,6},{8,9},{9,8},{10,11... | collective-permute-start | bytes 3145736 | tf_op jit(solution)/shard_map/ppermute | solution.py:564
  43.6 6.1 %collective-permute-start.2 = (bf16[1,256,2048]{2,1,0:T(8,128)(2,1)}, bf16[1,256,2048]{2,1,0:T(8,128)(2,1)}, u32[]{:S(2)}, u32[]{:S(2)}) collective-permute-start(bf16[1,256,2048]{2,1,0:T(8,128)(2,1)} %constant_dynamic-slice_fusion), channel_id=1, source_target_pairs={{0,1},{1,0},{2,3},{3,2},{4,5},{5,4},{6,7},{7,6},{8,9},{9,8},{10,11... | collective-permute-start | bytes 3145736 | tf_op jit(solution)/shard_map/ppermute | solution.py:564
  45.2 51.4 %all-to-all-start.2 = ((bf16[256,8,256]{2,0,1:T(8,128)(2,1)}), bf16[256,8,256]{2,0,1:T(8,128)(2,1)S(1)}, u32[]{:S(2)}, u32[]{:S(2)}) async-start(bf16[256,8,256]{2,0,1:T(8,128)(2,1)} %bitcast.28), calls=%async_computation.2 | async-start | bytes 2097152 | tf_op jit(solution)/shard_map/all_to_all | solution.py:569
  49.6 118.8 %reduce-scatter.2.cloned.1.call-start = ((), (), s32[]{:S(2)}) async-start(), calls=%async_computation.6 | async-start | bytes 2621440 | tf_op jit(solution)/shard_map/reduce_scatter | solution.py:574
  88.7 1.2 copy-start.4
  88.7 1.2 copy-start.6
  88.7 106.5 %all-gather.7.cloned.1.call-start = ((), (), s32[]{:S(2)}) async-start(), calls=%async_computation.8 | async-start | bytes 2359296 | tf_op jit(solution)/shard_map/all_gather | solution.py:590
  89.9 1.6 copy-start.3
  91.5 1.2 copy-start.5
  133.6 5.2 %collective-permute-start.3 = (bf16[2,64,512]{2,1,0:T(8,128)(2,1)S(1)}, bf16[2,64,512]{2,1,0:T(8,128)(2,1)S(1)}, u32[]{:S(2)}, u32[]{:S(2)}) collective-permute-start(bf16[2,64,512]{2,1,0:T(8,128)(2,1)S(1)} %get-tuple-element.28), channel_id=1, source_target_pairs={{0,8},{8,16},{16,24},{24,32},{32,40},{40,48},{48,56},{56,64},{64,7... | collective-permute-start | bytes 393224 | tf_op jit(solution)/shard_map/ppermute | solution.py:578
  169.5 1.6 collective-permute-start.4
  195.2 1.6 copy-start.1
Sparse Core Ops, SparseCore 0:
  39.6 40.9 all-gather.4
  88.8 28.7 reduce-scatter.1
  168.5 22.1 all-gather.6

commit v3 on v2

--- a/solution.py
+++ b/solution.py
@@ -160,58 +160,73 @@
     )(where, ids, tokens)
 
 
-def experts_kernel(where_ref, x_ref, *refs):
-    weights, out_ref = refs[:-1], refs[-1]
-    parts, peers, capacity, part = x_ref.shape
+def experts_kernel(where_ref, *refs):
+    step = pl.program_id(0)
+    shards, far_refs, weights = refs[0:3], refs[3:5], refs[5:11]
+    out_ref, total_ref = refs[11:]
+    peers, capacity, part = shards[0].shape
     rows = peers * capacity
-    hiddens = []
-    for gate_ref, up_ref in (weights[0:2], weights[3:5]):
-        gate = jnp.zeros((rows, gate_ref.shape[2]), F32)
-        up_val = jnp.zeros((rows, gate_ref.shape[2]), F32)
-        for index in range(parts):
-            x = x_ref[index].reshape(rows, part)
-            gate = gate + dot(x, gate_ref[0, index * part : (index + 1) * part, :])
-            up_val = up_val + dot(x, up_ref[0, index * part : (index + 1) * part, :])
-        hiddens.append((gate / (1.0 + jnp.exp(-gate)) * up_val).astype(BF16))
-    half = part // EXP_DEV
-    for index in range(parts):
-        at = index * part
-        piece = dot(hiddens[0], weights[2][0, :, at : at + part])
-        piece = (piece + dot(hiddens[1], weights[5][0, :, at : at + part])).astype(BF16)
+    ups = (weights[0], weights[1], weights[3], weights[4])
+
+    def add(x, start):
+        for index, weight in enumerate(ups):
+            product = dot(x, weight[0])
+            total_ref[index] = product if start else total_ref[index] + product
+
+    for turn, shard in enumerate(shards):
+
+        @pl.when(step == turn)
+        def _(shard=shard, start=turn == 0):
+            add(shard[...].reshape(rows, part), start)
+
+    @pl.when(step == len(shards))
+    def _():
+        add(jnp.concatenate([ref[...].reshape(rows // 2, part) for ref in far_refs], axis=0), False)
+        hiddens = []
         for side in range(EXP_DEV):
-            columns = piece[:, side * half : (side + 1) * half]
-            out_ref[index, side] = columns.reshape(peers, capacity, half)
-
-
-def run_experts(where, x, own, sibling):
-    parts, peers, capacity, part = x.shape
+            gate, up_val = total_ref[2 * side], total_ref[2 * side + 1]
+            hiddens.append((gate / (1.0 + jnp.exp(-gate)) * up_val).astype(BF16))
+        half = part // EXP_DEV
+        for index in range(out_ref.shape[0]):
+            at = index * part
+            piece = dot(hiddens[0], weights[2][0, :, at : at + part])
+            piece = (piece + dot(hiddens[1], weights[5][0, :, at : at + part])).astype(BF16)
+            for side in range(EXP_DEV):
+                columns = piece[:, side * half : (side + 1) * half]
+                out_ref[index, side] = columns.reshape(peers, capacity, half)
+
+
+def run_experts(where, shards, far, own, sibling):
+    peers, capacity, part = shards[0].shape
     width, hidden = own[0].shape[1:]
-    out = (parts, EXP_DEV, peers, capacity, part // EXP_DEV)
+    chips = width // part
+    out = (chips, EXP_DEV, peers, capacity, part // EXP_DEV)
     rows = peers * capacity
 
-    def mine(i, e):
-        return (e[1], 0, 0)
-
-    def first(i, e):
-        return (0, 0, 0)
-
-    up_block, down_block = (1, width, hidden), (1, hidden, width)
-    blocks = (up_block, up_block, down_block)
+    def rows_of(i, e):
+        ahead = jnp.where(i == 0, 0, jnp.where(i == 1, chips - 1, jnp.where(i == 2, 1, 2)))
+        return (e[0] + ahead) % chips
+
+    up_block, down_block = (1, part, hidden), (1, hidden, width)
+    own_up = pl.BlockSpec(up_block, lambda i, e: (e[1], rows_of(i, e), 0))
+    sibling_up = pl.BlockSpec(up_block, lambda i, e: (0, rows_of(i, e), 0))
+    own_down = pl.BlockSpec(down_block, lambda i, e: (e[1], 0, 0))
+    sibling_down = pl.BlockSpec(down_block, lambda i, e: (0, 0, 0))
     return pl.pallas_call(
         experts_kernel,
         grid_spec=pltpu.PrefetchScalarGridSpec(
             num_scalar_prefetch=1,
-            grid=(1,),
-            in_specs=[pl.BlockSpec(x.shape, lambda i, e: (0, 0, 0, 0))]
-            + [pl.BlockSpec(block, mine) for block in blocks]
-            + [pl.BlockSpec(block, first) for block in blocks],
+            grid=(len(shards) + 1,),
+            in_specs=[pl.BlockSpec(x.shape, lambda i, e: (0, 0, 0)) for x in (*shards, *far)]
+            + [own_up, own_up, own_down, sibling_up, sibling_up, sibling_down],
             out_specs=pl.BlockSpec(out, lambda i, e: (0, 0, 0, 0, 0)),
+            scratch_shapes=[pltpu.VMEM((4, rows, hidden), F32)],
         ),
         out_shape=jax.ShapeDtypeStruct(out, BF16),
         cost_estimate=cost(12 * rows * width * hidden, 10 << 20),
         compiler_params=BIG,
         name="experts",
-    )(where, x, *own, *sibling)
+    )(where, *shards, *far, *own, *sibling)
 
 
 def unpack_tokens_kernel(back_ref, slot_ref, out_ref):
@@ -508,27 +523,69 @@
     )(got, token)
 
 
-def project_kernel(heads_ref, weight_ref, out_ref):
-    span = heads_ref.shape[2]
-    total = jnp.zeros(out_ref.shape, F32)
-    for index in range(heads_ref.shape[0]):
-        total = total + dot(heads_ref[index], weight_ref[index * span : (index + 1) * span, :])
-    out_ref[...] = total.astype(BF16)
-
-
-def project(heads, weight):
-    parts, length, span = heads.shape
+def project_kernel(where_ref, own_ref, prev_ref, next_ref, far_a_ref, far_b_ref, *refs):
+    weights, (kept_ref, given_ref) = refs[:-2], refs[-2:]
+    far = jnp.concatenate([far_a_ref[...], far_b_ref[...]], axis=0)
+    total = dot(own_ref[...], weights[0][...]) + dot(prev_ref[...], weights[1][...])
+    total = total + dot(next_ref[...], weights[2][...]) + dot(far, weights[3][...])
+    half = kept_ref.shape[1]
+    for core in range(EXP_DEV):
+
+        @pl.when(where_ref[1] == core)
+        def _(core=core):
+            kept_ref[...] = total[:, core * half : (core + 1) * half]
+            other = 1 - core
+            given_ref[...] = total[:, other * half : (other + 1) * half].astype(BF16)
+
+
+def project(where, heads, w_out, others):
+    length, span = heads[0].shape
+    columns = others[0].shape[1]
+    half = columns // EXP_DEV
+    weights = (w_out, *others)
+    shapes = [x.shape for x in heads] + [(span, columns)] + [x.shape for x in others]
+
+    def first(i, e):
+        return (0, 0)
+
+    specs = [pl.BlockSpec(shape, first) for shape in shapes]
+    specs[len(heads)] = pl.BlockSpec((span, columns), lambda i, e: (0, e[0]))
     return pl.pallas_call(
         project_kernel,
-        out_shape=jax.ShapeDtypeStruct((length, weight.shape[1]), BF16),
-        cost_estimate=cost(2 * length * parts * span * weight.shape[1], 3 << 20),
+        grid_spec=pltpu.PrefetchScalarGridSpec(
+            num_scalar_prefetch=1,
+            grid=(1,),
+            in_specs=specs,
+            out_specs=[pl.BlockSpec((length, half), first)] * 2,
+        ),
+        out_shape=[
+            jax.ShapeDtypeStruct((length, half), F32),
+            jax.ShapeDtypeStruct((length, half), BF16),
+        ],
+        cost_estimate=cost(8 * length * span * columns, 3 << 20),
         compiler_params=BIG,
         name="project",
-    )(heads, weight)
+    )(where, *heads, *weights)
 
 
 def exchange(x, axis):
     return lax.all_to_all(x, axis, split_axis=0, concat_axis=0, tiled=True)
+
+
+def hop(x, by, chips):
+    pairs = []
+    for chip in range(chips):
+        for core in range(EXP_DEV):
+            there = (chip + by) % chips
+            pairs.append((chip * EXP_DEV + core, there * EXP_DEV + core))
+    return lax.ppermute(x, "exp", pairs)
+
+
+def spread(x, chips):
+    half = x.shape[0] // 2
+    before, behind = hop(x, 1, chips), hop(x, -1, chips)
+    far = (hop(before[:half], 1, chips), hop(behind[half:], -1, chips))
+    return (x, before, behind), far
 
 
 def after(x, *done):
@@ -556,27 +613,35 @@
     )
     received = exchange(dispatch.reshape(peers, capacity, part), "seq")
     outgoing, slot_token = pack_rows(me, perms, x_att, w_qk, w_val)
-    outgoing = after(outgoing, received)
-    gathered = lax.all_gather(received, "exp", axis=0, tiled=False, axis_index_groups=lines)
-    arrived = exchange(outgoing.reshape(peers, rounds * per_peer, outgoing.shape[1]), "seq")
     own = (w_gate, w_up, w_down)
     sibling = [
         lax.ppermute(
-            lax.dynamic_slice_in_dim(after(weight, received), 1 - core, 1, 0), "exp", siblings
+            lax.dynamic_slice_in_dim(after(weight, dispatch), 1 - core, 1, 0), "exp", siblings
         )
         for weight in own
     ]
-    w_columns = lax.all_to_all(
-        after(w_out, received), "exp", split_axis=1, concat_axis=0, tiled=True
-    )
-    expert_part = run_experts(where, gathered, own, sibling)
-    arrived = after(arrived, expert_part, w_columns)
+    columns = [
+        hop(
+            lax.dynamic_slice_in_dim(
+                after(w_out, dispatch), (where[0] + by) % chips * part, part, 1
+            ),
+            by,
+            chips,
+        )
+        for by in (1, chips - 1, 2)
+    ]
+    received = after(received, outgoing, *sibling, *columns)
+    outgoing = after(outgoing, received)
+    shards, far = spread(received, chips)
+    arrived = exchange(outgoing.reshape(peers, rounds * per_peer, outgoing.shape[1]), "seq")
+    expert_part = run_experts(where, shards, far, own, sibling)
+    arrived = after(arrived, expert_part)
     expert_rows = lax.psum_scatter(
         expert_part, "exp", scatter_dimension=0, tiled=False, axis_index_groups=lines
     )
     rows, last, row_slot = sort_rows(me, perms, arrived, length)
     last = lax.ppermute(last, "seq", [(i, (i + 1) % peers) for i in range(peers)])
-    later = attend_later(me, perms, rows)
+    later = attend_later(me, perms, rows) if length > TILE else rows
     last = after(last, later)
     packed = attend_first(me, perms, rows, last, row_slot, later, peers)
     got = exchange(packed, "seq")
@@ -585,14 +650,16 @@
     given = lax.dynamic_index_in_dim(expert_rows, 1 - core, 0, keepdims=False)
     taken = lax.ppermute(given, "exp", siblings)
     expert_rows = jnp.stack([kept, taken], axis=1)
-    mixed_heads = combine(got, slot_token)
-    expert_rows = after(expert_rows, mixed_heads)
-    all_heads = lax.all_gather(mixed_heads, "exp", axis=0, tiled=False)
-    expert_back = exchange(expert_rows, "seq")
+    mixed_heads = combine(after(got, expert_rows), slot_token)
+    expert_back = exchange(after(expert_rows, mixed_heads), "seq")
+    heads, far_heads = spread(mixed_heads, chips)
+    attn_kept, attn_given = project(where, (*heads, *far_heads), w_out, columns)
+    attended = attn_kept + lax.ppermute(attn_given, "exp", siblings).astype(F32)
+    attended = attended.astype(BF16)
+    expert_back = after(expert_back, attended)
     mixed = unpack_tokens(
         expert_back.reshape(peers * EXP_DEV * capacity, width // parts), token_slot
     )
-    attended = project(after(all_heads, mixed), w_columns)
     return (attended, mixed)
 
 

time: 205 us -> 182 us (0.89)
  blocking collectives: 112 us -> 34 us
  starting transfers between devices: 5.45 us -> 40.7 us
  waiting for transfers between devices: 34.4 us -> 49.3 us
    all_to_all x4 -> x1, blocking collectives: 112 us -> 34 us  [exchange(): return lax.all_to_all(x, axis, split_axis=0, concat_axis=0, tiled=True)]
    ppermute x3 -> x15, waiting for transfers between devices: 0.01 us -> 34.3 us  [the longest x11 32.7 us: hop(): return lax.ppermute(x, 'exp', pairs)]
    all_gather x2 -> x0, waiting for transfers between devices: 30.9 us -> none  [the longest x1 30.9 us: body(): lax.all_gather(received, 'exp', axis=0, tiled=False, axis_index_groups=li...]
    all_to_all x1 -> x3, starting transfers between devices: 4.47 us -> 23.3 us  [exchange(): return lax.all_to_all(x, axis, split_axis=0, concat_axis=0, tiled=True)]
    ppermute x3 -> x15, starting transfers between devices: 0.51 us -> 17.2 us  [the longest x11 16.6 us: hop(): return lax.ppermute(x, 'exp', pairs)]
    all_to_all x1 -> x3, waiting for transfers between devices: 0.01 us -> 11.5 us  [exchange(): return lax.all_to_all(x, axis, split_axis=0, concat_axis=0, tiled=True)]
    dynamic_slice x3 -> x4, local copies, waits for them, and re-layouts: 3.13 us -> 5.46 us  [the longest x3 4.59 us: body(): lax.dynamic_slice_in_dim(after(weight, dispatch), 1 - core, 1, 0)]
    unnamed x22 -> x26, local copies, waits for them, and re-layouts: 8.72 us -> 7.54 us
  transfers between devices with their start and end apart: 9 -> 21, of which waited for: 3 -> 11; matrix products, arithmetic and copies ran while one was open for 3% -> 3% of each run, Pallas kernels for 11% -> 7%
where the time goes in v3:
time: 182 us; the launch traced here: 180 us
  waiting for transfers between devices  49.3 us (27%)
  starting transfers between devices  40.7 us (22%)
  blocking collectives  34 us (19%)
  Pallas kernels  26 us (14%)
  between operations  14.3 us (8%)
  local copies, waits for them, and re-layouts  14.1 us (8%)
    all_to_all x1, blocking collectives, exchange(): return lax.all_to_all(x, axis, split_axis=0, concat_axis=0, tiled=True)  34 us
    ppermute x11, waiting for transfers between devices, hop(): return lax.ppermute(x, 'exp', pairs)  32.7 us
    all_to_all x3, starting transfers between devices, exchange(): return lax.all_to_all(x, axis, split_axis=0, concat_axis=0, tiled=True)  23.3 us
    ppermute x11, starting transfers between devices, hop(): return lax.ppermute(x, 'exp', pairs)  16.6 us
    all_to_all x3, waiting for transfers between devices, exchange(): return lax.all_to_all(x, axis, split_axis=0, concat_axis=0, tiled=True)  11.5 us
    pallas_call x1, Pallas kernels, run_experts(): pl.pallas_call(experts_kernel, grid_spec=pltpu.PrefetchScalarGridSpec(num...  8.59 us
    unnamed x26, local copies, waits for them, and re-layouts  7.54 us
    dynamic_slice x3, local copies, waits for them, and re-layouts, body(): lax.dynamic_slice_in_dim(after(weight, dispatch), 1 - core, 1, 0)  4.59 us
  transfers between devices with their start and end apart: 21, of which 11 were waited for; matrix products, arithmetic and copies ran while one was open for 3% of the time, Pallas kernels for 7%

profile of v3, /device:TPU:32, one launch (start us, length us, event | category | flops | bytes accessed | tf_op | source)
XLA Modules:
  0.0 180.1 jit_solution(9779936960654237781)
XLA Ops:
  7.2 0.1 pad_add_fusion.where_ref
  7.3 1.6 copy-done.1
  8.9 0.7 copy-done.2
  9.5 2.0 %pack_tokens.1 = (bf16[512,512]{1,0:T(8,128)(2,1)}, s32[8,512]{1,0:T(8,128)S(1)}) custom-call(s32[2]{0:T(128)S(1)} %pad_add_fusion.where_ref, s32[1,512]{1,0:T(1,128)S(1)} %bitcast.15, bf16[512,2048]{1,0:T(8,128)(2,1)S(1)} %copy-done.1), custom_call_target="tpu_custom_call" | custom-call | flops 268435456 | bytes 2097152 | tf_op jit(solution)/shard_map/pack_tokens/pallas_call | solution.py:139
  11.5 0.6 copy-done.7
  12.1 2.5 %constant_dynamic-slice_fusion.3 = bf16[1,256,2048]{2,1,0:T(8,128)(2,1)} fusion(bf16[2,256,2048]{2,1,0:T(8,128)(2,1)} %refs_7_.1, s32[]{:T(128)S(6)} %select_n.44), kind=kLoop, calls=%fused_computation.7 | loop fusion | bytes 2097156 | tf_op jit(solution)/shard_map/dynamic_slice | solution.py:619
  14.6 0.0 collective-permute-start.2
  14.6 1.0 constant_dynamic-slice_fusion.4
  15.7 0.5 collective-permute-start.1
  16.2 1.1 constant_dynamic-slice_fusion.5
  17.2 0.0 collective-permute-start
  17.2 11.2 %all-to-all-start = ((bf16[32,16,512]{2,1,0:T(8,128)(2,1)}), bf16[32,16,512]{2,1,0:T(8,128)(2,1)S(1)}, u32[]{:S(2)}, u32[]{:S(2)}) async-start(bf16[32,16,512]{2,1,0:T(8,128)(2,1)} %bitcast.4), calls=%async_computation | async-start | bytes 1048576 | tf_op jit(solution)/shard_map/all_to_all | solution.py:572
  28.4 0.0 reduce-scatter.2.cloned.1.call-start
  28.6 0.9 constant_dynamic-slice_fusion
  29.4 3.2 %collective-permute-start.5 = (bf16[256,512]{1,0:T(8,128)(2,1)S(1)}, bf16[256,512]{1,0:T(8,128)(2,1)S(1)}, u32[]{:S(2)}, u32[]{:S(2)}) collective-permute-start(bf16[256,512]{1,0:T(8,128)(2,1)S(1)} %get-tuple-element.44), channel_id=1, source_target_pairs={{0,4},{1,5},{2,6},{3,7},{4,0},{5,1},{6,2},{7,3},{8,12},{9,13},{10,... | collective-permute-start | bytes 786440 | tf_op jit(solution)/shard_map/ppermute | solution.py:581
  32.6 1.1 collective-permute-start.4
  33.7 5.4 %collective-permute-done.5.refs_3_ = bf16[256,512]{1,0:T(8,128)(2,1)S(1)} collective-permute-done((bf16[256,512]{1,0:T(8,128)(2,1)S(1)}, bf16[256,512]{1,0:T(8,128)(2,1)S(1)}, u32[]{:S(2)}, u32[]{:S(2)}) %collective-permute-start.5) | collective-permute-done | bytes 262176 | tf_op jit(solution)/shard_map/ppermute | solution.py:581
  39.1 2.7 %collective-permute-start.3 = (bf16[256,512]{1,0:T(8,128)(2,1)}, bf16[256,512]{1,0:T(8,128)(2,1)S(1)}, u32[]{:S(2)}, u32[]{:S(2)}) collective-permute-start(bf16[256,512]{1,0:T(8,128)(2,1)} %get-tuple-element.46), channel_id=1, source_target_pairs={{0,2},{1,3},{2,4},{3,5},{4,6},{5,7},{6,0},{7,1},{8,10},{9,11},{10,... | collective-permute-start | bytes 786440 | tf_op jit(solution)/shard_map/ppermute | solution.py:581
  41.7 1.6 copy-done.3
  43.3 1.2 copy-done.4
  44.6 1.2 copy-done.5
  45.8 3.8 %pack_rows.1 = (bf16[1024,512]{1,0:T(8,128)(2,1)S(1)}, s32[2,8,512]{2,1,0:T(8,128)S(1)}) custom-call(s32[1]{0:T(128)} %bitcast.2.me_ref, s32[2,16384]{1,0:T(2,128)S(1)} %copy-done.6, bf16[512,2048]{1,0:T(8,128)(2,1)S(1)} %copy-done.3, bf16[2048,256]{1,0:T(8,128)(2,1)S(1)} %copy-done.4, bf16[2048,256]{1,0:T(8,128)(2,1)S(1)} %copy-done.5), custom_call_target="tpu_custom_call" | custom-call | flops 1610612736 | bytes 6291456 | tf_op jit(solution)/shard_map/pack_rows/pallas_call | solution.py:89
  49.6 0.6 copy-done.9
  50.2 0.0 collective-permute-done.4.refs_2_
  50.2 0.0 collective-permute-done.3.refs_1_
  50.2 0.0 collective-permute-done.2.refs_10_
  50.3 0.0 collective-permute-done.1.refs_9_
  50.3 1.5 collective-permute-start.7
  51.8 0.6 collective-permute-start.6
  52.4 9.6 %collective-permute-done.7.refs_2_ = bf16[32,16,512]{2,1,0:T(8,128)(2,1)S(1)} collective-permute-done((bf16[32,16,512]{2,1,0:T(8,128)(2,1)S(1)}, bf16[32,16,512]{2,1,0:T(8,128)(2,1)S(1)}, u32[]{:S(2)}, u32[]{:S(2)}) %collective-permute-start.7) | collective-permute-done | bytes 524320 | tf_op jit(solution)/shard_map/ppermute | solution.py:581
  62.0 3.0 %collective-permute-start.9 = (bf16[16,16,512]{2,1,0:T(8,128)(2,1)S(1)}, bf16[16,16,512]{2,1,0:T(8,128)(2,1)S(1)}, u32[]{:S(2)}, u32[]{:S(2)}) collective-permute-start(bf16[16,16,512]{2,1,0:T(8,128)(2,1)S(1)} %slice.17), channel_id=1, source_target_pairs={{0,6},{1,7},{2,0},{3,1},{4,2},{5,3},{6,4},{7,5},{8,14},{9,15},{10,... | collective-permute-start | bytes 786440 | tf_op jit(solution)/shard_map/ppermute | solution.py:581
  65.0 0.3 collective-permute-start.8
  65.3 3.6 %collective-permute-done.9.refs_4_ = bf16[16,16,512]{2,1,0:T(8,128)(2,1)S(1)} collective-permute-done((bf16[16,16,512]{2,1,0:T(8,128)(2,1)S(1)}, bf16[16,16,512]{2,1,0:T(8,128)(2,1)S(1)}, u32[]{:S(2)}, u32[]{:S(2)}) %collective-permute-start.9) | collective-permute-done | bytes 262176 | tf_op jit(solution)/shard_map/ppermute | solution.py:581
  68.9 4.0 %collective-permute-done.8.refs_3_ = bf16[16,16,512]{2,1,0:T(8,128)(2,1)S(1)} collective-permute-done((bf16[16,16,512]{2,1,0:T(8,128)(2,1)S(1)}, bf16[16,16,512]{2,1,0:T(8,128)(2,1)S(1)}, u32[]{:S(2)}, u32[]{:S(2)}) %collective-permute-start.8) | collective-permute-done | bytes 262176 | tf_op jit(solution)/shard_map/ppermute | solution.py:581
  72.8 8.6 %experts.1 = bf16[4,2,32,16,256]{4,3,2,1,0:T(8,128)(2,1)} custom-call(s32[2]{0:T(128)S(1)} %pad_add_fusion.where_ref, bf16[32,16,512]{2,1,0:T(8,128)(2,1)S(1)} %all-to-all-done.refs_0_, bf16[32,16,512]{2,1,0:T(8,128)(2,1)S(1)} %collective-permute-done.6.refs_1_, bf16[32,16,512]{2,1,0:T(8,128)(2,1)S(1)} %collective-permute-done.7.refs_2_, ...), custom_call_target="tpu_custom_call" | custom-call | flops 3221225472 | bytes 10485760 | tf_op jit(solution)/shard_map/experts/pallas_call | solution.py:215
  81.4 0.0 reduce-scatter.2.cloned.1.call-update
  81.5 34.0 %all_to_all.20.arrived_ref = bf16[32,32,512]{2,1,0:T(8,128)(2,1)S(1)} all-to-all(bf16[32,32,512]{2,1,0:T(8,128)(2,1)S(1)} %bitcast.13), channel_id=1, replica_groups=mesh['seq'=32,'exp'=8] {'seq'}, dimensions={0} | all-to-all | bytes 2097152 | tf_op jit(solution)/shard_map/all_to_all | solution.py:572
  115.4 1.7 sort_rows.1
  117.2 0.1 collective-permute-start.10
  117.3 3.0 %attend_later.1.later_ref = bf16[2,384,384]{2,1,0:T(8,128)(2,1)S(1)} custom-call(s32[1]{0:T(128)} %bitcast.2.me_ref, s32[2,16384]{1,0:T(2,128)S(1)} %copy-done.6, bf16[2,512,512]{2,1,0:T(8,128)(2,1)S(1)} %get-tuple-element.32.rows_ref), custom_call_target="tpu_custom_call" | custom-call | flops 2147483648 | bytes 4194304 | tf_op jit(solution)/shard_map/attend_later/pallas_call | solution.py:421
  120.3 1.9 %collective-permute-done.10.last_ref = bf16[2,64,512]{2,1,0:T(8,128)(2,1)S(1)} collective-permute-done((bf16[2,64,512]{2,1,0:T(8,128)(2,1)S(1)}, bf16[2,64,512]{2,1,0:T(8,128)(2,1)S(1)}, u32[]{:S(2)}, u32[]{:S(2)}) %collective-permute-start.10) | collective-permute-done | bytes 131104 | tf_op jit(solution)/shard_map/ppermute | solution.py:643
  122.2 3.1 %attend_first.1 = bf16[32,40,256]{2,1,0:T(8,128)(2,1)} custom-call(s32[1]{0:T(128)} %bitcast.2.me_ref, s32[2,16384]{1,0:T(2,128)S(1)} %copy-done.6, s32[2,16384]{1,0:T(2,128)S(1)} %copy-done.6, bf16[2,512,512]{2,1,0:T(8,128)(2,1)S(1)} %get-tuple-element.32.rows_ref, bf16[2,64,512]{2,1,0:T(8,128)(2,1)S(1)} %collective-permute-done.10.last_ref, ...), custom_call_target="tpu_custom_call" | custom-call | flops 2147483648 | bytes 4194304 | tf_op jit(solution)/shard_map/attend_first/pallas_call | solution.py:449
  125.3 7.3 %all-to-all-start.2 = ((bf16[32,40,256]{2,1,0:T(8,128)(2,1)}), bf16[32,40,256]{2,1,0:T(8,128)(2,1)S(1)}, u32[]{:S(2)}, u32[]{:S(2)}) async-start(bf16[32,40,256]{2,1,0:T(8,128)(2,1)} %attend_first.1), calls=%async_computation.2 | async-start | bytes 1310720 | tf_op jit(solution)/shard_map/all_to_all | solution.py:572
  132.7 0.0 reduce-scatter.2.cloned.1.call-done
  132.7 1.1 dynamic-slice_bitcast_fusion.1
  133.8 0.1 collective-permute-start.11
  133.9 1.5 collective-permute-done.11
  135.4 0.8 pad_maximum_fusion
  136.2 11.5 %all-to-all-done.2.got_ref = bf16[32,40,256]{2,1,0:T(8,128)(2,1)S(1)} async-done(((bf16[32,40,256]{2,1,0:T(8,128)(2,1)}), bf16[32,40,256]{2,1,0:T(8,128)(2,1)S(1)}, u32[]{:S(2)}, u32[]{:S(2)}) %all-to-all-start.2) | async-done | bytes 655392 | tf_op jit(solution)/shard_map/all_to_all | solution.py:572
  147.7 1.1 combine.1.own_ref
  148.8 4.8 %all-to-all-start.3 = ((bf16[32,2,16,256]{3,2,1,0:T(8,128)(2,1)}), bf16[32,2,16,256]{3,2,1,0:T(8,128)(2,1)S(1)}, u32[]{:S(2)}, u32[]{:S(2)}) async-start(bf16[32,2,16,256]{3,2,1,0:T(8,128)(2,1)} %pad_maximum_fusion), calls=%async_computation.4 | async-start | bytes 1048576 | tf_op jit(solution)/shard_map/all_to_all | solution.py:572
  153.5 0.2 collective-permute-start.13
  153.7 1.9 %collective-permute-start.12 = (bf16[512,256]{1,0:T(8,128)(2,1)S(1)}, bf16[512,256]{1,0:T(8,128)(2,1)S(1)}, u32[]{:S(2)}, u32[]{:S(2)}) collective-permute-start(bf16[512,256]{1,0:T(8,128)(2,1)S(1)} %combine.1.own_ref), channel_id=1, source_target_pairs={{0,2},{1,3},{2,4},{3,5},{4,6},{5,7},{6,0},{7,1},{8,10},{9,11},{10,... | collective-permute-start | bytes 786440 | tf_op jit(solution)/shard_map/ppermute | solution.py:581
  155.6 4.3 %collective-permute-done.13.next_ref = bf16[512,256]{1,0:T(8,128)(2,1)S(1)} collective-permute-done((bf16[512,256]{1,0:T(8,128)(2,1)S(1)}, bf16[512,256]{1,0:T(8,128)(2,1)S(1)}, u32[]{:S(2)}, u32[]{:S(2)}) %collective-permute-start.13) | collective-permute-done | bytes 262176 | tf_op jit(solution)/shard_map/ppermute | solution.py:581
  160.0 1.8 collective-permute-start.15
  161.8 0.4 collective-permute-start.14
  162.2 2.8 %collective-permute-done.15.far_b_ref = bf16[256,256]{1,0:T(8,128)(2,1)S(1)} collective-permute-done((bf16[256,256]{1,0:T(8,128)(2,1)S(1)}, bf16[256,256]{1,0:T(8,128)(2,1)S(1)}, u32[]{:S(2)}, u32[]{:S(2)}) %collective-permute-start.15) | collective-permute-done | bytes 131104 | tf_op jit(solution)/shard_map/ppermute | solution.py:581
  165.1 3.0 %collective-permute-done.14.far_a_ref = bf16[256,256]{1,0:T(8,128)(2,1)S(1)} collective-permute-done((bf16[256,256]{1,0:T(8,128)(2,1)S(1)}, bf16[256,256]{1,0:T(8,128)(2,1)S(1)}, u32[]{:S(2)}, u32[]{:S(2)}) %collective-permute-start.14) | collective-permute-done | bytes 131104 | tf_op jit(solution)/shard_map/ppermute | solution.py:581
  168.1 1.3 project.1
  169.4 0.1 collective-permute-start.16
  169.5 1.5 collective-permute-done.16
  171.0 0.8 add_convert_fusion
  171.8 0.0 all-to-all-done.3
  171.8 1.4 unpack_tokens.1
  (27 shorter events, 0.1 us)
Async XLA Ops:
  7.3 1.6 copy-start.1
  8.9 0.7 copy-start.2
  9.5 5.1 %copy-start.12 = (bf16[2,2048,256]{2,1,0:T(8,128)(2,1)S(1)}, bf16[2,2048,256]{2,1,0:T(8,128)(2,1)}, u32[]{:S(2)}) copy-start(bf16[2,2048,256]{2,1,0:T(8,128)(2,1)} %refs_6_.1) | copy-start | bytes 6291460
  11.5 0.6 copy-start.7
  12.1 4.0 %copy-start.11 = (bf16[2,2048,256]{2,1,0:T(8,128)(2,1)S(1)}, bf16[2,2048,256]{2,1,0:T(8,128)(2,1)}, u32[]{:S(2)}) copy-start(bf16[2,2048,256]{2,1,0:T(8,128)(2,1)} %refs_5_.1) | copy-start | bytes 6291460
  14.6 35.6 %collective-permute-start.2 = (bf16[1,256,2048]{2,1,0:T(8,128)(2,1)}, bf16[1,256,2048]{2,1,0:T(8,128)(2,1)}, u32[]{:S(2)}, u32[]{:S(2)}) collective-permute-start(bf16[1,256,2048]{2,1,0:T(8,128)(2,1)} %constant_dynamic-slice_fusion.3), channel_id=1, source_target_pairs={{0,1},{1,0},{2,3},{3,2},{4,5},{5,4},{6,7},{7,6},{8,9},{9,8},{10,11... | collective-permute-start | bytes 3145736 | tf_op jit(solution)/shard_map/ppermute | solution.py:618
  15.7 12.9 %copy-start = (bf16[256,2048]{1,0:T(8,128)(2,1)S(1)}, bf16[256,2048]{1,0:T(8,128)(2,1)}, u32[]{:S(2)}) copy-start(bf16[256,2048]{1,0:T(8,128)(2,1)} %refs_0_.1) | copy-start | bytes 3145732
  15.7 26.1 %copy-start.6 = (s32[2,16384]{1,0:T(2,128)S(1)}, s32[2,16384]{1,0:T(2,128)}, u32[]{:S(2)}) copy-start(s32[2,16384]{1,0:T(2,128)} %earlier_ref.1) | copy-start | bytes 393220
  15.7 34.6 %collective-permute-start.1 = (bf16[1,2048,256]{2,1,0:T(8,128)(2,1)}, bf16[1,2048,256]{2,1,0:T(8,128)(2,1)}, u32[]{:S(2)}, u32[]{:S(2)}) collective-permute-start(bf16[1,2048,256]{2,1,0:T(8,128)(2,1)} %constant_dynamic-slice_fusion.4), channel_id=1, source_target_pairs={{0,1},{1,0},{2,3},{3,2},{4,5},{5,4},{6,7},{7,6},{8,9},{9,8},{10,11... | collective-permute-start | bytes 3145736 | tf_op jit(solution)/shard_map/ppermute | solution.py:618
  17.2 33.0 %collective-permute-start = (bf16[1,2048,256]{2,1,0:T(8,128)(2,1)}, bf16[1,2048,256]{2,1,0:T(8,128)(2,1)}, u32[]{:S(2)}, u32[]{:S(2)}) collective-permute-start(bf16[1,2048,256]{2,1,0:T(8,128)(2,1)} %constant_dynamic-slice_fusion.5), channel_id=1, source_target_pairs={{0,1},{1,0},{2,3},{3,2},{4,5},{5,4},{6,7},{7,6},{8,9},{9,8},{10,11... | collective-permute-start | bytes 3145736 | tf_op jit(solution)/shard_map/ppermute | solution.py:618
  17.2 33.0 %all-to-all-start = ((bf16[32,16,512]{2,1,0:T(8,128)(2,1)}), bf16[32,16,512]{2,1,0:T(8,128)(2,1)S(1)}, u32[]{:S(2)}, u32[]{:S(2)}) async-start(bf16[32,16,512]{2,1,0:T(8,128)(2,1)} %bitcast.4), calls=%async_computation | async-start | bytes 1048576 | tf_op jit(solution)/shard_map/all_to_all | solution.py:572
  28.4 104.2 %reduce-scatter.2.cloned.1.call-start = ((), (), s32[]{:S(2)}) async-start(), calls=%async_computation.5 | async-start | bytes 2621440 | tf_op jit(solution)/shard_map/reduce_scatter | solution.py:639
  29.4 9.7 %collective-permute-start.5 = (bf16[256,512]{1,0:T(8,128)(2,1)S(1)}, bf16[256,512]{1,0:T(8,128)(2,1)S(1)}, u32[]{:S(2)}, u32[]{:S(2)}) collective-permute-start(bf16[256,512]{1,0:T(8,128)(2,1)S(1)} %get-tuple-element.44), channel_id=1, source_target_pairs={{0,4},{1,5},{2,6},{3,7},{4,0},{5,1},{6,2},{7,3},{8,12},{9,13},{10,... | collective-permute-start | bytes 786440 | tf_op jit(solution)/shard_map/ppermute | solution.py:581
  32.6 17.6 %collective-permute-start.4 = (bf16[256,512]{1,0:T(8,128)(2,1)}, bf16[256,512]{1,0:T(8,128)(2,1)S(1)}, u32[]{:S(2)}, u32[]{:S(2)}) collective-permute-start(bf16[256,512]{1,0:T(8,128)(2,1)} %get-tuple-element.45), channel_id=1, source_target_pairs={{0,6},{1,7},{2,0},{3,1},{4,2},{5,3},{6,4},{7,5},{8,14},{9,15},{10,... | collective-permute-start | bytes 786440 | tf_op jit(solution)/shard_map/ppermute | solution.py:581
  39.1 11.2 %collective-permute-start.3 = (bf16[256,512]{1,0:T(8,128)(2,1)}, bf16[256,512]{1,0:T(8,128)(2,1)S(1)}, u32[]{:S(2)}, u32[]{:S(2)}) collective-permute-start(bf16[256,512]{1,0:T(8,128)(2,1)} %get-tuple-element.46), channel_id=1, source_target_pairs={{0,2},{1,3},{2,4},{3,5},{4,6},{5,7},{6,0},{7,1},{8,10},{9,11},{10,... | collective-permute-start | bytes 786440 | tf_op jit(solution)/shard_map/ppermute | solution.py:581
  41.7 1.6 copy-start.3
  43.3 1.2 copy-start.4
  44.6 1.2 copy-start.5
  49.6 0.6 copy-start.9
  50.3 11.7 %collective-permute-start.7 = (bf16[32,16,512]{2,1,0:T(8,128)(2,1)S(1)}, bf16[32,16,512]{2,1,0:T(8,128)(2,1)S(1)}, u32[]{:S(2)}, u32[]{:S(2)}) collective-permute-start(bf16[32,16,512]{2,1,0:T(8,128)(2,1)S(1)} %all-to-all-done.refs_0_), channel_id=1, source_target_pairs={{0,6},{1,7},{2,0},{3,1},{4,2},{5,3},{6,4},{7,5},{8,14},{9,15},{10,... | collective-permute-start | bytes 1572872 | tf_op jit(solution)/shard_map/ppermute | solution.py:581
  51.8 13.2 %collective-permute-start.6 = (bf16[32,16,512]{2,1,0:T(8,128)(2,1)S(1)}, bf16[32,16,512]{2,1,0:T(8,128)(2,1)S(1)}, u32[]{:S(2)}, u32[]{:S(2)}) collective-permute-start(bf16[32,16,512]{2,1,0:T(8,128)(2,1)S(1)} %all-to-all-done.refs_0_), channel_id=1, source_target_pairs={{0,2},{1,3},{2,4},{3,5},{4,6},{5,7},{6,0},{7,1},{8,10},{9,11},{10,... | collective-permute-start | bytes 1572872 | tf_op jit(solution)/shard_map/ppermute | solution.py:581
  62.0 6.9 %collective-permute-start.9 = (bf16[16,16,512]{2,1,0:T(8,128)(2,1)S(1)}, bf16[16,16,512]{2,1,0:T(8,128)(2,1)S(1)}, u32[]{:S(2)}, u32[]{:S(2)}) collective-permute-start(bf16[16,16,512]{2,1,0:T(8,128)(2,1)S(1)} %slice.17), channel_id=1, source_target_pairs={{0,6},{1,7},{2,0},{3,1},{4,2},{5,3},{6,4},{7,5},{8,14},{9,15},{10,... | collective-permute-start | bytes 786440 | tf_op jit(solution)/shard_map/ppermute | solution.py:581
  65.0 7.8 %collective-permute-start.8 = (bf16[16,16,512]{2,1,0:T(8,128)(2,1)S(1)}, bf16[16,16,512]{2,1,0:T(8,128)(2,1)S(1)}, u32[]{:S(2)}, u32[]{:S(2)}) collective-permute-start(bf16[16,16,512]{2,1,0:T(8,128)(2,1)S(1)} %slice.16), channel_id=1, source_target_pairs={{0,2},{1,3},{2,4},{3,5},{4,6},{5,7},{6,0},{7,1},{8,10},{9,11},{10,... | collective-permute-start | bytes 786440 | tf_op jit(solution)/shard_map/ppermute | solution.py:581
  117.2 5.0 %collective-permute-start.10 = (bf16[2,64,512]{2,1,0:T(8,128)(2,1)S(1)}, bf16[2,64,512]{2,1,0:T(8,128)(2,1)S(1)}, u32[]{:S(2)}, u32[]{:S(2)}) collective-permute-start(bf16[2,64,512]{2,1,0:T(8,128)(2,1)S(1)} %get-tuple-element.33), channel_id=1, source_target_pairs={{0,8},{8,16},{16,24},{24,32},{32,40},{40,48},{48,56},{56,64},{64,7... | collective-permute-start | bytes 393224 | tf_op jit(solution)/shard_map/ppermute | solution.py:643
  125.3 22.4 %copy-start.10 = (s32[2,8,512]{2,1,0:T(8,128)S(1)}, s32[2,8,512]{2,1,0:T(8,128)}, u32[]{:S(2)}) copy-start(s32[2,8,512]{2,1,0:T(8,128)} %copy-done.9) | copy-start | bytes 98308
  125.3 22.4 %all-to-all-start.2 = ((bf16[32,40,256]{2,1,0:T(8,128)(2,1)}), bf16[32,40,256]{2,1,0:T(8,128)(2,1)S(1)}, u32[]{:S(2)}, u32[]{:S(2)}) async-start(bf16[32,40,256]{2,1,0:T(8,128)(2,1)} %attend_first.1), calls=%async_computation.2 | async-start | bytes 1310720 | tf_op jit(solution)/shard_map/all_to_all | solution.py:572
  133.8 1.6 collective-permute-start.11
  148.8 23.0 %all-to-all-start.3 = ((bf16[32,2,16,256]{3,2,1,0:T(8,128)(2,1)}), bf16[32,2,16,256]{3,2,1,0:T(8,128)(2,1)S(1)}, u32[]{:S(2)}, u32[]{:S(2)}) async-start(bf16[32,2,16,256]{3,2,1,0:T(8,128)(2,1)} %pad_maximum_fusion), calls=%async_computation.4 | async-start | bytes 1048576 | tf_op jit(solution)/shard_map/all_to_all | solution.py:572
  153.5 6.4 %collective-permute-start.13 = (bf16[512,256]{1,0:T(8,128)(2,1)S(1)}, bf16[512,256]{1,0:T(8,128)(2,1)S(1)}, u32[]{:S(2)}, u32[]{:S(2)}) collective-permute-start(bf16[512,256]{1,0:T(8,128)(2,1)S(1)} %combine.1.own_ref), channel_id=1, source_target_pairs={{0,6},{1,7},{2,0},{3,1},{4,2},{5,3},{6,4},{7,5},{8,14},{9,15},{10,... | collective-permute-start | bytes 786440 | tf_op jit(solution)/shard_map/ppermute | solution.py:581
  153.7 8.1 %collective-permute-start.12 = (bf16[512,256]{1,0:T(8,128)(2,1)S(1)}, bf16[512,256]{1,0:T(8,128)(2,1)S(1)}, u32[]{:S(2)}, u32[]{:S(2)}) collective-permute-start(bf16[512,256]{1,0:T(8,128)(2,1)S(1)} %combine.1.own_ref), channel_id=1, source_target_pairs={{0,2},{1,3},{2,4},{3,5},{4,6},{5,7},{6,0},{7,1},{8,10},{9,11},{10,... | collective-permute-start | bytes 786440 | tf_op jit(solution)/shard_map/ppermute | solution.py:581
  160.0 11.8 %copy-start.8 = (s32[8,512]{1,0:T(8,128)S(1)}, s32[8,512]{1,0:T(8,128)}, u32[]{:S(2)}) copy-start(s32[8,512]{1,0:T(8,128)} %copy-done.7) | copy-start | bytes 49156
  160.0 5.0 %collective-permute-start.15 = (bf16[256,256]{1,0:T(8,128)(2,1)S(1)}, bf16[256,256]{1,0:T(8,128)(2,1)S(1)}, u32[]{:S(2)}, u32[]{:S(2)}) collective-permute-start(bf16[256,256]{1,0:T(8,128)(2,1)S(1)} %slice.19), channel_id=1, source_target_pairs={{0,6},{1,7},{2,0},{3,1},{4,2},{5,3},{6,4},{7,5},{8,14},{9,15},{10,... | collective-permute-start | bytes 393224 | tf_op jit(solution)/shard_map/ppermute | solution.py:581
  161.8 6.3 %collective-permute-start.14 = (bf16[256,256]{1,0:T(8,128)(2,1)S(1)}, bf16[256,256]{1,0:T(8,128)(2,1)S(1)}, u32[]{:S(2)}, u32[]{:S(2)}) collective-permute-start(bf16[256,256]{1,0:T(8,128)(2,1)S(1)} %slice.18), channel_id=1, source_target_pairs={{0,2},{1,3},{2,4},{3,5},{4,6},{5,7},{6,0},{7,1},{8,10},{9,11},{10,... | collective-permute-start | bytes 393224 | tf_op jit(solution)/shard_map/ppermute | solution.py:581
  169.4 1.6 collective-permute-start.16
Sparse Core Ops, SparseCore 0:
  81.6 30.8 reduce-scatter.1

commit v4 on v3

--- a/solution.py
+++ b/solution.py
@@ -581,9 +581,10 @@
     return lax.ppermute(x, "exp", pairs)
 
 
-def spread(x, chips):
+def spread(x, chips, ready=()):
     half = x.shape[0] // 2
     before, behind = hop(x, 1, chips), hop(x, -1, chips)
+    before, behind = (after(side, *ready) if ready else side for side in (before, behind))
     far = (hop(before[:half], 1, chips), hop(behind[half:], -1, chips))
     return (x, before, behind), far
 
@@ -613,13 +614,6 @@
     )
     received = exchange(dispatch.reshape(peers, capacity, part), "seq")
     outgoing, slot_token = pack_rows(me, perms, x_att, w_qk, w_val)
-    own = (w_gate, w_up, w_down)
-    sibling = [
-        lax.ppermute(
-            lax.dynamic_slice_in_dim(after(weight, dispatch), 1 - core, 1, 0), "exp", siblings
-        )
-        for weight in own
-    ]
     columns = [
         hop(
             lax.dynamic_slice_in_dim(
@@ -630,16 +624,27 @@
         )
         for by in (1, chips - 1, 2)
     ]
-    received = after(received, outgoing, *sibling, *columns)
+    received = after(received, outgoing, *columns)
     outgoing = after(outgoing, received)
+    own = (w_gate, w_up, w_down)
+    sibling = [
+        lax.ppermute(
+            lax.dynamic_slice_in_dim(after(weight, received), 1 - core, 1, 0), "exp", siblings
+        )
+        for weight in own
+    ]
     shards, far = spread(received, chips)
     arrived = exchange(outgoing.reshape(peers, rounds * per_peer, outgoing.shape[1]), "seq")
     expert_part = run_experts(where, shards, far, own, sibling)
     arrived = after(arrived, expert_part)
+    rows, last, row_slot = sort_rows(me, perms, arrived, length)
     expert_rows = lax.psum_scatter(
-        expert_part, "exp", scatter_dimension=0, tiled=False, axis_index_groups=lines
+        after(expert_part, last),
+        "exp",
+        scatter_dimension=0,
+        tiled=False,
+        axis_index_groups=lines,
     )
-    rows, last, row_slot = sort_rows(me, perms, arrived, length)
     last = lax.ppermute(last, "seq", [(i, (i + 1) % peers) for i in range(peers)])
     later = attend_later(me, perms, rows) if length > TILE else rows
     last = after(last, later)
@@ -650,9 +655,9 @@
     given = lax.dynamic_index_in_dim(expert_rows, 1 - core, 0, keepdims=False)
     taken = lax.ppermute(given, "exp", siblings)
     expert_rows = jnp.stack([kept, taken], axis=1)
-    mixed_heads = combine(after(got, expert_rows), slot_token)
+    mixed_heads = combine(got, slot_token)
     expert_back = exchange(after(expert_rows, mixed_heads), "seq")
-    heads, far_heads = spread(mixed_heads, chips)
+    heads, far_heads = spread(mixed_heads, chips, (expert_rows,))
     attn_kept, attn_given = project(where, (*heads, *far_heads), w_out, columns)
     attended = attn_kept + lax.ppermute(attn_given, "exp", siblings).astype(F32)
     attended = attended.astype(BF16)

time: 182 us -> 168 us (0.923)
  blocking collectives: 34 us -> 0 us
  starting transfers between devices: 40.7 us -> 55 us
  waiting for transfers between devices: 49.3 us -> 54.4 us
    all_to_all x1 -> x0, blocking collectives: 34 us -> none  [exchange(): return lax.all_to_all(x, axis, split_axis=0, concat_axis=0, tiled=True)]
    all_to_all x3 -> x4, starting transfers between devices: 23.3 us -> 36.3 us  [exchange(): return lax.all_to_all(x, axis, split_axis=0, concat_axis=0, tiled=True)]
    reduce_scatter x1, waiting for transfers between devices: 0.02 us -> 11.7 us  [body(): lax.psum_scatter(after(expert_part, last), 'exp', scatter_dimension=0, ti...]
    all_to_all x3 -> x4, waiting for transfers between devices: 11.5 us -> 6.43 us  [exchange(): return lax.all_to_all(x, axis, split_axis=0, concat_axis=0, tiled=True)]
    dynamic_slice x3, local copies, waits for them, and re-layouts: 4.59 us -> 1.62 us  [body(): lax.dynamic_slice_in_dim(after(weight, received), 1 - core, 1, 0)]
    unnamed x26 -> x34, local copies, waits for them, and re-layouts: 7.54 us -> 8.97 us
  transfers between devices with their start and end apart: 21 -> 22, of which waited for: 11 -> 13; matrix products, arithmetic and copies ran while one was open for 3% -> 3% of each run, Pallas kernels for 7% -> 13%
where the time goes in v4:
time: 168 us; the launch traced here: 165 us
  starting transfers between devices  55 us (33%)
  waiting for transfers between devices  54.4 us (32%)
  Pallas kernels  26.2 us (16%)
  between operations  14.3 us (9%)
  local copies, waits for them, and re-layouts  12.6 us (8%)
  other arithmetic  2.66 us (2%)
    all_to_all x4, starting transfers between devices, exchange(): return lax.all_to_all(x, axis, split_axis=0, concat_axis=0, tiled=True)  36.3 us
    ppermute x11, waiting for transfers between devices, hop(): return lax.ppermute(x, 'exp', pairs)  34.3 us
    ppermute x11, starting transfers between devices, hop(): return lax.ppermute(x, 'exp', pairs)  16.3 us
    reduce_scatter x1, waiting for transfers between devices, body(): lax.psum_scatter(after(expert_part, last), 'exp', scatter_dimension=0, ti...  11.7 us
    unnamed x34, local copies, waits for them, and re-layouts  8.97 us
    pallas_call x1, Pallas kernels, run_experts(): pl.pallas_call(experts_kernel, grid_spec=pltpu.PrefetchScalarGridSpec(num...  7.8 us
    all_to_all x4, waiting for transfers between devices, exchange(): return lax.all_to_all(x, axis, split_axis=0, concat_axis=0, tiled=True)  6.43 us
    pallas_call x1, Pallas kernels, pack_rows(): pl.pallas_call(pack_rows_kernel, grid_spec=pltpu.PrefetchScalarGridSpec(n...  4.81 us
  transfers between devices with their start and end apart: 22, of which 13 were waited for; matrix products, arithmetic and copies ran while one was open for 3% of the time, Pallas kernels for 13%

profile of v4, /device:TPU:32, one launch (start us, length us, event | category | flops | bytes accessed | tf_op | source)
XLA Modules:
  0.0 165.3 jit_solution(14613212338142225731)
XLA Ops:
  7.2 0.1 pad_add_fusion.where_ref
  7.3 1.7 %copy-done.1 = bf16[512,2048]{1,0:T(8,128)(2,1)S(1)} copy-done((bf16[512,2048]{1,0:T(8,128)(2,1)S(1)}, bf16[512,2048]{1,0:T(8,128)(2,1)}, u32[]{:S(2)}) %copy-start.1) | copy-done | bytes 2097176
  8.9 0.7 copy-done.2
  9.6 2.0 %pack_tokens.1 = (bf16[512,512]{1,0:T(8,128)(2,1)}, s32[8,512]{1,0:T(8,128)S(1)}) custom-call(s32[2]{0:T(128)S(1)} %pad_add_fusion.where_ref, s32[1,512]{1,0:T(1,128)S(1)} %bitcast.14, bf16[512,2048]{1,0:T(8,128)(2,1)S(1)} %copy-done.1), custom_call_target="tpu_custom_call" | custom-call | flops 268435456 | bytes 2097152 | tf_op jit(solution)/shard_map/pack_tokens/pallas_call | solution.py:139
  11.6 0.6 copy-done.7
  12.2 11.2 %all-to-all-start = ((bf16[32,16,512]{2,1,0:T(8,128)(2,1)}), bf16[32,16,512]{2,1,0:T(8,128)(2,1)S(1)}, u32[]{:S(2)}, u32[]{:S(2)}) async-start(bf16[32,16,512]{2,1,0:T(8,128)(2,1)} %bitcast.4), calls=%async_computation | async-start | bytes 1048576 | tf_op jit(solution)/shard_map/all_to_all | solution.py:572
  23.5 0.9 constant_dynamic-slice_fusion.3
  24.4 3.2 %collective-permute-start.2 = (bf16[256,512]{1,0:T(8,128)(2,1)}, bf16[256,512]{1,0:T(8,128)(2,1)S(1)}, u32[]{:S(2)}, u32[]{:S(2)}) collective-permute-start(bf16[256,512]{1,0:T(8,128)(2,1)} %get-tuple-element.48), channel_id=1, source_target_pairs={{0,4},{1,5},{2,6},{3,7},{4,0},{5,1},{6,2},{7,3},{8,12},{9,13},{10,... | collective-permute-start | bytes 786440 | tf_op jit(solution)/shard_map/ppermute | solution.py:581
  27.6 1.1 collective-permute-start.1
  28.6 1.0 collective-permute-start
  29.6 1.6 copy-done.3
  31.2 1.2 copy-done.5
  32.4 4.8 %pack_rows.1 = (bf16[1024,512]{1,0:T(8,128)(2,1)}, s32[2,8,512]{2,1,0:T(8,128)S(1)}) custom-call(s32[1]{0:T(128)} %bitcast.2.me_ref, s32[2,16384]{1,0:T(2,128)S(1)} %copy-done.6, bf16[512,2048]{1,0:T(8,128)(2,1)S(1)} %copy-done.3, bf16[2048,256]{1,0:T(8,128)(2,1)S(1)} %copy-done.4, bf16[2048,256]{1,0:T(8,128)(2,1)S(1)} %copy-done.5), custom_call_target="tpu_custom_call" | custom-call | flops 1610612736 | bytes 6291456 | tf_op jit(solution)/shard_map/pack_rows/pallas_call | solution.py:89
  37.2 0.6 copy-done.11
  37.9 1.7 %collective-permute-done.1.refs_2_ = bf16[256,512]{1,0:T(8,128)(2,1)S(1)} collective-permute-done((bf16[256,512]{1,0:T(8,128)(2,1)}, bf16[256,512]{1,0:T(8,128)(2,1)S(1)}, u32[]{:S(2)}, u32[]{:S(2)}) %collective-permute-start.1) | collective-permute-done | bytes 262176 | tf_op jit(solution)/shard_map/ppermute | solution.py:581
  39.6 1.4 all-to-all-done.refs_0_
  41.0 8.4 %all-to-all-start.1 = ((bf16[32,32,512]{2,1,0:T(8,128)(2,1)}), bf16[32,32,512]{2,1,0:T(8,128)(2,1)S(1)}, u32[]{:S(2)}, u32[]{:S(2)}) async-start(bf16[32,32,512]{2,1,0:T(8,128)(2,1)} %bitcast.5), calls=%async_computation.1 | async-start | bytes 2097152 | tf_op jit(solution)/shard_map/all_to_all | solution.py:572
  49.4 0.0 reduce-scatter.2.cloned.1.call-start
  49.4 0.0 copy-start.15
  49.5 0.0 copy-start.16
  49.5 1.4 constant_dynamic-slice_fusion.2
  50.9 0.4 copy-done.15
  51.4 0.1 constant_dynamic-slice_fusion.1
  51.4 0.6 copy-done.16
  52.0 0.1 constant_dynamic-slice_fusion
  52.1 0.1 collective-permute-start.9
  52.2 0.5 collective-permute-start.8
  52.7 0.1 collective-permute-start.7
  52.8 2.6 %collective-permute-start.4 = (bf16[32,16,512]{2,1,0:T(8,128)(2,1)S(1)}, bf16[32,16,512]{2,1,0:T(8,128)(2,1)S(1)}, u32[]{:S(2)}, u32[]{:S(2)}) collective-permute-start(bf16[32,16,512]{2,1,0:T(8,128)(2,1)S(1)} %all-to-all-done.refs_0_), channel_id=1, source_target_pairs={{0,6},{1,7},{2,0},{3,1},{4,2},{5,3},{6,4},{7,5},{8,14},{9,15},{10,... | collective-permute-start | bytes 1572872 | tf_op jit(solution)/shard_map/ppermute | solution.py:581
  55.4 11.8 %collective-permute-done.4.refs_2_ = bf16[32,16,512]{2,1,0:T(8,128)(2,1)S(1)} collective-permute-done((bf16[32,16,512]{2,1,0:T(8,128)(2,1)S(1)}, bf16[32,16,512]{2,1,0:T(8,128)(2,1)S(1)}, u32[]{:S(2)}, u32[]{:S(2)}) %collective-permute-start.4) | collective-permute-done | bytes 524320 | tf_op jit(solution)/shard_map/ppermute | solution.py:581
  67.2 3.8 %collective-permute-start.6 = (bf16[16,16,512]{2,1,0:T(8,128)(2,1)S(1)}, bf16[16,16,512]{2,1,0:T(8,128)(2,1)S(1)}, u32[]{:S(2)}, u32[]{:S(2)}) collective-permute-start(bf16[16,16,512]{2,1,0:T(8,128)(2,1)S(1)} %slice.17), channel_id=1, source_target_pairs={{0,6},{1,7},{2,0},{3,1},{4,2},{5,3},{6,4},{7,5},{8,14},{9,15},{10,... | collective-permute-start | bytes 786440 | tf_op jit(solution)/shard_map/ppermute | solution.py:581
  71.0 0.3 collective-permute-start.5
  71.3 5.1 %collective-permute-done.6.refs_4_ = bf16[16,16,512]{2,1,0:T(8,128)(2,1)S(1)} collective-permute-done((bf16[16,16,512]{2,1,0:T(8,128)(2,1)S(1)}, bf16[16,16,512]{2,1,0:T(8,128)(2,1)S(1)}, u32[]{:S(2)}, u32[]{:S(2)}) %collective-permute-start.6) | collective-permute-done | bytes 262176 | tf_op jit(solution)/shard_map/ppermute | solution.py:581
  76.4 3.7 %collective-permute-done.5.refs_3_ = bf16[16,16,512]{2,1,0:T(8,128)(2,1)S(1)} collective-permute-done((bf16[16,16,512]{2,1,0:T(8,128)(2,1)S(1)}, bf16[16,16,512]{2,1,0:T(8,128)(2,1)S(1)}, u32[]{:S(2)}, u32[]{:S(2)}) %collective-permute-start.5) | collective-permute-done | bytes 262176 | tf_op jit(solution)/shard_map/ppermute | solution.py:581
  80.1 7.8 %experts.1 = bf16[4,2,32,16,256]{4,3,2,1,0:T(8,128)(2,1)} custom-call(s32[2]{0:T(128)S(1)} %pad_add_fusion.where_ref, bf16[32,16,512]{2,1,0:T(8,128)(2,1)S(1)} %all-to-all-done.refs_0_, bf16[32,16,512]{2,1,0:T(8,128)(2,1)S(1)} %collective-permute-done.3.refs_1_, bf16[32,16,512]{2,1,0:T(8,128)(2,1)S(1)} %collective-permute-done.4.refs_2_, ...), custom_call_target="tpu_custom_call" | custom-call | flops 3221225472 | bytes 10485760 | tf_op jit(solution)/shard_map/experts/pallas_call | solution.py:215
  87.9 1.7 %sort_rows.1 = (bf16[2,512,512]{2,1,0:T(8,128)(2,1)S(1)}, bf16[2,64,512]{2,1,0:T(8,128)(2,1)S(1)}, s32[2,8,512]{2,1,0:T(8,128)S(1)}) custom-call(s32[1]{0:T(128)} %bitcast.2.me_ref, s32[2,16384]{1,0:T(2,128)S(1)} %copy-done.6, bf16[32,32,512]{2,1,0:T(8,128)(2,1)S(1)} %all-to-all-done.1.arrived_ref), custom_call_target="tpu_custom_call" | custom-call | flops 536870912 | bytes 4194304 | tf_op jit(solution)/shard_map/sort_rows/pallas_call | solution.py:270
  89.6 1.0 copy-done.9
  90.6 0.6 copy-done.13
  91.2 0.0 reduce-scatter.2.cloned.1.call-update
  91.2 1.5 collective-permute-start.10
  92.8 3.0 %attend_later.1.later_ref = bf16[2,384,384]{2,1,0:T(8,128)(2,1)S(1)} custom-call(s32[1]{0:T(128)} %bitcast.2.me_ref, s32[2,16384]{1,0:T(2,128)S(1)} %copy-done.6, bf16[2,512,512]{2,1,0:T(8,128)(2,1)S(1)} %copy-done.10), custom_call_target="tpu_custom_call" | custom-call | flops 2147483648 | bytes 4194304 | tf_op jit(solution)/shard_map/attend_later/pallas_call | solution.py:421
  95.8 0.5 collective-permute-done.10.last_ref
  96.3 3.1 %attend_first.1 = bf16[32,40,256]{2,1,0:T(8,128)(2,1)} custom-call(s32[1]{0:T(128)} %bitcast.2.me_ref, s32[2,16384]{1,0:T(2,128)S(1)} %copy-done.6, s32[2,16384]{1,0:T(2,128)S(1)} %copy-done.6, bf16[2,512,512]{2,1,0:T(8,128)(2,1)S(1)} %copy-done.10, bf16[2,64,512]{2,1,0:T(8,128)(2,1)S(1)} %collective-permute-done.10.last_ref, s32[2,8,512]{2,1,0:T(8,128)S(1)} %copy-done.14, ...), custom_call_target="tpu_custom_call" | custom-call | flops 2147483648 | bytes 4194304 | tf_op jit(solution)/shard_map/attend_first/pallas_call | solution.py:449
  99.4 11.1 %all-to-all-start.2 = ((bf16[32,40,256]{2,1,0:T(8,128)(2,1)}), bf16[32,40,256]{2,1,0:T(8,128)(2,1)S(1)}, u32[]{:S(2)}, u32[]{:S(2)}) async-start(bf16[32,40,256]{2,1,0:T(8,128)(2,1)} %attend_first.1), calls=%async_computation.2 | async-start | bytes 1310720 | tf_op jit(solution)/shard_map/all_to_all | solution.py:572
  110.5 11.7 %reduce-scatter.2.cloned.1.call-done = bf16[1,2,32,16,256]{4,3,2,1,0:T(8,128)(2,1)} async-done(((bf16[4,2,32,16,256]{4,3,2,1,0:T(8,128)(2,1)}), bf16[1,2,32,16,256]{4,3,2,1,0:T(8,128)(2,1)}) %reduce-scatter.2.cloned.1.call-update) | async-done | bytes 524304 | tf_op jit(solution)/shard_map/reduce_scatter | solution.py:641
  122.2 1.1 dynamic-slice_bitcast_fusion.1
  123.3 0.1 collective-permute-start.12
  123.4 5.0 %all-to-all-done.2.got_ref = bf16[32,40,256]{2,1,0:T(8,128)(2,1)S(1)} async-done(((bf16[32,40,256]{2,1,0:T(8,128)(2,1)}), bf16[32,40,256]{2,1,0:T(8,128)(2,1)S(1)}, u32[]{:S(2)}, u32[]{:S(2)}) %all-to-all-start.2) | async-done | bytes 655392 | tf_op jit(solution)/shard_map/all_to_all | solution.py:572
  128.4 1.1 combine.1.own_ref
  129.5 1.8 %pad_maximum_fusion = bf16[32,2,16,256]{3,2,1,0:T(8,128)(2,1)} fusion(bf16[32,1,16,256]{3,2,1,0:T(8,128)(2,1)} %bitcast.9, bf16[32,1,16,256]{3,2,1,0:T(8,128)(2,1)S(1)} %get-tuple-element.51), kind=kLoop, calls=%fused_computation | loop fusion | flops 262144 | bytes 1048576 | tf_op jit(solution)/shard_map/stack | solution.py:657
  131.3 5.6 %all-to-all-start.3 = ((bf16[32,2,16,256]{3,2,1,0:T(8,128)(2,1)}), bf16[32,2,16,256]{3,2,1,0:T(8,128)(2,1)S(1)}, u32[]{:S(2)}, u32[]{:S(2)}) async-start(bf16[32,2,16,256]{3,2,1,0:T(8,128)(2,1)} %pad_maximum_fusion), calls=%async_computation.4 | async-start | bytes 1048576 | tf_op jit(solution)/shard_map/all_to_all | solution.py:572
  136.9 1.1 collective-permute-start.13
  138.0 1.2 collective-permute-start.11
  139.2 5.8 %collective-permute-done.13.next_ref = bf16[512,256]{1,0:T(8,128)(2,1)S(1)} collective-permute-done((bf16[512,256]{1,0:T(8,128)(2,1)S(1)}, bf16[512,256]{1,0:T(8,128)(2,1)S(1)}, u32[]{:S(2)}, u32[]{:S(2)}) %collective-permute-start.13) | collective-permute-done | bytes 262176 | tf_op jit(solution)/shard_map/ppermute | solution.py:581
  145.0 1.8 %collective-permute-done.11.prev_ref = bf16[512,256]{1,0:T(8,128)(2,1)S(1)} collective-permute-done((bf16[512,256]{1,0:T(8,128)(2,1)S(1)}, bf16[512,256]{1,0:T(8,128)(2,1)S(1)}, u32[]{:S(2)}, u32[]{:S(2)}) %collective-permute-start.11) | collective-permute-done | bytes 262176 | tf_op jit(solution)/shard_map/ppermute | solution.py:581
  146.8 0.4 collective-permute-start.15
  147.1 1.7 %collective-permute-start.14 = (bf16[256,256]{1,0:T(8,128)(2,1)S(1)}, bf16[256,256]{1,0:T(8,128)(2,1)S(1)}, u32[]{:S(2)}, u32[]{:S(2)}) collective-permute-start(bf16[256,256]{1,0:T(8,128)(2,1)S(1)} %slice.14), channel_id=1, source_target_pairs={{0,2},{1,3},{2,4},{3,5},{4,6},{5,7},{6,0},{7,1},{8,10},{9,11},{10,... | collective-permute-start | bytes 393224 | tf_op jit(solution)/shard_map/ppermute | solution.py:581
  148.9 2.9 %collective-permute-done.15.far_b_ref = bf16[256,256]{1,0:T(8,128)(2,1)S(1)} collective-permute-done((bf16[256,256]{1,0:T(8,128)(2,1)S(1)}, bf16[256,256]{1,0:T(8,128)(2,1)S(1)}, u32[]{:S(2)}, u32[]{:S(2)}) %collective-permute-start.15) | collective-permute-done | bytes 131104 | tf_op jit(solution)/shard_map/ppermute | solution.py:581
  151.8 1.5 collective-permute-done.14.far_a_ref
  153.3 1.3 project.1
  154.6 0.1 collective-permute-start.16
  154.7 1.5 collective-permute-done.16
  156.3 0.8 add_convert_fusion
  157.0 1.4 unpack_tokens.1
  (36 shorter events, 0.1 us)
Async XLA Ops:
  7.2 16.3 %copy-start = (bf16[256,2048]{1,0:T(8,128)(2,1)S(1)}, bf16[256,2048]{1,0:T(8,128)(2,1)}, u32[]{:S(2)}) copy-start(bf16[256,2048]{1,0:T(8,128)(2,1)} %refs_0_.1) | copy-start | bytes 3145732
  7.3 1.7 %copy-start.1 = (bf16[512,2048]{1,0:T(8,128)(2,1)S(1)}, bf16[512,2048]{1,0:T(8,128)(2,1)}, u32[]{:S(2)}) copy-start(bf16[512,2048]{1,0:T(8,128)(2,1)} %tokens_ref.1) | copy-start | bytes 6291460
  8.9 0.7 copy-start.2
  9.6 20.0 %copy-start.4 = (bf16[2048,256]{1,0:T(8,128)(2,1)S(1)}, bf16[2048,256]{1,0:T(8,128)(2,1)}, u32[]{:S(2)}) copy-start(bf16[2048,256]{1,0:T(8,128)(2,1)} %qk_ref.1) | copy-start | bytes 3145732
  9.6 20.0 %copy-start.6 = (s32[2,16384]{1,0:T(2,128)S(1)}, s32[2,16384]{1,0:T(2,128)}, u32[]{:S(2)}) copy-start(s32[2,16384]{1,0:T(2,128)} %earlier_ref.1) | copy-start | bytes 393220
  11.6 0.6 copy-start.7
  12.2 28.8 %all-to-all-start = ((bf16[32,16,512]{2,1,0:T(8,128)(2,1)}), bf16[32,16,512]{2,1,0:T(8,128)(2,1)S(1)}, u32[]{:S(2)}, u32[]{:S(2)}) async-start(bf16[32,16,512]{2,1,0:T(8,128)(2,1)} %bitcast.4), calls=%async_computation | async-start | bytes 1048576 | tf_op jit(solution)/shard_map/all_to_all | solution.py:572
  24.4 13.5 %collective-permute-start.2 = (bf16[256,512]{1,0:T(8,128)(2,1)}, bf16[256,512]{1,0:T(8,128)(2,1)S(1)}, u32[]{:S(2)}, u32[]{:S(2)}) collective-permute-start(bf16[256,512]{1,0:T(8,128)(2,1)} %get-tuple-element.48), channel_id=1, source_target_pairs={{0,4},{1,5},{2,6},{3,7},{4,0},{5,1},{6,2},{7,3},{8,12},{9,13},{10,... | collective-permute-start | bytes 786440 | tf_op jit(solution)/shard_map/ppermute | solution.py:581
  27.6 12.0 %collective-permute-start.1 = (bf16[256,512]{1,0:T(8,128)(2,1)}, bf16[256,512]{1,0:T(8,128)(2,1)S(1)}, u32[]{:S(2)}, u32[]{:S(2)}) collective-permute-start(bf16[256,512]{1,0:T(8,128)(2,1)} %get-tuple-element.49), channel_id=1, source_target_pairs={{0,6},{1,7},{2,0},{3,1},{4,2},{5,3},{6,4},{7,5},{8,14},{9,15},{10,... | collective-permute-start | bytes 786440 | tf_op jit(solution)/shard_map/ppermute | solution.py:581
  28.6 11.0 %collective-permute-start = (bf16[256,512]{1,0:T(8,128)(2,1)}, bf16[256,512]{1,0:T(8,128)(2,1)S(1)}, u32[]{:S(2)}, u32[]{:S(2)}) collective-permute-start(bf16[256,512]{1,0:T(8,128)(2,1)} %get-tuple-element.50), channel_id=1, source_target_pairs={{0,2},{1,3},{2,4},{3,5},{4,6},{5,7},{6,0},{7,1},{8,10},{9,11},{10,... | collective-permute-start | bytes 786440 | tf_op jit(solution)/shard_map/ppermute | solution.py:581
  29.6 1.6 copy-start.3
  31.2 1.2 copy-start.5
  37.2 0.6 copy-start.11
  41.0 46.9 %all-to-all-start.1 = ((bf16[32,32,512]{2,1,0:T(8,128)(2,1)}), bf16[32,32,512]{2,1,0:T(8,128)(2,1)S(1)}, u32[]{:S(2)}, u32[]{:S(2)}) async-start(bf16[32,32,512]{2,1,0:T(8,128)(2,1)} %bitcast.5), calls=%async_computation.1 | async-start | bytes 2097152 | tf_op jit(solution)/shard_map/all_to_all | solution.py:572
  49.4 72.8 %reduce-scatter.2.cloned.1.call-start = ((), (), s32[]{:S(2)}) async-start(), calls=%async_computation.5 | async-start | bytes 2621440 | tf_op jit(solution)/shard_map/reduce_scatter | solution.py:641
  49.4 1.9 %copy-start.15 = (bf16[2,2048,256]{2,1,0:T(8,128)(2,1)S(1)}, bf16[2,2048,256]{2,1,0:T(8,128)(2,1)}, u32[]{:S(2)}) copy-start(bf16[2,2048,256]{2,1,0:T(8,128)(2,1)} %refs_6_.1) | copy-start | bytes 6291460
  49.5 2.5 %copy-start.16 = (bf16[2,256,2048]{2,1,0:T(8,128)(2,1)S(1)}, bf16[2,256,2048]{2,1,0:T(8,128)(2,1)}, u32[]{:S(2)}) copy-start(bf16[2,256,2048]{2,1,0:T(8,128)(2,1)} %refs_7_.1) | copy-start | bytes 6291460
  52.1 28.0 %collective-permute-start.9 = (bf16[1,256,2048]{2,1,0:T(8,128)(2,1)S(1)}, bf16[1,256,2048]{2,1,0:T(8,128)(2,1)S(1)}, u32[]{:S(2)}, u32[]{:S(2)}) collective-permute-start(bf16[1,256,2048]{2,1,0:T(8,128)(2,1)S(1)} %constant_dynamic-slice_fusion), channel_id=1, source_target_pairs={{0,1},{1,0},{2,3},{3,2},{4,5},{5,4},{6,7},{7,6},{8,9},{9,8},{10,11... | collective-permute-start | bytes 3145736 | tf_op jit(solution)/shard_map/ppermute | solution.py:631
  52.2 27.9 %collective-permute-start.8 = (bf16[1,2048,256]{2,1,0:T(8,128)(2,1)S(1)}, bf16[1,2048,256]{2,1,0:T(8,128)(2,1)S(1)}, u32[]{:S(2)}, u32[]{:S(2)}) collective-permute-start(bf16[1,2048,256]{2,1,0:T(8,128)(2,1)S(1)} %constant_dynamic-slice_fusion.1), channel_id=1, source_target_pairs={{0,1},{1,0},{2,3},{3,2},{4,5},{5,4},{6,7},{7,6},{8,9},{9,8},{10,11... | collective-permute-start | bytes 3145736 | tf_op jit(solution)/shard_map/ppermute | solution.py:631
  52.7 27.4 %collective-permute-start.7 = (bf16[1,2048,256]{2,1,0:T(8,128)(2,1)S(1)}, bf16[1,2048,256]{2,1,0:T(8,128)(2,1)S(1)}, u32[]{:S(2)}, u32[]{:S(2)}) collective-permute-start(bf16[1,2048,256]{2,1,0:T(8,128)(2,1)S(1)} %constant_dynamic-slice_fusion.2), channel_id=1, source_target_pairs={{0,1},{1,0},{2,3},{3,2},{4,5},{5,4},{6,7},{7,6},{8,9},{9,8},{10,11... | collective-permute-start | bytes 3145736 | tf_op jit(solution)/shard_map/ppermute | solution.py:631
  52.8 14.4 %collective-permute-start.4 = (bf16[32,16,512]{2,1,0:T(8,128)(2,1)S(1)}, bf16[32,16,512]{2,1,0:T(8,128)(2,1)S(1)}, u32[]{:S(2)}, u32[]{:S(2)}) collective-permute-start(bf16[32,16,512]{2,1,0:T(8,128)(2,1)S(1)} %all-to-all-done.refs_0_), channel_id=1, source_target_pairs={{0,6},{1,7},{2,0},{3,1},{4,2},{5,3},{6,4},{7,5},{8,14},{9,15},{10,... | collective-permute-start | bytes 1572872 | tf_op jit(solution)/shard_map/ppermute | solution.py:581
  55.4 15.6 %collective-permute-start.3 = (bf16[32,16,512]{2,1,0:T(8,128)(2,1)S(1)}, bf16[32,16,512]{2,1,0:T(8,128)(2,1)S(1)}, u32[]{:S(2)}, u32[]{:S(2)}) collective-permute-start(bf16[32,16,512]{2,1,0:T(8,128)(2,1)S(1)} %all-to-all-done.refs_0_), channel_id=1, source_target_pairs={{0,2},{1,3},{2,4},{3,5},{4,6},{5,7},{6,0},{7,1},{8,10},{9,11},{10,... | collective-permute-start | bytes 1572872 | tf_op jit(solution)/shard_map/ppermute | solution.py:581
  67.2 9.1 %collective-permute-start.6 = (bf16[16,16,512]{2,1,0:T(8,128)(2,1)S(1)}, bf16[16,16,512]{2,1,0:T(8,128)(2,1)S(1)}, u32[]{:S(2)}, u32[]{:S(2)}) collective-permute-start(bf16[16,16,512]{2,1,0:T(8,128)(2,1)S(1)} %slice.17), channel_id=1, source_target_pairs={{0,6},{1,7},{2,0},{3,1},{4,2},{5,3},{6,4},{7,5},{8,14},{9,15},{10,... | collective-permute-start | bytes 786440 | tf_op jit(solution)/shard_map/ppermute | solution.py:581
  71.0 9.0 %collective-permute-start.5 = (bf16[16,16,512]{2,1,0:T(8,128)(2,1)S(1)}, bf16[16,16,512]{2,1,0:T(8,128)(2,1)S(1)}, u32[]{:S(2)}, u32[]{:S(2)}) collective-permute-start(bf16[16,16,512]{2,1,0:T(8,128)(2,1)S(1)} %slice.16), channel_id=1, source_target_pairs={{0,2},{1,3},{2,4},{3,5},{4,6},{5,7},{6,0},{7,1},{8,10},{9,11},{10,... | collective-permute-start | bytes 786440 | tf_op jit(solution)/shard_map/ppermute | solution.py:581
  89.6 1.0 copy-start.9
  90.6 0.6 copy-start.13
  91.2 1.6 copy-start.10
  91.2 5.0 %collective-permute-start.10 = (bf16[2,64,512]{2,1,0:T(8,128)(2,1)S(1)}, bf16[2,64,512]{2,1,0:T(8,128)(2,1)S(1)}, u32[]{:S(2)}, u32[]{:S(2)}) collective-permute-start(bf16[2,64,512]{2,1,0:T(8,128)(2,1)S(1)} %get-tuple-element.35), channel_id=1, source_target_pairs={{0,8},{8,16},{16,24},{24,32},{32,40},{40,48},{48,56},{56,64},{64,7... | collective-permute-start | bytes 393224 | tf_op jit(solution)/shard_map/ppermute | solution.py:648
  92.8 3.5 %copy-start.14 = (s32[2,8,512]{2,1,0:T(8,128)S(1)}, s32[2,8,512]{2,1,0:T(8,128)}, u32[]{:S(2)}) copy-start(s32[2,8,512]{2,1,0:T(8,128)} %copy-done.13) | copy-start | bytes 98308
  99.3 29.1 %copy-start.12 = (s32[2,8,512]{2,1,0:T(8,128)S(1)}, s32[2,8,512]{2,1,0:T(8,128)}, u32[]{:S(2)}) copy-start(s32[2,8,512]{2,1,0:T(8,128)} %copy-done.11) | copy-start | bytes 98308
  99.4 29.1 %all-to-all-start.2 = ((bf16[32,40,256]{2,1,0:T(8,128)(2,1)}), bf16[32,40,256]{2,1,0:T(8,128)(2,1)S(1)}, u32[]{:S(2)}, u32[]{:S(2)}) async-start(bf16[32,40,256]{2,1,0:T(8,128)(2,1)} %attend_first.1), calls=%async_computation.2 | async-start | bytes 1310720 | tf_op jit(solution)/shard_map/all_to_all | solution.py:572
  123.3 6.2 %collective-permute-start.12 = (bf16[32,16,256]{2,1,0:T(8,128)(2,1)S(1)}, bf16[32,16,256]{2,1,0:T(8,128)(2,1)}, u32[]{:S(2)}, u32[]{:S(2)}) collective-permute-start(bf16[32,16,256]{2,1,0:T(8,128)(2,1)S(1)} %get-tuple-element.52), channel_id=1, source_target_pairs={{0,1},{1,0},{2,3},{3,2},{4,5},{5,4},{6,7},{7,6},{8,9},{9,8},{10,11... | collective-permute-start | bytes 786440 | tf_op jit(solution)/shard_map/ppermute | solution.py:656
  131.3 25.7 %all-to-all-start.3 = ((bf16[32,2,16,256]{3,2,1,0:T(8,128)(2,1)}), bf16[32,2,16,256]{3,2,1,0:T(8,128)(2,1)S(1)}, u32[]{:S(2)}, u32[]{:S(2)}) async-start(bf16[32,2,16,256]{3,2,1,0:T(8,128)(2,1)} %pad_maximum_fusion), calls=%async_computation.4 | async-start | bytes 1048576 | tf_op jit(solution)/shard_map/all_to_all | solution.py:572
  136.9 8.1 %collective-permute-start.13 = (bf16[512,256]{1,0:T(8,128)(2,1)S(1)}, bf16[512,256]{1,0:T(8,128)(2,1)S(1)}, u32[]{:S(2)}, u32[]{:S(2)}) collective-permute-start(bf16[512,256]{1,0:T(8,128)(2,1)S(1)} %combine.1.own_ref), channel_id=1, source_target_pairs={{0,6},{1,7},{2,0},{3,1},{4,2},{5,3},{6,4},{7,5},{8,14},{9,15},{10,... | collective-permute-start | bytes 786440 | tf_op jit(solution)/shard_map/ppermute | solution.py:581
  138.0 8.7 %collective-permute-start.11 = (bf16[512,256]{1,0:T(8,128)(2,1)S(1)}, bf16[512,256]{1,0:T(8,128)(2,1)S(1)}, u32[]{:S(2)}, u32[]{:S(2)}) collective-permute-start(bf16[512,256]{1,0:T(8,128)(2,1)S(1)} %combine.1.own_ref), channel_id=1, source_target_pairs={{0,2},{1,3},{2,4},{3,5},{4,6},{5,7},{6,0},{7,1},{8,10},{9,11},{10,... | collective-permute-start | bytes 786440 | tf_op jit(solution)/shard_map/ppermute | solution.py:581
  146.7 10.3 %copy-start.8 = (s32[8,512]{1,0:T(8,128)S(1)}, s32[8,512]{1,0:T(8,128)}, u32[]{:S(2)}) copy-start(s32[8,512]{1,0:T(8,128)} %copy-done.7) | copy-start | bytes 49156
  146.8 5.0 %collective-permute-start.15 = (bf16[256,256]{1,0:T(8,128)(2,1)S(1)}, bf16[256,256]{1,0:T(8,128)(2,1)S(1)}, u32[]{:S(2)}, u32[]{:S(2)}) collective-permute-start(bf16[256,256]{1,0:T(8,128)(2,1)S(1)} %slice.15), channel_id=1, source_target_pairs={{0,6},{1,7},{2,0},{3,1},{4,2},{5,3},{6,4},{7,5},{8,14},{9,15},{10,... | collective-permute-start | bytes 393224 | tf_op jit(solution)/shard_map/ppermute | solution.py:581
  147.1 6.2 %collective-permute-start.14 = (bf16[256,256]{1,0:T(8,128)(2,1)S(1)}, bf16[256,256]{1,0:T(8,128)(2,1)S(1)}, u32[]{:S(2)}, u32[]{:S(2)}) collective-permute-start(bf16[256,256]{1,0:T(8,128)(2,1)S(1)} %slice.14), channel_id=1, source_target_pairs={{0,2},{1,3},{2,4},{3,5},{4,6},{5,7},{6,0},{7,1},{8,10},{9,11},{10,... | collective-permute-start | bytes 393224 | tf_op jit(solution)/shard_map/ppermute | solution.py:581
  154.6 1.6 collective-permute-start.16
Sparse Core Ops, SparseCore 0:
  91.3 30.8 reduce-scatter.1

commit v5 on v4

--- a/solution.py
+++ b/solution.py
@@ -160,73 +160,75 @@
     )(where, ids, tokens)
 
 
-def experts_kernel(where_ref, *refs):
+def experts_kernel(where_ref, x_ref, *refs):
     step = pl.program_id(0)
-    shards, far_refs, weights = refs[0:3], refs[3:5], refs[5:11]
-    out_ref, total_ref = refs[11:]
-    peers, capacity, part = shards[0].shape
+    weights, (out_ref, total_ref, hidden_ref) = refs[:-3], refs[-3:]
+    parts = pl.num_programs(0) // 2
+    _, peers, capacity, part = x_ref.shape
     rows = peers * capacity
     ups = (weights[0], weights[1], weights[3], weights[4])
 
-    def add(x, start):
+    @pl.when(step == 0)
+    def _():
         for index, weight in enumerate(ups):
-            product = dot(x, weight[0])
-            total_ref[index] = product if start else total_ref[index] + product
-
-    for turn, shard in enumerate(shards):
-
-        @pl.when(step == turn)
-        def _(shard=shard, start=turn == 0):
-            add(shard[...].reshape(rows, part), start)
-
-    @pl.when(step == len(shards))
+            total_ref[index] = dot(x_ref[0].reshape(rows, part), weight[0])
+
+    @pl.when((step > 0) & (step < parts))
     def _():
-        add(jnp.concatenate([ref[...].reshape(rows // 2, part) for ref in far_refs], axis=0), False)
-        hiddens = []
+        for index, weight in enumerate(ups):
+            total_ref[index] += dot(x_ref[0].reshape(rows, part), weight[0])
+
+    @pl.when(step == parts - 1)
+    def _():
         for side in range(EXP_DEV):
             gate, up_val = total_ref[2 * side], total_ref[2 * side + 1]
-            hiddens.append((gate / (1.0 + jnp.exp(-gate)) * up_val).astype(BF16))
+            hidden_ref[side] = (gate / (1.0 + jnp.exp(-gate)) * up_val).astype(BF16)
+
+    @pl.when(step >= parts)
+    def _():
+        piece = dot(hidden_ref[0], weights[2][0]) + dot(hidden_ref[1], weights[5][0])
+        piece = piece.astype(BF16)
         half = part // EXP_DEV
-        for index in range(out_ref.shape[0]):
-            at = index * part
-            piece = dot(hiddens[0], weights[2][0, :, at : at + part])
-            piece = (piece + dot(hiddens[1], weights[5][0, :, at : at + part])).astype(BF16)
-            for side in range(EXP_DEV):
-                columns = piece[:, side * half : (side + 1) * half]
-                out_ref[index, side] = columns.reshape(peers, capacity, half)
-
-
-def run_experts(where, shards, far, own, sibling):
-    peers, capacity, part = shards[0].shape
+        for side in range(EXP_DEV):
+            columns = piece[:, side * half : (side + 1) * half]
+            out_ref[0, side] = columns.reshape(peers, capacity, half)
+
+
+def run_experts(where, x, own, sibling):
+    parts, peers, capacity, part = x.shape
     width, hidden = own[0].shape[1:]
-    chips = width // part
-    out = (chips, EXP_DEV, peers, capacity, part // EXP_DEV)
+    out = (parts, EXP_DEV, peers, capacity, part // EXP_DEV)
     rows = peers * capacity
 
-    def rows_of(i, e):
-        ahead = jnp.where(i == 0, 0, jnp.where(i == 1, chips - 1, jnp.where(i == 2, 1, 2)))
-        return (e[0] + ahead) % chips
-
-    up_block, down_block = (1, part, hidden), (1, hidden, width)
-    own_up = pl.BlockSpec(up_block, lambda i, e: (e[1], rows_of(i, e), 0))
-    sibling_up = pl.BlockSpec(up_block, lambda i, e: (0, rows_of(i, e), 0))
-    own_down = pl.BlockSpec(down_block, lambda i, e: (e[1], 0, 0))
-    sibling_down = pl.BlockSpec(down_block, lambda i, e: (0, 0, 0))
+    def early(i):
+        return jnp.minimum(i, parts - 1)
+
+    def late(i):
+        return jnp.maximum(i - parts, 0)
+
+    up_block, down_block = (1, part, hidden), (1, hidden, part)
+    own_up = pl.BlockSpec(up_block, lambda i, e: (e[1], early(i), 0))
+    sibling_up = pl.BlockSpec(up_block, lambda i, e: (0, early(i), 0))
+    own_down = pl.BlockSpec(down_block, lambda i, e: (e[1], 0, late(i)))
+    sibling_down = pl.BlockSpec(down_block, lambda i, e: (0, 0, late(i)))
     return pl.pallas_call(
         experts_kernel,
         grid_spec=pltpu.PrefetchScalarGridSpec(
             num_scalar_prefetch=1,
-            grid=(len(shards) + 1,),
-            in_specs=[pl.BlockSpec(x.shape, lambda i, e: (0, 0, 0)) for x in (*shards, *far)]
+            grid=(2 * parts,),
+            in_specs=[pl.BlockSpec((1, *x.shape[1:]), lambda i, e: (early(i), 0, 0, 0))]
             + [own_up, own_up, own_down, sibling_up, sibling_up, sibling_down],
-            out_specs=pl.BlockSpec(out, lambda i, e: (0, 0, 0, 0, 0)),
-            scratch_shapes=[pltpu.VMEM((4, rows, hidden), F32)],
+            out_specs=pl.BlockSpec((1, *out[1:]), lambda i, e: (late(i), 0, 0, 0, 0)),
+            scratch_shapes=[
+                pltpu.VMEM((2 * EXP_DEV, rows, hidden), F32),
+                pltpu.VMEM((EXP_DEV, rows, hidden), BF16),
+            ],
         ),
         out_shape=jax.ShapeDtypeStruct(out, BF16),
         cost_estimate=cost(12 * rows * width * hidden, 10 << 20),
         compiler_params=BIG,
         name="experts",
-    )(where, *shards, *far, *own, *sibling)
+    )(where, x, *own, *sibling)
 
 
 def unpack_tokens_kernel(back_ref, slot_ref, out_ref):
@@ -581,14 +583,6 @@
     return lax.ppermute(x, "exp", pairs)
 
 
-def spread(x, chips, ready=()):
-    half = x.shape[0] // 2
-    before, behind = hop(x, 1, chips), hop(x, -1, chips)
-    before, behind = (after(side, *ready) if ready else side for side in (before, behind))
-    far = (hop(before[:half], 1, chips), hop(behind[half:], -1, chips))
-    return (x, before, behind), far
-
-
 def after(x, *done):
     return lax.optimization_barrier((x, *done))[0]
 
@@ -633,9 +627,9 @@
         )
         for weight in own
     ]
-    shards, far = spread(received, chips)
+    gathered = lax.all_gather(received, "exp", axis=0, tiled=False, axis_index_groups=lines)
     arrived = exchange(outgoing.reshape(peers, rounds * per_peer, outgoing.shape[1]), "seq")
-    expert_part = run_experts(where, shards, far, own, sibling)
+    expert_part = run_experts(where, gathered, own, sibling)
     arrived = after(arrived, expert_part)
     rows, last, row_slot = sort_rows(me, perms, arrived, length)
     expert_rows = lax.psum_scatter(
@@ -656,9 +650,17 @@
     taken = lax.ppermute(given, "exp", siblings)
     expert_rows = jnp.stack([kept, taken], axis=1)
     mixed_heads = combine(got, slot_token)
-    expert_back = exchange(after(expert_rows, mixed_heads), "seq")
-    heads, far_heads = spread(mixed_heads, chips, (expert_rows,))
-    attn_kept, attn_given = project(where, (*heads, *far_heads), w_out, columns)
+    before, behind = hop(mixed_heads, 1, chips), hop(mixed_heads, -1, chips)
+    expert_back = exchange(after(expert_rows, before, behind), "seq")
+    middle = length // 2
+    heads = (
+        mixed_heads,
+        before,
+        behind,
+        hop(before[:middle], 1, chips),
+        hop(behind[middle:], -1, chips),
+    )
+    attn_kept, attn_given = project(where, heads, w_out, columns)
     attended = attn_kept + lax.ppermute(attn_given, "exp", siblings).astype(F32)
     attended = attended.astype(BF16)
     expert_back = after(expert_back, attended)

time: 168 us -> 171 us (1.018); the launches traced: 165 us -> 170 us
  starting transfers between devices: 55 us -> 50.1 us
  local copies, waits for them, and re-layouts: 12.6 us -> 17.3 us
  waiting for transfers between devices: 54.4 us -> 57.9 us
  Pallas kernels: 26.2 us -> 28 us
    ppermute x11 -> x7, waiting for transfers between devices: 34.3 us -> 10.7 us  [hop(): return lax.ppermute(x, 'exp', pairs)]
    all_gather x0 -> x1, waiting for transfers between devices: none -> 15 us  [body(): lax.all_gather(received, 'exp', axis=0, tiled=False, axis_index_groups=li...]
    all_to_all x4, waiting for transfers between devices: 6.43 us -> 13.5 us  [exchange(): return lax.all_to_all(x, axis, split_axis=0, concat_axis=0, tiled=True)]
    ppermute x11 -> x7, starting transfers between devices: 16.3 us -> 9.5 us  [hop(): return lax.ppermute(x, 'exp', pairs)]
    unnamed x34 -> x48, local copies, waits for them, and re-layouts: 8.97 us -> 13 us
    ppermute x3, waiting for transfers between devices: 0.01 us -> 4.07 us  [body(): lax.ppermute(lax.dynamic_slice_in_dim(after(weight, received), 1 - core,...]
    pallas_call x1, Pallas kernels: 7.8 us -> 9.55 us  [run_experts(): pl.pallas_call(experts_kernel, grid_spec=pltpu.PrefetchScalarGridSpec(num...]
  transfers between devices with their start and end apart: 22 -> 19, of which waited for: 13 -> 15; matrix products, arithmetic and copies ran while one was open for 3% -> 4% of each run, Pallas kernels for 13% -> 13%
where the time goes in v5:
time: 171 us; the launch traced here: 170 us
  waiting for transfers between devices  57.9 us (34%)
  starting transfers between devices  50.1 us (29%)
  Pallas kernels  28 us (16%)
  local copies, waits for them, and re-layouts  17.3 us (10%)
  between operations  14.3 us (8%)
  other arithmetic  2.65 us (2%)
    all_to_all x4, starting transfers between devices, exchange(): return lax.all_to_all(x, axis, split_axis=0, concat_axis=0, tiled=True)  37.9 us
    all_gather x1, waiting for transfers between devices, body(): lax.all_gather(received, 'exp', axis=0, tiled=False, axis_index_groups=li...  15 us
    all_to_all x4, waiting for transfers between devices, exchange(): return lax.all_to_all(x, axis, split_axis=0, concat_axis=0, tiled=True)  13.5 us
    unnamed x48, local copies, waits for them, and re-layouts  13 us
    reduce_scatter x1, waiting for transfers between devices, body(): lax.psum_scatter(after(expert_part, last), 'exp', scatter_dimension=0, ti...  12.4 us
    ppermute x7, waiting for transfers between devices, hop(): return lax.ppermute(x, 'exp', pairs)  10.7 us
    pallas_call x1, Pallas kernels, run_experts(): pl.pallas_call(experts_kernel, grid_spec=pltpu.PrefetchScalarGridSpec(num...  9.55 us
    ppermute x7, starting transfers between devices, hop(): return lax.ppermute(x, 'exp', pairs)  9.5 us
  transfers between devices with their start and end apart: 19, of which 15 were waited for; matrix products, arithmetic and copies ran while one was open for 4% of the time, Pallas kernels for 13%

profile of v5, /device:TPU:32, one launch (start us, length us, event | category | flops | bytes accessed | tf_op | source)
XLA Modules:
  0.0 170.4 jit_solution(14642935065182713326)
XLA Ops:
  7.2 0.1 pad_add_fusion.where_ref
  7.3 1.7 copy-done.1
  8.9 0.7 copy-done.10
  9.6 2.0 %pack_tokens.1 = (bf16[512,512]{1,0:T(8,128)(2,1)}, s32[8,512]{1,0:T(8,128)S(1)}) custom-call(s32[2]{0:T(128)S(1)} %pad_add_fusion.where_ref, s32[1,512]{1,0:T(1,128)S(1)} %bitcast.15, bf16[512,2048]{1,0:T(8,128)(2,1)S(1)} %copy-done.1), custom_call_target="tpu_custom_call" | custom-call | flops 268435456 | bytes 2097152 | tf_op jit(solution)/shard_map/pack_tokens/pallas_call | solution.py:139
  11.6 11.2 %all-to-all-start = ((bf16[32,16,512]{2,1,0:T(8,128)(2,1)}), bf16[32,16,512]{2,1,0:T(8,128)(2,1)S(1)}, u32[]{:S(2)}, u32[]{:S(2)}) async-start(bf16[32,16,512]{2,1,0:T(8,128)(2,1)} %bitcast.4), calls=%async_computation | async-start | bytes 1048576 | tf_op jit(solution)/shard_map/all_to_all | solution.py:574
  22.8 0.0 all-gather.3.cloned.1.call-start
  22.9 0.9 constant_dynamic-slice_fusion.3
  23.8 3.2 %collective-permute-start.2 = (bf16[256,512]{1,0:T(8,128)(2,1)}, bf16[256,512]{1,0:T(8,128)(2,1)S(1)}, u32[]{:S(2)}, u32[]{:S(2)}) collective-permute-start(bf16[256,512]{1,0:T(8,128)(2,1)} %get-tuple-element.44), channel_id=1, source_target_pairs={{0,4},{1,5},{2,6},{3,7},{4,0},{5,1},{6,2},{7,3},{8,12},{9,13},{10,... | collective-permute-start | bytes 786440 | tf_op jit(solution)/shard_map/ppermute | solution.py:583
  27.0 1.1 collective-permute-start.1
  28.1 1.0 collective-permute-start
  29.1 1.6 copy-done.11
  30.6 1.2 copy-done.13
  31.9 4.8 %pack_rows.1 = (bf16[1024,512]{1,0:T(8,128)(2,1)}, s32[2,8,512]{2,1,0:T(8,128)S(1)}) custom-call(s32[1]{0:T(128)} %bitcast.2.me_ref, s32[2,16384]{1,0:T(2,128)S(1)} %copy-done.14, bf16[512,2048]{1,0:T(8,128)(2,1)S(1)} %copy-done.11, bf16[2048,256]{1,0:T(8,128)(2,1)S(1)} %copy-done.12, bf16[2048,256]{1,0:T(8,128)(2,1)S(1)} %copy-done.13), custom_call_target="tpu_custom_call" | custom-call | flops 1610612736 | bytes 6291456 | tf_op jit(solution)/shard_map/pack_rows/pallas_call | solution.py:89
  36.7 0.6 copy-done.19
  37.3 1.7 %collective-permute-done.1.refs_2_ = bf16[256,512]{1,0:T(8,128)(2,1)S(1)} collective-permute-done((bf16[256,512]{1,0:T(8,128)(2,1)}, bf16[256,512]{1,0:T(8,128)(2,1)S(1)}, u32[]{:S(2)}, u32[]{:S(2)}) %collective-permute-start.1) | collective-permute-done | bytes 262176 | tf_op jit(solution)/shard_map/ppermute | solution.py:583
  39.0 1.4 all-to-all-done
  40.4 0.8 copy-done.23
  41.2 0.0 all-gather.3.cloned.1.call-update
  41.3 8.5 %all-to-all-start.1 = ((bf16[32,32,512]{2,1,0:T(8,128)(2,1)}), bf16[32,32,512]{2,1,0:T(8,128)(2,1)S(1)}, u32[]{:S(2)}, u32[]{:S(2)}) async-start(bf16[32,32,512]{2,1,0:T(8,128)(2,1)} %bitcast.5), calls=%async_computation.1 | async-start | bytes 2097152 | tf_op jit(solution)/shard_map/all_to_all | solution.py:574
  49.8 0.0 reduce-scatter.2.cloned.1.call-start
  49.8 1.4 constant_dynamic-slice_fusion.2
  51.3 0.4 copy-done.21
  51.7 0.1 constant_dynamic-slice_fusion.1
  51.8 0.6 copy-done.22
  52.4 0.1 constant_dynamic-slice_fusion
  52.5 0.1 collective-permute-start.5
  52.6 0.5 collective-permute-start.4
  53.1 0.1 collective-permute-start.3
  53.2 2.0 %collective-permute-done.5.refs_5_ = bf16[1,256,2048]{2,1,0:T(8,128)(2,1)S(1)} collective-permute-done((bf16[1,256,2048]{2,1,0:T(8,128)(2,1)S(1)}, bf16[1,256,2048]{2,1,0:T(8,128)(2,1)S(1)}, u32[]{:S(2)}, u32[]{:S(2)}) %collective-permute-start.5) | collective-permute-done | bytes 1048608 | tf_op jit(solution)/shard_map/ppermute | solution.py:625
  55.3 1.5 collective-permute-done.4.refs_4_
  56.8 1.0 copy-done.2
  57.8 0.5 collective-permute-done.3.refs_3_
  58.3 1.0 copy-done.4
  59.3 15.0 %all-gather.3.cloned.1.call-done = bf16[128,16,512]{2,1,0:T(8,128)(2,1)} async-done(((bf16[32,16,512]{2,1,0:T(8,128)(2,1)}), bf16[128,16,512]{2,1,0:T(8,128)(2,1)}) %all-gather.3.cloned.1.call-update) | async-done | bytes 2097168 | tf_op jit(solution)/shard_map/all_gather | solution.py:630
  74.3 1.2 copy-done.3
  75.5 1.2 copy-done.5
  76.7 9.6 %experts.1 = bf16[4,2,32,16,256]{4,3,2,1,0:T(8,128)(2,1)} custom-call(s32[2]{0:T(128)S(1)} %pad_add_fusion.where_ref, bf16[4,32,16,512]{3,2,1,0:T(8,128)(2,1)} %bitcast.16, bf16[2,2048,256]{2,1,0:T(8,128)(2,1)} %refs_0_.2, bf16[2,2048,256]{2,1,0:T(8,128)(2,1)} %refs_1_.1, bf16[2,256,2048]{2,1,0:T(8,128)(2,1)} %refs_2_.1, ...), custom_call_target="tpu_custom_call" | custom-call | flops 3221225472 | bytes 10485760 | tf_op jit(solution)/shard_map/experts/pallas_call | solution.py:214
  86.3 1.7 %sort_rows.1 = (bf16[2,512,512]{2,1,0:T(8,128)(2,1)S(1)}, bf16[2,64,512]{2,1,0:T(8,128)(2,1)S(1)}, s32[2,8,512]{2,1,0:T(8,128)S(1)}) custom-call(s32[1]{0:T(128)} %bitcast.2.me_ref, s32[2,16384]{1,0:T(2,128)S(1)} %copy-done.14, bf16[32,32,512]{2,1,0:T(8,128)(2,1)S(1)} %all-to-all-done.1.arrived_ref), custom_call_target="tpu_custom_call" | custom-call | flops 536870912 | bytes 4194304 | tf_op jit(solution)/shard_map/sort_rows/pallas_call | solution.py:272
  88.0 1.0 copy-done.17
  89.0 1.8 %collective-permute-start.6 = (bf16[2,64,512]{2,1,0:T(8,128)(2,1)S(1)}, bf16[2,64,512]{2,1,0:T(8,128)(2,1)S(1)}, u32[]{:S(2)}, u32[]{:S(2)}) collective-permute-start(bf16[2,64,512]{2,1,0:T(8,128)(2,1)S(1)} %get-tuple-element.33), channel_id=1, source_target_pairs={{0,8},{8,16},{16,24},{24,32},{32,40},{40,48},{48,56},{56,64},{64,7... | collective-permute-start | bytes 393224 | tf_op jit(solution)/shard_map/ppermute | solution.py:642
  90.8 3.0 %attend_later.1.later_ref = bf16[2,384,384]{2,1,0:T(8,128)(2,1)S(1)} custom-call(s32[1]{0:T(128)} %bitcast.2.me_ref, s32[2,16384]{1,0:T(2,128)S(1)} %copy-done.14, bf16[2,512,512]{2,1,0:T(8,128)(2,1)S(1)} %copy-done.18), custom_call_target="tpu_custom_call" | custom-call | flops 2147483648 | bytes 4194304 | tf_op jit(solution)/shard_map/attend_later/pallas_call | solution.py:423
  93.8 0.7 collective-permute-done.6.last_ref
  94.5 3.1 %attend_first.1 = bf16[32,40,256]{2,1,0:T(8,128)(2,1)} custom-call(s32[1]{0:T(128)} %bitcast.2.me_ref, s32[2,16384]{1,0:T(2,128)S(1)} %copy-done.14, s32[2,16384]{1,0:T(2,128)S(1)} %copy-done.14, bf16[2,512,512]{2,1,0:T(8,128)(2,1)S(1)} %copy-done.18, bf16[2,64,512]{2,1,0:T(8,128)(2,1)S(1)} %collective-permute-done.6.last_ref, ...), custom_call_target="tpu_custom_call" | custom-call | flops 2147483648 | bytes 4194304 | tf_op jit(solution)/shard_map/attend_first/pallas_call | solution.py:451
  97.6 11.4 %all-to-all-start.2 = ((bf16[32,40,256]{2,1,0:T(8,128)(2,1)}), bf16[32,40,256]{2,1,0:T(8,128)(2,1)S(1)}, u32[]{:S(2)}, u32[]{:S(2)}) async-start(bf16[32,40,256]{2,1,0:T(8,128)(2,1)} %attend_first.1), calls=%async_computation.2 | async-start | bytes 1310720 | tf_op jit(solution)/shard_map/all_to_all | solution.py:574
  109.0 12.4 %reduce-scatter.2.cloned.1.call-done = bf16[1,2,32,16,256]{4,3,2,1,0:T(8,128)(2,1)} async-done(((bf16[4,2,32,16,256]{4,3,2,1,0:T(8,128)(2,1)}), bf16[1,2,32,16,256]{4,3,2,1,0:T(8,128)(2,1)}) %reduce-scatter.2.cloned.1.call-update) | async-done | bytes 524304 | tf_op jit(solution)/shard_map/reduce_scatter | solution.py:635
  121.4 1.8 %dynamic-slice_bitcast_fusion.1 = (bf16[32,1,16,256]{3,2,1,0:T(8,128)(2,1)S(1)}, bf16[32,16,256]{2,1,0:T(8,128)(2,1)}) fusion(bf16[2,32,16,256]{3,2,1,0:T(8,128)(2,1)} %bitcast.17, s32[]{:T(128)S(6)} %select_n.51, s32[]{:T(128)S(6)} %select_n.50), kind=kLoop, calls=%fused_computation.3 | loop fusion | bytes 1048584 | tf_op jit(solution)/shard_map/stack | solution.py:651
  123.2 5.3 %all-to-all-done.2.got_ref = bf16[32,40,256]{2,1,0:T(8,128)(2,1)S(1)} async-done(((bf16[32,40,256]{2,1,0:T(8,128)(2,1)}), bf16[32,40,256]{2,1,0:T(8,128)(2,1)S(1)}, u32[]{:S(2)}, u32[]{:S(2)}) %all-to-all-start.2) | async-done | bytes 655392 | tf_op jit(solution)/shard_map/all_to_all | solution.py:574
  128.5 1.1 combine.1.own_ref
  129.6 0.9 collective-permute-start.8
  130.5 1.2 collective-permute-start.7
  131.7 1.8 %pad_maximum_fusion = bf16[32,2,16,256]{3,2,1,0:T(8,128)(2,1)} fusion(bf16[32,1,16,256]{3,2,1,0:T(8,128)(2,1)} %bitcast.10, bf16[32,1,16,256]{3,2,1,0:T(8,128)(2,1)S(1)} %get-tuple-element.47), kind=kLoop, calls=%fused_computation | loop fusion | flops 262144 | bytes 1048576 | tf_op jit(solution)/shard_map/stack | solution.py:651
  133.5 2.5 %collective-permute-done.8.next_ref = bf16[512,256]{1,0:T(8,128)(2,1)S(1)} collective-permute-done((bf16[512,256]{1,0:T(8,128)(2,1)S(1)}, bf16[512,256]{1,0:T(8,128)(2,1)S(1)}, u32[]{:S(2)}, u32[]{:S(2)}) %collective-permute-start.8) | collective-permute-done | bytes 262176 | tf_op jit(solution)/shard_map/ppermute | solution.py:583
  136.0 2.0 %collective-permute-done.7.prev_ref = bf16[512,256]{1,0:T(8,128)(2,1)S(1)} collective-permute-done((bf16[512,256]{1,0:T(8,128)(2,1)S(1)}, bf16[512,256]{1,0:T(8,128)(2,1)S(1)}, u32[]{:S(2)}, u32[]{:S(2)}) %collective-permute-start.7) | collective-permute-done | bytes 262176 | tf_op jit(solution)/shard_map/ppermute | solution.py:583
  138.0 6.8 %all-to-all-start.3 = ((bf16[32,2,16,256]{3,2,1,0:T(8,128)(2,1)}), bf16[32,2,16,256]{3,2,1,0:T(8,128)(2,1)S(1)}, u32[]{:S(2)}, u32[]{:S(2)}) async-start(bf16[32,2,16,256]{3,2,1,0:T(8,128)(2,1)} %pad_maximum_fusion), calls=%async_computation.4 | async-start | bytes 1048576 | tf_op jit(solution)/shard_map/all_to_all | solution.py:574
  144.9 0.4 collective-permute-start.10
  145.3 1.8 %collective-permute-start.9 = (bf16[256,256]{1,0:T(8,128)(2,1)S(1)}, bf16[256,256]{1,0:T(8,128)(2,1)S(1)}, u32[]{:S(2)}, u32[]{:S(2)}) collective-permute-start(bf16[256,256]{1,0:T(8,128)(2,1)S(1)} %slice.8), channel_id=1, source_target_pairs={{0,2},{1,3},{2,4},{3,5},{4,6},{5,7},{6,0},{7,1},{8,10},{9,11},{10,... | collective-permute-start | bytes 393224 | tf_op jit(solution)/shard_map/ppermute | solution.py:583
  147.1 2.9 %collective-permute-done.10.far_b_ref = bf16[256,256]{1,0:T(8,128)(2,1)S(1)} collective-permute-done((bf16[256,256]{1,0:T(8,128)(2,1)S(1)}, bf16[256,256]{1,0:T(8,128)(2,1)S(1)}, u32[]{:S(2)}, u32[]{:S(2)}) %collective-permute-start.10) | collective-permute-done | bytes 131104 | tf_op jit(solution)/shard_map/ppermute | solution.py:583
  150.0 1.6 collective-permute-done.9.far_a_ref
  151.6 1.3 project.1
  152.9 0.1 collective-permute-start.11
  153.0 1.5 collective-permute-done.11
  154.5 0.8 add_convert_fusion
  155.3 6.8 %all-to-all-done.3 = bf16[32,2,16,256]{3,2,1,0:T(8,128)(2,1)S(1)} async-done(((bf16[32,2,16,256]{3,2,1,0:T(8,128)(2,1)}), bf16[32,2,16,256]{3,2,1,0:T(8,128)(2,1)S(1)}, u32[]{:S(2)}, u32[]{:S(2)}) %all-to-all-start.3) | async-done | bytes 524320 | tf_op jit(solution)/shard_map/all_to_all | solution.py:574
  162.1 1.4 unpack_tokens.1
  (43 shorter events, 0.1 us)
Async XLA Ops:
  7.2 15.7 %copy-start = (bf16[256,2048]{1,0:T(8,128)(2,1)S(1)}, bf16[256,2048]{1,0:T(8,128)(2,1)}, u32[]{:S(2)}) copy-start(bf16[256,2048]{1,0:T(8,128)(2,1)} %refs_0_.3) | copy-start | bytes 3145732
  7.3 1.7 copy-start.1
  8.9 0.7 copy-start.10
  9.6 19.4 %copy-start.12 = (bf16[2048,256]{1,0:T(8,128)(2,1)S(1)}, bf16[2048,256]{1,0:T(8,128)(2,1)}, u32[]{:S(2)}) copy-start(bf16[2048,256]{1,0:T(8,128)(2,1)} %qk_ref.1) | copy-start | bytes 3145732
  9.6 19.4 %copy-start.14 = (s32[2,16384]{1,0:T(2,128)S(1)}, s32[2,16384]{1,0:T(2,128)}, u32[]{:S(2)}) copy-start(s32[2,16384]{1,0:T(2,128)} %earlier_ref.1) | copy-start | bytes 393220
  11.6 15.4 %copy-start.15 = (s32[8,512]{1,0:T(8,128)}, s32[8,512]{1,0:T(8,128)S(1)}, u32[]{:S(2)}) copy-start(s32[8,512]{1,0:T(8,128)S(1)} %get-tuple-element.43.slot_ref) | copy-start | bytes 49156
  11.6 28.8 %all-to-all-start = ((bf16[32,16,512]{2,1,0:T(8,128)(2,1)}), bf16[32,16,512]{2,1,0:T(8,128)(2,1)S(1)}, u32[]{:S(2)}, u32[]{:S(2)}) async-start(bf16[32,16,512]{2,1,0:T(8,128)(2,1)} %bitcast.4), calls=%async_computation | async-start | bytes 1048576 | tf_op jit(solution)/shard_map/all_to_all | solution.py:574
  22.8 51.5 %all-gather.3.cloned.1.call-start = ((), (), s32[]{:S(2)}) async-start(), calls=%async_computation.6 | async-start | bytes 2621440 | tf_op jit(solution)/shard_map/all_gather | solution.py:630
  23.8 13.5 %collective-permute-start.2 = (bf16[256,512]{1,0:T(8,128)(2,1)}, bf16[256,512]{1,0:T(8,128)(2,1)S(1)}, u32[]{:S(2)}, u32[]{:S(2)}) collective-permute-start(bf16[256,512]{1,0:T(8,128)(2,1)} %get-tuple-element.44), channel_id=1, source_target_pairs={{0,4},{1,5},{2,6},{3,7},{4,0},{5,1},{6,2},{7,3},{8,12},{9,13},{10,... | collective-permute-start | bytes 786440 | tf_op jit(solution)/shard_map/ppermute | solution.py:583
  27.0 12.0 %collective-permute-start.1 = (bf16[256,512]{1,0:T(8,128)(2,1)}, bf16[256,512]{1,0:T(8,128)(2,1)S(1)}, u32[]{:S(2)}, u32[]{:S(2)}) collective-permute-start(bf16[256,512]{1,0:T(8,128)(2,1)} %get-tuple-element.45), channel_id=1, source_target_pairs={{0,6},{1,7},{2,0},{3,1},{4,2},{5,3},{6,4},{7,5},{8,14},{9,15},{10,... | collective-permute-start | bytes 786440 | tf_op jit(solution)/shard_map/ppermute | solution.py:583
  28.1 11.0 %collective-permute-start = (bf16[256,512]{1,0:T(8,128)(2,1)}, bf16[256,512]{1,0:T(8,128)(2,1)S(1)}, u32[]{:S(2)}, u32[]{:S(2)}) collective-permute-start(bf16[256,512]{1,0:T(8,128)(2,1)} %get-tuple-element.46), channel_id=1, source_target_pairs={{0,2},{1,3},{2,4},{3,5},{4,6},{5,7},{6,0},{7,1},{8,10},{9,11},{10,... | collective-permute-start | bytes 786440 | tf_op jit(solution)/shard_map/ppermute | solution.py:583
  29.0 1.6 copy-start.11
  30.6 1.2 copy-start.13
  36.7 0.6 copy-start.19
  39.0 2.2 %copy-start.6 = (bf16[256,512]{1,0:T(8,128)(2,1)}, bf16[256,512]{1,0:T(8,128)(2,1)S(1)}, u32[]{:S(2)}) copy-start(bf16[256,512]{1,0:T(8,128)(2,1)S(1)} %collective-permute-done.1.refs_2_) | copy-start | bytes 786436
  39.0 2.2 %copy-start.8 = (bf16[256,512]{1,0:T(8,128)(2,1)}, bf16[256,512]{1,0:T(8,128)(2,1)S(1)}, u32[]{:S(2)}) copy-start(bf16[256,512]{1,0:T(8,128)(2,1)S(1)} %collective-permute-done.refs_1_) | copy-start | bytes 786436
  40.4 0.8 copy-start.23
  41.3 45.0 %all-to-all-start.1 = ((bf16[32,32,512]{2,1,0:T(8,128)(2,1)}), bf16[32,32,512]{2,1,0:T(8,128)(2,1)S(1)}, u32[]{:S(2)}, u32[]{:S(2)}) async-start(bf16[32,32,512]{2,1,0:T(8,128)(2,1)} %bitcast.5), calls=%async_computation.1 | async-start | bytes 2097152 | tf_op jit(solution)/shard_map/all_to_all | solution.py:574
  49.8 71.7 %reduce-scatter.2.cloned.1.call-start = ((), (), s32[]{:S(2)}) async-start(), calls=%async_computation.5 | async-start | bytes 2621440 | tf_op jit(solution)/shard_map/reduce_scatter | solution.py:635
  49.8 1.9 %copy-start.21 = (bf16[2,2048,256]{2,1,0:T(8,128)(2,1)S(1)}, bf16[2,2048,256]{2,1,0:T(8,128)(2,1)}, u32[]{:S(2)}) copy-start(bf16[2,2048,256]{2,1,0:T(8,128)(2,1)} %refs_1_.1) | copy-start | bytes 6291460
  49.8 2.6 %copy-start.22 = (bf16[2,256,2048]{2,1,0:T(8,128)(2,1)S(1)}, bf16[2,256,2048]{2,1,0:T(8,128)(2,1)}, u32[]{:S(2)}) copy-start(bf16[2,256,2048]{2,1,0:T(8,128)(2,1)} %refs_2_.1) | copy-start | bytes 6291460
  52.5 2.7 %collective-permute-start.5 = (bf16[1,256,2048]{2,1,0:T(8,128)(2,1)S(1)}, bf16[1,256,2048]{2,1,0:T(8,128)(2,1)S(1)}, u32[]{:S(2)}, u32[]{:S(2)}) collective-permute-start(bf16[1,256,2048]{2,1,0:T(8,128)(2,1)S(1)} %constant_dynamic-slice_fusion), channel_id=1, source_target_pairs={{0,1},{1,0},{2,3},{3,2},{4,5},{5,4},{6,7},{7,6},{8,9},{9,8},{10,11... | collective-permute-start | bytes 3145736 | tf_op jit(solution)/shard_map/ppermute | solution.py:625
  52.6 4.1 %collective-permute-start.4 = (bf16[1,2048,256]{2,1,0:T(8,128)(2,1)S(1)}, bf16[1,2048,256]{2,1,0:T(8,128)(2,1)S(1)}, u32[]{:S(2)}, u32[]{:S(2)}) collective-permute-start(bf16[1,2048,256]{2,1,0:T(8,128)(2,1)S(1)} %constant_dynamic-slice_fusion.1), channel_id=1, source_target_pairs={{0,1},{1,0},{2,3},{3,2},{4,5},{5,4},{6,7},{7,6},{8,9},{9,8},{10,11... | collective-permute-start | bytes 3145736 | tf_op jit(solution)/shard_map/ppermute | solution.py:625
  53.1 5.1 %collective-permute-start.3 = (bf16[1,2048,256]{2,1,0:T(8,128)(2,1)S(1)}, bf16[1,2048,256]{2,1,0:T(8,128)(2,1)S(1)}, u32[]{:S(2)}, u32[]{:S(2)}) collective-permute-start(bf16[1,2048,256]{2,1,0:T(8,128)(2,1)S(1)} %constant_dynamic-slice_fusion.2), channel_id=1, source_target_pairs={{0,1},{1,0},{2,3},{3,2},{4,5},{5,4},{6,7},{7,6},{8,9},{9,8},{10,11... | collective-permute-start | bytes 3145736 | tf_op jit(solution)/shard_map/ppermute | solution.py:625
  56.8 1.0 copy-start.2
  58.3 1.0 copy-start.4
  74.3 1.2 copy-start.3
  75.5 1.2 copy-start.5
  88.0 1.0 copy-start.17
  89.0 1.8 %copy-start.18 = (bf16[2,512,512]{2,1,0:T(8,128)(2,1)S(1)}, bf16[2,512,512]{2,1,0:T(8,128)(2,1)}, u32[]{:S(2)}) copy-start(bf16[2,512,512]{2,1,0:T(8,128)(2,1)} %copy-done.17) | copy-start | bytes 3145732
  89.0 5.5 %collective-permute-start.6 = (bf16[2,64,512]{2,1,0:T(8,128)(2,1)S(1)}, bf16[2,64,512]{2,1,0:T(8,128)(2,1)S(1)}, u32[]{:S(2)}, u32[]{:S(2)}) collective-permute-start(bf16[2,64,512]{2,1,0:T(8,128)(2,1)S(1)} %get-tuple-element.33), channel_id=1, source_target_pairs={{0,8},{8,16},{16,24},{24,32},{32,40},{40,48},{48,56},{56,64},{64,7... | collective-permute-start | bytes 393224 | tf_op jit(solution)/shard_map/ppermute | solution.py:642
  97.6 30.9 %copy-start.20 = (s32[2,8,512]{2,1,0:T(8,128)S(1)}, s32[2,8,512]{2,1,0:T(8,128)}, u32[]{:S(2)}) copy-start(s32[2,8,512]{2,1,0:T(8,128)} %copy-done.19) | copy-start | bytes 98308
  97.6 30.9 %all-to-all-start.2 = ((bf16[32,40,256]{2,1,0:T(8,128)(2,1)}), bf16[32,40,256]{2,1,0:T(8,128)(2,1)S(1)}, u32[]{:S(2)}, u32[]{:S(2)}) async-start(bf16[32,40,256]{2,1,0:T(8,128)(2,1)} %attend_first.1), calls=%async_computation.2 | async-start | bytes 1310720 | tf_op jit(solution)/shard_map/all_to_all | solution.py:574
  123.2 28.4 %copy-start.7 = (bf16[256,512]{1,0:T(8,128)(2,1)S(1)}, bf16[256,512]{1,0:T(8,128)(2,1)}, u32[]{:S(2)}) copy-start(bf16[256,512]{1,0:T(8,128)(2,1)} %copy-done.6) | copy-start | bytes 786436
  123.2 28.4 %copy-start.9 = (bf16[256,512]{1,0:T(8,128)(2,1)S(1)}, bf16[256,512]{1,0:T(8,128)(2,1)}, u32[]{:S(2)}) copy-start(bf16[256,512]{1,0:T(8,128)(2,1)} %copy-done.8) | copy-start | bytes 786436
  123.2 8.5 %collective-permute-start.12 = (bf16[32,16,256]{2,1,0:T(8,128)(2,1)}, bf16[32,16,256]{2,1,0:T(8,128)(2,1)}, u32[]{:S(2)}, u32[]{:S(2)}) collective-permute-start(bf16[32,16,256]{2,1,0:T(8,128)(2,1)} %get-tuple-element.48), channel_id=1, source_target_pairs={{0,1},{1,0},{2,3},{3,2},{4,5},{5,4},{6,7},{7,6},{8,9},{9,8},{10,11... | collective-permute-start | bytes 786440 | tf_op jit(solution)/shard_map/ppermute | solution.py:650
  129.6 6.4 %collective-permute-start.8 = (bf16[512,256]{1,0:T(8,128)(2,1)S(1)}, bf16[512,256]{1,0:T(8,128)(2,1)S(1)}, u32[]{:S(2)}, u32[]{:S(2)}) collective-permute-start(bf16[512,256]{1,0:T(8,128)(2,1)S(1)} %combine.1.own_ref), channel_id=1, source_target_pairs={{0,6},{1,7},{2,0},{3,1},{4,2},{5,3},{6,4},{7,5},{8,14},{9,15},{10,... | collective-permute-start | bytes 786440 | tf_op jit(solution)/shard_map/ppermute | solution.py:583
  130.5 7.6 %collective-permute-start.7 = (bf16[512,256]{1,0:T(8,128)(2,1)S(1)}, bf16[512,256]{1,0:T(8,128)(2,1)S(1)}, u32[]{:S(2)}, u32[]{:S(2)}) collective-permute-start(bf16[512,256]{1,0:T(8,128)(2,1)S(1)} %combine.1.own_ref), channel_id=1, source_target_pairs={{0,2},{1,3},{2,4},{3,5},{4,6},{5,7},{6,0},{7,1},{8,10},{9,11},{10,... | collective-permute-start | bytes 786440 | tf_op jit(solution)/shard_map/ppermute | solution.py:583
  138.0 24.0 %all-to-all-start.3 = ((bf16[32,2,16,256]{3,2,1,0:T(8,128)(2,1)}), bf16[32,2,16,256]{3,2,1,0:T(8,128)(2,1)S(1)}, u32[]{:S(2)}, u32[]{:S(2)}) async-start(bf16[32,2,16,256]{3,2,1,0:T(8,128)(2,1)} %pad_maximum_fusion), calls=%async_computation.4 | async-start | bytes 1048576 | tf_op jit(solution)/shard_map/all_to_all | solution.py:574
  144.9 17.2 %copy-start.16 = (s32[8,512]{1,0:T(8,128)S(1)}, s32[8,512]{1,0:T(8,128)}, u32[]{:S(2)}) copy-start(s32[8,512]{1,0:T(8,128)} %copy-done.15) | copy-start | bytes 49156
  144.9 5.0 %collective-permute-start.10 = (bf16[256,256]{1,0:T(8,128)(2,1)S(1)}, bf16[256,256]{1,0:T(8,128)(2,1)S(1)}, u32[]{:S(2)}, u32[]{:S(2)}) collective-permute-start(bf16[256,256]{1,0:T(8,128)(2,1)S(1)} %slice.9), channel_id=1, source_target_pairs={{0,6},{1,7},{2,0},{3,1},{4,2},{5,3},{6,4},{7,5},{8,14},{9,15},{10,... | collective-permute-start | bytes 393224 | tf_op jit(solution)/shard_map/ppermute | solution.py:583
  145.3 6.3 %collective-permute-start.9 = (bf16[256,256]{1,0:T(8,128)(2,1)S(1)}, bf16[256,256]{1,0:T(8,128)(2,1)S(1)}, u32[]{:S(2)}, u32[]{:S(2)}) collective-permute-start(bf16[256,256]{1,0:T(8,128)(2,1)S(1)} %slice.8), channel_id=1, source_target_pairs={{0,2},{1,3},{2,4},{3,5},{4,6},{5,7},{6,0},{7,1},{8,10},{9,11},{10,... | collective-permute-start | bytes 393224 | tf_op jit(solution)/shard_map/ppermute | solution.py:583
  152.9 1.6 collective-permute-start.11
Sparse Core Ops, SparseCore 0:
  41.4 32.8 all-gather.2
  89.1 32.2 reduce-scatter.1

commit v6 on v4

--- a/solution.py
+++ b/solution.py
@@ -13,6 +13,7 @@
 EXP_DEV = 2
 LANES = 128
 F32, BF16, I32 = jnp.float32, jnp.bfloat16, jnp.int32
+LONG = 1 << 35
 BIG = pltpu.CompilerParams(vmem_limit_bytes=48 * 1024 * 1024)
 
 
@@ -48,7 +49,7 @@
     return flag(iota((count, count), 0) <= iota((count, count), 1))
 
 
-def pack_rows_kernel(me_ref, perms_ref, x_ref, qk_ref, val_ref, out_ref, token_ref, scratch):
+def project_rows_kernel(me_ref, perms_ref, x_ref, qk_ref, val_ref, rows_ref, pick_ref, token_ref, scratch):
     length, span = x_ref.shape[0], qk_ref.shape[1]
     rounds, total = perms_ref.shape
     peers = total // length
@@ -70,13 +71,13 @@
     for turn in range(rounds):
         row = to_row(by_round[:, turn].reshape(peers * per_peer, 1)).astype(I32)
         token_ref[turn] = jnp.broadcast_to(row, token_ref.shape[1:])
-    pick = flag(column.astype(I32) == iota((groups * per_peer, length), 1))
+    pick_ref[...] = flag(column.astype(I32) == iota((groups * per_peer, length), 1))
     for part, weight in enumerate((qk_ref, val_ref)):
         rows = dot(x_ref[...], weight[...]).astype(BF16)
-        out_ref[:, part * span : (part + 1) * span] = dot(pick, rows).astype(BF16)
-
-
-def pack_rows(me, perms, x_att, w_qk, w_val):
+        rows_ref[:, part * span : (part + 1) * span] = rows
+
+
+def project_rows(me, perms, x_att, w_qk, w_val):
     length, width = x_att.shape
     rounds, total = perms.shape
     span = w_qk.shape[1]
@@ -87,7 +88,7 @@
         return pl.BlockSpec(shape, lambda i, me_ref: (0, 0))
 
     return pl.pallas_call(
-        pack_rows_kernel,
+        project_rows_kernel,
         grid_spec=pltpu.PrefetchScalarGridSpec(
             num_scalar_prefetch=1,
             grid=(1,),
@@ -98,19 +99,35 @@
                 whole((width, span)),
             ],
             out_specs=[
-                whole((slots, 2 * span)),
+                whole((length, 2 * span)),
+                whole((slots, length)),
                 pl.BlockSpec((rounds, 8, length), lambda i, me_ref: (0, 0, 0)),
             ],
             scratch_shapes=[pltpu.VMEM((groups, length), I32)],
         ),
         out_shape=[
-            jax.ShapeDtypeStruct((slots, 2 * span), BF16),
+            jax.ShapeDtypeStruct((length, 2 * span), BF16),
+            jax.ShapeDtypeStruct((slots, length), BF16),
             jax.ShapeDtypeStruct((rounds, 8, length), I32),
         ],
         cost_estimate=cost(4 * length * width * span + 4 * slots * length * span, 6 << 20),
         compiler_params=BIG,
+        name="project_rows",
+    )(me, perms, x_att, w_qk, w_val)
+
+
+def pack_rows_kernel(pick_ref, rows_ref, out_ref):
+    out_ref[...] = dot(pick_ref[...], rows_ref[...]).astype(BF16)
+
+
+def pack_rows(pick, rows):
+    return pl.pallas_call(
+        pack_rows_kernel,
+        out_shape=jax.ShapeDtypeStruct((pick.shape[0], rows.shape[1]), BF16),
+        cost_estimate=cost(LONG, 2 << 20),
+        compiler_params=BIG,
         name="pack_rows",
-    )(me, perms, x_att, w_qk, w_val)
+    )(pick, rows)
 
 
 def pack_tokens_kernel(peers, where_ref, ids_ref, tokens_ref, out_ref, slot_ref):
@@ -229,6 +246,32 @@
     )(where, *shards, *far, *own, *sibling)
 
 
+def place_rows_kernel(where_ref, rows_ref, taken_ref, out_ref):
+    out_ref[:, 0] = rows_ref[0]
+    out_ref[:, 1] = taken_ref[...]
+
+
+def place_rows(where, rows, taken):
+    peers, capacity, half = taken.shape
+    out = (peers, EXP_DEV, capacity, half)
+    return pl.pallas_call(
+        place_rows_kernel,
+        grid_spec=pltpu.PrefetchScalarGridSpec(
+            num_scalar_prefetch=1,
+            grid=(1,),
+            in_specs=[
+                pl.BlockSpec((1, *taken.shape), lambda i, e: (e[1], 0, 0, 0)),
+                pl.BlockSpec(taken.shape, lambda i, e: (0, 0, 0)),
+            ],
+            out_specs=pl.BlockSpec(out, lambda i, e: (0, 0, 0, 0)),
+        ),
+        out_shape=jax.ShapeDtypeStruct(out, BF16),
+        cost_estimate=cost(LONG, 1 << 20),
+        compiler_params=BIG,
+        name="place_rows",
+    )(where, rows, taken)
+
+
 def unpack_tokens_kernel(back_ref, slot_ref, out_ref):
     length = out_ref.shape[0]
     column = to_col(slot_ref[:1, :].astype(F32)).astype(I32)
@@ -287,7 +330,7 @@
             jax.ShapeDtypeStruct((rounds, BLOCK_LEN, width), BF16),
             jax.ShapeDtypeStruct((rounds, 8, length), I32),
         ],
-        cost_estimate=cost(2 * rounds * length * length * width, 4 << 20),
+        cost_estimate=cost(LONG, 4 << 20),
         compiler_params=BIG,
         name="sort_rows",
     )(me, perms, arrived)
@@ -430,7 +473,7 @@
             out_specs=pl.BlockSpec(out, lambda i, s: (0, 0, 0)),
         ),
         out_shape=jax.ShapeDtypeStruct(out, BF16),
-        cost_estimate=cost(2 << 30, 4 << 20),
+        cost_estimate=cost(LONG, 4 << 20),
         compiler_params=BIG,
         name="attend_later",
     )(me, perms, rows)
@@ -468,7 +511,7 @@
             out_specs=fixed(out),
         ),
         out_shape=jax.ShapeDtypeStruct(out, BF16),
-        cost_estimate=cost(2 << 30, 4 << 20),
+        cost_estimate=cost(LONG, 4 << 20),
         compiler_params=BIG,
         name="attend_first",
     )(me, perms, perms, rows, last, slot, later)
@@ -613,7 +656,7 @@
         where, expert_ids.reshape(1, tokb), tokens_b, peers, capacity, part
     )
     received = exchange(dispatch.reshape(peers, capacity, part), "seq")
-    outgoing, slot_token = pack_rows(me, perms, x_att, w_qk, w_val)
+    projected, pick, slot_token = project_rows(me, perms, x_att, w_qk, w_val)
     columns = [
         hop(
             lax.dynamic_slice_in_dim(
@@ -624,8 +667,8 @@
         )
         for by in (1, chips - 1, 2)
     ]
-    received = after(received, outgoing, *columns)
-    outgoing = after(outgoing, received)
+    received = after(received, projected, *columns)
+    outgoing = pack_rows(pick, after(projected, received))
     own = (w_gate, w_up, w_down)
     sibling = [
         lax.ppermute(
@@ -639,7 +682,7 @@
     arrived = after(arrived, expert_part)
     rows, last, row_slot = sort_rows(me, perms, arrived, length)
     expert_rows = lax.psum_scatter(
-        after(expert_part, last),
+        expert_part,
         "exp",
         scatter_dimension=0,
         tiled=False,
@@ -651,12 +694,11 @@
     packed = attend_first(me, perms, rows, last, row_slot, later, peers)
     got = exchange(packed, "seq")
     expert_rows = after(expert_rows, packed)
-    kept = lax.dynamic_index_in_dim(expert_rows, core, 0, keepdims=False)
     given = lax.dynamic_index_in_dim(expert_rows, 1 - core, 0, keepdims=False)
     taken = lax.ppermute(given, "exp", siblings)
-    expert_rows = jnp.stack([kept, taken], axis=1)
     mixed_heads = combine(got, slot_token)
-    expert_back = exchange(after(expert_rows, mixed_heads), "seq")
+    expert_rows = place_rows(where, expert_rows, after(taken, mixed_heads))
+    expert_back = exchange(expert_rows, "seq")
     heads, far_heads = spread(mixed_heads, chips, (expert_rows,))
     attn_kept, attn_given = project(where, (*heads, *far_heads), w_out, columns)
     attended = attn_kept + lax.ppermute(attn_given, "exp", siblings).astype(F32)

time: 168 us -> 167 us (level)
  local copies, waits for them, and re-layouts: 12.6 us -> 15.2 us
  other arithmetic: 2.66 us -> 0.84 us
    unnamed x34 -> x38, local copies, waits for them, and re-layouts: 8.97 us -> 11.7 us
    another operation x1 -> x0, other arithmetic: 1.82 us -> none  [body(): expert_rows = jnp.stack([kept, taken], axis=1)]
    all_to_all x4, waiting for transfers between devices: 6.43 us -> 8.22 us  [exchange(): return lax.all_to_all(x, axis, split_axis=0, concat_axis=0, tiled=True)]
    pallas_call x1 -> x3, Pallas kernels: 4.81 us -> 3.84 us  [the longest x1 1.76 us: project_rows(): pl.pallas_call(project_rows_kernel, grid_spec=pltpu.PrefetchScalarGridSpe...]
  transfers between devices with their start and end apart: 22 -> 22, of which waited for: 13 -> 12; matrix products, arithmetic and copies ran while one was open for 3% -> 3% of each run, Pallas kernels for 13% -> 12%
where the time goes in v6:
time: 167 us; the launch traced here: 165 us
  waiting for transfers between devices  54.9 us (33%)
  starting transfers between devices  54.4 us (33%)
  Pallas kernels  25.3 us (15%)
  local copies, waits for them, and re-layouts  15.2 us (9%)
  between operations  14.4 us (9%)
    all_to_all x4, starting transfers between devices, exchange(): return lax.all_to_all(x, axis, split_axis=0, concat_axis=0, tiled=True)  35.5 us
    ppermute x11, waiting for transfers between devices, hop(): return lax.ppermute(x, 'exp', pairs)  34.5 us
    ppermute x11, starting transfers between devices, hop(): return lax.ppermute(x, 'exp', pairs)  16.4 us
    unnamed x38, local copies, waits for them, and re-layouts  11.7 us
    reduce_scatter x1, waiting for transfers between devices, body(): lax.psum_scatter(expert_part, 'exp', scatter_dimension=0, tiled=False, ax...  10.1 us
    all_to_all x4, waiting for transfers between devices, exchange(): return lax.all_to_all(x, axis, split_axis=0, concat_axis=0, tiled=True)  8.22 us
    pallas_call x1, Pallas kernels, run_experts(): pl.pallas_call(experts_kernel, grid_spec=pltpu.PrefetchScalarGridSpec(num...  7.8 us
  transfers between devices with their start and end apart: 22, of which 12 were waited for; matrix products, arithmetic and copies ran while one was open for 3% of the time, Pallas kernels for 12%

profile of v6, /device:TPU:32, one launch (start us, length us, event | category | flops | bytes accessed | tf_op | source)
XLA Modules:
  0.0 165.0 jit_solution(1020029298954355777)
XLA Ops:
  7.2 0.1 pad_add_fusion.where_ref
  7.3 1.7 %copy-done.1 = bf16[512,2048]{1,0:T(8,128)(2,1)S(1)} copy-done((bf16[512,2048]{1,0:T(8,128)(2,1)S(1)}, bf16[512,2048]{1,0:T(8,128)(2,1)}, u32[]{:S(2)}) %copy-start.1) | copy-done | bytes 2097176
  8.9 0.7 copy-done.10
  9.6 2.0 %pack_tokens.1 = (bf16[512,512]{1,0:T(8,128)(2,1)}, s32[8,512]{1,0:T(8,128)S(1)}) custom-call(s32[2]{0:T(128)S(1)} %pad_add_fusion.where_ref, s32[1,512]{1,0:T(1,128)S(1)} %bitcast.14, bf16[512,2048]{1,0:T(8,128)(2,1)S(1)} %copy-done.1), custom_call_target="tpu_custom_call" | custom-call | flops 268435456 | bytes 2097152 | tf_op jit(solution)/shard_map/pack_tokens/pallas_call | solution.py:156
  11.6 11.2 %all-to-all-start = ((bf16[32,16,512]{2,1,0:T(8,128)(2,1)}), bf16[32,16,512]{2,1,0:T(8,128)(2,1)S(1)}, u32[]{:S(2)}, u32[]{:S(2)}) async-start(bf16[32,16,512]{2,1,0:T(8,128)(2,1)} %bitcast.4), calls=%async_computation | async-start | bytes 1048576 | tf_op jit(solution)/shard_map/all_to_all | solution.py:615
  22.9 0.9 constant_dynamic-slice_fusion.3
  23.8 3.2 %collective-permute-start.2 = (bf16[256,512]{1,0:T(8,128)(2,1)}, bf16[256,512]{1,0:T(8,128)(2,1)S(1)}, u32[]{:S(2)}, u32[]{:S(2)}) collective-permute-start(bf16[256,512]{1,0:T(8,128)(2,1)} %get-tuple-element.48), channel_id=1, source_target_pairs={{0,4},{1,5},{2,6},{3,7},{4,0},{5,1},{6,2},{7,3},{8,12},{9,13},{10,... | collective-permute-start | bytes 786440 | tf_op jit(solution)/shard_map/ppermute | solution.py:624
  26.9 1.1 collective-permute-start.1
  28.0 1.0 collective-permute-start
  29.0 1.6 copy-done.11
  30.6 1.2 copy-done.12
  31.8 1.2 copy-done.13
  33.0 1.8 %project_rows.1 = (bf16[512,512]{1,0:T(8,128)(2,1)S(1)}, bf16[1024,512]{1,0:T(8,128)(2,1)S(1)}, s32[2,8,512]{2,1,0:T(8,128)S(1)}) custom-call(s32[1]{0:T(128)} %bitcast.2.me_ref, s32[2,16384]{1,0:T(2,128)S(1)} %copy-done.14, bf16[512,2048]{1,0:T(8,128)(2,1)S(1)} %copy-done.11, bf16[2048,256]{1,0:T(8,128)(2,1)S(1)} %copy-done.12, bf16[2048,256]{1,0:T(8,128)(2,1)S(1)} %copy-done.13), custom_call_target="tpu_custom_call" | custom-call | flops 1610612736 | bytes 6291456 | tf_op jit(solution)/shard_map/project_rows/pallas_call | solution.py:90
  34.8 1.0 copy-done.15
  35.8 3.2 %collective-permute-done.1.refs_2_ = bf16[256,512]{1,0:T(8,128)(2,1)S(1)} collective-permute-done((bf16[256,512]{1,0:T(8,128)(2,1)}, bf16[256,512]{1,0:T(8,128)(2,1)S(1)}, u32[]{:S(2)}, u32[]{:S(2)}) %collective-permute-start.1) | collective-permute-done | bytes 262176 | tf_op jit(solution)/shard_map/ppermute | solution.py:624
  39.0 1.5 all-to-all-done.refs_0_
  40.4 1.2 copy-done.16
  41.7 0.7 pack_rows.1
  42.4 1.0 copy-done.2
  43.4 8.5 %all-to-all-start.1 = ((bf16[32,32,512]{2,1,0:T(8,128)(2,1)}), bf16[32,32,512]{2,1,0:T(8,128)(2,1)S(1)}, u32[]{:S(2)}, u32[]{:S(2)}) async-start(bf16[32,32,512]{2,1,0:T(8,128)(2,1)} %bitcast.10), calls=%async_computation.1 | async-start | bytes 2097152 | tf_op jit(solution)/shard_map/all_to_all | solution.py:615
  51.9 0.0 reduce-scatter.2.cloned.1.call-start
  51.9 0.0 copy-start.18
  52.0 1.4 constant_dynamic-slice_fusion.2
  53.4 0.4 copy-done.17
  53.8 0.1 constant_dynamic-slice_fusion.1
  53.9 0.6 copy-done.18
  54.5 0.1 constant_dynamic-slice_fusion
  54.6 0.1 collective-permute-start.9
  54.7 0.5 collective-permute-start.8
  55.2 0.1 collective-permute-start.7
  55.3 2.6 %collective-permute-start.4 = (bf16[32,16,512]{2,1,0:T(8,128)(2,1)S(1)}, bf16[32,16,512]{2,1,0:T(8,128)(2,1)S(1)}, u32[]{:S(2)}, u32[]{:S(2)}) collective-permute-start(bf16[32,16,512]{2,1,0:T(8,128)(2,1)S(1)} %all-to-all-done.refs_0_), channel_id=1, source_target_pairs={{0,6},{1,7},{2,0},{3,1},{4,2},{5,3},{6,4},{7,5},{8,14},{9,15},{10,... | collective-permute-start | bytes 1572872 | tf_op jit(solution)/shard_map/ppermute | solution.py:624
  57.9 11.8 %collective-permute-done.4.refs_2_ = bf16[32,16,512]{2,1,0:T(8,128)(2,1)S(1)} collective-permute-done((bf16[32,16,512]{2,1,0:T(8,128)(2,1)S(1)}, bf16[32,16,512]{2,1,0:T(8,128)(2,1)S(1)}, u32[]{:S(2)}, u32[]{:S(2)}) %collective-permute-start.4) | collective-permute-done | bytes 524320 | tf_op jit(solution)/shard_map/ppermute | solution.py:624
  69.7 3.8 %collective-permute-start.6 = (bf16[16,16,512]{2,1,0:T(8,128)(2,1)S(1)}, bf16[16,16,512]{2,1,0:T(8,128)(2,1)S(1)}, u32[]{:S(2)}, u32[]{:S(2)}) collective-permute-start(bf16[16,16,512]{2,1,0:T(8,128)(2,1)S(1)} %slice.17), channel_id=1, source_target_pairs={{0,6},{1,7},{2,0},{3,1},{4,2},{5,3},{6,4},{7,5},{8,14},{9,15},{10,... | collective-permute-start | bytes 786440 | tf_op jit(solution)/shard_map/ppermute | solution.py:624
  73.5 0.3 collective-permute-start.5
  73.8 5.1 %collective-permute-done.6.refs_4_ = bf16[16,16,512]{2,1,0:T(8,128)(2,1)S(1)} collective-permute-done((bf16[16,16,512]{2,1,0:T(8,128)(2,1)S(1)}, bf16[16,16,512]{2,1,0:T(8,128)(2,1)S(1)}, u32[]{:S(2)}, u32[]{:S(2)}) %collective-permute-start.6) | collective-permute-done | bytes 262176 | tf_op jit(solution)/shard_map/ppermute | solution.py:624
  78.8 3.7 %collective-permute-done.5.refs_3_ = bf16[16,16,512]{2,1,0:T(8,128)(2,1)S(1)} collective-permute-done((bf16[16,16,512]{2,1,0:T(8,128)(2,1)S(1)}, bf16[16,16,512]{2,1,0:T(8,128)(2,1)S(1)}, u32[]{:S(2)}, u32[]{:S(2)}) %collective-permute-start.5) | collective-permute-done | bytes 262176 | tf_op jit(solution)/shard_map/ppermute | solution.py:624
  82.5 7.8 %experts.1 = bf16[4,2,32,16,256]{4,3,2,1,0:T(8,128)(2,1)} custom-call(s32[2]{0:T(128)S(1)} %pad_add_fusion.where_ref, bf16[32,16,512]{2,1,0:T(8,128)(2,1)S(1)} %all-to-all-done.refs_0_, bf16[32,16,512]{2,1,0:T(8,128)(2,1)S(1)} %collective-permute-done.3.refs_1_, bf16[32,16,512]{2,1,0:T(8,128)(2,1)S(1)} %collective-permute-done.4.refs_2_, ...), custom_call_target="tpu_custom_call" | custom-call | flops 3221225472 | bytes 10485760 | tf_op jit(solution)/shard_map/experts/pallas_call | solution.py:232
  90.4 0.0 reduce-scatter.2.cloned.1.call-update
  90.4 1.7 %sort_rows.1 = (bf16[2,512,512]{2,1,0:T(8,128)(2,1)S(1)}, bf16[2,64,512]{2,1,0:T(8,128)(2,1)S(1)}, s32[2,8,512]{2,1,0:T(8,128)S(1)}) custom-call(s32[1]{0:T(128)} %bitcast.2.me_ref, s32[2,16384]{1,0:T(2,128)S(1)} %copy-done.14, bf16[32,32,512]{2,1,0:T(8,128)(2,1)S(1)} %all-to-all-done.1.arrived_ref), custom_call_target="tpu_custom_call" | custom-call | flops 34359738368 | bytes 4194304 | tf_op jit(solution)/shard_map/sort_rows/pallas_call | solution.py:313
  92.1 1.5 collective-permute-start.10
  93.6 3.0 %attend_later.1.later_ref = bf16[2,384,384]{2,1,0:T(8,128)(2,1)S(1)} custom-call(s32[1]{0:T(128)} %bitcast.2.me_ref, s32[2,16384]{1,0:T(2,128)S(1)} %copy-done.14, bf16[2,512,512]{2,1,0:T(8,128)(2,1)S(1)} %get-tuple-element.35.rows_ref), custom_call_target="tpu_custom_call" | custom-call | flops 34359738368 | bytes 4194304 | tf_op jit(solution)/shard_map/attend_later/pallas_call | solution.py:464
  96.7 0.5 collective-permute-done.10.last_ref
  97.2 3.1 %attend_first.1 = bf16[32,40,256]{2,1,0:T(8,128)(2,1)} custom-call(s32[1]{0:T(128)} %bitcast.2.me_ref, s32[2,16384]{1,0:T(2,128)S(1)} %copy-done.14, s32[2,16384]{1,0:T(2,128)S(1)} %copy-done.14, bf16[2,512,512]{2,1,0:T(8,128)(2,1)S(1)} %get-tuple-element.35.rows_ref, bf16[2,64,512]{2,1,0:T(8,128)(2,1)S(1)} %collective-permute-done.10.last_ref, ...), custom_call_target="tpu_custom_call" | custom-call | flops 34359738368 | bytes 4194304 | tf_op jit(solution)/shard_map/attend_first/pallas_call | solution.py:492
  100.3 11.0 %all-to-all-start.2 = ((bf16[32,40,256]{2,1,0:T(8,128)(2,1)}), bf16[32,40,256]{2,1,0:T(8,128)(2,1)S(1)}, u32[]{:S(2)}, u32[]{:S(2)}) async-start(bf16[32,40,256]{2,1,0:T(8,128)(2,1)} %attend_first.1), calls=%async_computation.2 | async-start | bytes 1310720 | tf_op jit(solution)/shard_map/all_to_all | solution.py:615
  111.3 10.1 %reduce-scatter.2.cloned.1.call-done = bf16[1,2,32,16,256]{4,3,2,1,0:T(8,128)(2,1)} async-done(((bf16[4,2,32,16,256]{4,3,2,1,0:T(8,128)(2,1)}), bf16[1,2,32,16,256]{4,3,2,1,0:T(8,128)(2,1)}) %reduce-scatter.2.cloned.1.call-update) | async-done | bytes 524304 | tf_op jit(solution)/shard_map/reduce_scatter | solution.py:684
  121.4 1.0 dynamic-slice_bitcast_fusion
  122.3 0.1 collective-permute-start.12
  122.4 6.7 %all-to-all-done.2.got_ref = bf16[32,40,256]{2,1,0:T(8,128)(2,1)S(1)} async-done(((bf16[32,40,256]{2,1,0:T(8,128)(2,1)}), bf16[32,40,256]{2,1,0:T(8,128)(2,1)S(1)}, u32[]{:S(2)}, u32[]{:S(2)}) %all-to-all-start.2) | async-done | bytes 655392 | tf_op jit(solution)/shard_map/all_to_all | solution.py:615
  129.2 1.1 combine.1.own_ref
  130.3 1.1 copy-done.9
  131.4 1.4 place_rows.1
  132.8 4.8 %all-to-all-start.3 = ((bf16[32,2,16,256]{3,2,1,0:T(8,128)(2,1)}), bf16[32,2,16,256]{3,2,1,0:T(8,128)(2,1)S(1)}, u32[]{:S(2)}, u32[]{:S(2)}) async-start(bf16[32,2,16,256]{3,2,1,0:T(8,128)(2,1)} %place_rows.1), calls=%async_computation.4 | async-start | bytes 1048576 | tf_op jit(solution)/shard_map/all_to_all | solution.py:615
  137.6 0.6 collective-permute-start.13
  138.2 1.7 %collective-permute-start.11 = (bf16[512,256]{1,0:T(8,128)(2,1)S(1)}, bf16[512,256]{1,0:T(8,128)(2,1)S(1)}, u32[]{:S(2)}, u32[]{:S(2)}) collective-permute-start(bf16[512,256]{1,0:T(8,128)(2,1)S(1)} %combine.1.own_ref), channel_id=1, source_target_pairs={{0,2},{1,3},{2,4},{3,5},{4,6},{5,7},{6,0},{7,1},{8,10},{9,11},{10,... | collective-permute-start | bytes 786440 | tf_op jit(solution)/shard_map/ppermute | solution.py:624
  139.9 4.6 %collective-permute-done.13.next_ref = bf16[512,256]{1,0:T(8,128)(2,1)S(1)} collective-permute-done((bf16[512,256]{1,0:T(8,128)(2,1)S(1)}, bf16[512,256]{1,0:T(8,128)(2,1)S(1)}, u32[]{:S(2)}, u32[]{:S(2)}) %collective-permute-start.13) | collective-permute-done | bytes 262176 | tf_op jit(solution)/shard_map/ppermute | solution.py:624
  144.6 2.1 %collective-permute-start.15 = (bf16[256,256]{1,0:T(8,128)(2,1)S(1)}, bf16[256,256]{1,0:T(8,128)(2,1)S(1)}, u32[]{:S(2)}, u32[]{:S(2)}) collective-permute-start(bf16[256,256]{1,0:T(8,128)(2,1)S(1)} %slice.15), channel_id=1, source_target_pairs={{0,6},{1,7},{2,0},{3,1},{4,2},{5,3},{6,4},{7,5},{8,14},{9,15},{10,... | collective-permute-start | bytes 393224 | tf_op jit(solution)/shard_map/ppermute | solution.py:624
  146.7 0.1 collective-permute-start.14
  146.8 2.8 %collective-permute-done.15.far_b_ref = bf16[256,256]{1,0:T(8,128)(2,1)S(1)} collective-permute-done((bf16[256,256]{1,0:T(8,128)(2,1)S(1)}, bf16[256,256]{1,0:T(8,128)(2,1)S(1)}, u32[]{:S(2)}, u32[]{:S(2)}) %collective-permute-start.15) | collective-permute-done | bytes 131104 | tf_op jit(solution)/shard_map/ppermute | solution.py:624
  149.6 3.4 %collective-permute-done.14.far_a_ref = bf16[256,256]{1,0:T(8,128)(2,1)S(1)} collective-permute-done((bf16[256,256]{1,0:T(8,128)(2,1)S(1)}, bf16[256,256]{1,0:T(8,128)(2,1)S(1)}, u32[]{:S(2)}, u32[]{:S(2)}) %collective-permute-start.14) | collective-permute-done | bytes 131104 | tf_op jit(solution)/shard_map/ppermute | solution.py:624
  153.0 1.3 project.1
  154.3 0.1 collective-permute-start.16
  154.4 1.5 collective-permute-done.16
  155.9 0.8 add_convert_fusion
  156.7 1.4 unpack_tokens.1
  (41 shorter events, 0.1 us)
Async XLA Ops:
  7.2 15.7 %copy-start = (bf16[256,2048]{1,0:T(8,128)(2,1)S(1)}, bf16[256,2048]{1,0:T(8,128)(2,1)}, u32[]{:S(2)}) copy-start(bf16[256,2048]{1,0:T(8,128)(2,1)} %refs_0_.1) | copy-start | bytes 3145732
  7.3 1.7 %copy-start.1 = (bf16[512,2048]{1,0:T(8,128)(2,1)S(1)}, bf16[512,2048]{1,0:T(8,128)(2,1)}, u32[]{:S(2)}) copy-start(bf16[512,2048]{1,0:T(8,128)(2,1)} %tokens_ref.1) | copy-start | bytes 6291460
  8.9 0.7 copy-start.10
  9.6 19.4 %copy-start.14 = (s32[2,16384]{1,0:T(2,128)S(1)}, s32[2,16384]{1,0:T(2,128)}, u32[]{:S(2)}) copy-start(s32[2,16384]{1,0:T(2,128)} %earlier_ref.1) | copy-start | bytes 393220
  11.6 28.8 %all-to-all-start = ((bf16[32,16,512]{2,1,0:T(8,128)(2,1)}), bf16[32,16,512]{2,1,0:T(8,128)(2,1)S(1)}, u32[]{:S(2)}, u32[]{:S(2)}) async-start(bf16[32,16,512]{2,1,0:T(8,128)(2,1)} %bitcast.4), calls=%async_computation | async-start | bytes 1048576 | tf_op jit(solution)/shard_map/all_to_all | solution.py:615
  23.8 12.0 %collective-permute-start.2 = (bf16[256,512]{1,0:T(8,128)(2,1)}, bf16[256,512]{1,0:T(8,128)(2,1)S(1)}, u32[]{:S(2)}, u32[]{:S(2)}) collective-permute-start(bf16[256,512]{1,0:T(8,128)(2,1)} %get-tuple-element.48), channel_id=1, source_target_pairs={{0,4},{1,5},{2,6},{3,7},{4,0},{5,1},{6,2},{7,3},{8,12},{9,13},{10,... | collective-permute-start | bytes 786440 | tf_op jit(solution)/shard_map/ppermute | solution.py:624
  26.9 12.0 %collective-permute-start.1 = (bf16[256,512]{1,0:T(8,128)(2,1)}, bf16[256,512]{1,0:T(8,128)(2,1)S(1)}, u32[]{:S(2)}, u32[]{:S(2)}) collective-permute-start(bf16[256,512]{1,0:T(8,128)(2,1)} %get-tuple-element.49), channel_id=1, source_target_pairs={{0,6},{1,7},{2,0},{3,1},{4,2},{5,3},{6,4},{7,5},{8,14},{9,15},{10,... | collective-permute-start | bytes 786440 | tf_op jit(solution)/shard_map/ppermute | solution.py:624
  28.0 11.0 %collective-permute-start = (bf16[256,512]{1,0:T(8,128)(2,1)S(1)}, bf16[256,512]{1,0:T(8,128)(2,1)S(1)}, u32[]{:S(2)}, u32[]{:S(2)}) collective-permute-start(bf16[256,512]{1,0:T(8,128)(2,1)S(1)} %get-tuple-element.50), channel_id=1, source_target_pairs={{0,2},{1,3},{2,4},{3,5},{4,6},{5,7},{6,0},{7,1},{8,10},{9,11},{10,... | collective-permute-start | bytes 786440 | tf_op jit(solution)/shard_map/ppermute | solution.py:624
  29.0 1.6 copy-start.11
  30.6 1.2 copy-start.12
  31.8 1.2 copy-start.13
  34.8 1.0 copy-start.15
  35.8 6.6 %copy-start.3 = (bf16[256,512]{1,0:T(8,128)(2,1)}, bf16[256,512]{1,0:T(8,128)(2,1)S(1)}, u32[]{:S(2)}) copy-start(bf16[256,512]{1,0:T(8,128)(2,1)S(1)} %collective-permute-done.2.refs_3_) | copy-start | bytes 786436
  39.0 3.4 %copy-start.5 = (bf16[256,512]{1,0:T(8,128)(2,1)}, bf16[256,512]{1,0:T(8,128)(2,1)S(1)}, u32[]{:S(2)}) copy-start(bf16[256,512]{1,0:T(8,128)(2,1)S(1)} %collective-permute-done.1.refs_2_) | copy-start | bytes 786436
  39.0 3.4 %copy-start.7 = (bf16[256,512]{1,0:T(8,128)(2,1)}, bf16[256,512]{1,0:T(8,128)(2,1)S(1)}, u32[]{:S(2)}) copy-start(bf16[256,512]{1,0:T(8,128)(2,1)S(1)} %collective-permute-done.refs_1_) | copy-start | bytes 786436
  40.4 1.2 copy-start.16
  42.4 1.0 copy-start.2
  43.4 47.0 %all-to-all-start.1 = ((bf16[32,32,512]{2,1,0:T(8,128)(2,1)}), bf16[32,32,512]{2,1,0:T(8,128)(2,1)S(1)}, u32[]{:S(2)}, u32[]{:S(2)}) async-start(bf16[32,32,512]{2,1,0:T(8,128)(2,1)} %bitcast.10), calls=%async_computation.1 | async-start | bytes 2097152 | tf_op jit(solution)/shard_map/all_to_all | solution.py:615
  51.9 69.5 %reduce-scatter.2.cloned.1.call-start = ((), (), s32[]{:S(2)}) async-start(), calls=%async_computation.5 | async-start | bytes 2621440 | tf_op jit(solution)/shard_map/reduce_scatter | solution.py:684
  51.9 1.9 %copy-start.17 = (bf16[2,2048,256]{2,1,0:T(8,128)(2,1)S(1)}, bf16[2,2048,256]{2,1,0:T(8,128)(2,1)}, u32[]{:S(2)}) copy-start(bf16[2,2048,256]{2,1,0:T(8,128)(2,1)} %refs_6_.1) | copy-start | bytes 6291460
  51.9 2.5 %copy-start.18 = (bf16[2,256,2048]{2,1,0:T(8,128)(2,1)S(1)}, bf16[2,256,2048]{2,1,0:T(8,128)(2,1)}, u32[]{:S(2)}) copy-start(bf16[2,256,2048]{2,1,0:T(8,128)(2,1)} %refs_7_.1) | copy-start | bytes 6291460
  54.6 28.0 %collective-permute-start.9 = (bf16[1,256,2048]{2,1,0:T(8,128)(2,1)S(1)}, bf16[1,256,2048]{2,1,0:T(8,128)(2,1)S(1)}, u32[]{:S(2)}, u32[]{:S(2)}) collective-permute-start(bf16[1,256,2048]{2,1,0:T(8,128)(2,1)S(1)} %constant_dynamic-slice_fusion), channel_id=1, source_target_pairs={{0,1},{1,0},{2,3},{3,2},{4,5},{5,4},{6,7},{7,6},{8,9},{9,8},{10,11... | collective-permute-start | bytes 3145736 | tf_op jit(solution)/shard_map/ppermute | solution.py:674
  54.7 27.9 %collective-permute-start.8 = (bf16[1,2048,256]{2,1,0:T(8,128)(2,1)S(1)}, bf16[1,2048,256]{2,1,0:T(8,128)(2,1)S(1)}, u32[]{:S(2)}, u32[]{:S(2)}) collective-permute-start(bf16[1,2048,256]{2,1,0:T(8,128)(2,1)S(1)} %constant_dynamic-slice_fusion.1), channel_id=1, source_target_pairs={{0,1},{1,0},{2,3},{3,2},{4,5},{5,4},{6,7},{7,6},{8,9},{9,8},{10,11... | collective-permute-start | bytes 3145736 | tf_op jit(solution)/shard_map/ppermute | solution.py:674
  55.2 27.4 %collective-permute-start.7 = (bf16[1,2048,256]{2,1,0:T(8,128)(2,1)S(1)}, bf16[1,2048,256]{2,1,0:T(8,128)(2,1)S(1)}, u32[]{:S(2)}, u32[]{:S(2)}) collective-permute-start(bf16[1,2048,256]{2,1,0:T(8,128)(2,1)S(1)} %constant_dynamic-slice_fusion.2), channel_id=1, source_target_pairs={{0,1},{1,0},{2,3},{3,2},{4,5},{5,4},{6,7},{7,6},{8,9},{9,8},{10,11... | collective-permute-start | bytes 3145736 | tf_op jit(solution)/shard_map/ppermute | solution.py:674
  55.3 14.4 %collective-permute-start.4 = (bf16[32,16,512]{2,1,0:T(8,128)(2,1)S(1)}, bf16[32,16,512]{2,1,0:T(8,128)(2,1)S(1)}, u32[]{:S(2)}, u32[]{:S(2)}) collective-permute-start(bf16[32,16,512]{2,1,0:T(8,128)(2,1)S(1)} %all-to-all-done.refs_0_), channel_id=1, source_target_pairs={{0,6},{1,7},{2,0},{3,1},{4,2},{5,3},{6,4},{7,5},{8,14},{9,15},{10,... | collective-permute-start | bytes 1572872 | tf_op jit(solution)/shard_map/ppermute | solution.py:624
  57.9 15.6 %collective-permute-start.3 = (bf16[32,16,512]{2,1,0:T(8,128)(2,1)S(1)}, bf16[32,16,512]{2,1,0:T(8,128)(2,1)S(1)}, u32[]{:S(2)}, u32[]{:S(2)}) collective-permute-start(bf16[32,16,512]{2,1,0:T(8,128)(2,1)S(1)} %all-to-all-done.refs_0_), channel_id=1, source_target_pairs={{0,2},{1,3},{2,4},{3,5},{4,6},{5,7},{6,0},{7,1},{8,10},{9,11},{10,... | collective-permute-start | bytes 1572872 | tf_op jit(solution)/shard_map/ppermute | solution.py:624
  69.7 9.1 %collective-permute-start.6 = (bf16[16,16,512]{2,1,0:T(8,128)(2,1)S(1)}, bf16[16,16,512]{2,1,0:T(8,128)(2,1)S(1)}, u32[]{:S(2)}, u32[]{:S(2)}) collective-permute-start(bf16[16,16,512]{2,1,0:T(8,128)(2,1)S(1)} %slice.17), channel_id=1, source_target_pairs={{0,6},{1,7},{2,0},{3,1},{4,2},{5,3},{6,4},{7,5},{8,14},{9,15},{10,... | collective-permute-start | bytes 786440 | tf_op jit(solution)/shard_map/ppermute | solution.py:624
  73.5 9.0 %collective-permute-start.5 = (bf16[16,16,512]{2,1,0:T(8,128)(2,1)S(1)}, bf16[16,16,512]{2,1,0:T(8,128)(2,1)S(1)}, u32[]{:S(2)}, u32[]{:S(2)}) collective-permute-start(bf16[16,16,512]{2,1,0:T(8,128)(2,1)S(1)} %slice.16), channel_id=1, source_target_pairs={{0,2},{1,3},{2,4},{3,5},{4,6},{5,7},{6,0},{7,1},{8,10},{9,11},{10,... | collective-permute-start | bytes 786440 | tf_op jit(solution)/shard_map/ppermute | solution.py:624
  92.1 5.0 %collective-permute-start.10 = (bf16[2,64,512]{2,1,0:T(8,128)(2,1)S(1)}, bf16[2,64,512]{2,1,0:T(8,128)(2,1)S(1)}, u32[]{:S(2)}, u32[]{:S(2)}) collective-permute-start(bf16[2,64,512]{2,1,0:T(8,128)(2,1)S(1)} %get-tuple-element.36), channel_id=1, source_target_pairs={{0,8},{8,16},{16,24},{24,32},{32,40},{40,48},{48,56},{56,64},{64,7... | collective-permute-start | bytes 393224 | tf_op jit(solution)/shard_map/ppermute | solution.py:691
  100.3 28.9 %all-to-all-start.2 = ((bf16[32,40,256]{2,1,0:T(8,128)(2,1)}), bf16[32,40,256]{2,1,0:T(8,128)(2,1)S(1)}, u32[]{:S(2)}, u32[]{:S(2)}) async-start(bf16[32,40,256]{2,1,0:T(8,128)(2,1)} %attend_first.1), calls=%async_computation.2 | async-start | bytes 1310720 | tf_op jit(solution)/shard_map/all_to_all | solution.py:615
  122.3 8.0 %collective-permute-start.12 = (bf16[32,16,256]{2,1,0:T(8,128)(2,1)S(1)}, bf16[32,16,256]{2,1,0:T(8,128)(2,1)S(1)}, u32[]{:S(2)}, u32[]{:S(2)}) collective-permute-start(bf16[32,16,256]{2,1,0:T(8,128)(2,1)S(1)} %dynamic-slice_bitcast_fusion), channel_id=1, source_target_pairs={{0,1},{1,0},{2,3},{3,2},{4,5},{5,4},{6,7},{7,6},{8,9},{9,8},{10,11... | collective-permute-start | bytes 786440 | tf_op jit(solution)/shard_map/ppermute | solution.py:698
  130.3 22.7 %copy-start.4 = (bf16[256,512]{1,0:T(8,128)(2,1)S(1)}, bf16[256,512]{1,0:T(8,128)(2,1)}, u32[]{:S(2)}) copy-start(bf16[256,512]{1,0:T(8,128)(2,1)} %copy-done.3) | copy-start | bytes 786436
  130.3 22.7 %copy-start.6 = (bf16[256,512]{1,0:T(8,128)(2,1)S(1)}, bf16[256,512]{1,0:T(8,128)(2,1)}, u32[]{:S(2)}) copy-start(bf16[256,512]{1,0:T(8,128)(2,1)} %copy-done.5) | copy-start | bytes 786436
  130.3 22.7 %copy-start.8 = (bf16[256,512]{1,0:T(8,128)(2,1)S(1)}, bf16[256,512]{1,0:T(8,128)(2,1)}, u32[]{:S(2)}) copy-start(bf16[256,512]{1,0:T(8,128)(2,1)} %copy-done.7) | copy-start | bytes 786436
  130.3 1.1 copy-start.9
  132.8 23.9 %all-to-all-start.3 = ((bf16[32,2,16,256]{3,2,1,0:T(8,128)(2,1)}), bf16[32,2,16,256]{3,2,1,0:T(8,128)(2,1)S(1)}, u32[]{:S(2)}, u32[]{:S(2)}) async-start(bf16[32,2,16,256]{3,2,1,0:T(8,128)(2,1)} %place_rows.1), calls=%async_computation.4 | async-start | bytes 1048576 | tf_op jit(solution)/shard_map/all_to_all | solution.py:615
  137.6 6.9 %collective-permute-start.13 = (bf16[512,256]{1,0:T(8,128)(2,1)S(1)}, bf16[512,256]{1,0:T(8,128)(2,1)S(1)}, u32[]{:S(2)}, u32[]{:S(2)}) collective-permute-start(bf16[512,256]{1,0:T(8,128)(2,1)S(1)} %combine.1.own_ref), channel_id=1, source_target_pairs={{0,6},{1,7},{2,0},{3,1},{4,2},{5,3},{6,4},{7,5},{8,14},{9,15},{10,... | collective-permute-start | bytes 786440 | tf_op jit(solution)/shard_map/ppermute | solution.py:624
  138.2 8.5 %collective-permute-start.11 = (bf16[512,256]{1,0:T(8,128)(2,1)S(1)}, bf16[512,256]{1,0:T(8,128)(2,1)S(1)}, u32[]{:S(2)}, u32[]{:S(2)}) collective-permute-start(bf16[512,256]{1,0:T(8,128)(2,1)S(1)} %combine.1.own_ref), channel_id=1, source_target_pairs={{0,2},{1,3},{2,4},{3,5},{4,6},{5,7},{6,0},{7,1},{8,10},{9,11},{10,... | collective-permute-start | bytes 786440 | tf_op jit(solution)/shard_map/ppermute | solution.py:624
  144.6 5.0 %collective-permute-start.15 = (bf16[256,256]{1,0:T(8,128)(2,1)S(1)}, bf16[256,256]{1,0:T(8,128)(2,1)S(1)}, u32[]{:S(2)}, u32[]{:S(2)}) collective-permute-start(bf16[256,256]{1,0:T(8,128)(2,1)S(1)} %slice.15), channel_id=1, source_target_pairs={{0,6},{1,7},{2,0},{3,1},{4,2},{5,3},{6,4},{7,5},{8,14},{9,15},{10,... | collective-permute-start | bytes 393224 | tf_op jit(solution)/shard_map/ppermute | solution.py:624
  146.7 6.3 %collective-permute-start.14 = (bf16[256,256]{1,0:T(8,128)(2,1)S(1)}, bf16[256,256]{1,0:T(8,128)(2,1)S(1)}, u32[]{:S(2)}, u32[]{:S(2)}) collective-permute-start(bf16[256,256]{1,0:T(8,128)(2,1)S(1)} %slice.14), channel_id=1, source_target_pairs={{0,2},{1,3},{2,4},{3,5},{4,6},{5,7},{6,0},{7,1},{8,10},{9,11},{10,... | collective-permute-start | bytes 393224 | tf_op jit(solution)/shard_map/ppermute | solution.py:624
  154.3 1.6 collective-permute-start.16
Sparse Core Ops, SparseCore 0:
  90.5 30.8 reduce-scatter.1

commit v7 on v6

--- a/solution.py
+++ b/solution.py
@@ -49,7 +49,7 @@
     return flag(iota((count, count), 0) <= iota((count, count), 1))
 
 
-def project_rows_kernel(me_ref, perms_ref, x_ref, qk_ref, val_ref, rows_ref, pick_ref, token_ref, scratch):
+def pack_rows_kernel(me_ref, perms_ref, x_ref, qk_ref, val_ref, out_ref, token_ref, scratch):
     length, span = x_ref.shape[0], qk_ref.shape[1]
     rounds, total = perms_ref.shape
     peers = total // length
@@ -71,13 +71,13 @@
     for turn in range(rounds):
         row = to_row(by_round[:, turn].reshape(peers * per_peer, 1)).astype(I32)
         token_ref[turn] = jnp.broadcast_to(row, token_ref.shape[1:])
-    pick_ref[...] = flag(column.astype(I32) == iota((groups * per_peer, length), 1))
+    pick = flag(column.astype(I32) == iota((groups * per_peer, length), 1))
     for part, weight in enumerate((qk_ref, val_ref)):
         rows = dot(x_ref[...], weight[...]).astype(BF16)
-        rows_ref[:, part * span : (part + 1) * span] = rows
-
-
-def project_rows(me, perms, x_att, w_qk, w_val):
+        out_ref[:, part * span : (part + 1) * span] = dot(pick, rows).astype(BF16)
+
+
+def pack_rows(me, perms, x_att, w_qk, w_val):
     length, width = x_att.shape
     rounds, total = perms.shape
     span = w_qk.shape[1]
@@ -88,7 +88,7 @@
         return pl.BlockSpec(shape, lambda i, me_ref: (0, 0))
 
     return pl.pallas_call(
-        project_rows_kernel,
+        pack_rows_kernel,
         grid_spec=pltpu.PrefetchScalarGridSpec(
             num_scalar_prefetch=1,
             grid=(1,),
@@ -99,35 +99,19 @@
                 whole((width, span)),
             ],
             out_specs=[
-                whole((length, 2 * span)),
-                whole((slots, length)),
+                whole((slots, 2 * span)),
                 pl.BlockSpec((rounds, 8, length), lambda i, me_ref: (0, 0, 0)),
             ],
             scratch_shapes=[pltpu.VMEM((groups, length), I32)],
         ),
         out_shape=[
-            jax.ShapeDtypeStruct((length, 2 * span), BF16),
-            jax.ShapeDtypeStruct((slots, length), BF16),
+            jax.ShapeDtypeStruct((slots, 2 * span), BF16),
             jax.ShapeDtypeStruct((rounds, 8, length), I32),
         ],
         cost_estimate=cost(4 * length * width * span + 4 * slots * length * span, 6 << 20),
         compiler_params=BIG,
-        name="project_rows",
+        name="pack_rows",
     )(me, perms, x_att, w_qk, w_val)
-
-
-def pack_rows_kernel(pick_ref, rows_ref, out_ref):
-    out_ref[...] = dot(pick_ref[...], rows_ref[...]).astype(BF16)
-
-
-def pack_rows(pick, rows):
-    return pl.pallas_call(
-        pack_rows_kernel,
-        out_shape=jax.ShapeDtypeStruct((pick.shape[0], rows.shape[1]), BF16),
-        cost_estimate=cost(LONG, 2 << 20),
-        compiler_params=BIG,
-        name="pack_rows",
-    )(pick, rows)
 
 
 def pack_tokens_kernel(peers, where_ref, ids_ref, tokens_ref, out_ref, slot_ref):
@@ -177,73 +161,69 @@
     )(where, ids, tokens)
 
 
-def experts_kernel(where_ref, *refs):
-    step = pl.program_id(0)
-    shards, far_refs, weights = refs[0:3], refs[3:5], refs[5:11]
-    out_ref, total_ref = refs[11:]
-    peers, capacity, part = shards[0].shape
+def chip_at(place, core, chips):
+    return jnp.where(core == 0, place, chips - 1 - place)
+
+
+def experts_kernel(where_ref, x_ref, *refs):
+    step, chips = pl.program_id(0), pl.num_programs(0)
+    weights, (out_ref, total_ref) = refs[:-2], refs[-2:]
+    _, peers, capacity, part = x_ref.shape
     rows = peers * capacity
     ups = (weights[0], weights[1], weights[3], weights[4])
 
-    def add(x, start):
+    @pl.when(step == 0)
+    def _():
         for index, weight in enumerate(ups):
-            product = dot(x, weight[0])
-            total_ref[index] = product if start else total_ref[index] + product
-
-    for turn, shard in enumerate(shards):
-
-        @pl.when(step == turn)
-        def _(shard=shard, start=turn == 0):
-            add(shard[...].reshape(rows, part), start)
-
-    @pl.when(step == len(shards))
+            total_ref[index] = dot(x_ref[0].reshape(rows, part), weight[0])
+
+    @pl.when(step > 0)
     def _():
-        add(jnp.concatenate([ref[...].reshape(rows // 2, part) for ref in far_refs], axis=0), False)
+        for index, weight in enumerate(ups):
+            total_ref[index] += dot(x_ref[0].reshape(rows, part), weight[0])
+
+    @pl.when(step == chips - 1)
+    def _():
         hiddens = []
         for side in range(EXP_DEV):
             gate, up_val = total_ref[2 * side], total_ref[2 * side + 1]
             hiddens.append((gate / (1.0 + jnp.exp(-gate)) * up_val).astype(BF16))
         half = part // EXP_DEV
         for index in range(out_ref.shape[0]):
-            at = index * part
-            piece = dot(hiddens[0], weights[2][0, :, at : at + part])
-            piece = (piece + dot(hiddens[1], weights[5][0, :, at : at + part])).astype(BF16)
+            chip = chip_at(index, where_ref[1], out_ref.shape[0])
+            columns = pl.ds(pl.multiple_of(chip * part, part), part)
+            piece = dot(hiddens[0], weights[2][0, :, columns])
+            piece = (piece + dot(hiddens[1], weights[5][0, :, columns])).astype(BF16)
             for side in range(EXP_DEV):
                 columns = piece[:, side * half : (side + 1) * half]
                 out_ref[index, side] = columns.reshape(peers, capacity, half)
 
 
-def run_experts(where, shards, far, own, sibling):
-    peers, capacity, part = shards[0].shape
+def run_experts(where, x, own, sibling):
+    chips, peers, capacity, part = x.shape
     width, hidden = own[0].shape[1:]
-    chips = width // part
     out = (chips, EXP_DEV, peers, capacity, part // EXP_DEV)
     rows = peers * capacity
-
-    def rows_of(i, e):
-        ahead = jnp.where(i == 0, 0, jnp.where(i == 1, chips - 1, jnp.where(i == 2, 1, 2)))
-        return (e[0] + ahead) % chips
-
     up_block, down_block = (1, part, hidden), (1, hidden, width)
-    own_up = pl.BlockSpec(up_block, lambda i, e: (e[1], rows_of(i, e), 0))
-    sibling_up = pl.BlockSpec(up_block, lambda i, e: (0, rows_of(i, e), 0))
+    own_up = pl.BlockSpec(up_block, lambda i, e: (e[1], chip_at(i, e[1], chips), 0))
+    sibling_up = pl.BlockSpec(up_block, lambda i, e: (0, chip_at(i, e[1], chips), 0))
     own_down = pl.BlockSpec(down_block, lambda i, e: (e[1], 0, 0))
     sibling_down = pl.BlockSpec(down_block, lambda i, e: (0, 0, 0))
     return pl.pallas_call(
         experts_kernel,
         grid_spec=pltpu.PrefetchScalarGridSpec(
             num_scalar_prefetch=1,
-            grid=(len(shards) + 1,),
-            in_specs=[pl.BlockSpec(x.shape, lambda i, e: (0, 0, 0)) for x in (*shards, *far)]
+            grid=(chips,),
+            in_specs=[pl.BlockSpec((1, *x.shape[1:]), lambda i, e: (i, 0, 0, 0))]
             + [own_up, own_up, own_down, sibling_up, sibling_up, sibling_down],
             out_specs=pl.BlockSpec(out, lambda i, e: (0, 0, 0, 0, 0)),
-            scratch_shapes=[pltpu.VMEM((4, rows, hidden), F32)],
+            scratch_shapes=[pltpu.VMEM((2 * EXP_DEV, rows, hidden), F32)],
         ),
         out_shape=jax.ShapeDtypeStruct(out, BF16),
         cost_estimate=cost(12 * rows * width * hidden, 10 << 20),
         compiler_params=BIG,
         name="experts",
-    )(where, *shards, *far, *own, *sibling)
+    )(where, x, *own, *sibling)
 
 
 def place_rows_kernel(where_ref, rows_ref, taken_ref, out_ref):
@@ -566,11 +546,13 @@
     )(got, token)
 
 
-def project_kernel(where_ref, own_ref, prev_ref, next_ref, far_a_ref, far_b_ref, *refs):
+def project_kernel(where_ref, heads_ref, *refs):
     weights, (kept_ref, given_ref) = refs[:-2], refs[-2:]
-    far = jnp.concatenate([far_a_ref[...], far_b_ref[...]], axis=0)
-    total = dot(own_ref[...], weights[0][...]) + dot(prev_ref[...], weights[1][...])
-    total = total + dot(next_ref[...], weights[2][...]) + dot(far, weights[3][...])
+    chips = heads_ref.shape[0]
+    total = jnp.zeros((kept_ref.shape[0], 2 * kept_ref.shape[1]), F32)
+    for ahead, weight in zip((0, chips - 1, 1, 2), weights):
+        place = chip_at((where_ref[0] + ahead) % chips, where_ref[1], chips)
+        total = total + dot(heads_ref[place], weight[...])
     half = kept_ref.shape[1]
     for core in range(EXP_DEV):
 
@@ -582,23 +564,23 @@
 
 
 def project(where, heads, w_out, others):
-    length, span = heads[0].shape
+    _, length, span = heads.shape
     columns = others[0].shape[1]
     half = columns // EXP_DEV
-    weights = (w_out, *others)
-    shapes = [x.shape for x in heads] + [(span, columns)] + [x.shape for x in others]
 
     def first(i, e):
         return (0, 0)
 
-    specs = [pl.BlockSpec(shape, first) for shape in shapes]
-    specs[len(heads)] = pl.BlockSpec((span, columns), lambda i, e: (0, e[0]))
     return pl.pallas_call(
         project_kernel,
         grid_spec=pltpu.PrefetchScalarGridSpec(
             num_scalar_prefetch=1,
             grid=(1,),
-            in_specs=specs,
+            in_specs=[
+                pl.BlockSpec(heads.shape, lambda i, e: (0, 0, 0)),
+                pl.BlockSpec((span, columns), lambda i, e: (0, e[0])),
+            ]
+            + [pl.BlockSpec(x.shape, first) for x in others],
             out_specs=[pl.BlockSpec((length, half), first)] * 2,
         ),
         out_shape=[
@@ -608,7 +590,7 @@
         cost_estimate=cost(8 * length * span * columns, 3 << 20),
         compiler_params=BIG,
         name="project",
-    )(where, *heads, *weights)
+    )(where, heads, w_out, *others)
 
 
 def exchange(x, axis):
@@ -622,14 +604,6 @@
             there = (chip + by) % chips
             pairs.append((chip * EXP_DEV + core, there * EXP_DEV + core))
     return lax.ppermute(x, "exp", pairs)
-
-
-def spread(x, chips, ready=()):
-    half = x.shape[0] // 2
-    before, behind = hop(x, 1, chips), hop(x, -1, chips)
-    before, behind = (after(side, *ready) if ready else side for side in (before, behind))
-    far = (hop(before[:half], 1, chips), hop(behind[half:], -1, chips))
-    return (x, before, behind), far
 
 
 def after(x, *done):
@@ -650,13 +624,14 @@
     capacity = tokb // peers
     part = width // chips
     lines = [[chip * EXP_DEV + side for chip in range(chips)] for side in range(EXP_DEV)]
+    lines[1].reverse()
     siblings = [(i, i ^ 1) for i in range(parts)]
 
     dispatch, token_slot = pack_tokens(
         where, expert_ids.reshape(1, tokb), tokens_b, peers, capacity, part
     )
     received = exchange(dispatch.reshape(peers, capacity, part), "seq")
-    projected, pick, slot_token = project_rows(me, perms, x_att, w_qk, w_val)
+    outgoing, slot_token = pack_rows(me, perms, x_att, w_qk, w_val)
     columns = [
         hop(
             lax.dynamic_slice_in_dim(
@@ -667,8 +642,8 @@
         )
         for by in (1, chips - 1, 2)
     ]
-    received = after(received, projected, *columns)
-    outgoing = pack_rows(pick, after(projected, received))
+    received = after(received, outgoing, *columns)
+    outgoing = after(outgoing, received)
     own = (w_gate, w_up, w_down)
     sibling = [
         lax.ppermute(
@@ -676,9 +651,9 @@
         )
         for weight in own
     ]
-    shards, far = spread(received, chips)
+    gathered = lax.all_gather(received, "exp", axis=0, tiled=False, axis_index_groups=lines)
     arrived = exchange(outgoing.reshape(peers, rounds * per_peer, outgoing.shape[1]), "seq")
-    expert_part = run_experts(where, shards, far, own, sibling)
+    expert_part = run_experts(where, gathered, own, sibling)
     arrived = after(arrived, expert_part)
     rows, last, row_slot = sort_rows(me, perms, arrived, length)
     expert_rows = lax.psum_scatter(
@@ -696,11 +671,11 @@
     expert_rows = after(expert_rows, packed)
     given = lax.dynamic_index_in_dim(expert_rows, 1 - core, 0, keepdims=False)
     taken = lax.ppermute(given, "exp", siblings)
-    mixed_heads = combine(got, slot_token)
+    mixed_heads = combine(after(got, expert_rows), slot_token)
     expert_rows = place_rows(where, expert_rows, after(taken, mixed_heads))
     expert_back = exchange(expert_rows, "seq")
-    heads, far_heads = spread(mixed_heads, chips, (expert_rows,))
-    attn_kept, attn_given = project(where, (*heads, *far_heads), w_out, columns)
+    heads = lax.all_gather(mixed_heads, "exp", axis=0, tiled=False, axis_index_groups=lines)
+    attn_kept, attn_given = project(where, heads, w_out, columns)
     attended = attn_kept + lax.ppermute(attn_given, "exp", siblings).astype(F32)
     attended = attended.astype(BF16)
     expert_back = after(expert_back, attended)

time: 167 us -> 165 us (0.988)
  starting transfers between devices: 54.4 us -> 44.6 us
  Pallas kernels: 25.3 us -> 28.9 us
  waiting for transfers between devices: 54.9 us -> 57.9 us
    ppermute x11 -> x3, waiting for transfers between devices: 34.5 us -> 2.32 us  [hop(): return lax.ppermute(x, 'exp', pairs)]
    all_gather x0 -> x2, waiting for transfers between devices: none -> 29.8 us  [the longest x1 15.4 us: body(): lax.all_gather(received, 'exp', axis=0, tiled=False, axis_index_groups=li...]
    ppermute x11 -> x3, starting transfers between devices: 16.4 us -> 5.22 us  [hop(): return lax.ppermute(x, 'exp', pairs)]
    ppermute x3, waiting for transfers between devices: 0.01 us -> 4.08 us  [body(): lax.ppermute(lax.dynamic_slice_in_dim(after(weight, received), 1 - core,...]
    pallas_call x2 -> x1, Pallas kernels: 2.46 us -> 4.83 us  [pack_rows(): pl.pallas_call(pack_rows_kernel, grid_spec=pltpu.PrefetchScalarGridSpec(n...]
    unnamed x38 -> x42, local copies, waits for them, and re-layouts: 11.7 us -> 12.6 us
  transfers between devices with their start and end apart: 22 -> 16, of which waited for: 12 -> 11; matrix products, arithmetic and copies ran while one was open for 3% -> 3% of each run, Pallas kernels for 12% -> 16%
where the time goes in v7:
time: 165 us; the launch traced here: 162 us
  waiting for transfers between devices  57.9 us (35%)
  starting transfers between devices  44.6 us (27%)
  Pallas kernels  28.9 us (18%)
  local copies, waits for them, and re-layouts  16.1 us (10%)
  between operations  14.1 us (9%)
    all_to_all x4, starting transfers between devices, exchange(): return lax.all_to_all(x, axis, split_axis=0, concat_axis=0, tiled=True)  36.6 us
    all_gather x1, waiting for transfers between devices, body(): lax.all_gather(received, 'exp', axis=0, tiled=False, axis_index_groups=li...  15.4 us
    all_gather x1, waiting for transfers between devices, body(): lax.all_gather(mixed_heads, 'exp', axis=0, tiled=False, axis_index_groups...  14.5 us
    unnamed x42, local copies, waits for them, and re-layouts  12.6 us
    reduce_scatter x1, waiting for transfers between devices, body(): lax.psum_scatter(expert_part, 'exp', scatter_dimension=0, tiled=False, ax...  9.98 us
    all_to_all x4, waiting for transfers between devices, exchange(): return lax.all_to_all(x, axis, split_axis=0, concat_axis=0, tiled=True)  9.23 us
    pallas_call x1, Pallas kernels, run_experts(): pl.pallas_call(experts_kernel, grid_spec=pltpu.PrefetchScalarGridSpec(num...  8.31 us
    ppermute x3, starting transfers between devices, hop(): return lax.ppermute(x, 'exp', pairs)  5.22 us
  transfers between devices with their start and end apart: 16, of which 11 were waited for; matrix products, arithmetic and copies ran while one was open for 3% of the time, Pallas kernels for 16%

profile of v7, /device:TPU:32, one launch (start us, length us, event | category | flops | bytes accessed | tf_op | source)
XLA Modules:
  0.0 162.4 jit_solution(5126339701218953771)
XLA Ops:
  7.2 0.1 pad_add_fusion.where_ref
  7.3 1.7 %copy-done.1 = bf16[512,2048]{1,0:T(8,128)(2,1)S(1)} copy-done((bf16[512,2048]{1,0:T(8,128)(2,1)S(1)}, bf16[512,2048]{1,0:T(8,128)(2,1)}, u32[]{:S(2)}) %copy-start.1) | copy-done | bytes 2097176
  8.9 0.7 copy-done.14
  9.6 2.0 %pack_tokens.1 = (bf16[512,512]{1,0:T(8,128)(2,1)}, s32[8,512]{1,0:T(8,128)S(1)}) custom-call(s32[2]{0:T(128)S(1)} %pad_add_fusion.where_ref, s32[1,512]{1,0:T(1,128)S(1)} %bitcast.16, bf16[512,2048]{1,0:T(8,128)(2,1)S(1)} %copy-done.1), custom_call_target="tpu_custom_call" | custom-call | flops 268435456 | bytes 2097152 | tf_op jit(solution)/shard_map/pack_tokens/pallas_call | solution.py:140
  11.6 11.2 %all-to-all-start = ((bf16[32,16,512]{2,1,0:T(8,128)(2,1)}), bf16[32,16,512]{2,1,0:T(8,128)(2,1)}, u32[]{:S(2)}, u32[]{:S(2)}) async-start(bf16[32,16,512]{2,1,0:T(8,128)(2,1)} %bitcast.4), calls=%async_computation | async-start | bytes 1048576 | tf_op jit(solution)/shard_map/all_to_all | solution.py:597
  22.9 0.0 all-gather.5.cloned.1.call-start
  23.0 0.9 constant_dynamic-slice_fusion.3
  23.8 3.2 %collective-permute-start.2 = (bf16[256,512]{1,0:T(8,128)(2,1)}, bf16[256,512]{1,0:T(8,128)(2,1)S(1)}, u32[]{:S(2)}, u32[]{:S(2)}) collective-permute-start(bf16[256,512]{1,0:T(8,128)(2,1)} %get-tuple-element.44), channel_id=1, source_target_pairs={{0,4},{1,5},{2,6},{3,7},{4,0},{5,1},{6,2},{7,3},{8,12},{9,13},{10,... | collective-permute-start | bytes 786440 | tf_op jit(solution)/shard_map/ppermute | solution.py:606
  27.0 1.1 collective-permute-start.1
  28.1 1.0 collective-permute-start
  29.1 1.6 copy-done.15
  30.7 1.2 copy-done.17
  31.9 4.8 %pack_rows.1 = (bf16[1024,512]{1,0:T(8,128)(2,1)}, s32[2,8,512]{2,1,0:T(8,128)S(1)}) custom-call(s32[1]{0:T(128)} %bitcast.2.me_ref, s32[2,16384]{1,0:T(2,128)S(1)} %copy-done.18, bf16[512,2048]{1,0:T(8,128)(2,1)S(1)} %copy-done.15, bf16[2048,256]{1,0:T(8,128)(2,1)S(1)} %copy-done.16, bf16[2048,256]{1,0:T(8,128)(2,1)S(1)} %copy-done.17), custom_call_target="tpu_custom_call" | custom-call | flops 1610612736 | bytes 6291456 | tf_op jit(solution)/shard_map/pack_rows/pallas_call | solution.py:90
  36.7 2.3 %collective-permute-done.1.refs_2_ = bf16[256,512]{1,0:T(8,128)(2,1)S(1)} collective-permute-done((bf16[256,512]{1,0:T(8,128)(2,1)}, bf16[256,512]{1,0:T(8,128)(2,1)S(1)}, u32[]{:S(2)}, u32[]{:S(2)}) %collective-permute-start.1) | collective-permute-done | bytes 262176 | tf_op jit(solution)/shard_map/ppermute | solution.py:606
  39.1 0.7 copy-done.11
  39.8 0.7 all-to-all-done
  40.5 0.0 all-gather.5.cloned.1.call-update
  40.6 9.1 %all-to-all-start.1 = ((bf16[32,32,512]{2,1,0:T(8,128)(2,1)}), bf16[32,32,512]{2,1,0:T(8,128)(2,1)S(1)}, u32[]{:S(2)}, u32[]{:S(2)}) async-start(bf16[32,32,512]{2,1,0:T(8,128)(2,1)} %bitcast.5), calls=%async_computation.1 | async-start | bytes 2097152 | tf_op jit(solution)/shard_map/all_to_all | solution.py:597
  49.7 0.0 reduce-scatter.2.cloned.1.call-start
  49.7 0.0 copy-start.19
  49.7 0.0 copy-start.20
  49.7 1.4 constant_dynamic-slice_fusion.2
  51.2 0.4 copy-done.19
  51.6 0.1 constant_dynamic-slice_fusion.1
  51.7 0.6 copy-done.20
  52.3 0.1 constant_dynamic-slice_fusion
  52.4 0.1 collective-permute-start.5
  52.5 0.5 collective-permute-start.4
  53.0 0.1 collective-permute-start.3
  53.1 2.0 %collective-permute-done.5.refs_5_ = bf16[1,256,2048]{2,1,0:T(8,128)(2,1)S(1)} collective-permute-done((bf16[1,256,2048]{2,1,0:T(8,128)(2,1)S(1)}, bf16[1,256,2048]{2,1,0:T(8,128)(2,1)S(1)}, u32[]{:S(2)}, u32[]{:S(2)}) %collective-permute-start.5) | collective-permute-done | bytes 1048608 | tf_op jit(solution)/shard_map/ppermute | solution.py:649
  55.2 1.5 collective-permute-done.4.refs_4_
  56.7 1.0 copy-done.3
  57.6 0.5 collective-permute-done.3.refs_3_
  58.2 1.0 copy-done.5
  59.1 15.4 %all-gather.5.cloned.1.call-done = bf16[128,16,512]{2,1,0:T(8,128)(2,1)} async-done(((bf16[32,16,512]{2,1,0:T(8,128)(2,1)}), bf16[128,16,512]{2,1,0:T(8,128)(2,1)}) %all-gather.5.cloned.1.call-update) | async-done | bytes 2097168 | tf_op jit(solution)/shard_map/all_gather | solution.py:654
  74.5 1.2 copy-done.4
  75.7 1.2 copy-done.6
  76.9 8.3 %experts.1 = bf16[4,2,32,16,256]{4,3,2,1,0:T(8,128)(2,1)} custom-call(s32[2]{0:T(128)S(1)} %pad_add_fusion.where_ref, bf16[4,32,16,512]{3,2,1,0:T(8,128)(2,1)} %bitcast.17, bf16[2,2048,256]{2,1,0:T(8,128)(2,1)} %refs_0_.2, bf16[2,2048,256]{2,1,0:T(8,128)(2,1)} %refs_1_.1, bf16[2,256,2048]{2,1,0:T(8,128)(2,1)} %refs_2_.1, ...), custom_call_target="tpu_custom_call" | custom-call | flops 3221225472 | bytes 10485760 | tf_op jit(solution)/shard_map/experts/pallas_call | solution.py:212
  85.2 0.0 reduce-scatter.2.cloned.1.call-update
  85.3 0.0 all-to-all-done.1.arrived_ref
  85.3 1.7 %sort_rows.1 = (bf16[2,512,512]{2,1,0:T(8,128)(2,1)S(1)}, bf16[2,64,512]{2,1,0:T(8,128)(2,1)S(1)}, s32[2,8,512]{2,1,0:T(8,128)S(1)}) custom-call(s32[1]{0:T(128)} %bitcast.2.me_ref, s32[2,16384]{1,0:T(2,128)S(1)} %copy-done.18, bf16[32,32,512]{2,1,0:T(8,128)(2,1)S(1)} %all-to-all-done.1.arrived_ref), custom_call_target="tpu_custom_call" | custom-call | flops 34359738368 | bytes 4194304 | tf_op jit(solution)/shard_map/sort_rows/pallas_call | solution.py:293
  87.0 1.8 %collective-permute-start.6 = (bf16[2,64,512]{2,1,0:T(8,128)(2,1)S(1)}, bf16[2,64,512]{2,1,0:T(8,128)(2,1)S(1)}, u32[]{:S(2)}, u32[]{:S(2)}) collective-permute-start(bf16[2,64,512]{2,1,0:T(8,128)(2,1)S(1)} %get-tuple-element.33), channel_id=1, source_target_pairs={{0,8},{8,16},{16,24},{24,32},{32,40},{40,48},{48,56},{56,64},{64,7... | collective-permute-start | bytes 393224 | tf_op jit(solution)/shard_map/ppermute | solution.py:666
  88.8 3.0 %attend_later.1.later_ref = bf16[2,384,384]{2,1,0:T(8,128)(2,1)S(1)} custom-call(s32[1]{0:T(128)} %bitcast.2.me_ref, s32[2,16384]{1,0:T(2,128)S(1)} %copy-done.18, bf16[2,512,512]{2,1,0:T(8,128)(2,1)S(1)} %get-tuple-element.32.rows_ref), custom_call_target="tpu_custom_call" | custom-call | flops 34359738368 | bytes 4194304 | tf_op jit(solution)/shard_map/attend_later/pallas_call | solution.py:444
  91.8 0.9 collective-permute-done.6.last_ref
  92.7 3.1 %attend_first.1 = bf16[32,40,256]{2,1,0:T(8,128)(2,1)} custom-call(s32[1]{0:T(128)} %bitcast.2.me_ref, s32[2,16384]{1,0:T(2,128)S(1)} %copy-done.18, s32[2,16384]{1,0:T(2,128)S(1)} %copy-done.18, bf16[2,512,512]{2,1,0:T(8,128)(2,1)S(1)} %get-tuple-element.32.rows_ref, bf16[2,64,512]{2,1,0:T(8,128)(2,1)S(1)} %collective-permute-done.6.last_ref, ...), custom_call_target="tpu_custom_call" | custom-call | flops 34359738368 | bytes 4194304 | tf_op jit(solution)/shard_map/attend_first/pallas_call | solution.py:472
  95.8 11.3 %all-to-all-start.2 = ((bf16[32,40,256]{2,1,0:T(8,128)(2,1)}), bf16[32,40,256]{2,1,0:T(8,128)(2,1)S(1)}, u32[]{:S(2)}, u32[]{:S(2)}) async-start(bf16[32,40,256]{2,1,0:T(8,128)(2,1)} %attend_first.1), calls=%async_computation.2 | async-start | bytes 1310720 | tf_op jit(solution)/shard_map/all_to_all | solution.py:597
  107.1 0.0 all-gather.7.cloned.1.call-start
  107.1 10.0 %reduce-scatter.2.cloned.1.call-done = bf16[1,2,32,16,256]{4,3,2,1,0:T(8,128)(2,1)} async-done(((bf16[4,2,32,16,256]{4,3,2,1,0:T(8,128)(2,1)}), bf16[1,2,32,16,256]{4,3,2,1,0:T(8,128)(2,1)}) %reduce-scatter.2.cloned.1.call-update) | async-done | bytes 524304 | tf_op jit(solution)/shard_map/reduce_scatter | solution.py:659
  117.1 1.0 dynamic-slice_bitcast_fusion
  118.1 0.1 collective-permute-start.8
  118.2 8.5 %all-to-all-done.2.got_ref = bf16[32,40,256]{2,1,0:T(8,128)(2,1)S(1)} async-done(((bf16[32,40,256]{2,1,0:T(8,128)(2,1)}), bf16[32,40,256]{2,1,0:T(8,128)(2,1)S(1)}, u32[]{:S(2)}, u32[]{:S(2)}) %all-to-all-start.2) | async-done | bytes 655392 | tf_op jit(solution)/shard_map/all_to_all | solution.py:597
  126.7 1.8 %combine.1 = bf16[512,256]{1,0:T(8,128)(2,1)} custom-call(bf16[32,40,256]{2,1,0:T(8,128)(2,1)S(1)} %all-to-all-done.2.got_ref, s32[2,8,512]{2,1,0:T(8,128)S(1)} %get-tuple-element.38.token_ref), custom_call_target="tpu_custom_call" | custom-call | flops 402653184 | bytes 1048576 | tf_op jit(solution)/shard_map/combine/pallas_call | solution.py:540
  128.5 0.0 all-gather.7.cloned.1.call-update
  128.5 0.0 copy-start.12
  128.6 0.0 collective-permute-done.8.taken_ref
  128.6 1.4 place_rows.1
  130.0 5.0 %all-to-all-start.3 = ((bf16[32,2,16,256]{3,2,1,0:T(8,128)(2,1)}), bf16[32,2,16,256]{3,2,1,0:T(8,128)(2,1)S(1)}, u32[]{:S(2)}, u32[]{:S(2)}) async-start(bf16[32,2,16,256]{3,2,1,0:T(8,128)(2,1)} %place_rows.1), calls=%async_computation.4 | async-start | bytes 1048576 | tf_op jit(solution)/shard_map/all_to_all | solution.py:597
  135.0 14.5 %all-gather.7.cloned.1.call-done = bf16[2048,256]{1,0:T(8,128)(2,1)} async-done(((bf16[512,256]{1,0:T(8,128)(2,1)}), bf16[2048,256]{1,0:T(8,128)(2,1)}) %all-gather.7.cloned.1.call-update) | async-done | bytes 1048592 | tf_op jit(solution)/shard_map/all_gather | solution.py:677
  149.4 1.2 copy-done.2
  150.7 1.3 project.1
  152.0 0.1 collective-permute-start.7
  152.1 1.5 collective-permute-done.7
  153.6 0.8 add_convert_fusion
  154.4 1.4 unpack_tokens.1
  (30 shorter events, 0.1 us)
Async XLA Ops:
  7.2 15.8 %copy-start = (bf16[256,2048]{1,0:T(8,128)(2,1)S(1)}, bf16[256,2048]{1,0:T(8,128)(2,1)}, u32[]{:S(2)}) copy-start(bf16[256,2048]{1,0:T(8,128)(2,1)} %refs_0_.3) | copy-start | bytes 3145732
  7.3 1.7 %copy-start.1 = (bf16[512,2048]{1,0:T(8,128)(2,1)S(1)}, bf16[512,2048]{1,0:T(8,128)(2,1)}, u32[]{:S(2)}) copy-start(bf16[512,2048]{1,0:T(8,128)(2,1)} %tokens_ref.1) | copy-start | bytes 6291460
  8.9 0.7 copy-start.14
  9.6 19.5 %copy-start.16 = (bf16[2048,256]{1,0:T(8,128)(2,1)S(1)}, bf16[2048,256]{1,0:T(8,128)(2,1)}, u32[]{:S(2)}) copy-start(bf16[2048,256]{1,0:T(8,128)(2,1)} %qk_ref.1) | copy-start | bytes 3145732
  9.6 19.5 %copy-start.18 = (s32[2,16384]{1,0:T(2,128)S(1)}, s32[2,16384]{1,0:T(2,128)}, u32[]{:S(2)}) copy-start(s32[2,16384]{1,0:T(2,128)} %earlier_ref.1) | copy-start | bytes 393220
  11.6 28.9 %all-to-all-start = ((bf16[32,16,512]{2,1,0:T(8,128)(2,1)}), bf16[32,16,512]{2,1,0:T(8,128)(2,1)}, u32[]{:S(2)}, u32[]{:S(2)}) async-start(bf16[32,16,512]{2,1,0:T(8,128)(2,1)} %bitcast.4), calls=%async_computation | async-start | bytes 1048576 | tf_op jit(solution)/shard_map/all_to_all | solution.py:597
  22.9 51.6 %all-gather.5.cloned.1.call-start = ((), (), s32[]{:S(2)}) async-start(), calls=%async_computation.6 | async-start | bytes 2621440 | tf_op jit(solution)/shard_map/all_gather | solution.py:654
  23.8 12.9 %collective-permute-start.2 = (bf16[256,512]{1,0:T(8,128)(2,1)}, bf16[256,512]{1,0:T(8,128)(2,1)S(1)}, u32[]{:S(2)}, u32[]{:S(2)}) collective-permute-start(bf16[256,512]{1,0:T(8,128)(2,1)} %get-tuple-element.44), channel_id=1, source_target_pairs={{0,4},{1,5},{2,6},{3,7},{4,0},{5,1},{6,2},{7,3},{8,12},{9,13},{10,... | collective-permute-start | bytes 786440 | tf_op jit(solution)/shard_map/ppermute | solution.py:606
  27.0 12.0 %collective-permute-start.1 = (bf16[256,512]{1,0:T(8,128)(2,1)}, bf16[256,512]{1,0:T(8,128)(2,1)S(1)}, u32[]{:S(2)}, u32[]{:S(2)}) collective-permute-start(bf16[256,512]{1,0:T(8,128)(2,1)} %get-tuple-element.45), channel_id=1, source_target_pairs={{0,6},{1,7},{2,0},{3,1},{4,2},{5,3},{6,4},{7,5},{8,14},{9,15},{10,... | collective-permute-start | bytes 786440 | tf_op jit(solution)/shard_map/ppermute | solution.py:606
  28.1 11.0 %collective-permute-start = (bf16[256,512]{1,0:T(8,128)(2,1)S(1)}, bf16[256,512]{1,0:T(8,128)(2,1)S(1)}, u32[]{:S(2)}, u32[]{:S(2)}) collective-permute-start(bf16[256,512]{1,0:T(8,128)(2,1)S(1)} %get-tuple-element.46), channel_id=1, source_target_pairs={{0,2},{1,3},{2,4},{3,5},{4,6},{5,7},{6,0},{7,1},{8,10},{9,11},{10,... | collective-permute-start | bytes 786440 | tf_op jit(solution)/shard_map/ppermute | solution.py:606
  29.1 1.6 copy-start.15
  30.7 1.2 copy-start.17
  36.7 3.8 %copy-start.7 = (bf16[256,512]{1,0:T(8,128)(2,1)}, bf16[256,512]{1,0:T(8,128)(2,1)S(1)}, u32[]{:S(2)}) copy-start(bf16[256,512]{1,0:T(8,128)(2,1)S(1)} %collective-permute-done.2.refs_3_) | copy-start | bytes 786436
  39.1 1.5 copy-start.9
  39.1 0.7 copy-start.11
  40.6 44.7 %all-to-all-start.1 = ((bf16[32,32,512]{2,1,0:T(8,128)(2,1)}), bf16[32,32,512]{2,1,0:T(8,128)(2,1)S(1)}, u32[]{:S(2)}, u32[]{:S(2)}) async-start(bf16[32,32,512]{2,1,0:T(8,128)(2,1)} %bitcast.5), calls=%async_computation.1 | async-start | bytes 2097152 | tf_op jit(solution)/shard_map/all_to_all | solution.py:597
  49.7 67.4 %reduce-scatter.2.cloned.1.call-start = ((), (), s32[]{:S(2)}) async-start(), calls=%async_computation.5 | async-start | bytes 2621440 | tf_op jit(solution)/shard_map/reduce_scatter | solution.py:659
  49.7 1.9 %copy-start.19 = (bf16[2,2048,256]{2,1,0:T(8,128)(2,1)S(1)}, bf16[2,2048,256]{2,1,0:T(8,128)(2,1)}, u32[]{:S(2)}) copy-start(bf16[2,2048,256]{2,1,0:T(8,128)(2,1)} %refs_1_.1) | copy-start | bytes 6291460
  49.7 2.6 %copy-start.20 = (bf16[2,256,2048]{2,1,0:T(8,128)(2,1)S(1)}, bf16[2,256,2048]{2,1,0:T(8,128)(2,1)}, u32[]{:S(2)}) copy-start(bf16[2,256,2048]{2,1,0:T(8,128)(2,1)} %refs_2_.1) | copy-start | bytes 6291460
  52.4 2.7 %collective-permute-start.5 = (bf16[1,256,2048]{2,1,0:T(8,128)(2,1)S(1)}, bf16[1,256,2048]{2,1,0:T(8,128)(2,1)S(1)}, u32[]{:S(2)}, u32[]{:S(2)}) collective-permute-start(bf16[1,256,2048]{2,1,0:T(8,128)(2,1)S(1)} %constant_dynamic-slice_fusion), channel_id=1, source_target_pairs={{0,1},{1,0},{2,3},{3,2},{4,5},{5,4},{6,7},{7,6},{8,9},{9,8},{10,11... | collective-permute-start | bytes 3145736 | tf_op jit(solution)/shard_map/ppermute | solution.py:649
  52.5 4.1 %collective-permute-start.4 = (bf16[1,2048,256]{2,1,0:T(8,128)(2,1)S(1)}, bf16[1,2048,256]{2,1,0:T(8,128)(2,1)S(1)}, u32[]{:S(2)}, u32[]{:S(2)}) collective-permute-start(bf16[1,2048,256]{2,1,0:T(8,128)(2,1)S(1)} %constant_dynamic-slice_fusion.1), channel_id=1, source_target_pairs={{0,1},{1,0},{2,3},{3,2},{4,5},{5,4},{6,7},{7,6},{8,9},{9,8},{10,11... | collective-permute-start | bytes 3145736 | tf_op jit(solution)/shard_map/ppermute | solution.py:649
  53.0 5.1 %collective-permute-start.3 = (bf16[1,2048,256]{2,1,0:T(8,128)(2,1)S(1)}, bf16[1,2048,256]{2,1,0:T(8,128)(2,1)S(1)}, u32[]{:S(2)}, u32[]{:S(2)}) collective-permute-start(bf16[1,2048,256]{2,1,0:T(8,128)(2,1)S(1)} %constant_dynamic-slice_fusion.2), channel_id=1, source_target_pairs={{0,1},{1,0},{2,3},{3,2},{4,5},{5,4},{6,7},{7,6},{8,9},{9,8},{10,11... | collective-permute-start | bytes 3145736 | tf_op jit(solution)/shard_map/ppermute | solution.py:649
  56.7 1.0 copy-start.3
  58.2 1.0 copy-start.5
  74.5 1.2 copy-start.4
  75.7 1.2 copy-start.6
  87.0 5.7 %collective-permute-start.6 = (bf16[2,64,512]{2,1,0:T(8,128)(2,1)S(1)}, bf16[2,64,512]{2,1,0:T(8,128)(2,1)S(1)}, u32[]{:S(2)}, u32[]{:S(2)}) collective-permute-start(bf16[2,64,512]{2,1,0:T(8,128)(2,1)S(1)} %get-tuple-element.33), channel_id=1, source_target_pairs={{0,8},{8,16},{16,24},{24,32},{32,40},{40,48},{48,56},{56,64},{64,7... | collective-permute-start | bytes 393224 | tf_op jit(solution)/shard_map/ppermute | solution.py:666
  95.8 30.9 %all-to-all-start.2 = ((bf16[32,40,256]{2,1,0:T(8,128)(2,1)}), bf16[32,40,256]{2,1,0:T(8,128)(2,1)S(1)}, u32[]{:S(2)}, u32[]{:S(2)}) async-start(bf16[32,40,256]{2,1,0:T(8,128)(2,1)} %attend_first.1), calls=%async_computation.2 | async-start | bytes 1310720 | tf_op jit(solution)/shard_map/all_to_all | solution.py:597
  107.1 42.4 %all-gather.7.cloned.1.call-start = ((), (), s32[]{:S(2)}) async-start(), calls=%async_computation.7 | async-start | bytes 1310720 | tf_op jit(solution)/shard_map/all_gather | solution.py:677
  117.1 11.5 %copy-start.13 = (bf16[1,2,32,16,256]{4,3,2,1,0:T(8,128)(2,1)S(1)}, bf16[1,2,32,16,256]{4,3,2,1,0:T(8,128)(2,1)}, u32[]{:S(2)}) copy-start(bf16[1,2,32,16,256]{4,3,2,1,0:T(8,128)(2,1)} %reduce-scatter.2.cloned.1.call-done) | copy-start | bytes 1572868
  118.1 10.4 %collective-permute-start.8 = (bf16[32,16,256]{2,1,0:T(8,128)(2,1)S(1)}, bf16[32,16,256]{2,1,0:T(8,128)(2,1)S(1)}, u32[]{:S(2)}, u32[]{:S(2)}) collective-permute-start(bf16[32,16,256]{2,1,0:T(8,128)(2,1)S(1)} %dynamic-slice_bitcast_fusion), channel_id=1, source_target_pairs={{0,1},{1,0},{2,3},{3,2},{4,5},{5,4},{6,7},{7,6},{8,9},{9,8},{10,11... | collective-permute-start | bytes 786440 | tf_op jit(solution)/shard_map/ppermute | solution.py:673
  128.5 20.9 %copy-start.8 = (bf16[256,512]{1,0:T(8,128)(2,1)S(1)}, bf16[256,512]{1,0:T(8,128)(2,1)}, u32[]{:S(2)}) copy-start(bf16[256,512]{1,0:T(8,128)(2,1)} %copy-done.7) | copy-start | bytes 786436
  128.5 20.9 %copy-start.10 = (bf16[256,512]{1,0:T(8,128)(2,1)S(1)}, bf16[256,512]{1,0:T(8,128)(2,1)}, u32[]{:S(2)}) copy-start(bf16[256,512]{1,0:T(8,128)(2,1)} %copy-done.9) | copy-start | bytes 786436
  128.5 20.9 %copy-start.12 = (bf16[256,512]{1,0:T(8,128)(2,1)S(1)}, bf16[256,512]{1,0:T(8,128)(2,1)}, u32[]{:S(2)}) copy-start(bf16[256,512]{1,0:T(8,128)(2,1)} %copy-done.11) | copy-start | bytes 786436
  130.0 24.4 %all-to-all-start.3 = ((bf16[32,2,16,256]{3,2,1,0:T(8,128)(2,1)}), bf16[32,2,16,256]{3,2,1,0:T(8,128)(2,1)S(1)}, u32[]{:S(2)}, u32[]{:S(2)}) async-start(bf16[32,2,16,256]{3,2,1,0:T(8,128)(2,1)} %place_rows.1), calls=%async_computation.4 | async-start | bytes 1048576 | tf_op jit(solution)/shard_map/all_to_all | solution.py:597
  149.4 1.2 copy-start.2
  152.0 1.6 collective-permute-start.7
Sparse Core Ops, SparseCore 0:
  40.7 33.7 all-gather.4
  85.4 31.6 reduce-scatter.1
  128.6 20.7 all-gather.6

commit v8 on v6

--- a/solution.py
+++ b/solution.py
@@ -49,7 +49,7 @@
     return flag(iota((count, count), 0) <= iota((count, count), 1))
 
 
-def project_rows_kernel(me_ref, perms_ref, x_ref, qk_ref, val_ref, rows_ref, pick_ref, token_ref, scratch):
+def pack_rows_kernel(me_ref, perms_ref, x_ref, qk_ref, val_ref, out_ref, token_ref, scratch):
     length, span = x_ref.shape[0], qk_ref.shape[1]
     rounds, total = perms_ref.shape
     peers = total // length
@@ -71,13 +71,13 @@
     for turn in range(rounds):
         row = to_row(by_round[:, turn].reshape(peers * per_peer, 1)).astype(I32)
         token_ref[turn] = jnp.broadcast_to(row, token_ref.shape[1:])
-    pick_ref[...] = flag(column.astype(I32) == iota((groups * per_peer, length), 1))
+    pick = flag(column.astype(I32) == iota((groups * per_peer, length), 1))
     for part, weight in enumerate((qk_ref, val_ref)):
         rows = dot(x_ref[...], weight[...]).astype(BF16)
-        rows_ref[:, part * span : (part + 1) * span] = rows
-
-
-def project_rows(me, perms, x_att, w_qk, w_val):
+        out_ref[:, part * span : (part + 1) * span] = dot(pick, rows).astype(BF16)
+
+
+def pack_rows(me, perms, x_att, w_qk, w_val):
     length, width = x_att.shape
     rounds, total = perms.shape
     span = w_qk.shape[1]
@@ -88,7 +88,7 @@
         return pl.BlockSpec(shape, lambda i, me_ref: (0, 0))
 
     return pl.pallas_call(
-        project_rows_kernel,
+        pack_rows_kernel,
         grid_spec=pltpu.PrefetchScalarGridSpec(
             num_scalar_prefetch=1,
             grid=(1,),
@@ -99,35 +99,19 @@
                 whole((width, span)),
             ],
             out_specs=[
-                whole((length, 2 * span)),
-                whole((slots, length)),
+                whole((slots, 2 * span)),
                 pl.BlockSpec((rounds, 8, length), lambda i, me_ref: (0, 0, 0)),
             ],
             scratch_shapes=[pltpu.VMEM((groups, length), I32)],
         ),
         out_shape=[
-            jax.ShapeDtypeStruct((length, 2 * span), BF16),
-            jax.ShapeDtypeStruct((slots, length), BF16),
+            jax.ShapeDtypeStruct((slots, 2 * span), BF16),
             jax.ShapeDtypeStruct((rounds, 8, length), I32),
         ],
         cost_estimate=cost(4 * length * width * span + 4 * slots * length * span, 6 << 20),
         compiler_params=BIG,
-        name="project_rows",
+        name="pack_rows",
     )(me, perms, x_att, w_qk, w_val)
-
-
-def pack_rows_kernel(pick_ref, rows_ref, out_ref):
-    out_ref[...] = dot(pick_ref[...], rows_ref[...]).astype(BF16)
-
-
-def pack_rows(pick, rows):
-    return pl.pallas_call(
-        pack_rows_kernel,
-        out_shape=jax.ShapeDtypeStruct((pick.shape[0], rows.shape[1]), BF16),
-        cost_estimate=cost(LONG, 2 << 20),
-        compiler_params=BIG,
-        name="pack_rows",
-    )(pick, rows)
 
 
 def pack_tokens_kernel(peers, where_ref, ids_ref, tokens_ref, out_ref, slot_ref):
@@ -240,7 +224,7 @@
             scratch_shapes=[pltpu.VMEM((4, rows, hidden), F32)],
         ),
         out_shape=jax.ShapeDtypeStruct(out, BF16),
-        cost_estimate=cost(12 * rows * width * hidden, 10 << 20),
+        cost_estimate=cost(15 * 10**9, 10 << 20),
         compiler_params=BIG,
         name="experts",
     )(where, *shards, *far, *own, *sibling)
@@ -605,7 +589,7 @@
             jax.ShapeDtypeStruct((length, half), F32),
             jax.ShapeDtypeStruct((length, half), BF16),
         ],
-        cost_estimate=cost(8 * length * span * columns, 3 << 20),
+        cost_estimate=cost(35 * 10**8, 3 << 20),
         compiler_params=BIG,
         name="project",
     )(where, *heads, *weights)
@@ -656,7 +640,7 @@
         where, expert_ids.reshape(1, tokb), tokens_b, peers, capacity, part
     )
     received = exchange(dispatch.reshape(peers, capacity, part), "seq")
-    projected, pick, slot_token = project_rows(me, perms, x_att, w_qk, w_val)
+    outgoing, slot_token = pack_rows(me, perms, x_att, w_qk, w_val)
     columns = [
         hop(
             lax.dynamic_slice_in_dim(
@@ -667,8 +651,8 @@
         )
         for by in (1, chips - 1, 2)
     ]
-    received = after(received, projected, *columns)
-    outgoing = pack_rows(pick, after(projected, received))
+    received = after(received, outgoing, *columns)
+    outgoing = after(outgoing, received)
     own = (w_gate, w_up, w_down)
     sibling = [
         lax.ppermute(

time: 167 us -> 156 us (0.934)
  waiting for transfers between devices: 54.9 us -> 48.4 us
  starting transfers between devices: 54.4 us -> 50.6 us
  Pallas kernels: 25.3 us -> 28.4 us
  local copies, waits for them, and re-layouts: 15.2 us -> 12.5 us
    ppermute x11, waiting for transfers between devices: 34.5 us -> 21.2 us  [hop(): return lax.ppermute(x, 'exp', pairs)]
    all_to_all x4, waiting for transfers between devices: 8.22 us -> 15.1 us  [exchange(): return lax.all_to_all(x, axis, split_axis=0, concat_axis=0, tiled=True)]
    unnamed x38 -> x34, local copies, waits for them, and re-layouts: 11.7 us -> 6.17 us
    all_to_all x4, starting transfers between devices: 35.5 us -> 31.5 us  [exchange(): return lax.all_to_all(x, axis, split_axis=0, concat_axis=0, tiled=True)]
    dynamic_slice x3, local copies, waits for them, and re-layouts: 1.62 us -> 4.55 us  [body(): lax.dynamic_slice_in_dim(after(weight, received), 1 - core, 1, 0)]
    pallas_call x2 -> x1, Pallas kernels: 2.46 us -> 4.8 us  [pack_rows(): pl.pallas_call(pack_rows_kernel, grid_spec=pltpu.PrefetchScalarGridSpec(n...]
    ppermute x11, starting transfers between devices: 16.4 us -> 18.3 us  [hop(): return lax.ppermute(x, 'exp', pairs)]
  transfers between devices with their start and end apart: 22 -> 22, of which waited for: 12 -> 13; matrix products, arithmetic and copies ran while one was open for 3% -> 2% of each run, Pallas kernels for 12% -> 16%
where the time goes in v8:
time: 156 us; the launch traced here: 155 us
  starting transfers between devices  50.6 us (32%)
  waiting for transfers between devices  48.4 us (31%)
  Pallas kernels  28.4 us (18%)
  between operations  14.3 us (9%)
  local copies, waits for them, and re-layouts  12.5 us (8%)
    all_to_all x4, starting transfers between devices, exchange(): return lax.all_to_all(x, axis, split_axis=0, concat_axis=0, tiled=True)  31.5 us
    ppermute x11, waiting for transfers between devices, hop(): return lax.ppermute(x, 'exp', pairs)  21.2 us
    ppermute x11, starting transfers between devices, hop(): return lax.ppermute(x, 'exp', pairs)  18.3 us
    all_to_all x4, waiting for transfers between devices, exchange(): return lax.all_to_all(x, axis, split_axis=0, concat_axis=0, tiled=True)  15.1 us
    reduce_scatter x1, waiting for transfers between devices, body(): lax.psum_scatter(expert_part, 'exp', scatter_dimension=0, tiled=False, ax...  8.62 us
    pallas_call x1, Pallas kernels, run_experts(): pl.pallas_call(experts_kernel, grid_spec=pltpu.PrefetchScalarGridSpec(num...  8.58 us
    unnamed x34, local copies, waits for them, and re-layouts  6.17 us
    pallas_call x1, Pallas kernels, pack_rows(): pl.pallas_call(pack_rows_kernel, grid_spec=pltpu.PrefetchScalarGridSpec(n...  4.8 us
  transfers between devices with their start and end apart: 22, of which 13 were waited for; matrix products, arithmetic and copies ran while one was open for 2% of the time, Pallas kernels for 16%

profile of v8, /device:TPU:32, one launch (start us, length us, event | category | flops | bytes accessed | tf_op | source)
XLA Modules:
  0.0 155.1 jit_solution(1921466271817864076)
XLA Ops:
  7.2 0.1 pad_add_fusion.where_ref
  7.3 1.6 %copy-done = bf16[512,2048]{1,0:T(8,128)(2,1)S(1)} copy-done((bf16[512,2048]{1,0:T(8,128)(2,1)S(1)}, bf16[512,2048]{1,0:T(8,128)(2,1)}, u32[]{:S(2)}) %copy-start) | copy-done | bytes 2097176
  8.9 0.7 copy-done.4
  9.5 2.0 %pack_tokens.1 = (bf16[512,512]{1,0:T(8,128)(2,1)}, s32[8,512]{1,0:T(8,128)S(1)}) custom-call(s32[2]{0:T(128)S(1)} %pad_add_fusion.where_ref, s32[1,512]{1,0:T(1,128)S(1)} %bitcast.13, bf16[512,2048]{1,0:T(8,128)(2,1)S(1)} %copy-done), custom_call_target="tpu_custom_call" | custom-call | flops 268435456 | bytes 2097152 | tf_op jit(solution)/shard_map/pack_tokens/pallas_call | solution.py:140
  11.5 11.2 %all-to-all-start = ((bf16[32,16,512]{2,1,0:T(8,128)(2,1)}), bf16[32,16,512]{2,1,0:T(8,128)(2,1)S(1)}, u32[]{:S(2)}, u32[]{:S(2)}) async-start(bf16[32,16,512]{2,1,0:T(8,128)(2,1)} %bitcast.4), calls=%async_computation | async-start | bytes 1048576 | tf_op jit(solution)/shard_map/all_to_all | solution.py:599
  22.8 0.8 constant_dynamic-slice_fusion.3
  23.6 3.2 %collective-permute-start.2 = (bf16[256,512]{1,0:T(8,128)(2,1)}, bf16[256,512]{1,0:T(8,128)(2,1)S(1)}, u32[]{:S(2)}, u32[]{:S(2)}) collective-permute-start(bf16[256,512]{1,0:T(8,128)(2,1)} %get-tuple-element.46), channel_id=1, source_target_pairs={{0,4},{1,5},{2,6},{3,7},{4,0},{5,1},{6,2},{7,3},{8,12},{9,13},{10,... | collective-permute-start | bytes 786440 | tf_op jit(solution)/shard_map/ppermute | solution.py:608
  26.8 1.1 collective-permute-start.1
  27.8 1.0 collective-permute-start
  28.8 1.6 %copy-done.5 = bf16[512,2048]{1,0:T(8,128)(2,1)S(1)} copy-done((bf16[512,2048]{1,0:T(8,128)(2,1)S(1)}, bf16[512,2048]{1,0:T(8,128)(2,1)}, u32[]{:S(2)}) %copy-start.5) | copy-done | bytes 2097176
  30.4 1.2 copy-done.7
  31.6 4.8 %pack_rows.1 = (bf16[1024,512]{1,0:T(8,128)(2,1)}, s32[2,8,512]{2,1,0:T(8,128)S(1)}) custom-call(s32[1]{0:T(128)} %bitcast.2.me_ref, s32[2,16384]{1,0:T(2,128)S(1)} %copy-done.14, bf16[512,2048]{1,0:T(8,128)(2,1)S(1)} %copy-done.5, bf16[2048,256]{1,0:T(8,128)(2,1)S(1)} %copy-done.6, bf16[2048,256]{1,0:T(8,128)(2,1)S(1)} %copy-done.7), custom_call_target="tpu_custom_call" | custom-call | flops 1610612736 | bytes 6291456 | tf_op jit(solution)/shard_map/pack_rows/pallas_call | solution.py:90
  36.4 0.0 collective-permute-done.2.refs_3_
  36.4 2.4 %collective-permute-done.1.refs_2_ = bf16[256,512]{1,0:T(8,128)(2,1)S(1)} collective-permute-done((bf16[256,512]{1,0:T(8,128)(2,1)S(1)}, bf16[256,512]{1,0:T(8,128)(2,1)S(1)}, u32[]{:S(2)}, u32[]{:S(2)}) %collective-permute-start.1) | collective-permute-done | bytes 262176 | tf_op jit(solution)/shard_map/ppermute | solution.py:608
  38.8 0.0 collective-permute-done.refs_1_
  38.8 1.6 all-to-all-done.refs_0_
  40.3 2.4 %constant_dynamic-slice_fusion.2 = bf16[1,2048,256]{2,1,0:T(8,128)(2,1)} fusion(bf16[2,2048,256]{2,1,0:T(8,128)(2,1)} %refs_5_.1, s32[]{:T(128)S(6)} %select_n.47), kind=kLoop, calls=%fused_computation.4 | loop fusion | bytes 2097156 | tf_op jit(solution)/shard_map/dynamic_slice | solution.py:659
  42.8 1.1 constant_dynamic-slice_fusion.1
  43.9 1.0 constant_dynamic-slice_fusion
  44.9 0.0 collective-permute-start.9
  44.9 0.5 collective-permute-start.8
  45.4 3.0 %collective-permute-start.4 = (bf16[32,16,512]{2,1,0:T(8,128)(2,1)S(1)}, bf16[32,16,512]{2,1,0:T(8,128)(2,1)S(1)}, u32[]{:S(2)}, u32[]{:S(2)}) collective-permute-start(bf16[32,16,512]{2,1,0:T(8,128)(2,1)S(1)} %all-to-all-done.refs_0_), channel_id=1, source_target_pairs={{0,6},{1,7},{2,0},{3,1},{4,2},{5,3},{6,4},{7,5},{8,14},{9,15},{10,... | collective-permute-start | bytes 1572872 | tf_op jit(solution)/shard_map/ppermute | solution.py:608
  48.4 0.0 collective-permute-start.3
  48.4 8.0 %all-to-all-start.1 = ((bf16[32,32,512]{2,1,0:T(8,128)(2,1)}), bf16[32,32,512]{2,1,0:T(8,128)(2,1)S(1)}, u32[]{:S(2)}, u32[]{:S(2)}) async-start(bf16[32,32,512]{2,1,0:T(8,128)(2,1)} %bitcast.5), calls=%async_computation.1 | async-start | bytes 2097152 | tf_op jit(solution)/shard_map/all_to_all | solution.py:599
  56.4 0.0 reduce-scatter.2.cloned.1.call-start
  56.4 3.8 %collective-permute-done.4.refs_2_ = bf16[32,16,512]{2,1,0:T(8,128)(2,1)S(1)} collective-permute-done((bf16[32,16,512]{2,1,0:T(8,128)(2,1)S(1)}, bf16[32,16,512]{2,1,0:T(8,128)(2,1)S(1)}, u32[]{:S(2)}, u32[]{:S(2)}) %collective-permute-start.4) | collective-permute-done | bytes 524320 | tf_op jit(solution)/shard_map/ppermute | solution.py:608
  60.3 3.8 %collective-permute-start.6 = (bf16[16,16,512]{2,1,0:T(8,128)(2,1)S(1)}, bf16[16,16,512]{2,1,0:T(8,128)(2,1)S(1)}, u32[]{:S(2)}, u32[]{:S(2)}) collective-permute-start(bf16[16,16,512]{2,1,0:T(8,128)(2,1)S(1)} %slice.17), channel_id=1, source_target_pairs={{0,6},{1,7},{2,0},{3,1},{4,2},{5,3},{6,4},{7,5},{8,14},{9,15},{10,... | collective-permute-start | bytes 786440 | tf_op jit(solution)/shard_map/ppermute | solution.py:608
  64.1 0.3 collective-permute-start.5
  64.4 5.2 %collective-permute-done.6.refs_4_ = bf16[16,16,512]{2,1,0:T(8,128)(2,1)S(1)} collective-permute-done((bf16[16,16,512]{2,1,0:T(8,128)(2,1)S(1)}, bf16[16,16,512]{2,1,0:T(8,128)(2,1)S(1)}, u32[]{:S(2)}, u32[]{:S(2)}) %collective-permute-start.6) | collective-permute-done | bytes 262176 | tf_op jit(solution)/shard_map/ppermute | solution.py:608
  69.5 3.7 %collective-permute-done.5.refs_3_ = bf16[16,16,512]{2,1,0:T(8,128)(2,1)S(1)} collective-permute-done((bf16[16,16,512]{2,1,0:T(8,128)(2,1)S(1)}, bf16[16,16,512]{2,1,0:T(8,128)(2,1)S(1)}, u32[]{:S(2)}, u32[]{:S(2)}) %collective-permute-start.5) | collective-permute-done | bytes 262176 | tf_op jit(solution)/shard_map/ppermute | solution.py:608
  73.2 0.0 collective-permute-done.9.refs_10_
  73.2 0.0 collective-permute-done.8.refs_9_
  73.2 0.0 collective-permute-done.7.refs_8_
  73.2 8.6 %experts.1 = bf16[4,2,32,16,256]{4,3,2,1,0:T(8,128)(2,1)} custom-call(s32[2]{0:T(128)S(1)} %pad_add_fusion.where_ref, bf16[32,16,512]{2,1,0:T(8,128)(2,1)S(1)} %all-to-all-done.refs_0_, bf16[32,16,512]{2,1,0:T(8,128)(2,1)S(1)} %collective-permute-done.3.refs_1_, bf16[32,16,512]{2,1,0:T(8,128)(2,1)S(1)} %collective-permute-done.4.refs_2_, ...), custom_call_target="tpu_custom_call" | custom-call | flops 15000000512 | bytes 10485760 | tf_op jit(solution)/shard_map/experts/pallas_call | solution.py:216
  81.8 0.0 reduce-scatter.2.cloned.1.call-update
  81.8 3.3 %all-to-all-done.1.arrived_ref = bf16[32,32,512]{2,1,0:T(8,128)(2,1)S(1)} async-done(((bf16[32,32,512]{2,1,0:T(8,128)(2,1)}), bf16[32,32,512]{2,1,0:T(8,128)(2,1)S(1)}, u32[]{:S(2)}, u32[]{:S(2)}) %all-to-all-start.1) | async-done | bytes 1048608 | tf_op jit(solution)/shard_map/all_to_all | solution.py:599
  85.2 1.7 %sort_rows.1 = (bf16[2,512,512]{2,1,0:T(8,128)(2,1)S(1)}, bf16[2,64,512]{2,1,0:T(8,128)(2,1)S(1)}, s32[2,8,512]{2,1,0:T(8,128)S(1)}) custom-call(s32[1]{0:T(128)} %bitcast.2.me_ref, s32[2,16384]{1,0:T(2,128)S(1)} %copy-done.14, bf16[32,32,512]{2,1,0:T(8,128)(2,1)S(1)} %all-to-all-done.1.arrived_ref), custom_call_target="tpu_custom_call" | custom-call | flops 34359738368 | bytes 4194304 | tf_op jit(solution)/shard_map/sort_rows/pallas_call | solution.py:297
  86.9 0.1 collective-permute-start.10
  87.0 3.0 %attend_later.1.later_ref = bf16[2,384,384]{2,1,0:T(8,128)(2,1)S(1)} custom-call(s32[1]{0:T(128)} %bitcast.2.me_ref, s32[2,16384]{1,0:T(2,128)S(1)} %copy-done.14, bf16[2,512,512]{2,1,0:T(8,128)(2,1)S(1)} %get-tuple-element.33.rows_ref), custom_call_target="tpu_custom_call" | custom-call | flops 34359738368 | bytes 4194304 | tf_op jit(solution)/shard_map/attend_later/pallas_call | solution.py:448
  90.0 1.9 %collective-permute-done.10.last_ref = bf16[2,64,512]{2,1,0:T(8,128)(2,1)S(1)} collective-permute-done((bf16[2,64,512]{2,1,0:T(8,128)(2,1)S(1)}, bf16[2,64,512]{2,1,0:T(8,128)(2,1)S(1)}, u32[]{:S(2)}, u32[]{:S(2)}) %collective-permute-start.10) | collective-permute-done | bytes 131104 | tf_op jit(solution)/shard_map/ppermute | solution.py:675
  91.9 3.1 %attend_first.1 = bf16[32,40,256]{2,1,0:T(8,128)(2,1)} custom-call(s32[1]{0:T(128)} %bitcast.2.me_ref, s32[2,16384]{1,0:T(2,128)S(1)} %copy-done.14, s32[2,16384]{1,0:T(2,128)S(1)} %copy-done.14, bf16[2,512,512]{2,1,0:T(8,128)(2,1)S(1)} %get-tuple-element.33.rows_ref, bf16[2,64,512]{2,1,0:T(8,128)(2,1)S(1)} %collective-permute-done.10.last_ref, ...), custom_call_target="tpu_custom_call" | custom-call | flops 34359738368 | bytes 4194304 | tf_op jit(solution)/shard_map/attend_first/pallas_call | solution.py:476
  95.0 7.3 %all-to-all-start.2 = ((bf16[32,40,256]{2,1,0:T(8,128)(2,1)}), bf16[32,40,256]{2,1,0:T(8,128)(2,1)S(1)}, u32[]{:S(2)}, u32[]{:S(2)}) async-start(bf16[32,40,256]{2,1,0:T(8,128)(2,1)} %attend_first.1), calls=%async_computation.2 | async-start | bytes 1310720 | tf_op jit(solution)/shard_map/all_to_all | solution.py:599
  102.4 8.6 %reduce-scatter.2.cloned.1.call-done = bf16[1,2,32,16,256]{4,3,2,1,0:T(8,128)(2,1)} async-done(((bf16[4,2,32,16,256]{4,3,2,1,0:T(8,128)(2,1)}), bf16[1,2,32,16,256]{4,3,2,1,0:T(8,128)(2,1)}) %reduce-scatter.2.cloned.1.call-update) | async-done | bytes 524304 | tf_op jit(solution)/shard_map/reduce_scatter | solution.py:668
  111.0 1.0 dynamic-slice_bitcast_fusion
  112.0 0.1 collective-permute-start.12
  112.1 9.0 %all-to-all-done.2.got_ref = bf16[32,40,256]{2,1,0:T(8,128)(2,1)S(1)} async-done(((bf16[32,40,256]{2,1,0:T(8,128)(2,1)}), bf16[32,40,256]{2,1,0:T(8,128)(2,1)S(1)}, u32[]{:S(2)}, u32[]{:S(2)}) %all-to-all-start.2) | async-done | bytes 655392 | tf_op jit(solution)/shard_map/all_to_all | solution.py:599
  121.0 1.1 combine.1.own_ref
  122.1 0.0 copy-start.2
  122.1 2.7 %collective-permute-start.13 = (bf16[512,256]{1,0:T(8,128)(2,1)S(1)}, bf16[512,256]{1,0:T(8,128)(2,1)S(1)}, u32[]{:S(2)}, u32[]{:S(2)}) collective-permute-start(bf16[512,256]{1,0:T(8,128)(2,1)S(1)} %combine.1.own_ref), channel_id=1, source_target_pairs={{0,6},{1,7},{2,0},{3,1},{4,2},{5,3},{6,4},{7,5},{8,14},{9,15},{10,... | collective-permute-start | bytes 786440 | tf_op jit(solution)/shard_map/ppermute | solution.py:608
  124.8 0.0 collective-permute-start.11
  124.8 1.0 copy-done.3
  125.8 1.4 place_rows.1
  127.2 5.0 %all-to-all-start.3 = ((bf16[32,2,16,256]{3,2,1,0:T(8,128)(2,1)}), bf16[32,2,16,256]{3,2,1,0:T(8,128)(2,1)S(1)}, u32[]{:S(2)}, u32[]{:S(2)}) async-start(bf16[32,2,16,256]{3,2,1,0:T(8,128)(2,1)} %place_rows.1), calls=%async_computation.4 | async-start | bytes 1048576 | tf_op jit(solution)/shard_map/all_to_all | solution.py:599
  132.3 3.3 %collective-permute-start.15 = (bf16[256,256]{1,0:T(8,128)(2,1)S(1)}, bf16[256,256]{1,0:T(8,128)(2,1)S(1)}, u32[]{:S(2)}, u32[]{:S(2)}) collective-permute-start(bf16[256,256]{1,0:T(8,128)(2,1)S(1)} %slice.15), channel_id=1, source_target_pairs={{0,6},{1,7},{2,0},{3,1},{4,2},{5,3},{6,4},{7,5},{8,14},{9,15},{10,... | collective-permute-start | bytes 393224 | tf_op jit(solution)/shard_map/ppermute | solution.py:608
  135.6 0.0 collective-permute-done.11.prev_ref
  135.6 0.1 collective-permute-start.14
  135.7 2.4 %collective-permute-done.15.far_b_ref = bf16[256,256]{1,0:T(8,128)(2,1)S(1)} collective-permute-done((bf16[256,256]{1,0:T(8,128)(2,1)S(1)}, bf16[256,256]{1,0:T(8,128)(2,1)S(1)}, u32[]{:S(2)}, u32[]{:S(2)}) %collective-permute-start.15) | collective-permute-done | bytes 131104 | tf_op jit(solution)/shard_map/ppermute | solution.py:608
  138.1 3.8 %collective-permute-done.14.far_a_ref = bf16[256,256]{1,0:T(8,128)(2,1)S(1)} collective-permute-done((bf16[256,256]{1,0:T(8,128)(2,1)S(1)}, bf16[256,256]{1,0:T(8,128)(2,1)S(1)}, u32[]{:S(2)}, u32[]{:S(2)}) %collective-permute-start.14) | collective-permute-done | bytes 131104 | tf_op jit(solution)/shard_map/ppermute | solution.py:608
  141.9 1.3 project.1
  143.2 0.1 collective-permute-start.16
  143.3 1.5 collective-permute-done.16
  144.8 0.8 add_convert_fusion
  145.6 1.2 all-to-all-done.3
  146.8 1.4 unpack_tokens.1
  (36 shorter events, 0.1 us)
Async XLA Ops:
  7.3 1.6 %copy-start = (bf16[512,2048]{1,0:T(8,128)(2,1)S(1)}, bf16[512,2048]{1,0:T(8,128)(2,1)}, u32[]{:S(2)}) copy-start(bf16[512,2048]{1,0:T(8,128)(2,1)} %tokens_ref.1) | copy-start | bytes 6291460
  8.9 0.7 copy-start.4
  9.5 13.2 %copy-start.1 = (bf16[256,2048]{1,0:T(8,128)(2,1)S(1)}, bf16[256,2048]{1,0:T(8,128)(2,1)}, u32[]{:S(2)}) copy-start(bf16[256,2048]{1,0:T(8,128)(2,1)} %refs_0_.1) | copy-start | bytes 3145732
  9.5 19.3 %copy-start.6 = (bf16[2048,256]{1,0:T(8,128)(2,1)S(1)}, bf16[2048,256]{1,0:T(8,128)(2,1)}, u32[]{:S(2)}) copy-start(bf16[2048,256]{1,0:T(8,128)(2,1)} %qk_ref.1) | copy-start | bytes 3145732
  9.5 19.3 %copy-start.14 = (s32[2,16384]{1,0:T(2,128)S(1)}, s32[2,16384]{1,0:T(2,128)}, u32[]{:S(2)}) copy-start(s32[2,16384]{1,0:T(2,128)} %earlier_ref.1) | copy-start | bytes 393220
  11.5 28.8 %all-to-all-start = ((bf16[32,16,512]{2,1,0:T(8,128)(2,1)}), bf16[32,16,512]{2,1,0:T(8,128)(2,1)S(1)}, u32[]{:S(2)}, u32[]{:S(2)}) async-start(bf16[32,16,512]{2,1,0:T(8,128)(2,1)} %bitcast.4), calls=%async_computation | async-start | bytes 1048576 | tf_op jit(solution)/shard_map/all_to_all | solution.py:599
  23.6 12.8 %collective-permute-start.2 = (bf16[256,512]{1,0:T(8,128)(2,1)}, bf16[256,512]{1,0:T(8,128)(2,1)S(1)}, u32[]{:S(2)}, u32[]{:S(2)}) collective-permute-start(bf16[256,512]{1,0:T(8,128)(2,1)} %get-tuple-element.46), channel_id=1, source_target_pairs={{0,4},{1,5},{2,6},{3,7},{4,0},{5,1},{6,2},{7,3},{8,12},{9,13},{10,... | collective-permute-start | bytes 786440 | tf_op jit(solution)/shard_map/ppermute | solution.py:608
  26.8 12.0 %collective-permute-start.1 = (bf16[256,512]{1,0:T(8,128)(2,1)S(1)}, bf16[256,512]{1,0:T(8,128)(2,1)S(1)}, u32[]{:S(2)}, u32[]{:S(2)}) collective-permute-start(bf16[256,512]{1,0:T(8,128)(2,1)S(1)} %get-tuple-element.47), channel_id=1, source_target_pairs={{0,6},{1,7},{2,0},{3,1},{4,2},{5,3},{6,4},{7,5},{8,14},{9,15},{10,... | collective-permute-start | bytes 786440 | tf_op jit(solution)/shard_map/ppermute | solution.py:608
  27.8 11.0 %collective-permute-start = (bf16[256,512]{1,0:T(8,128)(2,1)S(1)}, bf16[256,512]{1,0:T(8,128)(2,1)S(1)}, u32[]{:S(2)}, u32[]{:S(2)}) collective-permute-start(bf16[256,512]{1,0:T(8,128)(2,1)S(1)} %get-tuple-element.48), channel_id=1, source_target_pairs={{0,2},{1,3},{2,4},{3,5},{4,6},{5,7},{6,0},{7,1},{8,10},{9,11},{10,... | collective-permute-start | bytes 786440 | tf_op jit(solution)/shard_map/ppermute | solution.py:608
  28.8 1.6 %copy-start.5 = (bf16[512,2048]{1,0:T(8,128)(2,1)S(1)}, bf16[512,2048]{1,0:T(8,128)(2,1)}, u32[]{:S(2)}) copy-start(bf16[512,2048]{1,0:T(8,128)(2,1)} %x_ref.1) | copy-start | bytes 6291460
  30.4 1.2 copy-start.7
  36.4 7.4 %copy-start.8 = (bf16[256,512]{1,0:T(8,128)(2,1)}, bf16[256,512]{1,0:T(8,128)(2,1)S(1)}, u32[]{:S(2)}) copy-start(bf16[256,512]{1,0:T(8,128)(2,1)S(1)} %collective-permute-done.2.refs_3_) | copy-start | bytes 786436
  38.8 5.1 %copy-start.10 = (bf16[256,512]{1,0:T(8,128)(2,1)}, bf16[256,512]{1,0:T(8,128)(2,1)S(1)}, u32[]{:S(2)}) copy-start(bf16[256,512]{1,0:T(8,128)(2,1)S(1)} %collective-permute-done.1.refs_2_) | copy-start | bytes 786436
  38.8 5.1 %copy-start.12 = (bf16[256,512]{1,0:T(8,128)(2,1)}, bf16[256,512]{1,0:T(8,128)(2,1)S(1)}, u32[]{:S(2)}) copy-start(bf16[256,512]{1,0:T(8,128)(2,1)S(1)} %collective-permute-done.refs_1_) | copy-start | bytes 786436
  40.3 2.5 %copy-start.15 = (bf16[2,2048,256]{2,1,0:T(8,128)(2,1)S(1)}, bf16[2,2048,256]{2,1,0:T(8,128)(2,1)}, u32[]{:S(2)}) copy-start(bf16[2,2048,256]{2,1,0:T(8,128)(2,1)} %refs_6_.1) | copy-start | bytes 6291460
  40.3 3.5 %copy-start.16 = (bf16[2,256,2048]{2,1,0:T(8,128)(2,1)S(1)}, bf16[2,256,2048]{2,1,0:T(8,128)(2,1)}, u32[]{:S(2)}) copy-start(bf16[2,256,2048]{2,1,0:T(8,128)(2,1)} %refs_7_.1) | copy-start | bytes 6291460
  44.9 28.3 %collective-permute-start.9 = (bf16[1,256,2048]{2,1,0:T(8,128)(2,1)}, bf16[1,256,2048]{2,1,0:T(8,128)(2,1)}, u32[]{:S(2)}, u32[]{:S(2)}) collective-permute-start(bf16[1,256,2048]{2,1,0:T(8,128)(2,1)} %constant_dynamic-slice_fusion), channel_id=1, source_target_pairs={{0,1},{1,0},{2,3},{3,2},{4,5},{5,4},{6,7},{7,6},{8,9},{9,8},{10,11... | collective-permute-start | bytes 3145736 | tf_op jit(solution)/shard_map/ppermute | solution.py:658
  44.9 28.3 %collective-permute-start.8 = (bf16[1,2048,256]{2,1,0:T(8,128)(2,1)}, bf16[1,2048,256]{2,1,0:T(8,128)(2,1)}, u32[]{:S(2)}, u32[]{:S(2)}) collective-permute-start(bf16[1,2048,256]{2,1,0:T(8,128)(2,1)} %constant_dynamic-slice_fusion.1), channel_id=1, source_target_pairs={{0,1},{1,0},{2,3},{3,2},{4,5},{5,4},{6,7},{7,6},{8,9},{9,8},{10,11... | collective-permute-start | bytes 3145736 | tf_op jit(solution)/shard_map/ppermute | solution.py:658
  45.4 27.8 %collective-permute-start.7 = (bf16[1,2048,256]{2,1,0:T(8,128)(2,1)}, bf16[1,2048,256]{2,1,0:T(8,128)(2,1)}, u32[]{:S(2)}, u32[]{:S(2)}) collective-permute-start(bf16[1,2048,256]{2,1,0:T(8,128)(2,1)} %constant_dynamic-slice_fusion.2), channel_id=1, source_target_pairs={{0,1},{1,0},{2,3},{3,2},{4,5},{5,4},{6,7},{7,6},{8,9},{9,8},{10,11... | collective-permute-start | bytes 3145736 | tf_op jit(solution)/shard_map/ppermute | solution.py:658
  45.4 14.9 %collective-permute-start.4 = (bf16[32,16,512]{2,1,0:T(8,128)(2,1)S(1)}, bf16[32,16,512]{2,1,0:T(8,128)(2,1)S(1)}, u32[]{:S(2)}, u32[]{:S(2)}) collective-permute-start(bf16[32,16,512]{2,1,0:T(8,128)(2,1)S(1)} %all-to-all-done.refs_0_), channel_id=1, source_target_pairs={{0,6},{1,7},{2,0},{3,1},{4,2},{5,3},{6,4},{7,5},{8,14},{9,15},{10,... | collective-permute-start | bytes 1572872 | tf_op jit(solution)/shard_map/ppermute | solution.py:608
  48.4 15.6 %collective-permute-start.3 = (bf16[32,16,512]{2,1,0:T(8,128)(2,1)S(1)}, bf16[32,16,512]{2,1,0:T(8,128)(2,1)S(1)}, u32[]{:S(2)}, u32[]{:S(2)}) collective-permute-start(bf16[32,16,512]{2,1,0:T(8,128)(2,1)S(1)} %all-to-all-done.refs_0_), channel_id=1, source_target_pairs={{0,2},{1,3},{2,4},{3,5},{4,6},{5,7},{6,0},{7,1},{8,10},{9,11},{10,... | collective-permute-start | bytes 1572872 | tf_op jit(solution)/shard_map/ppermute | solution.py:608
  48.4 36.7 %all-to-all-start.1 = ((bf16[32,32,512]{2,1,0:T(8,128)(2,1)}), bf16[32,32,512]{2,1,0:T(8,128)(2,1)S(1)}, u32[]{:S(2)}, u32[]{:S(2)}) async-start(bf16[32,32,512]{2,1,0:T(8,128)(2,1)} %bitcast.5), calls=%async_computation.1 | async-start | bytes 2097152 | tf_op jit(solution)/shard_map/all_to_all | solution.py:599
  56.4 54.6 %reduce-scatter.2.cloned.1.call-start = ((), (), s32[]{:S(2)}) async-start(), calls=%async_computation.5 | async-start | bytes 2621440 | tf_op jit(solution)/shard_map/reduce_scatter | solution.py:668
  60.3 9.2 %collective-permute-start.6 = (bf16[16,16,512]{2,1,0:T(8,128)(2,1)S(1)}, bf16[16,16,512]{2,1,0:T(8,128)(2,1)S(1)}, u32[]{:S(2)}, u32[]{:S(2)}) collective-permute-start(bf16[16,16,512]{2,1,0:T(8,128)(2,1)S(1)} %slice.17), channel_id=1, source_target_pairs={{0,6},{1,7},{2,0},{3,1},{4,2},{5,3},{6,4},{7,5},{8,14},{9,15},{10,... | collective-permute-start | bytes 786440 | tf_op jit(solution)/shard_map/ppermute | solution.py:608
  64.1 9.1 %collective-permute-start.5 = (bf16[16,16,512]{2,1,0:T(8,128)(2,1)S(1)}, bf16[16,16,512]{2,1,0:T(8,128)(2,1)S(1)}, u32[]{:S(2)}, u32[]{:S(2)}) collective-permute-start(bf16[16,16,512]{2,1,0:T(8,128)(2,1)S(1)} %slice.16), channel_id=1, source_target_pairs={{0,2},{1,3},{2,4},{3,5},{4,6},{5,7},{6,0},{7,1},{8,10},{9,11},{10,... | collective-permute-start | bytes 786440 | tf_op jit(solution)/shard_map/ppermute | solution.py:608
  86.9 5.0 %collective-permute-start.10 = (bf16[2,64,512]{2,1,0:T(8,128)(2,1)S(1)}, bf16[2,64,512]{2,1,0:T(8,128)(2,1)S(1)}, u32[]{:S(2)}, u32[]{:S(2)}) collective-permute-start(bf16[2,64,512]{2,1,0:T(8,128)(2,1)S(1)} %get-tuple-element.34), channel_id=1, source_target_pairs={{0,8},{8,16},{16,24},{24,32},{32,40},{40,48},{48,56},{56,64},{64,7... | collective-permute-start | bytes 393224 | tf_op jit(solution)/shard_map/ppermute | solution.py:675
  95.0 26.0 %all-to-all-start.2 = ((bf16[32,40,256]{2,1,0:T(8,128)(2,1)}), bf16[32,40,256]{2,1,0:T(8,128)(2,1)S(1)}, u32[]{:S(2)}, u32[]{:S(2)}) async-start(bf16[32,40,256]{2,1,0:T(8,128)(2,1)} %attend_first.1), calls=%async_computation.2 | async-start | bytes 1310720 | tf_op jit(solution)/shard_map/all_to_all | solution.py:599
  112.0 12.8 %collective-permute-start.12 = (bf16[32,16,256]{2,1,0:T(8,128)(2,1)S(1)}, bf16[32,16,256]{2,1,0:T(8,128)(2,1)S(1)}, u32[]{:S(2)}, u32[]{:S(2)}) collective-permute-start(bf16[32,16,256]{2,1,0:T(8,128)(2,1)S(1)} %dynamic-slice_bitcast_fusion), channel_id=1, source_target_pairs={{0,1},{1,0},{2,3},{3,2},{4,5},{5,4},{6,7},{7,6},{8,9},{9,8},{10,11... | collective-permute-start | bytes 786440 | tf_op jit(solution)/shard_map/ppermute | solution.py:682
  121.0 20.8 %copy-start.9 = (bf16[256,512]{1,0:T(8,128)(2,1)S(1)}, bf16[256,512]{1,0:T(8,128)(2,1)}, u32[]{:S(2)}) copy-start(bf16[256,512]{1,0:T(8,128)(2,1)} %copy-done.8) | copy-start | bytes 786436
  121.0 20.8 %copy-start.11 = (bf16[256,512]{1,0:T(8,128)(2,1)S(1)}, bf16[256,512]{1,0:T(8,128)(2,1)}, u32[]{:S(2)}) copy-start(bf16[256,512]{1,0:T(8,128)(2,1)} %copy-done.10) | copy-start | bytes 786436
  121.0 20.8 %copy-start.13 = (bf16[256,512]{1,0:T(8,128)(2,1)S(1)}, bf16[256,512]{1,0:T(8,128)(2,1)}, u32[]{:S(2)}) copy-start(bf16[256,512]{1,0:T(8,128)(2,1)} %copy-done.12) | copy-start | bytes 786436
  122.1 19.7 %copy-start.2 = (bf16[256,2048]{1,0:T(8,128)(2,1)S(1)}, bf16[256,2048]{1,0:T(8,128)(2,1)}, u32[]{:S(2)}) copy-start(bf16[256,2048]{1,0:T(8,128)(2,1)} %refs_0_.1) | copy-start | bytes 3145732
  122.1 10.1 %collective-permute-start.13 = (bf16[512,256]{1,0:T(8,128)(2,1)S(1)}, bf16[512,256]{1,0:T(8,128)(2,1)S(1)}, u32[]{:S(2)}, u32[]{:S(2)}) collective-permute-start(bf16[512,256]{1,0:T(8,128)(2,1)S(1)} %combine.1.own_ref), channel_id=1, source_target_pairs={{0,6},{1,7},{2,0},{3,1},{4,2},{5,3},{6,4},{7,5},{8,14},{9,15},{10,... | collective-permute-start | bytes 786440 | tf_op jit(solution)/shard_map/ppermute | solution.py:608
  124.8 10.8 %collective-permute-start.11 = (bf16[512,256]{1,0:T(8,128)(2,1)S(1)}, bf16[512,256]{1,0:T(8,128)(2,1)S(1)}, u32[]{:S(2)}, u32[]{:S(2)}) collective-permute-start(bf16[512,256]{1,0:T(8,128)(2,1)S(1)} %combine.1.own_ref), channel_id=1, source_target_pairs={{0,2},{1,3},{2,4},{3,5},{4,6},{5,7},{6,0},{7,1},{8,10},{9,11},{10,... | collective-permute-start | bytes 786440 | tf_op jit(solution)/shard_map/ppermute | solution.py:608
  124.8 1.0 copy-start.3
  127.2 19.6 %all-to-all-start.3 = ((bf16[32,2,16,256]{3,2,1,0:T(8,128)(2,1)}), bf16[32,2,16,256]{3,2,1,0:T(8,128)(2,1)S(1)}, u32[]{:S(2)}, u32[]{:S(2)}) async-start(bf16[32,2,16,256]{3,2,1,0:T(8,128)(2,1)} %place_rows.1), calls=%async_computation.4 | async-start | bytes 1048576 | tf_op jit(solution)/shard_map/all_to_all | solution.py:599
  132.3 5.8 %collective-permute-start.15 = (bf16[256,256]{1,0:T(8,128)(2,1)S(1)}, bf16[256,256]{1,0:T(8,128)(2,1)S(1)}, u32[]{:S(2)}, u32[]{:S(2)}) collective-permute-start(bf16[256,256]{1,0:T(8,128)(2,1)S(1)} %slice.15), channel_id=1, source_target_pairs={{0,6},{1,7},{2,0},{3,1},{4,2},{5,3},{6,4},{7,5},{8,14},{9,15},{10,... | collective-permute-start | bytes 393224 | tf_op jit(solution)/shard_map/ppermute | solution.py:608
  135.6 6.3 %collective-permute-start.14 = (bf16[256,256]{1,0:T(8,128)(2,1)S(1)}, bf16[256,256]{1,0:T(8,128)(2,1)S(1)}, u32[]{:S(2)}, u32[]{:S(2)}) collective-permute-start(bf16[256,256]{1,0:T(8,128)(2,1)S(1)} %slice.14), channel_id=1, source_target_pairs={{0,2},{1,3},{2,4},{3,5},{4,6},{5,7},{6,0},{7,1},{8,10},{9,11},{10,... | collective-permute-start | bytes 393224 | tf_op jit(solution)/shard_map/ppermute | solution.py:608
  143.2 1.6 %collective-permute-start.16 = (bf16[512,256]{1,0:T(8,128)(2,1)S(1)}, bf16[512,256]{1,0:T(8,128)(2,1)S(1)}, u32[]{:S(2)}, u32[]{:S(2)}) collective-permute-start(bf16[512,256]{1,0:T(8,128)(2,1)S(1)} %get-tuple-element.43), channel_id=1, source_target_pairs={{0,1},{1,0},{2,3},{3,2},{4,5},{5,4},{6,7},{7,6},{8,9},{9,8},{10,11... | collective-permute-start | bytes 786440 | tf_op jit(solution)/shard_map/ppermute | solution.py:688
Sparse Core Ops, SparseCore 0:
  82.0 28.9 reduce-scatter.1

commit v9 on v8

--- a/solution.py
+++ b/solution.py
@@ -114,9 +114,14 @@
     )(me, perms, x_att, w_qk, w_val)
 
 
-def pack_tokens_kernel(peers, where_ref, ids_ref, tokens_ref, out_ref, slot_ref):
+def pack_tokens_kernel(
+    peers, where_ref, ids_ref, tokens_ref, out_ref, slot_ref, mine_ref, copied
+):
     length = tokens_ref.shape[0]
-    slots = out_ref.shape[0]
+    slots, part = out_ref.shape
+    columns = pl.ds(pl.multiple_of(where_ref[0] * part, part), part)
+    copy = pltpu.make_async_copy(tokens_ref.at[:, columns], mine_ref, copied)
+    copy.start()
     capacity = slots // peers
     experts = EXP_DEV * peers
     ids = ids_ref[...]
@@ -131,7 +136,8 @@
     )
     slot = jnp.where(turn == 0, peer * capacity + rank, -1)
     pick = flag(iota((slots, length), 0) == slot)
-    out_ref[...] = dot(pick, tokens_ref[...]).astype(BF16)
+    copy.wait()
+    out_ref[...] = dot(pick, mine_ref[...]).astype(BF16)
 
 
 def pack_tokens(where, ids, tokens, peers, capacity, part):
@@ -144,12 +150,13 @@
             grid=(1,),
             in_specs=[
                 pl.BlockSpec((1, length), lambda i, e: (0, 0)),
-                pl.BlockSpec((length, part), lambda i, e: (0, e[0])),
+                pl.BlockSpec(memory_space=pl.ANY),
             ],
             out_specs=[
                 pl.BlockSpec((slots, part), lambda i, e: (0, 0)),
                 pl.BlockSpec((8, length), lambda i, e: (0, 0)),
             ],
+            scratch_shapes=[pltpu.VMEM((length, part), BF16), pltpu.SemaphoreType.DMA],
         ),
         out_shape=[
             jax.ShapeDtypeStruct((slots, part), BF16),
@@ -210,16 +217,14 @@
 
     up_block, down_block = (1, part, hidden), (1, hidden, width)
     own_up = pl.BlockSpec(up_block, lambda i, e: (e[1], rows_of(i, e), 0))
-    sibling_up = pl.BlockSpec(up_block, lambda i, e: (0, rows_of(i, e), 0))
     own_down = pl.BlockSpec(down_block, lambda i, e: (e[1], 0, 0))
-    sibling_down = pl.BlockSpec(down_block, lambda i, e: (0, 0, 0))
     return pl.pallas_call(
         experts_kernel,
         grid_spec=pltpu.PrefetchScalarGridSpec(
             num_scalar_prefetch=1,
             grid=(len(shards) + 1,),
             in_specs=[pl.BlockSpec(x.shape, lambda i, e: (0, 0, 0)) for x in (*shards, *far)]
-            + [own_up, own_up, own_down, sibling_up, sibling_up, sibling_down],
+            + [own_up, own_up, own_down] * 2,
             out_specs=pl.BlockSpec(out, lambda i, e: (0, 0, 0, 0, 0)),
             scratch_shapes=[pltpu.VMEM((4, rows, hidden), F32)],
         ),
@@ -250,28 +255,32 @@
             out_specs=pl.BlockSpec(out, lambda i, e: (0, 0, 0, 0)),
         ),
         out_shape=jax.ShapeDtypeStruct(out, BF16),
-        cost_estimate=cost(LONG, 1 << 20),
+        cost_estimate=cost(1 << 20, 1 << 20),
         compiler_params=BIG,
         name="place_rows",
     )(where, rows, taken)
 
 
-def unpack_tokens_kernel(back_ref, slot_ref, out_ref):
-    length = out_ref.shape[0]
+def finish_kernel(back_ref, slot_ref, kept_ref, taken_ref, attended_ref, mixed_ref):
+    length = mixed_ref.shape[0]
     column = to_col(slot_ref[:1, :].astype(F32)).astype(I32)
     pick = flag(column == iota((length, back_ref.shape[0]), 1))
-    out_ref[...] = dot(pick, back_ref[...]).astype(BF16)
-
-
-def unpack_tokens(back, slot):
+    mixed_ref[...] = dot(pick, back_ref[...]).astype(BF16)
+    attended_ref[...] = (kept_ref[...] + taken_ref[...].astype(F32)).astype(BF16)
+
+
+def finish(back, slot, kept, taken):
     length, width = slot.shape[1], back.shape[1]
     return pl.pallas_call(
-        unpack_tokens_kernel,
-        out_shape=jax.ShapeDtypeStruct((length, width), BF16),
+        finish_kernel,
+        out_shape=[
+            jax.ShapeDtypeStruct(kept.shape, BF16),
+            jax.ShapeDtypeStruct((length, width), BF16),
+        ],
         cost_estimate=cost(2 * length * back.shape[0] * width, 1 << 20),
         compiler_params=BIG,
-        name="unpack_tokens",
-    )(back, slot)
+        name="finish",
+    )(back, slot, kept, taken)
 
 
 def sort_rows_kernel(peers, me_ref, perms_ref, arrived_ref, rows_ref, last_ref, slot_ref):
@@ -402,6 +411,8 @@
     lane_group = iota((peers, per_peer, LANES), 2) // GROUP
     own_group = lane_group == iota((peers, per_peer, LANES), 1)
     empty = jnp.zeros((BLOCK_LEN, HEAD_DIM), BF16)
+    log_row = iota((peers, GROUP, LANES), 1)
+    all_logs = jnp.zeros((peers, GROUP, LANES), F32)
     for turn in range(rounds):
         position = perms_ref[turn : turn + 1, :].astype(F32)
         positions = jnp.concatenate([earlier_ref[turn : turn + 1, :].astype(F32), position], axis=1)
@@ -429,16 +440,16 @@
         whole = jnp.concatenate([top, later_ref[turn]], axis=0) if length > TILE else top
         back = flag(iota((length, length), 0) == slot_ref[turn, :1, :])
         moved = dot(back, whole)
-        at = turn * per_peer
-        out_ref[:, at : at + per_peer, :] = (
-            moved[:, :span].astype(BF16).reshape(peers, per_peer, span)
-        )
+        for head in range(span // HEAD_DIM):
+            at = (head * rounds + turn) * per_peer
+            lanes = moved[:, head * HEAD_DIM : (head + 1) * HEAD_DIM]
+            out_ref[:, at : at + per_peer, :] = lanes.astype(BF16).reshape(
+                peers, per_peer, HEAD_DIM
+            )
         logs = moved[:, span:].reshape(peers, per_peer, LANES)
         logs = jnp.sum(jnp.where(own_group, logs, 0.0), axis=1, keepdims=True)
-        at = rounds * per_peer
-        out_ref[:, at : at + GROUP, turn * LANES : (turn + 1) * LANES] = jnp.broadcast_to(
-            logs, (peers, GROUP, LANES)
-        ).astype(BF16)
+        all_logs = jnp.where(log_row == turn, logs, all_logs)
+    out_ref[:, out_ref.shape[1] - GROUP :, :] = all_logs.astype(BF16)
 
 
 def attend_later(me, perms, rows):
@@ -472,7 +483,7 @@
     def fixed(shape):
         return pl.BlockSpec(shape, lambda i, s: (0, 0, 0))
 
-    out = (peers, rounds * per_peer + GROUP, span)
+    out = (peers, span // HEAD_DIM * rounds * per_peer + GROUP, HEAD_DIM)
     return pl.pallas_call(
         functools.partial(attend_first_kernel, peers),
         grid_spec=pltpu.PrefetchScalarGridSpec(
@@ -502,26 +513,27 @@
 
 
 def combine_kernel(got_ref, token_ref, mixed_ref):
-    peers, _, span = got_ref.shape
+    peers = got_ref.shape[0]
     rounds, _, length = token_ref.shape
     per_peer = length // peers
-    heads = span // HEAD_DIM
+    heads = mixed_ref.shape[1] // HEAD_DIM
     lane_group = iota((peers, per_peer, LANES), 2) // GROUP
     own_group = lane_group == iota((peers, per_peer, LANES), 1)
     lane = iota((length, LANES), 1) % GROUP // PIECES
     column = iota((length, length), 0)
+    log_row = iota((peers, GROUP, LANES), 1)
+    all_logs = got_ref[:, got_ref.shape[1] - GROUP :, :].astype(F32)
     outs, lses = [], []
     for turn in range(rounds):
         pick = flag(token_ref[turn, :1, :] == column)
-        at = turn * per_peer
-        rows = got_ref[:, at : at + per_peer, :].reshape(length, span)
-        logs = got_ref[
-            :, rounds * per_peer : rounds * per_peer + GROUP, turn * LANES : (turn + 1) * LANES
-        ]
-        logs = jnp.concatenate([logs] * (per_peer // GROUP), axis=1)
-        logs = jnp.where(own_group, logs, jnp.zeros_like(logs)).reshape(length, LANES)
-        outs.append(dot(pick, rows))
-        moved = dot(pick, logs)
+        logs = jnp.sum(jnp.where(log_row == turn, all_logs, 0.0), axis=1, keepdims=True)
+        logs = jnp.where(own_group, logs, 0.0).astype(BF16)
+        sides = []
+        for head in range(heads):
+            at = (head * rounds + turn) * per_peer
+            sides.append(got_ref[:, at : at + per_peer, :].reshape(length, HEAD_DIM))
+        outs.append(dot(pick, jnp.concatenate(sides, axis=1)))
+        moved = dot(pick, logs.reshape(length, LANES))
         lses.append(
             [
                 jnp.sum(jnp.where(lane == head, moved, 0.0), axis=1, keepdims=True)
@@ -539,12 +551,12 @@
         mixed_ref[:, at : at + HEAD_DIM] = mixed.astype(BF16)
 
 
-def combine(got, token):
+def combine(got, token, span):
     rounds, _, length = token.shape
     return pl.pallas_call(
         combine_kernel,
-        out_shape=jax.ShapeDtypeStruct((length, got.shape[2]), BF16),
-        cost_estimate=cost(2 * rounds * length * length * (got.shape[2] + LANES), 1 << 20),
+        out_shape=jax.ShapeDtypeStruct((length, span), BF16),
+        cost_estimate=cost(2 * rounds * length * length * (span + LANES), 1 << 20),
         compiler_params=BIG,
         name="combine",
     )(got, token)
@@ -641,28 +653,18 @@
     )
     received = exchange(dispatch.reshape(peers, capacity, part), "seq")
     outgoing, slot_token = pack_rows(me, perms, x_att, w_qk, w_val)
-    columns = [
-        hop(
-            lax.dynamic_slice_in_dim(
-                after(w_out, dispatch), (where[0] + by) % chips * part, part, 1
-            ),
-            by,
-            chips,
-        )
-        for by in (1, chips - 1, 2)
-    ]
-    received = after(received, outgoing, *columns)
+    def columns_of(by, *ready):
+        start = (where[0] + by) % chips * part
+        return hop(lax.dynamic_slice_in_dim(after(w_out, *ready), start, part, 1), by, chips)
+
+    near = [columns_of(by, dispatch) for by in (1, chips - 1)]
+    received = after(received, outgoing, *near)
     outgoing = after(outgoing, received)
     own = (w_gate, w_up, w_down)
-    sibling = [
-        lax.ppermute(
-            lax.dynamic_slice_in_dim(after(weight, received), 1 - core, 1, 0), "exp", siblings
-        )
-        for weight in own
-    ]
-    shards, far = spread(received, chips)
+    sibling = [lax.ppermute(after(weight, received), "exp", siblings) for weight in own]
+    shards, far_shards = spread(received, chips)
     arrived = exchange(outgoing.reshape(peers, rounds * per_peer, outgoing.shape[1]), "seq")
-    expert_part = run_experts(where, shards, far, own, sibling)
+    expert_part = run_experts(where, shards, far_shards, own, sibling)
     arrived = after(arrived, expert_part)
     rows, last, row_slot = sort_rows(me, perms, arrived, length)
     expert_rows = lax.psum_scatter(
@@ -677,21 +679,23 @@
     last = after(last, later)
     packed = attend_first(me, perms, rows, last, row_slot, later, peers)
     got = exchange(packed, "seq")
+    far = columns_of(2, packed)
     expert_rows = after(expert_rows, packed)
     given = lax.dynamic_index_in_dim(expert_rows, 1 - core, 0, keepdims=False)
     taken = lax.ppermute(given, "exp", siblings)
-    mixed_heads = combine(got, slot_token)
-    expert_rows = place_rows(where, expert_rows, after(taken, mixed_heads))
-    expert_back = exchange(expert_rows, "seq")
-    heads, far_heads = spread(mixed_heads, chips, (expert_rows,))
-    attn_kept, attn_given = project(where, (*heads, *far_heads), w_out, columns)
-    attended = attn_kept + lax.ppermute(attn_given, "exp", siblings).astype(F32)
-    attended = attended.astype(BF16)
-    expert_back = after(expert_back, attended)
-    mixed = unpack_tokens(
-        expert_back.reshape(peers * EXP_DEV * capacity, width // parts), token_slot
+    expert_rows = place_rows(where, expert_rows, taken)
+    mixed_heads = combine(after(got, expert_rows, far), slot_token, w_qk.shape[1])
+    expert_back = exchange(after(expert_rows, mixed_heads), "seq")
+    heads, far_heads = spread(mixed_heads, chips)
+    attn_kept, attn_given = project(where, (*heads, *far_heads), w_out, (*near, far))
+    attn_taken = lax.ppermute(attn_given, "exp", siblings)
+    expert_back = after(expert_back, attn_taken)
+    return finish(
+        expert_back.reshape(peers * EXP_DEV * capacity, width // parts),
+        token_slot,
+        attn_kept,
+        attn_taken,
     )
-    return (attended, mixed)
 
 
 def solution(mesh):

time: 156 us -> 157 us (level)
  waiting for transfers between devices: 48.4 us -> 51 us
  local copies, waits for them, and re-layouts: 12.5 us -> 10.5 us
    ppermute x11, waiting for transfers between devices: 21.2 us -> 34.6 us  [hop(): return lax.ppermute(x, 'exp', pairs)]
    all_to_all x4, waiting for transfers between devices: 15.1 us -> 4.4 us  [exchange(): return lax.all_to_all(x, axis, split_axis=0, concat_axis=0, tiled=True)]
    dynamic_slice x4 -> x2, local copies, waits for them, and re-layouts: 5.33 us -> 0.86 us  [columns_of(): lax.dynamic_slice_in_dim(after(w_out, *ready), start, part, 1)]
    ppermute x11, starting transfers between devices: 18.3 us -> 15.9 us  [hop(): return lax.ppermute(x, 'exp', pairs)]
    unnamed x34 -> x22, local copies, waits for them, and re-layouts: 6.17 us -> 7.71 us
  transfers between devices with their start and end apart: 22 -> 22, of which waited for: 13 -> 12; matrix products, arithmetic and copies ran while one was open for 2% -> 2% of each run, Pallas kernels for 16% -> 16%
where the time goes in v9:
time: 157 us; the launch traced here: 155 us
  waiting for transfers between devices  51 us (32%)
  starting transfers between devices  49.9 us (32%)
  Pallas kernels  28.9 us (18%)
  between operations  14.3 us (9%)
  local copies, waits for them, and re-layouts  10.5 us (7%)
    ppermute x11, waiting for transfers between devices, hop(): return lax.ppermute(x, 'exp', pairs)  34.6 us
    all_to_all x4, starting transfers between devices, exchange(): return lax.all_to_all(x, axis, split_axis=0, concat_axis=0, tiled=True)  32.7 us
    ppermute x11, starting transfers between devices, hop(): return lax.ppermute(x, 'exp', pairs)  15.9 us
    reduce_scatter x1, waiting for transfers between devices, body(): lax.psum_scatter(expert_part, 'exp', scatter_dimension=0, tiled=False, ax...  8.94 us
    pallas_call x1, Pallas kernels, run_experts(): pl.pallas_call(experts_kernel, grid_spec=pltpu.PrefetchScalarGridSpec(num...  8.74 us
    unnamed x22, local copies, waits for them, and re-layouts  7.71 us
    pallas_call x1, Pallas kernels, pack_rows(): pl.pallas_call(pack_rows_kernel, grid_spec=pltpu.PrefetchScalarGridSpec(n...  4.81 us
    all_to_all x4, waiting for transfers between devices, exchange(): return lax.all_to_all(x, axis, split_axis=0, concat_axis=0, tiled=True)  4.4 us
  transfers between devices with their start and end apart: 22, of which 12 were waited for; matrix products, arithmetic and copies ran while one was open for 2% of the time, Pallas kernels for 16%

profile of v9, /device:TPU:32, one launch (start us, length us, event | category | flops | bytes accessed | tf_op | source)
XLA Modules:
  0.0 154.6 jit_solution(10304877120084025961)
XLA Ops:
  7.2 0.1 pad_add_fusion.where_ref
  7.3 1.6 %copy-done = bf16[512,2048]{1,0:T(8,128)(2,1)S(1)} copy-done((bf16[512,2048]{1,0:T(8,128)(2,1)S(1)}, bf16[512,2048]{1,0:T(8,128)(2,1)}, u32[]{:S(2)}) %copy-start) | copy-done | bytes 2097176
  8.9 0.7 copy-done.3
  9.5 2.2 %pack_tokens.1 = (bf16[512,512]{1,0:T(8,128)(2,1)}, s32[8,512]{1,0:T(8,128)S(1)}) custom-call(s32[2]{0:T(128)S(1)} %pad_add_fusion.where_ref, s32[1,512]{1,0:T(1,128)S(1)} %bitcast.13, bf16[512,2048]{1,0:T(8,128)(2,1)S(1)} %copy-done), custom_call_target="tpu_custom_call" | custom-call | flops 268435456 | bytes 2097152 | tf_op jit(solution)/shard_map/pack_tokens/pallas_call | solution.py:146
  11.8 11.2 %all-to-all-start = ((bf16[32,16,512]{2,1,0:T(8,128)(2,1)}), bf16[32,16,512]{2,1,0:T(8,128)(2,1)S(1)}, u32[]{:S(2)}, u32[]{:S(2)}) async-start(bf16[32,16,512]{2,1,0:T(8,128)(2,1)} %bitcast.3), calls=%async_computation | async-start | bytes 1048576 | tf_op jit(solution)/shard_map/all_to_all | solution.py:611
  23.0 0.8 constant_dynamic-slice_fusion.1
  23.9 3.0 %collective-permute-start.1 = (bf16[256,512]{1,0:T(8,128)(2,1)}, bf16[256,512]{1,0:T(8,128)(2,1)S(1)}, u32[]{:S(2)}, u32[]{:S(2)}) collective-permute-start(bf16[256,512]{1,0:T(8,128)(2,1)} %get-tuple-element.46), channel_id=1, source_target_pairs={{0,6},{1,7},{2,0},{3,1},{4,2},{5,3},{6,4},{7,5},{8,14},{9,15},{10,... | collective-permute-start | bytes 786440 | tf_op jit(solution)/shard_map/ppermute | solution.py:620
  26.9 0.0 copy-start.4
  26.9 1.6 %copy-done.4 = bf16[512,2048]{1,0:T(8,128)(2,1)S(1)} copy-done((bf16[512,2048]{1,0:T(8,128)(2,1)S(1)}, bf16[512,2048]{1,0:T(8,128)(2,1)}, u32[]{:S(2)}) %copy-start.4) | copy-done | bytes 2097176
  28.5 1.2 copy-done.6
  29.7 4.8 %pack_rows.1 = (bf16[1024,512]{1,0:T(8,128)(2,1)}, s32[2,8,512]{2,1,0:T(8,128)S(1)}) custom-call(s32[1]{0:T(128)} %bitcast.4.me_ref, s32[2,16384]{1,0:T(2,128)S(1)} %copy-done.9, bf16[512,2048]{1,0:T(8,128)(2,1)S(1)} %copy-done.4, bf16[2048,256]{1,0:T(8,128)(2,1)S(1)} %copy-done.5, bf16[2048,256]{1,0:T(8,128)(2,1)S(1)} %copy-done.6), custom_call_target="tpu_custom_call" | custom-call | flops 1610612736 | bytes 6291456 | tf_op jit(solution)/shard_map/pack_rows/pallas_call | solution.py:90
  34.5 1.0 collective-permute-done.refs_1_
  35.5 0.7 copy-done.7
  36.2 4.4 %all-to-all-done.refs_0_ = bf16[32,16,512]{2,1,0:T(8,128)(2,1)S(1)} async-done(((bf16[32,16,512]{2,1,0:T(8,128)(2,1)}), bf16[32,16,512]{2,1,0:T(8,128)(2,1)S(1)}, u32[]{:S(2)}, u32[]{:S(2)}) %all-to-all-start) | async-done | bytes 524320 | tf_op jit(solution)/shard_map/all_to_all | solution.py:611
  40.6 0.0 collective-permute-start.6
  40.6 0.5 collective-permute-start.7
  41.1 0.0 collective-permute-start.8
  41.1 3.0 %collective-permute-start.3 = (bf16[32,16,512]{2,1,0:T(8,128)(2,1)S(1)}, bf16[32,16,512]{2,1,0:T(8,128)(2,1)S(1)}, u32[]{:S(2)}, u32[]{:S(2)}) collective-permute-start(bf16[32,16,512]{2,1,0:T(8,128)(2,1)S(1)} %all-to-all-done.refs_0_), channel_id=1, source_target_pairs={{0,6},{1,7},{2,0},{3,1},{4,2},{5,3},{6,4},{7,5},{8,14},{9,15},{10,... | collective-permute-start | bytes 1572872 | tf_op jit(solution)/shard_map/ppermute | solution.py:620
  44.1 0.0 collective-permute-start.2
  44.1 4.9 %all-to-all-start.1 = ((bf16[32,32,512]{2,1,0:T(8,128)(2,1)}), bf16[32,32,512]{2,1,0:T(8,128)(2,1)S(1)}, u32[]{:S(2)}, u32[]{:S(2)}) async-start(bf16[32,32,512]{2,1,0:T(8,128)(2,1)} %bitcast.6), calls=%async_computation.2 | async-start | bytes 2097152 | tf_op jit(solution)/shard_map/all_to_all | solution.py:611
  49.0 0.0 reduce-scatter.2.cloned.1.call-start
  49.0 6.9 %collective-permute-done.3.refs_2_ = bf16[32,16,512]{2,1,0:T(8,128)(2,1)S(1)} collective-permute-done((bf16[32,16,512]{2,1,0:T(8,128)(2,1)S(1)}, bf16[32,16,512]{2,1,0:T(8,128)(2,1)S(1)}, u32[]{:S(2)}, u32[]{:S(2)}) %collective-permute-start.3) | collective-permute-done | bytes 524320 | tf_op jit(solution)/shard_map/ppermute | solution.py:620
  56.0 3.8 %collective-permute-start.5 = (bf16[16,16,512]{2,1,0:T(8,128)(2,1)S(1)}, bf16[16,16,512]{2,1,0:T(8,128)(2,1)S(1)}, u32[]{:S(2)}, u32[]{:S(2)}) collective-permute-start(bf16[16,16,512]{2,1,0:T(8,128)(2,1)S(1)} %slice.17), channel_id=1, source_target_pairs={{0,6},{1,7},{2,0},{3,1},{4,2},{5,3},{6,4},{7,5},{8,14},{9,15},{10,... | collective-permute-start | bytes 786440 | tf_op jit(solution)/shard_map/ppermute | solution.py:620
  59.8 0.0 collective-permute-done.2.refs_1_
  59.8 1.0 slice.16
  60.7 0.3 collective-permute-start.4
  61.0 4.2 %collective-permute-done.5.refs_4_ = bf16[16,16,512]{2,1,0:T(8,128)(2,1)S(1)} collective-permute-done((bf16[16,16,512]{2,1,0:T(8,128)(2,1)S(1)}, bf16[16,16,512]{2,1,0:T(8,128)(2,1)S(1)}, u32[]{:S(2)}, u32[]{:S(2)}) %collective-permute-start.5) | collective-permute-done | bytes 262176 | tf_op jit(solution)/shard_map/ppermute | solution.py:620
  65.2 4.6 %collective-permute-done.4.refs_3_ = bf16[16,16,512]{2,1,0:T(8,128)(2,1)S(1)} collective-permute-done((bf16[16,16,512]{2,1,0:T(8,128)(2,1)S(1)}, bf16[16,16,512]{2,1,0:T(8,128)(2,1)S(1)}, u32[]{:S(2)}, u32[]{:S(2)}) %collective-permute-start.4) | collective-permute-done | bytes 262176 | tf_op jit(solution)/shard_map/ppermute | solution.py:620
  69.9 0.0 collective-permute-done.6.refs_8_
  69.9 0.0 collective-permute-done.7.refs_9_
  69.9 0.0 collective-permute-done.8.refs_10_
  69.9 8.7 %experts.1 = bf16[4,2,32,16,256]{4,3,2,1,0:T(8,128)(2,1)} custom-call(s32[2]{0:T(128)S(1)} %pad_add_fusion.where_ref, bf16[32,16,512]{2,1,0:T(8,128)(2,1)S(1)} %all-to-all-done.refs_0_, bf16[32,16,512]{2,1,0:T(8,128)(2,1)} %collective-permute-done.2.refs_1_, bf16[32,16,512]{2,1,0:T(8,128)(2,1)S(1)} %collective-permute-done.3.refs_2_, ...), custom_call_target="tpu_custom_call" | custom-call | flops 15000000512 | bytes 10485760 | tf_op jit(solution)/shard_map/experts/pallas_call | solution.py:221
  78.6 0.0 reduce-scatter.2.cloned.1.call-update
  78.7 0.9 copy-done.10
  79.5 1.7 %sort_rows.1 = (bf16[2,512,512]{2,1,0:T(8,128)(2,1)S(1)}, bf16[2,64,512]{2,1,0:T(8,128)(2,1)S(1)}, s32[2,8,512]{2,1,0:T(8,128)S(1)}) custom-call(s32[1]{0:T(128)} %bitcast.4.me_ref, s32[2,16384]{1,0:T(2,128)S(1)} %copy-done.10, bf16[32,32,512]{2,1,0:T(8,128)(2,1)S(1)} %all-to-all-done.1.arrived_ref), custom_call_target="tpu_custom_call" | custom-call | flops 34359738368 | bytes 4194304 | tf_op jit(solution)/shard_map/sort_rows/pallas_call | solution.py:306
  81.2 0.5 collective-permute-start.9
  81.8 3.0 %attend_later.1.later_ref = bf16[2,384,384]{2,1,0:T(8,128)(2,1)S(1)} custom-call(s32[1]{0:T(128)} %bitcast.4.me_ref, s32[2,16384]{1,0:T(2,128)S(1)} %copy-done.10, bf16[2,512,512]{2,1,0:T(8,128)(2,1)S(1)} %get-tuple-element.33.rows_ref), custom_call_target="tpu_custom_call" | custom-call | flops 34359738368 | bytes 4194304 | tf_op jit(solution)/shard_map/attend_later/pallas_call | solution.py:459
  84.8 1.5 collective-permute-done.9.last_ref
  86.3 3.1 %attend_first.1 = bf16[32,72,128]{2,1,0:T(8,128)(2,1)} custom-call(s32[1]{0:T(128)} %bitcast.4.me_ref, s32[2,16384]{1,0:T(2,128)S(1)} %copy-done.10, s32[2,16384]{1,0:T(2,128)S(1)} %copy-done.10, bf16[2,512,512]{2,1,0:T(8,128)(2,1)S(1)} %get-tuple-element.33.rows_ref, bf16[2,64,512]{2,1,0:T(8,128)(2,1)S(1)} %collective-permute-done.9.last_ref, ...), custom_call_target="tpu_custom_call" | custom-call | flops 34359738368 | bytes 4194304 | tf_op jit(solution)/shard_map/attend_first/pallas_call | solution.py:487
  89.4 6.4 %all-to-all-start.2 = ((bf16[32,72,128]{2,1,0:T(8,128)(2,1)}), bf16[32,72,128]{2,1,0:T(8,128)(2,1)S(1)}, u32[]{:S(2)}, u32[]{:S(2)}) async-start(bf16[32,72,128]{2,1,0:T(8,128)(2,1)} %attend_first.1), calls=%async_computation.3 | async-start | bytes 1179648 | tf_op jit(solution)/shard_map/all_to_all | solution.py:611
  95.8 8.9 %reduce-scatter.2.cloned.1.call-done = bf16[1,2,32,16,256]{4,3,2,1,0:T(8,128)(2,1)} async-done(((bf16[4,2,32,16,256]{4,3,2,1,0:T(8,128)(2,1)}), bf16[1,2,32,16,256]{4,3,2,1,0:T(8,128)(2,1)}) %reduce-scatter.2.cloned.1.call-update) | async-done | bytes 524304 | tf_op jit(solution)/shard_map/reduce_scatter | solution.py:670
  104.7 1.0 dynamic-slice_bitcast_fusion
  105.7 0.1 collective-permute-start.10
  105.8 0.0 copy-start.8
  105.8 1.5 collective-permute-start.11
  107.4 0.0 collective-permute-done.10.taken_ref
  107.4 1.0 copy-done.1
  108.4 1.4 place_rows.1
  109.8 6.3 %collective-permute-done.11.refs_3_ = bf16[256,512]{1,0:T(8,128)(2,1)S(1)} collective-permute-done((bf16[256,512]{1,0:T(8,128)(2,1)S(1)}, bf16[256,512]{1,0:T(8,128)(2,1)S(1)}, u32[]{:S(2)}, u32[]{:S(2)}) %collective-permute-start.11) | collective-permute-done | bytes 262176 | tf_op jit(solution)/shard_map/ppermute | solution.py:620
  116.1 0.0 all-to-all-done.2.got_ref
  116.1 1.1 combine.1.own_ref
  117.2 10.3 %all-to-all-start.3 = ((bf16[32,2,16,256]{3,2,1,0:T(8,128)(2,1)}), bf16[32,2,16,256]{3,2,1,0:T(8,128)(2,1)S(1)}, u32[]{:S(2)}, u32[]{:S(2)}) async-start(bf16[32,2,16,256]{3,2,1,0:T(8,128)(2,1)} %place_rows.1), calls=%async_computation.4 | async-start | bytes 1048576 | tf_op jit(solution)/shard_map/all_to_all | solution.py:611
  127.5 0.9 collective-permute-start.13
  128.4 1.2 collective-permute-start.12
  129.6 5.3 %collective-permute-done.13.next_ref = bf16[512,256]{1,0:T(8,128)(2,1)S(1)} collective-permute-done((bf16[512,256]{1,0:T(8,128)(2,1)S(1)}, bf16[512,256]{1,0:T(8,128)(2,1)S(1)}, u32[]{:S(2)}, u32[]{:S(2)}) %collective-permute-start.13) | collective-permute-done | bytes 262176 | tf_op jit(solution)/shard_map/ppermute | solution.py:620
  134.9 2.1 %collective-permute-start.15 = (bf16[256,256]{1,0:T(8,128)(2,1)S(1)}, bf16[256,256]{1,0:T(8,128)(2,1)S(1)}, u32[]{:S(2)}, u32[]{:S(2)}) collective-permute-start(bf16[256,256]{1,0:T(8,128)(2,1)S(1)} %slice.19), channel_id=1, source_target_pairs={{0,6},{1,7},{2,0},{3,1},{4,2},{5,3},{6,4},{7,5},{8,14},{9,15},{10,... | collective-permute-start | bytes 393224 | tf_op jit(solution)/shard_map/ppermute | solution.py:620
  137.0 0.1 collective-permute-start.14
  137.1 2.8 %collective-permute-done.15.far_b_ref = bf16[256,256]{1,0:T(8,128)(2,1)S(1)} collective-permute-done((bf16[256,256]{1,0:T(8,128)(2,1)S(1)}, bf16[256,256]{1,0:T(8,128)(2,1)S(1)}, u32[]{:S(2)}, u32[]{:S(2)}) %collective-permute-start.15) | collective-permute-done | bytes 131104 | tf_op jit(solution)/shard_map/ppermute | solution.py:620
  139.9 3.3 %collective-permute-done.14.far_a_ref = bf16[256,256]{1,0:T(8,128)(2,1)S(1)} collective-permute-done((bf16[256,256]{1,0:T(8,128)(2,1)S(1)}, bf16[256,256]{1,0:T(8,128)(2,1)S(1)}, u32[]{:S(2)}, u32[]{:S(2)}) %collective-permute-start.14) | collective-permute-done | bytes 131104 | tf_op jit(solution)/shard_map/ppermute | solution.py:620
  143.3 1.3 project.1
  144.6 0.1 collective-permute-start.16
  144.7 1.5 collective-permute-done.16.taken_ref
  146.2 0.0 all-to-all-done.3
  146.2 1.6 %finish.1 = (bf16[512,256]{1,0:T(8,128)(2,1)}, bf16[512,256]{1,0:T(8,128)(2,1)}) custom-call(bf16[1024,256]{1,0:T(8,128)(2,1)S(1)} %bitcast.10, s32[8,512]{1,0:T(8,128)S(1)} %get-tuple-element.44.slot_ref, f32[512,256]{1,0:T(8,128)S(1)} %get-tuple-element.45.kept_ref, bf16[512,256]{1,0:T(8,128)(2,1)S(1)} %collective-permute-done.16.taken_ref), custom_call_target="tpu_custom_call" | custom-call | flops 268435456 | bytes 1048576 | tf_op jit(solution)/shard_map/finish/pallas_call | solution.py:274
  (21 shorter events, 0.1 us)
Async XLA Ops:
  7.3 1.6 %copy-start = (bf16[512,2048]{1,0:T(8,128)(2,1)S(1)}, bf16[512,2048]{1,0:T(8,128)(2,1)}, u32[]{:S(2)}) copy-start(bf16[512,2048]{1,0:T(8,128)(2,1)} %tokens_ref.1) | copy-start | bytes 6291460
  8.9 0.7 copy-start.3
  9.5 13.5 %copy-start.2 = (bf16[256,2048]{1,0:T(8,128)(2,1)S(1)}, bf16[256,2048]{1,0:T(8,128)(2,1)}, u32[]{:S(2)}) copy-start(bf16[256,2048]{1,0:T(8,128)(2,1)} %refs_0_.1) | copy-start | bytes 3145732
  9.5 17.3 %copy-start.5 = (bf16[2048,256]{1,0:T(8,128)(2,1)S(1)}, bf16[2048,256]{1,0:T(8,128)(2,1)}, u32[]{:S(2)}) copy-start(bf16[2048,256]{1,0:T(8,128)(2,1)} %qk_ref.1) | copy-start | bytes 3145732
  9.5 17.3 %copy-start.9 = (s32[2,16384]{1,0:T(2,128)S(1)}, s32[2,16384]{1,0:T(2,128)}, u32[]{:S(2)}) copy-start(s32[2,16384]{1,0:T(2,128)} %earlier_ref.1) | copy-start | bytes 393220
  11.8 28.8 %all-to-all-start = ((bf16[32,16,512]{2,1,0:T(8,128)(2,1)}), bf16[32,16,512]{2,1,0:T(8,128)(2,1)S(1)}, u32[]{:S(2)}, u32[]{:S(2)}) async-start(bf16[32,16,512]{2,1,0:T(8,128)(2,1)} %bitcast.3), calls=%async_computation | async-start | bytes 1048576 | tf_op jit(solution)/shard_map/all_to_all | solution.py:611
  23.9 10.7 %collective-permute-start.1 = (bf16[256,512]{1,0:T(8,128)(2,1)}, bf16[256,512]{1,0:T(8,128)(2,1)S(1)}, u32[]{:S(2)}, u32[]{:S(2)}) collective-permute-start(bf16[256,512]{1,0:T(8,128)(2,1)} %get-tuple-element.46), channel_id=1, source_target_pairs={{0,6},{1,7},{2,0},{3,1},{4,2},{5,3},{6,4},{7,5},{8,14},{9,15},{10,... | collective-permute-start | bytes 786440 | tf_op jit(solution)/shard_map/ppermute | solution.py:620
  26.9 8.6 %collective-permute-start = (bf16[256,512]{1,0:T(8,128)(2,1)}, bf16[256,512]{1,0:T(8,128)(2,1)S(1)}, u32[]{:S(2)}, u32[]{:S(2)}) collective-permute-start(bf16[256,512]{1,0:T(8,128)(2,1)} %get-tuple-element.47), channel_id=1, source_target_pairs={{0,2},{1,3},{2,4},{3,5},{4,6},{5,7},{6,0},{7,1},{8,10},{9,11},{10,... | collective-permute-start | bytes 786440 | tf_op jit(solution)/shard_map/ppermute | solution.py:620
  26.9 1.6 %copy-start.4 = (bf16[512,2048]{1,0:T(8,128)(2,1)S(1)}, bf16[512,2048]{1,0:T(8,128)(2,1)}, u32[]{:S(2)}) copy-start(bf16[512,2048]{1,0:T(8,128)(2,1)} %x_ref.1) | copy-start | bytes 6291460
  28.5 1.2 copy-start.6
  35.5 0.7 copy-start.7
  40.6 29.3 %collective-permute-start.6 = (bf16[2,2048,256]{2,1,0:T(8,128)(2,1)}, bf16[2,2048,256]{2,1,0:T(8,128)(2,1)}, u32[]{:S(2)}, u32[]{:S(2)}) collective-permute-start(bf16[2,2048,256]{2,1,0:T(8,128)(2,1)} %refs_5_.1), channel_id=1, source_target_pairs={{0,1},{1,0},{2,3},{3,2},{4,5},{5,4},{6,7},{7,6},{8,9},{9,8},{10,11... | collective-permute-start | bytes 6291464 | tf_op jit(solution)/shard_map/ppermute | solution.py:664
  40.6 29.3 %collective-permute-start.7 = (bf16[2,2048,256]{2,1,0:T(8,128)(2,1)}, bf16[2,2048,256]{2,1,0:T(8,128)(2,1)}, u32[]{:S(2)}, u32[]{:S(2)}) collective-permute-start(bf16[2,2048,256]{2,1,0:T(8,128)(2,1)} %refs_6_.1), channel_id=1, source_target_pairs={{0,1},{1,0},{2,3},{3,2},{4,5},{5,4},{6,7},{7,6},{8,9},{9,8},{10,11... | collective-permute-start | bytes 6291464 | tf_op jit(solution)/shard_map/ppermute | solution.py:664
  41.1 28.8 %collective-permute-start.8 = (bf16[2,256,2048]{2,1,0:T(8,128)(2,1)}, bf16[2,256,2048]{2,1,0:T(8,128)(2,1)}, u32[]{:S(2)}, u32[]{:S(2)}) collective-permute-start(bf16[2,256,2048]{2,1,0:T(8,128)(2,1)} %refs_7_.1), channel_id=1, source_target_pairs={{0,1},{1,0},{2,3},{3,2},{4,5},{5,4},{6,7},{7,6},{8,9},{9,8},{10,11... | collective-permute-start | bytes 6291464 | tf_op jit(solution)/shard_map/ppermute | solution.py:664
  41.1 14.9 %collective-permute-start.3 = (bf16[32,16,512]{2,1,0:T(8,128)(2,1)S(1)}, bf16[32,16,512]{2,1,0:T(8,128)(2,1)S(1)}, u32[]{:S(2)}, u32[]{:S(2)}) collective-permute-start(bf16[32,16,512]{2,1,0:T(8,128)(2,1)S(1)} %all-to-all-done.refs_0_), channel_id=1, source_target_pairs={{0,6},{1,7},{2,0},{3,1},{4,2},{5,3},{6,4},{7,5},{8,14},{9,15},{10,... | collective-permute-start | bytes 1572872 | tf_op jit(solution)/shard_map/ppermute | solution.py:620
  44.1 15.6 %collective-permute-start.2 = (bf16[32,16,512]{2,1,0:T(8,128)(2,1)S(1)}, bf16[32,16,512]{2,1,0:T(8,128)(2,1)}, u32[]{:S(2)}, u32[]{:S(2)}) collective-permute-start(bf16[32,16,512]{2,1,0:T(8,128)(2,1)S(1)} %all-to-all-done.refs_0_), channel_id=1, source_target_pairs={{0,2},{1,3},{2,4},{3,5},{4,6},{5,7},{6,0},{7,1},{8,10},{9,11},{10,... | collective-permute-start | bytes 1572872 | tf_op jit(solution)/shard_map/ppermute | solution.py:620
  44.1 34.5 %all-to-all-start.1 = ((bf16[32,32,512]{2,1,0:T(8,128)(2,1)}), bf16[32,32,512]{2,1,0:T(8,128)(2,1)S(1)}, u32[]{:S(2)}, u32[]{:S(2)}) async-start(bf16[32,32,512]{2,1,0:T(8,128)(2,1)} %bitcast.6), calls=%async_computation.2 | async-start | bytes 2097152 | tf_op jit(solution)/shard_map/all_to_all | solution.py:611
  49.0 55.7 %reduce-scatter.2.cloned.1.call-start = ((), (), s32[]{:S(2)}) async-start(), calls=%async_computation.5 | async-start | bytes 2621440 | tf_op jit(solution)/shard_map/reduce_scatter | solution.py:670
  56.0 9.2 %collective-permute-start.5 = (bf16[16,16,512]{2,1,0:T(8,128)(2,1)S(1)}, bf16[16,16,512]{2,1,0:T(8,128)(2,1)S(1)}, u32[]{:S(2)}, u32[]{:S(2)}) collective-permute-start(bf16[16,16,512]{2,1,0:T(8,128)(2,1)S(1)} %slice.17), channel_id=1, source_target_pairs={{0,6},{1,7},{2,0},{3,1},{4,2},{5,3},{6,4},{7,5},{8,14},{9,15},{10,... | collective-permute-start | bytes 786440 | tf_op jit(solution)/shard_map/ppermute | solution.py:620
  60.7 9.1 %collective-permute-start.4 = (bf16[16,16,512]{2,1,0:T(8,128)(2,1)S(1)}, bf16[16,16,512]{2,1,0:T(8,128)(2,1)S(1)}, u32[]{:S(2)}, u32[]{:S(2)}) collective-permute-start(bf16[16,16,512]{2,1,0:T(8,128)(2,1)S(1)} %slice.16), channel_id=1, source_target_pairs={{0,2},{1,3},{2,4},{3,5},{4,6},{5,7},{6,0},{7,1},{8,10},{9,11},{10,... | collective-permute-start | bytes 786440 | tf_op jit(solution)/shard_map/ppermute | solution.py:620
  78.6 0.9 copy-start.10
  81.2 5.0 %collective-permute-start.9 = (bf16[2,64,512]{2,1,0:T(8,128)(2,1)S(1)}, bf16[2,64,512]{2,1,0:T(8,128)(2,1)S(1)}, u32[]{:S(2)}, u32[]{:S(2)}) collective-permute-start(bf16[2,64,512]{2,1,0:T(8,128)(2,1)S(1)} %get-tuple-element.34), channel_id=1, source_target_pairs={{0,8},{8,16},{16,24},{24,32},{32,40},{40,48},{48,56},{56,64},{64,7... | collective-permute-start | bytes 393224 | tf_op jit(solution)/shard_map/ppermute | solution.py:677
  89.4 26.7 %all-to-all-start.2 = ((bf16[32,72,128]{2,1,0:T(8,128)(2,1)}), bf16[32,72,128]{2,1,0:T(8,128)(2,1)S(1)}, u32[]{:S(2)}, u32[]{:S(2)}) async-start(bf16[32,72,128]{2,1,0:T(8,128)(2,1)} %attend_first.1), calls=%async_computation.3 | async-start | bytes 1179648 | tf_op jit(solution)/shard_map/all_to_all | solution.py:611
  105.7 1.7 %collective-permute-start.10 = (bf16[32,16,256]{2,1,0:T(8,128)(2,1)S(1)}, bf16[32,16,256]{2,1,0:T(8,128)(2,1)S(1)}, u32[]{:S(2)}, u32[]{:S(2)}) collective-permute-start(bf16[32,16,256]{2,1,0:T(8,128)(2,1)S(1)} %dynamic-slice_bitcast_fusion), channel_id=1, source_target_pairs={{0,1},{1,0},{2,3},{3,2},{4,5},{5,4},{6,7},{7,6},{8,9},{9,8},{10,11... | collective-permute-start | bytes 786440 | tf_op jit(solution)/shard_map/ppermute | solution.py:685
  105.8 37.5 %copy-start.8 = (bf16[256,512]{1,0:T(8,128)(2,1)S(1)}, bf16[256,512]{1,0:T(8,128)(2,1)}, u32[]{:S(2)}) copy-start(bf16[256,512]{1,0:T(8,128)(2,1)} %copy-done.7) | copy-start | bytes 786436
  105.8 10.3 %collective-permute-start.11 = (bf16[256,512]{1,0:T(8,128)(2,1)S(1)}, bf16[256,512]{1,0:T(8,128)(2,1)S(1)}, u32[]{:S(2)}, u32[]{:S(2)}) collective-permute-start(bf16[256,512]{1,0:T(8,128)(2,1)S(1)} %constant_dynamic-slice_fusion), channel_id=1, source_target_pairs={{0,4},{1,5},{2,6},{3,7},{4,0},{5,1},{6,2},{7,3},{8,12},{9,13},{10,... | collective-permute-start | bytes 786440 | tf_op jit(solution)/shard_map/ppermute | solution.py:620
  107.4 1.0 copy-start.1
  117.2 29.0 %all-to-all-start.3 = ((bf16[32,2,16,256]{3,2,1,0:T(8,128)(2,1)}), bf16[32,2,16,256]{3,2,1,0:T(8,128)(2,1)S(1)}, u32[]{:S(2)}, u32[]{:S(2)}) async-start(bf16[32,2,16,256]{3,2,1,0:T(8,128)(2,1)} %place_rows.1), calls=%async_computation.4 | async-start | bytes 1048576 | tf_op jit(solution)/shard_map/all_to_all | solution.py:611
  127.5 7.4 %collective-permute-start.13 = (bf16[512,256]{1,0:T(8,128)(2,1)S(1)}, bf16[512,256]{1,0:T(8,128)(2,1)S(1)}, u32[]{:S(2)}, u32[]{:S(2)}) collective-permute-start(bf16[512,256]{1,0:T(8,128)(2,1)S(1)} %combine.1.own_ref), channel_id=1, source_target_pairs={{0,6},{1,7},{2,0},{3,1},{4,2},{5,3},{6,4},{7,5},{8,14},{9,15},{10,... | collective-permute-start | bytes 786440 | tf_op jit(solution)/shard_map/ppermute | solution.py:620
  128.4 8.6 %collective-permute-start.12 = (bf16[512,256]{1,0:T(8,128)(2,1)S(1)}, bf16[512,256]{1,0:T(8,128)(2,1)S(1)}, u32[]{:S(2)}, u32[]{:S(2)}) collective-permute-start(bf16[512,256]{1,0:T(8,128)(2,1)S(1)} %combine.1.own_ref), channel_id=1, source_target_pairs={{0,2},{1,3},{2,4},{3,5},{4,6},{5,7},{6,0},{7,1},{8,10},{9,11},{10,... | collective-permute-start | bytes 786440 | tf_op jit(solution)/shard_map/ppermute | solution.py:620
  134.9 5.0 %collective-permute-start.15 = (bf16[256,256]{1,0:T(8,128)(2,1)S(1)}, bf16[256,256]{1,0:T(8,128)(2,1)S(1)}, u32[]{:S(2)}, u32[]{:S(2)}) collective-permute-start(bf16[256,256]{1,0:T(8,128)(2,1)S(1)} %slice.19), channel_id=1, source_target_pairs={{0,6},{1,7},{2,0},{3,1},{4,2},{5,3},{6,4},{7,5},{8,14},{9,15},{10,... | collective-permute-start | bytes 393224 | tf_op jit(solution)/shard_map/ppermute | solution.py:620
  137.0 6.3 %collective-permute-start.14 = (bf16[256,256]{1,0:T(8,128)(2,1)S(1)}, bf16[256,256]{1,0:T(8,128)(2,1)S(1)}, u32[]{:S(2)}, u32[]{:S(2)}) collective-permute-start(bf16[256,256]{1,0:T(8,128)(2,1)S(1)} %slice.18), channel_id=1, source_target_pairs={{0,2},{1,3},{2,4},{3,5},{4,6},{5,7},{6,0},{7,1},{8,10},{9,11},{10,... | collective-permute-start | bytes 393224 | tf_op jit(solution)/shard_map/ppermute | solution.py:620
  144.6 1.6 %collective-permute-start.16 = (bf16[512,256]{1,0:T(8,128)(2,1)S(1)}, bf16[512,256]{1,0:T(8,128)(2,1)S(1)}, u32[]{:S(2)}, u32[]{:S(2)}) collective-permute-start(bf16[512,256]{1,0:T(8,128)(2,1)S(1)} %get-tuple-element.42), channel_id=1, source_target_pairs={{0,1},{1,0},{2,3},{3,2},{4,5},{5,4},{6,7},{7,6},{8,9},{9,8},{10,11... | collective-permute-start | bytes 786440 | tf_op jit(solution)/shard_map/ppermute | solution.py:691
Sparse Core Ops, SparseCore 0:
  78.8 25.8 reduce-scatter.1

commit v10 on v9

--- a/solution.py
+++ b/solution.py
@@ -150,7 +150,7 @@
             grid=(1,),
             in_specs=[
                 pl.BlockSpec((1, length), lambda i, e: (0, 0)),
-                pl.BlockSpec(memory_space=pl.ANY),
+                pl.BlockSpec(memory_space=pltpu.HBM),
             ],
             out_specs=[
                 pl.BlockSpec((slots, part), lambda i, e: (0, 0)),
@@ -201,7 +201,8 @@
             piece = (piece + dot(hiddens[1], weights[5][0, :, at : at + part])).astype(BF16)
             for side in range(EXP_DEV):
                 columns = piece[:, side * half : (side + 1) * half]
-                out_ref[index, side] = columns.reshape(peers, capacity, half)
+                turn = (side + where_ref[1]) % EXP_DEV
+                out_ref[index, turn] = columns.reshape(peers, capacity, half)
 
 
 def run_experts(where, shards, far, own, sibling):
@@ -235,30 +236,29 @@
     )(where, *shards, *far, *own, *sibling)
 
 
-def place_rows_kernel(where_ref, rows_ref, taken_ref, out_ref):
-    out_ref[:, 0] = rows_ref[0]
-    out_ref[:, 1] = taken_ref[...]
-
-
-def place_rows(where, rows, taken):
+def place_rows_kernel(rows_ref, taken_ref, out_ref, copied):
+    copies = (
+        pltpu.make_async_copy(rows_ref.at[0], out_ref.at[:, 0], copied.at[0]),
+        pltpu.make_async_copy(taken_ref, out_ref.at[:, 1], copied.at[1]),
+    )
+    for copy in copies:
+        copy.start()
+    for copy in copies:
+        copy.wait()
+
+
+def place_rows(rows, taken):
     peers, capacity, half = taken.shape
-    out = (peers, EXP_DEV, capacity, half)
     return pl.pallas_call(
         place_rows_kernel,
-        grid_spec=pltpu.PrefetchScalarGridSpec(
-            num_scalar_prefetch=1,
-            grid=(1,),
-            in_specs=[
-                pl.BlockSpec((1, *taken.shape), lambda i, e: (e[1], 0, 0, 0)),
-                pl.BlockSpec(taken.shape, lambda i, e: (0, 0, 0)),
-            ],
-            out_specs=pl.BlockSpec(out, lambda i, e: (0, 0, 0, 0)),
-        ),
-        out_shape=jax.ShapeDtypeStruct(out, BF16),
+        in_specs=[pl.BlockSpec(memory_space=pltpu.HBM)] * 2,
+        out_specs=pl.BlockSpec(memory_space=pltpu.HBM),
+        out_shape=jax.ShapeDtypeStruct((peers, EXP_DEV, capacity, half), BF16),
+        scratch_shapes=[pltpu.SemaphoreType.DMA((2,))],
         cost_estimate=cost(1 << 20, 1 << 20),
         compiler_params=BIG,
         name="place_rows",
-    )(where, rows, taken)
+    )(rows, taken)
 
 
 def finish_kernel(back_ref, slot_ref, kept_ref, taken_ref, attended_ref, mixed_ref):
@@ -335,22 +335,33 @@
     return to_row(lax.rsqrt(squares + 1e-06) / math.sqrt(HEAD_DIM))
 
 
-def attend_tile(query, keys, values, scale, pos_q, pos_k):
-    tile, window = query.shape[0], keys.shape[0]
-    block_q = iota((tile, window), 0) // BLOCK_LEN
-    block_k = iota((tile, window), 1) // BLOCK_LEN
-    met = (block_k == block_q + 1) | (block_k == block_q + 2)
-    scores = dot_t(query, keys) * scale
+def windows(row, first, last):
+    moved = jnp.concatenate([row[:, BLOCK_LEN:], row[:, :BLOCK_LEN]], axis=1)
+    spans = []
+    for start in range(first, last, BLOCK_LEN):
+        odd = start % LANES
+        span = (moved if odd else row)[:, start - odd : start - odd + WINDOW]
+        spans.append(jnp.broadcast_to(span, (BLOCK_LEN, WINDOW)))
+    return jnp.concatenate(spans, axis=0)
+
+
+def attend_blocks(queries, keys, values, scale, pos_q, pos_k):
+    starts = range(0, queries.shape[0], BLOCK_LEN)
+    scores = jnp.concatenate(
+        [dot_t(queries[at : at + BLOCK_LEN], keys[at : at + WINDOW]) for at in starts], axis=0
+    )
+    scores = scores * scale
     scores = jnp.where(pos_k == pos_q, scores - 10000.0, scores)
-    scores = jnp.where(met & (pos_k <= pos_q), scores, -1e30)
+    scores = jnp.where(pos_k <= pos_q, scores, -1e30)
     peak = jnp.max(scores, axis=-1, keepdims=True)
     exponent = jnp.exp(scores - peak)
     total = jnp.sum(exponent, axis=-1, keepdims=True)
     weights = (exponent / total).astype(BF16)
-    return dot(weights, values).astype(BF16), peak + jnp.log(total)
-
-
-TILE, WINDOW, PIECES, GROUP = 2 * BLOCK_LEN, 4 * BLOCK_LEN, 3, 8
+    outs = [dot(weights[at : at + BLOCK_LEN], values[at : at + WINDOW]) for at in starts]
+    return jnp.concatenate(outs, axis=0).astype(BF16), peak + jnp.log(total)
+
+
+TILE, WINDOW, PIECES, GROUP = BLOCK_LEN, 2 * BLOCK_LEN, 3, 8
 
 
 def put_logs(totals):
@@ -365,33 +376,31 @@
     return logs.astype(BF16)
 
 
-def attend_later_kernel(me_ref, perms_ref, rows_ref, out_ref):
+def attend_later_kernel(me_ref, perms_ref, rows_ref, slot_ref, out_ref):
     rounds, length = perms_ref.shape
     span = rows_ref.shape[2] // 2
     for turn in range(rounds):
         position = perms_ref[turn : turn + 1, :].astype(F32)
-        position_col = to_col(position)
-        scales = []
+        pos_q = to_col(position)[TILE:]
+        pos_k = windows(position, 0, length - TILE)
+        outs, totals = [], []
         for head in range(span // HEAD_DIM):
             at = head * HEAD_DIM
-            scales.append(window_scale(rows_ref[turn, :, at : at + HEAD_DIM]))
-        for first in range(TILE, length, TILE):
-            totals = []
-            window = slice(first + TILE - WINDOW, first + TILE)
-            queries = slice(first, first + TILE)
-            for head in range(span // HEAD_DIM):
-                at = head * HEAD_DIM
-                out, total = attend_tile(
-                    rows_ref[turn, queries, at : at + HEAD_DIM],
-                    rows_ref[turn, window, at : at + HEAD_DIM],
-                    rows_ref[turn, window, span + at : span + at + HEAD_DIM],
-                    scales[head][:, window],
-                    position_col[queries],
-                    position[:, window],
-                )
-                out_ref[turn, first - TILE : first, at : at + HEAD_DIM] = out
-                totals.append(total)
-            out_ref[turn, first - TILE : first, span:] = put_logs(totals)
+            keys = rows_ref[turn, :, at : at + HEAD_DIM]
+            out, total = attend_blocks(
+                keys[TILE:],
+                keys,
+                rows_ref[turn, :, span + at : span + at + HEAD_DIM],
+                windows(window_scale(keys), 0, length - TILE),
+                pos_q,
+                pos_k,
+            )
+            outs.append(out)
+            totals.append(total)
+        whole = jnp.concatenate(outs + [put_logs(totals)], axis=1)
+        back = flag(iota((length, length), 0) == slot_ref[turn, :1, :])
+        whole = jnp.concatenate([jnp.zeros((TILE, whole.shape[1]), BF16), whole], axis=0)
+        out_ref[turn] = dot(back, whole).astype(BF16)
 
 
 def attend_first_kernel(
@@ -410,36 +419,36 @@
     span = rows_ref.shape[2] // 2
     lane_group = iota((peers, per_peer, LANES), 2) // GROUP
     own_group = lane_group == iota((peers, per_peer, LANES), 1)
-    empty = jnp.zeros((BLOCK_LEN, HEAD_DIM), BF16)
     log_row = iota((peers, GROUP, LANES), 1)
     all_logs = jnp.zeros((peers, GROUP, LANES), F32)
+    lane = iota((1, LANES), 1)
     for turn in range(rounds):
         position = perms_ref[turn : turn + 1, :].astype(F32)
-        positions = jnp.concatenate([earlier_ref[turn : turn + 1, :].astype(F32), position], axis=1)
-        position_col = to_col(position)
+        earlier = earlier_ref[turn : turn + 1, :].astype(F32)
+        swapped = jnp.concatenate([position[:, BLOCK_LEN:], position[:, :BLOCK_LEN]], axis=1)
+        earlier = jnp.concatenate([earlier[:, BLOCK_LEN:], earlier[:, :BLOCK_LEN]], axis=1)
+        pos_k = jnp.where(lane < BLOCK_LEN, earlier, swapped)
+        pos_q = to_col(position)[:TILE]
         totals, outs = [], []
         for head in range(span // HEAD_DIM):
             at = head * HEAD_DIM
-            own = rows_ref[turn, :, at : at + HEAD_DIM]
-            keys = jnp.concatenate([empty, last_ref[turn, :, at : at + HEAD_DIM], own], axis=0)
+            own = rows_ref[turn, :TILE, at : at + HEAD_DIM]
+            keys = jnp.concatenate([last_ref[turn, :, at : at + HEAD_DIM], own], axis=0)
             at = span + at
             values = jnp.concatenate(
                 [
-                    empty,
                     last_ref[turn, :, at : at + HEAD_DIM],
-                    rows_ref[turn, :, at : at + HEAD_DIM],
+                    rows_ref[turn, :TILE, at : at + HEAD_DIM],
                 ],
                 axis=0,
             )
-            out, total = attend_tile(
-                own, keys, values, window_scale(keys), position_col, positions
-            )
+            out, total = attend_blocks(own, keys, values, window_scale(keys), pos_q, pos_k)
             outs.append(out)
             totals.append(total)
         top = jnp.concatenate(outs + [put_logs(totals)], axis=1)
-        whole = jnp.concatenate([top, later_ref[turn]], axis=0) if length > TILE else top
-        back = flag(iota((length, length), 0) == slot_ref[turn, :1, :])
-        moved = dot(back, whole)
+        top = jnp.concatenate([top, jnp.zeros((LANES - TILE, top.shape[1]), BF16)], axis=0)
+        back = flag(iota((length, LANES), 0) == slot_ref[turn, :1, :LANES])
+        moved = dot(back, top) + later_ref[turn].astype(F32)
         for head in range(span // HEAD_DIM):
             at = (head * rounds + turn) * per_peer
             lanes = moved[:, head * HEAD_DIM : (head + 1) * HEAD_DIM]
@@ -452,10 +461,10 @@
     out_ref[:, out_ref.shape[1] - GROUP :, :] = all_logs.astype(BF16)
 
 
-def attend_later(me, perms, rows):
+def attend_later(me, perms, rows, slot):
     rounds, length, width = rows.shape
     span = width // 2
-    out = (rounds, length - TILE, span + LANES)
+    out = (rounds, length, span + LANES)
     return pl.pallas_call(
         attend_later_kernel,
         grid_spec=pltpu.PrefetchScalarGridSpec(
@@ -464,6 +473,7 @@
             in_specs=[
                 pl.BlockSpec((rounds, length), lambda i, s: (0, s[0])),
                 pl.BlockSpec(rows.shape, lambda i, s: (0, 0, 0)),
+                pl.BlockSpec(slot.shape, lambda i, s: (0, 0, 0)),
             ],
             out_specs=pl.BlockSpec(out, lambda i, s: (0, 0, 0)),
         ),
@@ -471,7 +481,7 @@
         cost_estimate=cost(LONG, 4 << 20),
         compiler_params=BIG,
         name="attend_later",
-    )(me, perms, rows)
+    )(me, perms, rows, slot)
 
 
 def attend_first(me, perms, rows, last, slot, later, peers):
@@ -490,7 +500,7 @@
             num_scalar_prefetch=1,
             grid=(1,),
             in_specs=[
-                pl.BlockSpec((rounds, TILE), lambda i, s: (0, s[0] * lane_blocks)),
+                pl.BlockSpec((rounds, LANES), lambda i, s: (0, s[0] * lane_blocks)),
                 pl.BlockSpec(
                     (rounds, LANES),
                     lambda i, s: (
@@ -498,7 +508,7 @@
                         jnp.where(s[0] == 0, peers * lane_blocks - 1, s[0] * lane_blocks - 1),
                     ),
                 ),
-                fixed((rounds, TILE, width)),
+                fixed((rounds, LANES, width)),
                 fixed(last.shape),
                 fixed(slot.shape),
                 fixed(later.shape),
@@ -601,7 +611,7 @@
             jax.ShapeDtypeStruct((length, half), F32),
             jax.ShapeDtypeStruct((length, half), BF16),
         ],
-        cost_estimate=cost(35 * 10**8, 3 << 20),
+        cost_estimate=cost(55 * 10**8, 3 << 20),
         compiler_params=BIG,
         name="project",
     )(where, *heads, *weights)
@@ -664,8 +674,9 @@
     sibling = [lax.ppermute(after(weight, received), "exp", siblings) for weight in own]
     shards, far_shards = spread(received, chips)
     arrived = exchange(outgoing.reshape(peers, rounds * per_peer, outgoing.shape[1]), "seq")
+    far = columns_of(2, *far_shards)
     expert_part = run_experts(where, shards, far_shards, own, sibling)
-    arrived = after(arrived, expert_part)
+    arrived = after(arrived, expert_part, far)
     rows, last, row_slot = sort_rows(me, perms, arrived, length)
     expert_rows = lax.psum_scatter(
         expert_part,
@@ -675,16 +686,14 @@
         axis_index_groups=lines,
     )
     last = lax.ppermute(last, "seq", [(i, (i + 1) % peers) for i in range(peers)])
-    later = attend_later(me, perms, rows) if length > TILE else rows
+    later = attend_later(me, perms, rows, row_slot)
     last = after(last, later)
     packed = attend_first(me, perms, rows, last, row_slot, later, peers)
     got = exchange(packed, "seq")
-    far = columns_of(2, packed)
     expert_rows = after(expert_rows, packed)
-    given = lax.dynamic_index_in_dim(expert_rows, 1 - core, 0, keepdims=False)
-    taken = lax.ppermute(given, "exp", siblings)
-    expert_rows = place_rows(where, expert_rows, taken)
-    mixed_heads = combine(after(got, expert_rows, far), slot_token, w_qk.shape[1])
+    taken = lax.ppermute(expert_rows[1], "exp", siblings)
+    expert_rows = place_rows(expert_rows, taken)
+    mixed_heads = combine(after(got, expert_rows), slot_token, w_qk.shape[1])
     expert_back = exchange(after(expert_rows, mixed_heads), "seq")
     heads, far_heads = spread(mixed_heads, chips)
     attn_kept, attn_given = project(where, (*heads, *far_heads), w_out, (*near, far))

time: 157 us -> 153 us (0.975); the launches traced: 155 us -> 152 us
  waiting for transfers between devices: 51 us -> 44.3 us
  local copies, waits for them, and re-layouts: 10.5 us -> 12.7 us
    ppermute x11, waiting for transfers between devices: 34.6 us -> 15.9 us  [hop(): return lax.ppermute(x, 'exp', pairs)]
    all_to_all x4, waiting for transfers between devices: 4.4 us -> 13.6 us  [exchange(): return lax.all_to_all(x, axis, split_axis=0, concat_axis=0, tiled=True)]
    ppermute x11, starting transfers between devices: 15.9 us -> 18.9 us  [hop(): return lax.ppermute(x, 'exp', pairs)]
    reduce_scatter x1, waiting for transfers between devices: 8.94 us -> 11 us  [body(): lax.psum_scatter(expert_part, 'exp', scatter_dimension=0, tiled=False, ax...]
  transfers between devices with their start and end apart: 22 -> 22, of which waited for: 12 -> 11; matrix products, arithmetic and copies ran while one was open for 2% -> 3% of each run, Pallas kernels for 16% -> 16%
where the time goes in v10:
time: 153 us; the launch traced here: 152 us
  starting transfers between devices  51.4 us (34%)
  waiting for transfers between devices  44.3 us (29%)
  Pallas kernels  29.7 us (19%)
  between operations  14.3 us (9%)
  local copies, waits for them, and re-layouts  12.7 us (8%)
    all_to_all x4, starting transfers between devices, exchange(): return lax.all_to_all(x, axis, split_axis=0, concat_axis=0, tiled=True)  31.2 us
    ppermute x11, starting transfers between devices, hop(): return lax.ppermute(x, 'exp', pairs)  18.9 us
    ppermute x11, waiting for transfers between devices, hop(): return lax.ppermute(x, 'exp', pairs)  15.9 us
    all_to_all x4, waiting for transfers between devices, exchange(): return lax.all_to_all(x, axis, split_axis=0, concat_axis=0, tiled=True)  13.6 us
    reduce_scatter x1, waiting for transfers between devices, body(): lax.psum_scatter(expert_part, 'exp', scatter_dimension=0, tiled=False, ax...  11 us
    pallas_call x1, Pallas kernels, run_experts(): pl.pallas_call(experts_kernel, grid_spec=pltpu.PrefetchScalarGridSpec(num...  8.94 us
    unnamed x22, local copies, waits for them, and re-layouts  7.71 us
    pallas_call x1, Pallas kernels, pack_rows(): pl.pallas_call(pack_rows_kernel, grid_spec=pltpu.PrefetchScalarGridSpec(n...  4.81 us
  transfers between devices with their start and end apart: 22, of which 11 were waited for; matrix products, arithmetic and copies ran while one was open for 3% of the time, Pallas kernels for 16%

profile of v10, /device:TPU:32, one launch (start us, length us, event | category | flops | bytes accessed | tf_op | source)
XLA Modules:
  0.0 152.4 jit_solution(12185527797237050403)
XLA Ops:
  7.2 0.1 pad_add_fusion.where_ref
  7.3 1.6 %copy-done = bf16[512,2048]{1,0:T(8,128)(2,1)S(1)} copy-done((bf16[512,2048]{1,0:T(8,128)(2,1)S(1)}, bf16[512,2048]{1,0:T(8,128)(2,1)}, u32[]{:S(2)}) %copy-start) | copy-done | bytes 2097176
  8.9 0.7 copy-done.3
  9.5 2.2 %pack_tokens.1 = (bf16[512,512]{1,0:T(8,128)(2,1)}, s32[8,512]{1,0:T(8,128)S(1)}) custom-call(s32[2]{0:T(128)S(1)} %pad_add_fusion.where_ref, s32[1,512]{1,0:T(1,128)S(1)} %bitcast.13, bf16[512,2048]{1,0:T(8,128)(2,1)S(1)} %copy-done), custom_call_target="tpu_custom_call" | custom-call | flops 268435456 | bytes 2097152 | tf_op jit(solution)/shard_map/pack_tokens/pallas_call | solution.py:146
  11.8 11.2 %all-to-all-start = ((bf16[32,16,512]{2,1,0:T(8,128)(2,1)}), bf16[32,16,512]{2,1,0:T(8,128)(2,1)S(1)}, u32[]{:S(2)}, u32[]{:S(2)}) async-start(bf16[32,16,512]{2,1,0:T(8,128)(2,1)} %bitcast.3), calls=%async_computation | async-start | bytes 1048576 | tf_op jit(solution)/shard_map/all_to_all | solution.py:621
  23.0 0.8 constant_dynamic-slice_fusion.1
  23.9 1.6 %collective-permute-start = (bf16[256,512]{1,0:T(8,128)(2,1)}, bf16[256,512]{1,0:T(8,128)(2,1)S(1)}, u32[]{:S(2)}, u32[]{:S(2)}) collective-permute-start(bf16[256,512]{1,0:T(8,128)(2,1)} %get-tuple-element.47), channel_id=1, source_target_pairs={{0,2},{1,3},{2,4},{3,5},{4,6},{5,7},{6,0},{7,1},{8,10},{9,11},{10,... | collective-permute-start | bytes 786440 | tf_op jit(solution)/shard_map/ppermute | solution.py:630
  25.4 1.7 %collective-permute-start.1 = (bf16[256,512]{1,0:T(8,128)(2,1)}, bf16[256,512]{1,0:T(8,128)(2,1)S(1)}, u32[]{:S(2)}, u32[]{:S(2)}) collective-permute-start(bf16[256,512]{1,0:T(8,128)(2,1)} %get-tuple-element.46), channel_id=1, source_target_pairs={{0,6},{1,7},{2,0},{3,1},{4,2},{5,3},{6,4},{7,5},{8,14},{9,15},{10,... | collective-permute-start | bytes 786440 | tf_op jit(solution)/shard_map/ppermute | solution.py:630
  27.1 1.6 %copy-done.4 = bf16[512,2048]{1,0:T(8,128)(2,1)S(1)} copy-done((bf16[512,2048]{1,0:T(8,128)(2,1)S(1)}, bf16[512,2048]{1,0:T(8,128)(2,1)}, u32[]{:S(2)}) %copy-start.4) | copy-done | bytes 2097176
  28.7 1.2 copy-done.6
  29.9 4.8 %pack_rows.1 = (bf16[1024,512]{1,0:T(8,128)(2,1)}, s32[2,8,512]{2,1,0:T(8,128)S(1)}) custom-call(s32[1]{0:T(128)} %bitcast.4.me_ref, s32[2,16384]{1,0:T(2,128)S(1)} %copy-done.9, bf16[512,2048]{1,0:T(8,128)(2,1)S(1)} %copy-done.4, bf16[2048,256]{1,0:T(8,128)(2,1)S(1)} %copy-done.5, bf16[2048,256]{1,0:T(8,128)(2,1)S(1)} %copy-done.6), custom_call_target="tpu_custom_call" | custom-call | flops 1610612736 | bytes 6291456 | tf_op jit(solution)/shard_map/pack_rows/pallas_call | solution.py:90
  34.7 0.0 collective-permute-done.refs_1_
  34.7 0.0 collective-permute-done.1.refs_2_
  34.7 0.7 copy-done.7
  35.4 5.1 %all-to-all-done.refs_0_ = bf16[32,16,512]{2,1,0:T(8,128)(2,1)S(1)} async-done(((bf16[32,16,512]{2,1,0:T(8,128)(2,1)}), bf16[32,16,512]{2,1,0:T(8,128)(2,1)S(1)}, u32[]{:S(2)}, u32[]{:S(2)}) %all-to-all-start) | async-done | bytes 524320 | tf_op jit(solution)/shard_map/all_to_all | solution.py:621
  40.6 0.5 collective-permute-start.7
  41.1 0.0 collective-permute-start.8
  41.1 1.6 %collective-permute-start.2 = (bf16[32,16,512]{2,1,0:T(8,128)(2,1)S(1)}, bf16[32,16,512]{2,1,0:T(8,128)(2,1)S(1)}, u32[]{:S(2)}, u32[]{:S(2)}) collective-permute-start(bf16[32,16,512]{2,1,0:T(8,128)(2,1)S(1)} %all-to-all-done.refs_0_), channel_id=1, source_target_pairs={{0,2},{1,3},{2,4},{3,5},{4,6},{5,7},{6,0},{7,1},{8,10},{9,11},{10,... | collective-permute-start | bytes 1572872 | tf_op jit(solution)/shard_map/ppermute | solution.py:630
  42.7 1.7 %collective-permute-start.3 = (bf16[32,16,512]{2,1,0:T(8,128)(2,1)S(1)}, bf16[32,16,512]{2,1,0:T(8,128)(2,1)}, u32[]{:S(2)}, u32[]{:S(2)}) collective-permute-start(bf16[32,16,512]{2,1,0:T(8,128)(2,1)S(1)} %all-to-all-done.refs_0_), channel_id=1, source_target_pairs={{0,6},{1,7},{2,0},{3,1},{4,2},{5,3},{6,4},{7,5},{8,14},{9,15},{10,... | collective-permute-start | bytes 1572872 | tf_op jit(solution)/shard_map/ppermute | solution.py:630
  44.3 4.9 %all-to-all-start.1 = ((bf16[32,32,512]{2,1,0:T(8,128)(2,1)}), bf16[32,32,512]{2,1,0:T(8,128)(2,1)S(1)}, u32[]{:S(2)}, u32[]{:S(2)}) async-start(bf16[32,32,512]{2,1,0:T(8,128)(2,1)} %bitcast.6), calls=%async_computation.2 | async-start | bytes 2097152 | tf_op jit(solution)/shard_map/all_to_all | solution.py:621
  49.2 0.0 reduce-scatter.2.cloned.1.call-start
  49.3 7.5 %collective-permute-done.2.refs_1_ = bf16[32,16,512]{2,1,0:T(8,128)(2,1)S(1)} collective-permute-done((bf16[32,16,512]{2,1,0:T(8,128)(2,1)S(1)}, bf16[32,16,512]{2,1,0:T(8,128)(2,1)S(1)}, u32[]{:S(2)}, u32[]{:S(2)}) %collective-permute-start.2) | collective-permute-done | bytes 524320 | tf_op jit(solution)/shard_map/ppermute | solution.py:630
  56.7 0.7 slice.20
  57.4 0.3 collective-permute-start.4
  57.7 0.0 collective-permute-done.3.refs_2_
  57.7 1.7 %slice.21 = bf16[16,16,512]{2,1,0:T(8,128)(2,1)} slice(bf16[32,16,512]{2,1,0:T(8,128)(2,1)} %collective-permute-done.3.refs_2_), slice={[16:32], [0:16], [0:512]} | slice | bytes 524288 | tf_op jit(solution)/shard_map/slice | solution.py:637
  59.4 2.9 %collective-permute-start.5 = (bf16[16,16,512]{2,1,0:T(8,128)(2,1)}, bf16[16,16,512]{2,1,0:T(8,128)(2,1)}, u32[]{:S(2)}, u32[]{:S(2)}) collective-permute-start(bf16[16,16,512]{2,1,0:T(8,128)(2,1)} %slice.21), channel_id=1, source_target_pairs={{0,6},{1,7},{2,0},{3,1},{4,2},{5,3},{6,4},{7,5},{8,14},{9,15},{10,... | collective-permute-start | bytes 786440 | tf_op jit(solution)/shard_map/ppermute | solution.py:630
  62.3 4.6 %collective-permute-done.4.refs_3_ = bf16[16,16,512]{2,1,0:T(8,128)(2,1)} collective-permute-done((bf16[16,16,512]{2,1,0:T(8,128)(2,1)}, bf16[16,16,512]{2,1,0:T(8,128)(2,1)}, u32[]{:S(2)}, u32[]{:S(2)}) %collective-permute-start.4) | collective-permute-done | bytes 262176 | tf_op jit(solution)/shard_map/ppermute | solution.py:630
  67.0 0.9 collective-permute-done.5.refs_4_
  67.9 0.7 constant_dynamic-slice_fusion
  68.6 2.5 %collective-permute-start.9 = (bf16[256,512]{1,0:T(8,128)(2,1)}, bf16[256,512]{1,0:T(8,128)(2,1)}, u32[]{:S(2)}, u32[]{:S(2)}) collective-permute-start(bf16[256,512]{1,0:T(8,128)(2,1)} %constant_dynamic-slice_fusion), channel_id=1, source_target_pairs={{0,4},{1,5},{2,6},{3,7},{4,0},{5,1},{6,2},{7,3},{8,12},{9,13},{10,... | collective-permute-start | bytes 786440 | tf_op jit(solution)/shard_map/ppermute | solution.py:630
  71.1 0.0 collective-permute-done.8.refs_10_
  71.1 8.9 %experts.1 = bf16[4,2,32,16,256]{4,3,2,1,0:T(8,128)(2,1)} custom-call(s32[2]{0:T(128)S(1)} %pad_add_fusion.where_ref, bf16[32,16,512]{2,1,0:T(8,128)(2,1)S(1)} %all-to-all-done.refs_0_, bf16[32,16,512]{2,1,0:T(8,128)(2,1)S(1)} %collective-permute-done.2.refs_1_, bf16[32,16,512]{2,1,0:T(8,128)(2,1)} %collective-permute-done.3.refs_2_, ...), custom_call_target="tpu_custom_call" | custom-call | flops 15000000512 | bytes 10485760 | tf_op jit(solution)/shard_map/experts/pallas_call | solution.py:222
  80.1 0.0 reduce-scatter.2.cloned.1.call-update
  80.1 0.0 collective-permute-done.9.refs_3_
  80.1 0.9 copy-done.10
  81.0 1.7 %sort_rows.1 = (bf16[2,512,512]{2,1,0:T(8,128)(2,1)S(1)}, bf16[2,64,512]{2,1,0:T(8,128)(2,1)S(1)}, s32[2,8,512]{2,1,0:T(8,128)S(1)}) custom-call(s32[1]{0:T(128)} %bitcast.4.me_ref, s32[2,16384]{1,0:T(2,128)S(1)} %copy-done.10, bf16[32,32,512]{2,1,0:T(8,128)(2,1)S(1)} %all-to-all-done.1.arrived_ref), custom_call_target="tpu_custom_call" | custom-call | flops 34359738368 | bytes 4194304 | tf_op jit(solution)/shard_map/sort_rows/pallas_call | solution.py:306
  82.7 0.5 collective-permute-start.10
  83.2 3.8 %attend_later.1.later_ref = bf16[2,512,384]{2,1,0:T(8,128)(2,1)S(1)} custom-call(s32[1]{0:T(128)} %bitcast.4.me_ref, s32[2,16384]{1,0:T(2,128)S(1)} %copy-done.10, bf16[2,512,512]{2,1,0:T(8,128)(2,1)S(1)} %get-tuple-element.34.rows_ref, s32[2,8,512]{2,1,0:T(8,128)S(1)} %get-tuple-element.36.slot_ref), custom_call_target="tpu_custom_call" | custom-call | flops 34359738368 | bytes 4194304 | tf_op jit(solution)/shard_map/attend_later/pallas_call | solution.py:468
  87.1 0.6 collective-permute-done.10.last_ref
  87.7 2.5 %attend_first.1 = bf16[32,72,128]{2,1,0:T(8,128)(2,1)} custom-call(s32[1]{0:T(128)} %bitcast.4.me_ref, s32[2,16384]{1,0:T(2,128)S(1)} %copy-done.10, s32[2,16384]{1,0:T(2,128)S(1)} %copy-done.10, bf16[2,512,512]{2,1,0:T(8,128)(2,1)S(1)} %get-tuple-element.34.rows_ref, bf16[2,64,512]{2,1,0:T(8,128)(2,1)S(1)} %collective-permute-done.10.last_ref, ...), custom_call_target="tpu_custom_call" | custom-call | flops 34359738368 | bytes 4194304 | tf_op jit(solution)/shard_map/attend_first/pallas_call | solution.py:497
  90.2 6.4 %all-to-all-start.2 = ((bf16[32,72,128]{2,1,0:T(8,128)(2,1)}), bf16[32,72,128]{2,1,0:T(8,128)(2,1)S(1)}, u32[]{:S(2)}, u32[]{:S(2)}) async-start(bf16[32,72,128]{2,1,0:T(8,128)(2,1)} %attend_first.1), calls=%async_computation.3 | async-start | bytes 1179648 | tf_op jit(solution)/shard_map/all_to_all | solution.py:621
  96.6 11.0 %reduce-scatter.2.cloned.1.call-done = bf16[1,2,32,16,256]{4,3,2,1,0:T(8,128)(2,1)} async-done(((bf16[4,2,32,16,256]{4,3,2,1,0:T(8,128)(2,1)}), bf16[1,2,32,16,256]{4,3,2,1,0:T(8,128)(2,1)}) %reduce-scatter.2.cloned.1.call-update) | async-done | bytes 524304 | tf_op jit(solution)/shard_map/reduce_scatter | solution.py:681
  107.6 1.0 slice_bitcast_fusion
  108.7 0.1 collective-permute-start.11
  108.8 1.5 collective-permute-done.11.taken_ref
  110.3 1.0 copy-done.1
  111.3 0.8 place_rows.1
  112.1 1.3 all-to-all-done.2.got_ref
  113.4 1.1 combine.1.own_ref
  114.5 2.1 %collective-permute-start.12 = (bf16[512,256]{1,0:T(8,128)(2,1)S(1)}, bf16[512,256]{1,0:T(8,128)(2,1)S(1)}, u32[]{:S(2)}, u32[]{:S(2)}) collective-permute-start(bf16[512,256]{1,0:T(8,128)(2,1)S(1)} %combine.1.own_ref), channel_id=1, source_target_pairs={{0,2},{1,3},{2,4},{3,5},{4,6},{5,7},{6,0},{7,1},{8,10},{9,11},{10,... | collective-permute-start | bytes 786440 | tf_op jit(solution)/shard_map/ppermute | solution.py:630
  116.7 1.2 collective-permute-start.13
  117.8 8.8 %all-to-all-start.3 = ((bf16[32,2,16,256]{3,2,1,0:T(8,128)(2,1)}), bf16[32,2,16,256]{3,2,1,0:T(8,128)(2,1)S(1)}, u32[]{:S(2)}, u32[]{:S(2)}) async-start(bf16[32,2,16,256]{3,2,1,0:T(8,128)(2,1)} %place_rows.1), calls=%async_computation.4 | async-start | bytes 1048576 | tf_op jit(solution)/shard_map/all_to_all | solution.py:621
  126.6 0.0 collective-permute-done.12.prev_ref
  126.7 0.1 collective-permute-start.14
  126.7 0.0 collective-permute-done.13.next_ref
  126.8 3.3 %collective-permute-start.15 = (bf16[256,256]{1,0:T(8,128)(2,1)S(1)}, bf16[256,256]{1,0:T(8,128)(2,1)S(1)}, u32[]{:S(2)}, u32[]{:S(2)}) collective-permute-start(bf16[256,256]{1,0:T(8,128)(2,1)S(1)} %slice.23), channel_id=1, source_target_pairs={{0,6},{1,7},{2,0},{3,1},{4,2},{5,3},{6,4},{7,5},{8,14},{9,15},{10,... | collective-permute-start | bytes 393224 | tf_op jit(solution)/shard_map/ppermute | solution.py:630
  130.1 2.8 %collective-permute-done.14.far_a_ref = bf16[256,256]{1,0:T(8,128)(2,1)S(1)} collective-permute-done((bf16[256,256]{1,0:T(8,128)(2,1)S(1)}, bf16[256,256]{1,0:T(8,128)(2,1)S(1)}, u32[]{:S(2)}, u32[]{:S(2)}) %collective-permute-start.14) | collective-permute-done | bytes 131104 | tf_op jit(solution)/shard_map/ppermute | solution.py:630
  132.9 0.0 collective-permute-done.15.far_b_ref
  132.9 2.3 %project.1 = (f32[512,256]{1,0:T(8,128)S(1)}, bf16[512,256]{1,0:T(8,128)(2,1)S(1)}) custom-call(s32[2]{0:T(128)S(1)} %pad_add_fusion.where_ref, bf16[512,256]{1,0:T(8,128)(2,1)S(1)} %combine.1.own_ref, bf16[512,256]{1,0:T(8,128)(2,1)S(1)} %collective-permute-done.12.prev_ref, bf16[512,256]{1,0:T(8,128)(2,1)S(1)} %collective-permute-done.13.next_ref, ...), custom_call_target="tpu_custom_call" | custom-call | flops 5500000256 | bytes 3145728 | tf_op jit(solution)/shard_map/project/pallas_call | solution.py:602
  135.2 0.1 collective-permute-start.16
  135.3 1.5 collective-permute-done.16.taken_ref
  136.8 7.2 %all-to-all-done.3 = bf16[32,2,16,256]{3,2,1,0:T(8,128)(2,1)S(1)} async-done(((bf16[32,2,16,256]{3,2,1,0:T(8,128)(2,1)}), bf16[32,2,16,256]{3,2,1,0:T(8,128)(2,1)S(1)}, u32[]{:S(2)}, u32[]{:S(2)}) %all-to-all-start.3) | async-done | bytes 524320 | tf_op jit(solution)/shard_map/all_to_all | solution.py:621
  144.0 1.6 %finish.1 = (bf16[512,256]{1,0:T(8,128)(2,1)}, bf16[512,256]{1,0:T(8,128)(2,1)}) custom-call(bf16[1024,256]{1,0:T(8,128)(2,1)S(1)} %bitcast.10, s32[8,512]{1,0:T(8,128)S(1)} %get-tuple-element.44.slot_ref, f32[512,256]{1,0:T(8,128)S(1)} %get-tuple-element.45.kept_ref, bf16[512,256]{1,0:T(8,128)(2,1)S(1)} %collective-permute-done.16.taken_ref), custom_call_target="tpu_custom_call" | custom-call | flops 268435456 | bytes 1048576 | tf_op jit(solution)/shard_map/finish/pallas_call | solution.py:274
  (21 shorter events, 0.1 us)
Async XLA Ops:
  7.3 1.6 %copy-start = (bf16[512,2048]{1,0:T(8,128)(2,1)S(1)}, bf16[512,2048]{1,0:T(8,128)(2,1)}, u32[]{:S(2)}) copy-start(bf16[512,2048]{1,0:T(8,128)(2,1)} %tokens_ref.1) | copy-start | bytes 6291460
  8.9 0.7 copy-start.3
  9.5 13.5 %copy-start.2 = (bf16[256,2048]{1,0:T(8,128)(2,1)S(1)}, bf16[256,2048]{1,0:T(8,128)(2,1)}, u32[]{:S(2)}) copy-start(bf16[256,2048]{1,0:T(8,128)(2,1)} %refs_0_.1) | copy-start | bytes 3145732
  9.5 17.6 %copy-start.5 = (bf16[2048,256]{1,0:T(8,128)(2,1)S(1)}, bf16[2048,256]{1,0:T(8,128)(2,1)}, u32[]{:S(2)}) copy-start(bf16[2048,256]{1,0:T(8,128)(2,1)} %qk_ref.1) | copy-start | bytes 3145732
  9.5 17.6 %copy-start.9 = (s32[2,16384]{1,0:T(2,128)S(1)}, s32[2,16384]{1,0:T(2,128)}, u32[]{:S(2)}) copy-start(s32[2,16384]{1,0:T(2,128)} %earlier_ref.1) | copy-start | bytes 393220
  11.8 28.8 %all-to-all-start = ((bf16[32,16,512]{2,1,0:T(8,128)(2,1)}), bf16[32,16,512]{2,1,0:T(8,128)(2,1)S(1)}, u32[]{:S(2)}, u32[]{:S(2)}) async-start(bf16[32,16,512]{2,1,0:T(8,128)(2,1)} %bitcast.3), calls=%async_computation | async-start | bytes 1048576 | tf_op jit(solution)/shard_map/all_to_all | solution.py:621
  23.9 10.9 %collective-permute-start = (bf16[256,512]{1,0:T(8,128)(2,1)}, bf16[256,512]{1,0:T(8,128)(2,1)S(1)}, u32[]{:S(2)}, u32[]{:S(2)}) collective-permute-start(bf16[256,512]{1,0:T(8,128)(2,1)} %get-tuple-element.47), channel_id=1, source_target_pairs={{0,2},{1,3},{2,4},{3,5},{4,6},{5,7},{6,0},{7,1},{8,10},{9,11},{10,... | collective-permute-start | bytes 786440 | tf_op jit(solution)/shard_map/ppermute | solution.py:630
  25.4 9.3 %collective-permute-start.1 = (bf16[256,512]{1,0:T(8,128)(2,1)}, bf16[256,512]{1,0:T(8,128)(2,1)S(1)}, u32[]{:S(2)}, u32[]{:S(2)}) collective-permute-start(bf16[256,512]{1,0:T(8,128)(2,1)} %get-tuple-element.46), channel_id=1, source_target_pairs={{0,6},{1,7},{2,0},{3,1},{4,2},{5,3},{6,4},{7,5},{8,14},{9,15},{10,... | collective-permute-start | bytes 786440 | tf_op jit(solution)/shard_map/ppermute | solution.py:630
  27.1 1.6 %copy-start.4 = (bf16[512,2048]{1,0:T(8,128)(2,1)S(1)}, bf16[512,2048]{1,0:T(8,128)(2,1)}, u32[]{:S(2)}) copy-start(bf16[512,2048]{1,0:T(8,128)(2,1)} %x_ref.1) | copy-start | bytes 6291460
  28.7 1.2 copy-start.6
  34.7 0.7 copy-start.7
  40.6 30.5 %collective-permute-start.6 = (bf16[2,2048,256]{2,1,0:T(8,128)(2,1)}, bf16[2,2048,256]{2,1,0:T(8,128)(2,1)}, u32[]{:S(2)}, u32[]{:S(2)}) collective-permute-start(bf16[2,2048,256]{2,1,0:T(8,128)(2,1)} %refs_5_.1), channel_id=1, source_target_pairs={{0,1},{1,0},{2,3},{3,2},{4,5},{5,4},{6,7},{7,6},{8,9},{9,8},{10,11... | collective-permute-start | bytes 6291464 | tf_op jit(solution)/shard_map/ppermute | solution.py:674
  40.6 30.5 %collective-permute-start.7 = (bf16[2,2048,256]{2,1,0:T(8,128)(2,1)}, bf16[2,2048,256]{2,1,0:T(8,128)(2,1)}, u32[]{:S(2)}, u32[]{:S(2)}) collective-permute-start(bf16[2,2048,256]{2,1,0:T(8,128)(2,1)} %refs_6_.1), channel_id=1, source_target_pairs={{0,1},{1,0},{2,3},{3,2},{4,5},{5,4},{6,7},{7,6},{8,9},{9,8},{10,11... | collective-permute-start | bytes 6291464 | tf_op jit(solution)/shard_map/ppermute | solution.py:674
  41.1 30.0 %collective-permute-start.8 = (bf16[2,256,2048]{2,1,0:T(8,128)(2,1)}, bf16[2,256,2048]{2,1,0:T(8,128)(2,1)}, u32[]{:S(2)}, u32[]{:S(2)}) collective-permute-start(bf16[2,256,2048]{2,1,0:T(8,128)(2,1)} %refs_7_.1), channel_id=1, source_target_pairs={{0,1},{1,0},{2,3},{3,2},{4,5},{5,4},{6,7},{7,6},{8,9},{9,8},{10,11... | collective-permute-start | bytes 6291464 | tf_op jit(solution)/shard_map/ppermute | solution.py:674
  41.1 15.6 %collective-permute-start.2 = (bf16[32,16,512]{2,1,0:T(8,128)(2,1)S(1)}, bf16[32,16,512]{2,1,0:T(8,128)(2,1)S(1)}, u32[]{:S(2)}, u32[]{:S(2)}) collective-permute-start(bf16[32,16,512]{2,1,0:T(8,128)(2,1)S(1)} %all-to-all-done.refs_0_), channel_id=1, source_target_pairs={{0,2},{1,3},{2,4},{3,5},{4,6},{5,7},{6,0},{7,1},{8,10},{9,11},{10,... | collective-permute-start | bytes 1572872 | tf_op jit(solution)/shard_map/ppermute | solution.py:630
  42.7 15.1 %collective-permute-start.3 = (bf16[32,16,512]{2,1,0:T(8,128)(2,1)S(1)}, bf16[32,16,512]{2,1,0:T(8,128)(2,1)}, u32[]{:S(2)}, u32[]{:S(2)}) collective-permute-start(bf16[32,16,512]{2,1,0:T(8,128)(2,1)S(1)} %all-to-all-done.refs_0_), channel_id=1, source_target_pairs={{0,6},{1,7},{2,0},{3,1},{4,2},{5,3},{6,4},{7,5},{8,14},{9,15},{10,... | collective-permute-start | bytes 1572872 | tf_op jit(solution)/shard_map/ppermute | solution.py:630
  44.3 35.8 %all-to-all-start.1 = ((bf16[32,32,512]{2,1,0:T(8,128)(2,1)}), bf16[32,32,512]{2,1,0:T(8,128)(2,1)S(1)}, u32[]{:S(2)}, u32[]{:S(2)}) async-start(bf16[32,32,512]{2,1,0:T(8,128)(2,1)} %bitcast.6), calls=%async_computation.2 | async-start | bytes 2097152 | tf_op jit(solution)/shard_map/all_to_all | solution.py:621
  49.2 58.4 %reduce-scatter.2.cloned.1.call-start = ((), (), s32[]{:S(2)}) async-start(), calls=%async_computation.5 | async-start | bytes 2621440 | tf_op jit(solution)/shard_map/reduce_scatter | solution.py:681
  57.4 9.5 %collective-permute-start.4 = (bf16[16,16,512]{2,1,0:T(8,128)(2,1)}, bf16[16,16,512]{2,1,0:T(8,128)(2,1)}, u32[]{:S(2)}, u32[]{:S(2)}) collective-permute-start(bf16[16,16,512]{2,1,0:T(8,128)(2,1)} %slice.20), channel_id=1, source_target_pairs={{0,2},{1,3},{2,4},{3,5},{4,6},{5,7},{6,0},{7,1},{8,10},{9,11},{10,... | collective-permute-start | bytes 786440 | tf_op jit(solution)/shard_map/ppermute | solution.py:630
  59.4 8.5 %collective-permute-start.5 = (bf16[16,16,512]{2,1,0:T(8,128)(2,1)}, bf16[16,16,512]{2,1,0:T(8,128)(2,1)}, u32[]{:S(2)}, u32[]{:S(2)}) collective-permute-start(bf16[16,16,512]{2,1,0:T(8,128)(2,1)} %slice.21), channel_id=1, source_target_pairs={{0,6},{1,7},{2,0},{3,1},{4,2},{5,3},{6,4},{7,5},{8,14},{9,15},{10,... | collective-permute-start | bytes 786440 | tf_op jit(solution)/shard_map/ppermute | solution.py:630
  68.6 11.5 %collective-permute-start.9 = (bf16[256,512]{1,0:T(8,128)(2,1)}, bf16[256,512]{1,0:T(8,128)(2,1)}, u32[]{:S(2)}, u32[]{:S(2)}) collective-permute-start(bf16[256,512]{1,0:T(8,128)(2,1)} %constant_dynamic-slice_fusion), channel_id=1, source_target_pairs={{0,4},{1,5},{2,6},{3,7},{4,0},{5,1},{6,2},{7,3},{8,12},{9,13},{10,... | collective-permute-start | bytes 786440 | tf_op jit(solution)/shard_map/ppermute | solution.py:630
  80.1 0.9 copy-start.10
  82.7 5.0 %collective-permute-start.10 = (bf16[2,64,512]{2,1,0:T(8,128)(2,1)S(1)}, bf16[2,64,512]{2,1,0:T(8,128)(2,1)S(1)}, u32[]{:S(2)}, u32[]{:S(2)}) collective-permute-start(bf16[2,64,512]{2,1,0:T(8,128)(2,1)S(1)} %get-tuple-element.35), channel_id=1, source_target_pairs={{0,8},{8,16},{16,24},{24,32},{32,40},{40,48},{48,56},{56,64},{64,7... | collective-permute-start | bytes 393224 | tf_op jit(solution)/shard_map/ppermute | solution.py:688
  90.2 23.2 %all-to-all-start.2 = ((bf16[32,72,128]{2,1,0:T(8,128)(2,1)}), bf16[32,72,128]{2,1,0:T(8,128)(2,1)S(1)}, u32[]{:S(2)}, u32[]{:S(2)}) async-start(bf16[32,72,128]{2,1,0:T(8,128)(2,1)} %attend_first.1), calls=%async_computation.3 | async-start | bytes 1179648 | tf_op jit(solution)/shard_map/all_to_all | solution.py:621
  107.6 25.3 %copy-start.8 = (bf16[256,512]{1,0:T(8,128)(2,1)S(1)}, bf16[256,512]{1,0:T(8,128)(2,1)}, u32[]{:S(2)}) copy-start(bf16[256,512]{1,0:T(8,128)(2,1)} %copy-done.7) | copy-start | bytes 786436
  108.7 1.6 %collective-permute-start.11 = (bf16[32,16,256]{2,1,0:T(8,128)(2,1)S(1)}, bf16[32,16,256]{2,1,0:T(8,128)(2,1)S(1)}, u32[]{:S(2)}, u32[]{:S(2)}) collective-permute-start(bf16[32,16,256]{2,1,0:T(8,128)(2,1)S(1)} %slice_bitcast_fusion), channel_id=1, source_target_pairs={{0,1},{1,0},{2,3},{3,2},{4,5},{5,4},{6,7},{7,6},{8,9},{9,8},{10,11... | collective-permute-start | bytes 786440 | tf_op jit(solution)/shard_map/ppermute | solution.py:694
  110.3 1.0 copy-start.1
  114.5 12.1 %collective-permute-start.12 = (bf16[512,256]{1,0:T(8,128)(2,1)S(1)}, bf16[512,256]{1,0:T(8,128)(2,1)S(1)}, u32[]{:S(2)}, u32[]{:S(2)}) collective-permute-start(bf16[512,256]{1,0:T(8,128)(2,1)S(1)} %combine.1.own_ref), channel_id=1, source_target_pairs={{0,2},{1,3},{2,4},{3,5},{4,6},{5,7},{6,0},{7,1},{8,10},{9,11},{10,... | collective-permute-start | bytes 786440 | tf_op jit(solution)/shard_map/ppermute | solution.py:630
  116.7 10.1 %collective-permute-start.13 = (bf16[512,256]{1,0:T(8,128)(2,1)S(1)}, bf16[512,256]{1,0:T(8,128)(2,1)S(1)}, u32[]{:S(2)}, u32[]{:S(2)}) collective-permute-start(bf16[512,256]{1,0:T(8,128)(2,1)S(1)} %combine.1.own_ref), channel_id=1, source_target_pairs={{0,6},{1,7},{2,0},{3,1},{4,2},{5,3},{6,4},{7,5},{8,14},{9,15},{10,... | collective-permute-start | bytes 786440 | tf_op jit(solution)/shard_map/ppermute | solution.py:630
  117.8 26.2 %all-to-all-start.3 = ((bf16[32,2,16,256]{3,2,1,0:T(8,128)(2,1)}), bf16[32,2,16,256]{3,2,1,0:T(8,128)(2,1)S(1)}, u32[]{:S(2)}, u32[]{:S(2)}) async-start(bf16[32,2,16,256]{3,2,1,0:T(8,128)(2,1)} %place_rows.1), calls=%async_computation.4 | async-start | bytes 1048576 | tf_op jit(solution)/shard_map/all_to_all | solution.py:621
  126.7 6.3 %collective-permute-start.14 = (bf16[256,256]{1,0:T(8,128)(2,1)S(1)}, bf16[256,256]{1,0:T(8,128)(2,1)S(1)}, u32[]{:S(2)}, u32[]{:S(2)}) collective-permute-start(bf16[256,256]{1,0:T(8,128)(2,1)S(1)} %slice.22), channel_id=1, source_target_pairs={{0,2},{1,3},{2,4},{3,5},{4,6},{5,7},{6,0},{7,1},{8,10},{9,11},{10,... | collective-permute-start | bytes 393224 | tf_op jit(solution)/shard_map/ppermute | solution.py:630
  126.8 6.1 %collective-permute-start.15 = (bf16[256,256]{1,0:T(8,128)(2,1)S(1)}, bf16[256,256]{1,0:T(8,128)(2,1)S(1)}, u32[]{:S(2)}, u32[]{:S(2)}) collective-permute-start(bf16[256,256]{1,0:T(8,128)(2,1)S(1)} %slice.23), channel_id=1, source_target_pairs={{0,6},{1,7},{2,0},{3,1},{4,2},{5,3},{6,4},{7,5},{8,14},{9,15},{10,... | collective-permute-start | bytes 393224 | tf_op jit(solution)/shard_map/ppermute | solution.py:630
  135.2 1.6 %collective-permute-start.16 = (bf16[512,256]{1,0:T(8,128)(2,1)S(1)}, bf16[512,256]{1,0:T(8,128)(2,1)S(1)}, u32[]{:S(2)}, u32[]{:S(2)}) collective-permute-start(bf16[512,256]{1,0:T(8,128)(2,1)S(1)} %get-tuple-element.42), channel_id=1, source_target_pairs={{0,1},{1,0},{2,3},{3,2},{4,5},{5,4},{6,7},{7,6},{8,9},{9,8},{10,11... | collective-permute-start | bytes 786440 | tf_op jit(solution)/shard_map/ppermute | solution.py:700
Sparse Core Ops, SparseCore 0:
  80.2 27.3 reduce-scatter.1

commit v11 on v10

--- a/solution.py
+++ b/solution.py
@@ -49,11 +49,26 @@
     return flag(iota((count, count), 0) <= iota((count, count), 1))
 
 
-def pack_rows_kernel(me_ref, perms_ref, x_ref, qk_ref, val_ref, out_ref, token_ref, scratch):
+def pack_rows_kernel(
+    me_ref,
+    perms_ref,
+    x_ref,
+    qk_ref,
+    val_ref,
+    out_ref,
+    token_ref,
+    order_ref,
+    earlier_ref,
+    scratch,
+):
     length, span = x_ref.shape[0], qk_ref.shape[1]
     rounds, total = perms_ref.shape
     peers = total // length
     per_peer = length // peers
+    start = me_ref[0] * length
+    order_ref[...] = perms_ref[:, pl.ds(pl.multiple_of(start, length), length)]
+    start = jnp.where(start == 0, total, start) - LANES
+    earlier_ref[...] = perms_ref[:, pl.ds(pl.multiple_of(start, LANES), LANES)]
     for peer in range(peers):
         scratch[peer * rounds : (peer + 1) * rounds, :] = perms_ref[
             :, peer * length : (peer + 1) * length
@@ -101,12 +116,16 @@
             out_specs=[
                 whole((slots, 2 * span)),
                 pl.BlockSpec((rounds, 8, length), lambda i, me_ref: (0, 0, 0)),
+                whole((rounds, length)),
+                whole((rounds, LANES)),
             ],
             scratch_shapes=[pltpu.VMEM((groups, length), I32)],
         ),
         out_shape=[
             jax.ShapeDtypeStruct((slots, 2 * span), BF16),
             jax.ShapeDtypeStruct((rounds, 8, length), I32),
+            jax.ShapeDtypeStruct((rounds, length), I32),
+            jax.ShapeDtypeStruct((rounds, LANES), I32),
         ],
         cost_estimate=cost(4 * length * width * span + 4 * slots * length * span, 6 << 20),
         compiler_params=BIG,
@@ -114,14 +133,9 @@
     )(me, perms, x_att, w_qk, w_val)
 
 
-def pack_tokens_kernel(
-    peers, where_ref, ids_ref, tokens_ref, out_ref, slot_ref, mine_ref, copied
-):
+def pack_tokens_kernel(peers, where_ref, ids_ref, tokens_ref, out_ref, slot_ref):
     length = tokens_ref.shape[0]
-    slots, part = out_ref.shape
-    columns = pl.ds(pl.multiple_of(where_ref[0] * part, part), part)
-    copy = pltpu.make_async_copy(tokens_ref.at[:, columns], mine_ref, copied)
-    copy.start()
+    slots = out_ref.shape[0]
     capacity = slots // peers
     experts = EXP_DEV * peers
     ids = ids_ref[...]
@@ -136,12 +150,11 @@
     )
     slot = jnp.where(turn == 0, peer * capacity + rank, -1)
     pick = flag(iota((slots, length), 0) == slot)
-    copy.wait()
-    out_ref[...] = dot(pick, mine_ref[...]).astype(BF16)
-
-
-def pack_tokens(where, ids, tokens, peers, capacity, part):
-    length = tokens.shape[0]
+    out_ref[...] = dot(pick, tokens_ref[...]).astype(BF16)
+
+
+def pack_tokens(where, ids, tokens, peers, capacity):
+    length, part = tokens.shape
     slots = peers * capacity
     return pl.pallas_call(
         functools.partial(pack_tokens_kernel, peers),
@@ -150,13 +163,12 @@
             grid=(1,),
             in_specs=[
                 pl.BlockSpec((1, length), lambda i, e: (0, 0)),
-                pl.BlockSpec(memory_space=pltpu.HBM),
+                pl.BlockSpec((length, part), lambda i, e: (0, 0)),
             ],
             out_specs=[
                 pl.BlockSpec((slots, part), lambda i, e: (0, 0)),
                 pl.BlockSpec((8, length), lambda i, e: (0, 0)),
             ],
-            scratch_shapes=[pltpu.VMEM((length, part), BF16), pltpu.SemaphoreType.DMA],
         ),
         out_shape=[
             jax.ShapeDtypeStruct((slots, part), BF16),
@@ -224,7 +236,7 @@
         grid_spec=pltpu.PrefetchScalarGridSpec(
             num_scalar_prefetch=1,
             grid=(len(shards) + 1,),
-            in_specs=[pl.BlockSpec(x.shape, lambda i, e: (0, 0, 0)) for x in (*shards, *far)]
+            in_specs=[pl.BlockSpec(memory_space=pltpu.VMEM)] * 5
             + [own_up, own_up, own_down] * 2,
             out_specs=pl.BlockSpec(out, lambda i, e: (0, 0, 0, 0, 0)),
             scratch_shapes=[pltpu.VMEM((4, rows, hidden), F32)],
@@ -239,7 +251,7 @@
 def place_rows_kernel(rows_ref, taken_ref, out_ref, copied):
     copies = (
         pltpu.make_async_copy(rows_ref.at[0], out_ref.at[:, 0], copied.at[0]),
-        pltpu.make_async_copy(taken_ref, out_ref.at[:, 1], copied.at[1]),
+        pltpu.make_async_copy(taken_ref.at[1], out_ref.at[:, 1], copied.at[1]),
     )
     for copy in copies:
         copy.start()
@@ -248,7 +260,7 @@
 
 
 def place_rows(rows, taken):
-    peers, capacity, half = taken.shape
+    _, peers, capacity, half = taken.shape
     return pl.pallas_call(
         place_rows_kernel,
         in_specs=[pl.BlockSpec(memory_space=pltpu.HBM)] * 2,
@@ -261,16 +273,13 @@
     )(rows, taken)
 
 
-def finish_kernel(back_ref, slot_ref, kept_ref, taken_ref, attended_ref, mixed_ref):
-    length = mixed_ref.shape[0]
-    column = to_col(slot_ref[:1, :].astype(F32)).astype(I32)
-    pick = flag(column == iota((length, back_ref.shape[0]), 1))
-    mixed_ref[...] = dot(pick, back_ref[...]).astype(BF16)
+def finish_kernel(back_ref, pick_ref, kept_ref, taken_ref, attended_ref, mixed_ref):
+    mixed_ref[...] = dot(pick_ref[...], back_ref[...]).astype(BF16)
     attended_ref[...] = (kept_ref[...] + taken_ref[...].astype(F32)).astype(BF16)
 
 
-def finish(back, slot, kept, taken):
-    length, width = slot.shape[1], back.shape[1]
+def finish(back, pick, kept, taken):
+    length, width = pick.shape[0], back.shape[1]
     return pl.pallas_call(
         finish_kernel,
         out_shape=[
@@ -280,10 +289,10 @@
         cost_estimate=cost(2 * length * back.shape[0] * width, 1 << 20),
         compiler_params=BIG,
         name="finish",
-    )(back, slot, kept, taken)
-
-
-def sort_rows_kernel(peers, me_ref, perms_ref, arrived_ref, rows_ref, last_ref, slot_ref):
+    )(back, pick, kept, taken)
+
+
+def sort_rows_kernel(peers, perms_ref, arrived_ref, rows_ref, last_ref, slot_ref):
     rounds, length = perms_ref.shape
     per_peer = length // peers
     for turn in range(rounds):
@@ -300,24 +309,11 @@
         last_ref[turn] = rows[length - BLOCK_LEN :]
 
 
-def sort_rows(me, perms, arrived, length):
-    rounds = perms.shape[0]
+def sort_rows(order, arrived):
+    rounds, length = order.shape
     peers, _, width = arrived.shape
     return pl.pallas_call(
         functools.partial(sort_rows_kernel, peers),
-        grid_spec=pltpu.PrefetchScalarGridSpec(
-            num_scalar_prefetch=1,
-            grid=(1,),
-            in_specs=[
-                pl.BlockSpec((rounds, length), lambda i, s: (0, s[0])),
-                pl.BlockSpec(arrived.shape, lambda i, s: (0, 0, 0)),
-            ],
-            out_specs=[
-                pl.BlockSpec((rounds, length, width), lambda i, s: (0, 0, 0)),
-                pl.BlockSpec((rounds, BLOCK_LEN, width), lambda i, s: (0, 0, 0)),
-                pl.BlockSpec((rounds, 8, length), lambda i, s: (0, 0, 0)),
-            ],
-        ),
         out_shape=[
             jax.ShapeDtypeStruct((rounds, length, width), BF16),
             jax.ShapeDtypeStruct((rounds, BLOCK_LEN, width), BF16),
@@ -326,7 +322,7 @@
         cost_estimate=cost(LONG, 4 << 20),
         compiler_params=BIG,
         name="sort_rows",
-    )(me, perms, arrived)
+    )(order, arrived)
 
 
 def window_scale(keys):
@@ -376,7 +372,7 @@
     return logs.astype(BF16)
 
 
-def attend_later_kernel(me_ref, perms_ref, rows_ref, slot_ref, out_ref):
+def attend_later_kernel(perms_ref, rows_ref, slot_ref, out_ref):
     rounds, length = perms_ref.shape
     span = rows_ref.shape[2] // 2
     for turn in range(rounds):
@@ -405,7 +401,6 @@
 
 def attend_first_kernel(
     peers,
-    me_ref,
     perms_ref,
     earlier_ref,
     rows_ref,
@@ -423,7 +418,7 @@
     all_logs = jnp.zeros((peers, GROUP, LANES), F32)
     lane = iota((1, LANES), 1)
     for turn in range(rounds):
-        position = perms_ref[turn : turn + 1, :].astype(F32)
+        position = perms_ref[turn : turn + 1, :LANES].astype(F32)
         earlier = earlier_ref[turn : turn + 1, :].astype(F32)
         swapped = jnp.concatenate([position[:, BLOCK_LEN:], position[:, :BLOCK_LEN]], axis=1)
         earlier = jnp.concatenate([earlier[:, BLOCK_LEN:], earlier[:, :BLOCK_LEN]], axis=1)
@@ -461,65 +456,41 @@
     out_ref[:, out_ref.shape[1] - GROUP :, :] = all_logs.astype(BF16)
 
 
-def attend_later(me, perms, rows, slot):
+def attend_later(order, rows, slot):
     rounds, length, width = rows.shape
-    span = width // 2
-    out = (rounds, length, span + LANES)
     return pl.pallas_call(
         attend_later_kernel,
-        grid_spec=pltpu.PrefetchScalarGridSpec(
-            num_scalar_prefetch=1,
-            grid=(1,),
-            in_specs=[
-                pl.BlockSpec((rounds, length), lambda i, s: (0, s[0])),
-                pl.BlockSpec(rows.shape, lambda i, s: (0, 0, 0)),
-                pl.BlockSpec(slot.shape, lambda i, s: (0, 0, 0)),
-            ],
-            out_specs=pl.BlockSpec(out, lambda i, s: (0, 0, 0)),
-        ),
+        out_shape=jax.ShapeDtypeStruct((rounds, length, width // 2 + LANES), BF16),
+        cost_estimate=cost(LONG, 4 << 20),
+        compiler_params=BIG,
+        name="attend_later",
+    )(order, rows, slot)
+
+
+def attend_first(order, earlier, rows, last, slot, later, peers):
+    rounds, length, width = rows.shape
+    out = (peers, width // 2 // HEAD_DIM * rounds * (length // peers) + GROUP, HEAD_DIM)
+
+    def fixed(x):
+        return pl.BlockSpec(x.shape, lambda i: (0,) * x.ndim)
+
+    return pl.pallas_call(
+        functools.partial(attend_first_kernel, peers),
+        grid=(1,),
+        in_specs=[
+            fixed(order),
+            fixed(earlier),
+            pl.BlockSpec((rounds, LANES, width), lambda i: (0, 0, 0)),
+            fixed(last),
+            fixed(slot),
+            fixed(later),
+        ],
+        out_specs=pl.BlockSpec(out, lambda i: (0, 0, 0)),
         out_shape=jax.ShapeDtypeStruct(out, BF16),
         cost_estimate=cost(LONG, 4 << 20),
         compiler_params=BIG,
-        name="attend_later",
-    )(me, perms, rows, slot)
-
-
-def attend_first(me, perms, rows, last, slot, later, peers):
-    rounds, length, width = rows.shape
-    span = width // 2
-    per_peer = length // peers
-    lane_blocks = length // LANES
-
-    def fixed(shape):
-        return pl.BlockSpec(shape, lambda i, s: (0, 0, 0))
-
-    out = (peers, span // HEAD_DIM * rounds * per_peer + GROUP, HEAD_DIM)
-    return pl.pallas_call(
-        functools.partial(attend_first_kernel, peers),
-        grid_spec=pltpu.PrefetchScalarGridSpec(
-            num_scalar_prefetch=1,
-            grid=(1,),
-            in_specs=[
-                pl.BlockSpec((rounds, LANES), lambda i, s: (0, s[0] * lane_blocks)),
-                pl.BlockSpec(
-                    (rounds, LANES),
-                    lambda i, s: (
-                        0,
-                        jnp.where(s[0] == 0, peers * lane_blocks - 1, s[0] * lane_blocks - 1),
-                    ),
-                ),
-                fixed((rounds, LANES, width)),
-                fixed(last.shape),
-                fixed(slot.shape),
-                fixed(later.shape),
-            ],
-            out_specs=fixed(out),
-        ),
-        out_shape=jax.ShapeDtypeStruct(out, BF16),
-        cost_estimate=cost(LONG, 4 << 20),
-        compiler_params=BIG,
         name="attend_first",
-    )(me, perms, perms, rows, last, slot, later)
+    )(order, earlier, rows, last, slot, later)
 
 
 def combine_kernel(got_ref, token_ref, mixed_ref):
@@ -573,7 +544,9 @@
 
 
 def project_kernel(where_ref, own_ref, prev_ref, next_ref, far_a_ref, far_b_ref, *refs):
-    weights, (kept_ref, given_ref) = refs[:-2], refs[-2:]
+    slot_ref, weights, (kept_ref, given_ref, pick_ref) = refs[0], refs[1:-3], refs[-3:]
+    column = to_col(slot_ref[:1, :].astype(F32)).astype(I32)
+    pick_ref[...] = flag(column == iota(pick_ref.shape, 1))
     far = jnp.concatenate([far_a_ref[...], far_b_ref[...]], axis=0)
     total = dot(own_ref[...], weights[0][...]) + dot(prev_ref[...], weights[1][...])
     total = total + dot(next_ref[...], weights[2][...]) + dot(far, weights[3][...])
@@ -587,34 +560,36 @@
             given_ref[...] = total[:, other * half : (other + 1) * half].astype(BF16)
 
 
-def project(where, heads, w_out, others):
+def project(where, heads, w_out, others, slot, slots):
     length, span = heads[0].shape
     columns = others[0].shape[1]
     half = columns // EXP_DEV
     weights = (w_out, *others)
-    shapes = [x.shape for x in heads] + [(span, columns)] + [x.shape for x in others]
+    shapes = [x.shape for x in (*heads, slot)] + [(span, columns)] + [x.shape for x in others]
 
     def first(i, e):
         return (0, 0)
 
     specs = [pl.BlockSpec(shape, first) for shape in shapes]
-    specs[len(heads)] = pl.BlockSpec((span, columns), lambda i, e: (0, e[0]))
+    specs[len(heads) + 1] = pl.BlockSpec((span, columns), lambda i, e: (0, e[0]))
     return pl.pallas_call(
         project_kernel,
         grid_spec=pltpu.PrefetchScalarGridSpec(
             num_scalar_prefetch=1,
             grid=(1,),
             in_specs=specs,
-            out_specs=[pl.BlockSpec((length, half), first)] * 2,
+            out_specs=[pl.BlockSpec((length, half), first)] * 2
+            + [pl.BlockSpec((slot.shape[1], slots), first)],
         ),
         out_shape=[
             jax.ShapeDtypeStruct((length, half), F32),
             jax.ShapeDtypeStruct((length, half), BF16),
+            jax.ShapeDtypeStruct((slot.shape[1], slots), BF16),
         ],
         cost_estimate=cost(55 * 10**8, 3 << 20),
         compiler_params=BIG,
         name="project",
-    )(where, *heads, *weights)
+    )(where, *heads, slot, *weights)
 
 
 def exchange(x, axis):
@@ -658,11 +633,12 @@
     lines = [[chip * EXP_DEV + side for chip in range(chips)] for side in range(EXP_DEV)]
     siblings = [(i, i ^ 1) for i in range(parts)]
 
+    token_part = lax.dynamic_slice_in_dim(tokens_b, where[0] * part, part, 1)
     dispatch, token_slot = pack_tokens(
-        where, expert_ids.reshape(1, tokb), tokens_b, peers, capacity, part
+        where, expert_ids.reshape(1, tokb), token_part, peers, capacity
     )
     received = exchange(dispatch.reshape(peers, capacity, part), "seq")
-    outgoing, slot_token = pack_rows(me, perms, x_att, w_qk, w_val)
+    outgoing, slot_token, order, earlier = pack_rows(me, perms, x_att, w_qk, w_val)
     def columns_of(by, *ready):
         start = (where[0] + by) % chips * part
         return hop(lax.dynamic_slice_in_dim(after(w_out, *ready), start, part, 1), by, chips)
@@ -674,10 +650,9 @@
     sibling = [lax.ppermute(after(weight, received), "exp", siblings) for weight in own]
     shards, far_shards = spread(received, chips)
     arrived = exchange(outgoing.reshape(peers, rounds * per_peer, outgoing.shape[1]), "seq")
-    far = columns_of(2, *far_shards)
     expert_part = run_experts(where, shards, far_shards, own, sibling)
-    arrived = after(arrived, expert_part, far)
-    rows, last, row_slot = sort_rows(me, perms, arrived, length)
+    arrived = after(arrived, expert_part)
+    rows, last, row_slot = sort_rows(order, arrived)
     expert_rows = lax.psum_scatter(
         expert_part,
         "exp",
@@ -686,22 +661,26 @@
         axis_index_groups=lines,
     )
     last = lax.ppermute(last, "seq", [(i, (i + 1) % peers) for i in range(peers)])
-    later = attend_later(me, perms, rows, row_slot)
+    later = attend_later(order, rows, row_slot)
     last = after(last, later)
-    packed = attend_first(me, perms, rows, last, row_slot, later, peers)
+    packed = attend_first(order, earlier, rows, last, row_slot, later, peers)
     got = exchange(packed, "seq")
-    expert_rows = after(expert_rows, packed)
-    taken = lax.ppermute(expert_rows[1], "exp", siblings)
+    far = columns_of(2, packed)
+    expert_rows = after(expert_rows, packed, far)
+    taken = lax.ppermute(expert_rows, "exp", siblings)
     expert_rows = place_rows(expert_rows, taken)
     mixed_heads = combine(after(got, expert_rows), slot_token, w_qk.shape[1])
     expert_back = exchange(after(expert_rows, mixed_heads), "seq")
     heads, far_heads = spread(mixed_heads, chips)
-    attn_kept, attn_given = project(where, (*heads, *far_heads), w_out, (*near, far))
+    slots = peers * EXP_DEV * capacity
+    attn_kept, attn_given, token_pick = project(
+        where, (*heads, *far_heads), w_out, (*near, far), token_slot, slots
+    )
     attn_taken = lax.ppermute(attn_given, "exp", siblings)
     expert_back = after(expert_back, attn_taken)
     return finish(
-        expert_back.reshape(peers * EXP_DEV * capacity, width // parts),
-        token_slot,
+        expert_back.reshape(slots, width // parts),
+        token_pick,
         attn_kept,
         attn_taken,
     )

time: 153 us -> 161 us (1.052); the launches traced: 152 us -> 159 us
  local copies, waits for them, and re-layouts: 12.7 us -> 23.4 us
  Pallas kernels: 29.7 us -> 26.4 us
    ppermute x11, waiting for transfers between devices: 15.9 us -> 34.9 us  [hop(): return lax.ppermute(x, 'exp', pairs)]
    unnamed x22 -> x46, local copies, waits for them, and re-layouts: 7.71 us -> 19.6 us
    reduce_scatter x1, waiting for transfers between devices: 11 us -> 0.01 us  [body(): lax.psum_scatter(expert_part, 'exp', scatter_dimension=0, tiled=False, ax...]
    all_to_all x4, waiting for transfers between devices: 13.6 us -> 3.53 us  [exchange(): return lax.all_to_all(x, axis, split_axis=0, concat_axis=0, tiled=True)]
    all_to_all x4, starting transfers between devices: 31.2 us -> 35.5 us  [exchange(): return lax.all_to_all(x, axis, split_axis=0, concat_axis=0, tiled=True)]
    ppermute x11, starting transfers between devices: 18.9 us -> 15.2 us  [hop(): return lax.ppermute(x, 'exp', pairs)]
  transfers between devices with their start and end apart: 22 -> 22, of which waited for: 11 -> 10; matrix products, arithmetic and copies ran while one was open for 3% -> 2% of each run, Pallas kernels for 16% -> 14%
where the time goes in v11:
time: 161 us; the launch traced here: 159 us
  starting transfers between devices  51.7 us (32%)
  waiting for transfers between devices  42.8 us (27%)
  Pallas kernels  26.4 us (16%)
  local copies, waits for them, and re-layouts  23.4 us (15%)
  between operations  14.4 us (9%)
    all_to_all x4, starting transfers between devices, exchange(): return lax.all_to_all(x, axis, split_axis=0, concat_axis=0, tiled=True)  35.5 us
    ppermute x11, waiting for transfers between devices, hop(): return lax.ppermute(x, 'exp', pairs)  34.9 us
    unnamed x46, local copies, waits for them, and re-layouts  19.6 us
    ppermute x11, starting transfers between devices, hop(): return lax.ppermute(x, 'exp', pairs)  15.2 us
    pallas_call x1, Pallas kernels, run_experts(): pl.pallas_call(experts_kernel, grid_spec=pltpu.PrefetchScalarGridSpec(num...  7.81 us
    pallas_call x1, Pallas kernels, pack_rows(): pl.pallas_call(pack_rows_kernel, grid_spec=pltpu.PrefetchScalarGridSpec(n...  4.81 us
    pallas_call x1, Pallas kernels, attend_later(): pl.pallas_call(attend_later_kernel, out_shape=jax.ShapeDtypeStruct((round...  3.85 us
    all_to_all x4, waiting for transfers between devices, exchange(): return lax.all_to_all(x, axis, split_axis=0, concat_axis=0, tiled=True)  3.53 us
  transfers between devices with their start and end apart: 22, of which 10 were waited for; matrix products, arithmetic and copies ran while one was open for 2% of the time, Pallas kernels for 14%

profile of v11, /device:TPU:32, one launch (start us, length us, event | category | flops | bytes accessed | tf_op | source)
XLA Modules:
  0.0 158.7 jit_solution(5558719827573005497)
XLA Ops:
  7.2 0.0 copy-start
  7.2 0.0 copy-start.4
  7.2 0.1 pad_add_fusion.where_ref
  7.3 1.5 copy-done
  8.8 0.0 copy-start.22
  8.8 0.7 copy-done.22
  9.5 1.2 pack_tokens.1
  10.7 0.8 copy-done.7
  11.5 11.2 %all-to-all-start = ((bf16[32,16,512]{2,1,0:T(8,128)(2,1)}), bf16[32,16,512]{2,1,0:T(8,128)(2,1)}, u32[]{:S(2)}, u32[]{:S(2)}) async-start(bf16[32,16,512]{2,1,0:T(8,128)(2,1)} %bitcast.11), calls=%async_computation | async-start | bytes 1048576 | tf_op jit(solution)/shard_map/all_to_all | solution.py:596
  22.8 0.8 constant_dynamic-slice_fusion.1
  23.6 3.0 %collective-permute-start.1 = (bf16[256,512]{1,0:T(8,128)(2,1)}, bf16[256,512]{1,0:T(8,128)(2,1)S(1)}, u32[]{:S(2)}, u32[]{:S(2)}) collective-permute-start(bf16[256,512]{1,0:T(8,128)(2,1)} %get-tuple-element.52), channel_id=1, source_target_pairs={{0,6},{1,7},{2,0},{3,1},{4,2},{5,3},{6,4},{7,5},{8,14},{9,15},{10,... | collective-permute-start | bytes 786440 | tf_op jit(solution)/shard_map/ppermute | solution.py:605
  26.6 1.6 %copy-done.10 = bf16[512,2048]{1,0:T(8,128)(2,1)S(1)} copy-done((bf16[512,2048]{1,0:T(8,128)(2,1)S(1)}, bf16[512,2048]{1,0:T(8,128)(2,1)}, u32[]{:S(2)}) %copy-start.10) | copy-done | bytes 2097176
  28.2 1.2 copy-done.11
  29.4 1.2 copy-done.12
  30.7 4.8 %pack_rows.1 = (bf16[1024,512]{1,0:T(8,128)(2,1)}, s32[2,8,512]{2,1,0:T(8,128)S(1)}, s32[2,512]{1,0:T(2,128)S(1)}, s32[2,128]{1,0:T(2,128)S(1)}) custom-call(s32[1]{0:T(128)} %bitcast.4.me_ref, s32[2,16384]{1,0:T(2,128)S(1)} %copy-done.21, bf16[512,2048]{1,0:T(8,128)(2,1)S(1)} %copy-done.10, bf16[2048,256]{1,0:T(8,128)(2,1)S(1)} %copy-done.11, ...), custom_call_target="tpu_custom_call" | custom-call | flops 1610612736 | bytes 6291456 | tf_op jit(solution)/shard_map/pack_rows/pallas_call | solution.py:105
  35.5 0.7 copy-done.13
  36.2 0.7 copy-done.15
  36.9 3.5 %all-to-all-done.refs_0_ = bf16[32,16,512]{2,1,0:T(8,128)(2,1)} async-done(((bf16[32,16,512]{2,1,0:T(8,128)(2,1)}), bf16[32,16,512]{2,1,0:T(8,128)(2,1)}, u32[]{:S(2)}, u32[]{:S(2)}) %all-to-all-start) | async-done | bytes 524320 | tf_op jit(solution)/shard_map/all_to_all | solution.py:596
  40.4 0.5 collective-permute-start.7
  40.9 3.0 %collective-permute-start.3 = (bf16[32,16,512]{2,1,0:T(8,128)(2,1)}, bf16[32,16,512]{2,1,0:T(8,128)(2,1)}, u32[]{:S(2)}, u32[]{:S(2)}) collective-permute-start(bf16[32,16,512]{2,1,0:T(8,128)(2,1)} %all-to-all-done.refs_0_), channel_id=1, source_target_pairs={{0,6},{1,7},{2,0},{3,1},{4,2},{5,3},{6,4},{7,5},{8,14},{9,15},{10,... | collective-permute-start | bytes 1572872 | tf_op jit(solution)/shard_map/ppermute | solution.py:605
  43.9 6.5 %all-to-all-start.1 = ((bf16[32,32,512]{2,1,0:T(8,128)(2,1)}), bf16[32,32,512]{2,1,0:T(8,128)(2,1)S(1)}, u32[]{:S(2)}, u32[]{:S(2)}) async-start(bf16[32,32,512]{2,1,0:T(8,128)(2,1)} %bitcast.6), calls=%async_computation.2 | async-start | bytes 2097152 | tf_op jit(solution)/shard_map/all_to_all | solution.py:596
  50.4 0.0 reduce-scatter.2.cloned.1.call-start
  50.5 5.6 %collective-permute-done.3.refs_2_ = bf16[32,16,512]{2,1,0:T(8,128)(2,1)} collective-permute-done((bf16[32,16,512]{2,1,0:T(8,128)(2,1)}, bf16[32,16,512]{2,1,0:T(8,128)(2,1)}, u32[]{:S(2)}, u32[]{:S(2)}) %collective-permute-start.3) | collective-permute-done | bytes 524320 | tf_op jit(solution)/shard_map/ppermute | solution.py:605
  56.1 1.0 slice.17
  57.0 3.8 %collective-permute-start.5 = (bf16[16,16,512]{2,1,0:T(8,128)(2,1)S(1)}, bf16[16,16,512]{2,1,0:T(8,128)(2,1)S(1)}, u32[]{:S(2)}, u32[]{:S(2)}) collective-permute-start(bf16[16,16,512]{2,1,0:T(8,128)(2,1)S(1)} %slice.17), channel_id=1, source_target_pairs={{0,6},{1,7},{2,0},{3,1},{4,2},{5,3},{6,4},{7,5},{8,14},{9,15},{10,... | collective-permute-start | bytes 786440 | tf_op jit(solution)/shard_map/ppermute | solution.py:605
  60.8 1.0 slice.16
  61.8 0.3 collective-permute-start.4
  62.1 4.2 %collective-permute-done.5.refs_4_ = bf16[16,16,512]{2,1,0:T(8,128)(2,1)S(1)} collective-permute-done((bf16[16,16,512]{2,1,0:T(8,128)(2,1)S(1)}, bf16[16,16,512]{2,1,0:T(8,128)(2,1)S(1)}, u32[]{:S(2)}, u32[]{:S(2)}) %collective-permute-start.5) | collective-permute-done | bytes 262176 | tf_op jit(solution)/shard_map/ppermute | solution.py:605
  66.3 4.6 %collective-permute-done.4.refs_3_ = bf16[16,16,512]{2,1,0:T(8,128)(2,1)S(1)} collective-permute-done((bf16[16,16,512]{2,1,0:T(8,128)(2,1)S(1)}, bf16[16,16,512]{2,1,0:T(8,128)(2,1)S(1)}, u32[]{:S(2)}, u32[]{:S(2)}) %collective-permute-start.4) | collective-permute-done | bytes 262176 | tf_op jit(solution)/shard_map/ppermute | solution.py:605
  70.9 7.8 %experts.1 = bf16[4,2,32,16,256]{4,3,2,1,0:T(8,128)(2,1)S(1)} custom-call(s32[2]{0:T(128)S(1)} %pad_add_fusion.where_ref, bf16[32,16,512]{2,1,0:T(8,128)(2,1)} %all-to-all-done.refs_0_, bf16[32,16,512]{2,1,0:T(8,128)(2,1)} %collective-permute-done.2.refs_1_, bf16[32,16,512]{2,1,0:T(8,128)(2,1)} %collective-permute-done.3.refs_2_, ...), custom_call_target="tpu_custom_call" | custom-call | flops 15000000512 | bytes 10485760 | tf_op jit(solution)/shard_map/experts/pallas_call | solution.py:234
  78.8 1.3 copy-done.1
  80.1 0.0 reduce-scatter.2.cloned.1.call-update
  80.1 1.7 %sort_rows.1 = (bf16[2,512,512]{2,1,0:T(8,128)(2,1)S(1)}, bf16[2,64,512]{2,1,0:T(8,128)(2,1)S(1)}, s32[2,8,512]{2,1,0:T(8,128)S(1)}) custom-call(s32[2,512]{1,0:T(2,128)S(1)} %get-tuple-element.34.perms_ref, bf16[32,32,512]{2,1,0:T(8,128)(2,1)S(1)} %all-to-all-done.1.arrived_ref), custom_call_target="tpu_custom_call" | custom-call | flops 34359738368 | bytes 4194304 | tf_op jit(solution)/shard_map/sort_rows/pallas_call | solution.py:315
  81.8 0.5 collective-permute-start.9
  82.4 3.9 %attend_later.1.later_ref = bf16[2,512,384]{2,1,0:T(8,128)(2,1)S(1)} custom-call(s32[2,512]{1,0:T(2,128)S(1)} %get-tuple-element.34.perms_ref, bf16[2,512,512]{2,1,0:T(8,128)(2,1)S(1)} %get-tuple-element.38.rows_ref, s32[2,8,512]{2,1,0:T(8,128)S(1)} %get-tuple-element.40.slot_ref), custom_call_target="tpu_custom_call" | custom-call | flops 34359738368 | bytes 4194304 | tf_op jit(solution)/shard_map/attend_later/pallas_call | solution.py:461
  86.2 0.7 collective-permute-done.9.last_ref
  86.9 2.5 %attend_first.1 = bf16[32,72,128]{2,1,0:T(8,128)(2,1)} custom-call(s32[2,512]{1,0:T(2,128)S(1)} %get-tuple-element.34.perms_ref, s32[2,128]{1,0:T(2,128)S(1)} %get-tuple-element.35.earlier_ref, bf16[2,512,512]{2,1,0:T(8,128)(2,1)S(1)} %get-tuple-element.38.rows_ref, bf16[2,64,512]{2,1,0:T(8,128)(2,1)S(1)} %collective-permute-done.9.last_ref, ...), custom_call_target="tpu_custom_call" | custom-call | flops 34359738368 | bytes 4194304 | tf_op jit(solution)/shard_map/attend_first/pallas_call | solution.py:477
  89.4 7.7 %all-to-all-start.2 = ((bf16[32,72,128]{2,1,0:T(8,128)(2,1)}), bf16[32,72,128]{2,1,0:T(8,128)(2,1)S(1)}, u32[]{:S(2)}, u32[]{:S(2)}) async-start(bf16[32,72,128]{2,1,0:T(8,128)(2,1)} %attend_first.1), calls=%async_computation.3 | async-start | bytes 1179648 | tf_op jit(solution)/shard_map/all_to_all | solution.py:596
  97.1 1.0 constant_dynamic-slice_fusion
  98.1 0.2 collective-permute-start.10
  98.3 14.2 %collective-permute-done.10.refs_4_ = bf16[256,512]{1,0:T(8,128)(2,1)S(1)} collective-permute-done((bf16[256,512]{1,0:T(8,128)(2,1)S(1)}, bf16[256,512]{1,0:T(8,128)(2,1)S(1)}, u32[]{:S(2)}, u32[]{:S(2)}) %collective-permute-start.10) | collective-permute-done | bytes 262176 | tf_op jit(solution)/shard_map/ppermute | solution.py:605
  112.6 0.7 copy-done.17
  113.3 2.1 %collective-permute-done.11.taken_ref = bf16[2,32,16,256]{3,2,1,0:T(8,128)(2,1)S(1)} collective-permute-done((bf16[2,32,16,256]{3,2,1,0:T(8,128)(2,1)}, bf16[2,32,16,256]{3,2,1,0:T(8,128)(2,1)S(1)}, u32[]{:S(2)}, u32[]{:S(2)}) %collective-permute-start.11) | collective-permute-done | bytes 524320 | tf_op jit(solution)/shard_map/ppermute | solution.py:670
  115.4 1.0 copy-done.6
  116.4 0.8 place_rows.1
  117.3 1.1 combine.1.own_ref
  118.4 1.4 collective-permute-start.13
  119.8 0.9 collective-permute-start.12
  120.7 10.1 %all-to-all-start.3 = ((bf16[32,2,16,256]{3,2,1,0:T(8,128)(2,1)}), bf16[32,2,16,256]{3,2,1,0:T(8,128)(2,1)S(1)}, u32[]{:S(2)}, u32[]{:S(2)}) async-start(bf16[32,2,16,256]{3,2,1,0:T(8,128)(2,1)} %place_rows.1), calls=%async_computation.4 | async-start | bytes 1048576 | tf_op jit(solution)/shard_map/all_to_all | solution.py:596
  130.8 2.4 %collective-permute-start.15 = (bf16[256,256]{1,0:T(8,128)(2,1)S(1)}, bf16[256,256]{1,0:T(8,128)(2,1)S(1)}, u32[]{:S(2)}, u32[]{:S(2)}) collective-permute-start(bf16[256,256]{1,0:T(8,128)(2,1)S(1)} %slice.19), channel_id=1, source_target_pairs={{0,6},{1,7},{2,0},{3,1},{4,2},{5,3},{6,4},{7,5},{8,14},{9,15},{10,... | collective-permute-start | bytes 393224 | tf_op jit(solution)/shard_map/ppermute | solution.py:605
  133.3 0.1 collective-permute-start.14
  133.3 2.5 %collective-permute-done.15.far_b_ref = bf16[256,256]{1,0:T(8,128)(2,1)S(1)} collective-permute-done((bf16[256,256]{1,0:T(8,128)(2,1)S(1)}, bf16[256,256]{1,0:T(8,128)(2,1)S(1)}, u32[]{:S(2)}, u32[]{:S(2)}) %collective-permute-start.15) | collective-permute-done | bytes 131104 | tf_op jit(solution)/shard_map/ppermute | solution.py:605
  135.9 3.7 %collective-permute-done.14.far_a_ref = bf16[256,256]{1,0:T(8,128)(2,1)S(1)} collective-permute-done((bf16[256,256]{1,0:T(8,128)(2,1)S(1)}, bf16[256,256]{1,0:T(8,128)(2,1)S(1)}, u32[]{:S(2)}, u32[]{:S(2)}) %collective-permute-start.14) | collective-permute-done | bytes 131104 | tf_op jit(solution)/shard_map/ppermute | solution.py:605
  139.5 1.2 copy-done.5
  140.7 0.9 copy-done.9
  141.7 0.9 copy-done.14
  142.7 0.9 copy-done.16
  143.6 0.9 copy-done.18
  144.6 0.9 copy-done.20
  145.5 1.3 project.1
  146.8 1.0 copy-done.2
  147.8 1.5 collective-permute-done.16.taken_ref
  149.4 1.2 copy-done.3
  150.6 1.3 finish.1
  (45 shorter events, 0.1 us)
Async XLA Ops:
  7.2 1.6 %copy-start = (bf16[512,2048]{1,0:T(8,128)(2,1)S(1)}, bf16[512,2048]{1,0:T(8,128)(2,1)}, u32[]{:S(2)}) copy-start(bf16[512,2048]{1,0:T(8,128)(2,1)} %param.15) | copy-start | bytes 6291460
  7.2 15.6 %copy-start.4 = (bf16[256,2048]{1,0:T(8,128)(2,1)S(1)}, bf16[256,2048]{1,0:T(8,128)(2,1)}, u32[]{:S(2)}) copy-start(bf16[256,2048]{1,0:T(8,128)(2,1)} %refs_1_.1) | copy-start | bytes 3145732
  8.8 17.9 %copy-start.21 = (s32[2,16384]{1,0:T(2,128)S(1)}, s32[2,16384]{1,0:T(2,128)}, u32[]{:S(2)}) copy-start(s32[2,16384]{1,0:T(2,128)} %perms_ref.1) | copy-start | bytes 393220
  8.8 0.7 copy-start.22
  10.7 0.8 copy-start.7
  11.5 28.9 %all-to-all-start = ((bf16[32,16,512]{2,1,0:T(8,128)(2,1)}), bf16[32,16,512]{2,1,0:T(8,128)(2,1)}, u32[]{:S(2)}, u32[]{:S(2)}) async-start(bf16[32,16,512]{2,1,0:T(8,128)(2,1)} %bitcast.11), calls=%async_computation | async-start | bytes 1048576 | tf_op jit(solution)/shard_map/all_to_all | solution.py:596
  23.6 11.9 %collective-permute-start.1 = (bf16[256,512]{1,0:T(8,128)(2,1)}, bf16[256,512]{1,0:T(8,128)(2,1)S(1)}, u32[]{:S(2)}, u32[]{:S(2)}) collective-permute-start(bf16[256,512]{1,0:T(8,128)(2,1)} %get-tuple-element.52), channel_id=1, source_target_pairs={{0,6},{1,7},{2,0},{3,1},{4,2},{5,3},{6,4},{7,5},{8,14},{9,15},{10,... | collective-permute-start | bytes 786440 | tf_op jit(solution)/shard_map/ppermute | solution.py:605
  26.6 9.6 %collective-permute-start = (bf16[256,512]{1,0:T(8,128)(2,1)}, bf16[256,512]{1,0:T(8,128)(2,1)S(1)}, u32[]{:S(2)}, u32[]{:S(2)}) collective-permute-start(bf16[256,512]{1,0:T(8,128)(2,1)} %get-tuple-element.53), channel_id=1, source_target_pairs={{0,2},{1,3},{2,4},{3,5},{4,6},{5,7},{6,0},{7,1},{8,10},{9,11},{10,... | collective-permute-start | bytes 786440 | tf_op jit(solution)/shard_map/ppermute | solution.py:605
  26.6 1.6 %copy-start.10 = (bf16[512,2048]{1,0:T(8,128)(2,1)S(1)}, bf16[512,2048]{1,0:T(8,128)(2,1)}, u32[]{:S(2)}) copy-start(bf16[512,2048]{1,0:T(8,128)(2,1)} %x_ref.1) | copy-start | bytes 6291460
  28.2 1.2 copy-start.11
  29.4 1.2 copy-start.12
  35.5 0.7 copy-start.13
  36.2 0.7 copy-start.15
  40.4 30.5 %collective-permute-start.6 = (bf16[2,2048,256]{2,1,0:T(8,128)(2,1)}, bf16[2,2048,256]{2,1,0:T(8,128)(2,1)}, u32[]{:S(2)}, u32[]{:S(2)}) collective-permute-start(bf16[2,2048,256]{2,1,0:T(8,128)(2,1)} %refs_5_.1), channel_id=1, source_target_pairs={{0,1},{1,0},{2,3},{3,2},{4,5},{5,4},{6,7},{7,6},{8,9},{9,8},{10,11... | collective-permute-start | bytes 6291464 | tf_op jit(solution)/shard_map/ppermute | solution.py:650
  40.4 30.5 %collective-permute-start.7 = (bf16[2,2048,256]{2,1,0:T(8,128)(2,1)}, bf16[2,2048,256]{2,1,0:T(8,128)(2,1)}, u32[]{:S(2)}, u32[]{:S(2)}) collective-permute-start(bf16[2,2048,256]{2,1,0:T(8,128)(2,1)} %refs_6_.1), channel_id=1, source_target_pairs={{0,1},{1,0},{2,3},{3,2},{4,5},{5,4},{6,7},{7,6},{8,9},{9,8},{10,11... | collective-permute-start | bytes 6291464 | tf_op jit(solution)/shard_map/ppermute | solution.py:650
  40.9 30.0 %collective-permute-start.8 = (bf16[2,256,2048]{2,1,0:T(8,128)(2,1)}, bf16[2,256,2048]{2,1,0:T(8,128)(2,1)}, u32[]{:S(2)}, u32[]{:S(2)}) collective-permute-start(bf16[2,256,2048]{2,1,0:T(8,128)(2,1)} %refs_7_.1), channel_id=1, source_target_pairs={{0,1},{1,0},{2,3},{3,2},{4,5},{5,4},{6,7},{7,6},{8,9},{9,8},{10,11... | collective-permute-start | bytes 6291464 | tf_op jit(solution)/shard_map/ppermute | solution.py:650
  40.9 15.2 %collective-permute-start.3 = (bf16[32,16,512]{2,1,0:T(8,128)(2,1)}, bf16[32,16,512]{2,1,0:T(8,128)(2,1)}, u32[]{:S(2)}, u32[]{:S(2)}) collective-permute-start(bf16[32,16,512]{2,1,0:T(8,128)(2,1)} %all-to-all-done.refs_0_), channel_id=1, source_target_pairs={{0,6},{1,7},{2,0},{3,1},{4,2},{5,3},{6,4},{7,5},{8,14},{9,15},{10,... | collective-permute-start | bytes 1572872 | tf_op jit(solution)/shard_map/ppermute | solution.py:605
  43.9 16.9 %collective-permute-start.2 = (bf16[32,16,512]{2,1,0:T(8,128)(2,1)}, bf16[32,16,512]{2,1,0:T(8,128)(2,1)}, u32[]{:S(2)}, u32[]{:S(2)}) collective-permute-start(bf16[32,16,512]{2,1,0:T(8,128)(2,1)} %all-to-all-done.refs_0_), channel_id=1, source_target_pairs={{0,2},{1,3},{2,4},{3,5},{4,6},{5,7},{6,0},{7,1},{8,10},{9,11},{10,... | collective-permute-start | bytes 1572872 | tf_op jit(solution)/shard_map/ppermute | solution.py:605
  43.9 36.2 %all-to-all-start.1 = ((bf16[32,32,512]{2,1,0:T(8,128)(2,1)}), bf16[32,32,512]{2,1,0:T(8,128)(2,1)S(1)}, u32[]{:S(2)}, u32[]{:S(2)}) async-start(bf16[32,32,512]{2,1,0:T(8,128)(2,1)} %bitcast.6), calls=%async_computation.2 | async-start | bytes 2097152 | tf_op jit(solution)/shard_map/all_to_all | solution.py:596
  50.4 62.9 %reduce-scatter.2.cloned.1.call-start = ((), (), s32[]{:S(2)}) async-start(), calls=%async_computation.5 | async-start | bytes 2621440 | tf_op jit(solution)/shard_map/reduce_scatter | solution.py:656
  57.0 9.2 %collective-permute-start.5 = (bf16[16,16,512]{2,1,0:T(8,128)(2,1)S(1)}, bf16[16,16,512]{2,1,0:T(8,128)(2,1)S(1)}, u32[]{:S(2)}, u32[]{:S(2)}) collective-permute-start(bf16[16,16,512]{2,1,0:T(8,128)(2,1)S(1)} %slice.17), channel_id=1, source_target_pairs={{0,6},{1,7},{2,0},{3,1},{4,2},{5,3},{6,4},{7,5},{8,14},{9,15},{10,... | collective-permute-start | bytes 786440 | tf_op jit(solution)/shard_map/ppermute | solution.py:605
  61.8 9.1 %collective-permute-start.4 = (bf16[16,16,512]{2,1,0:T(8,128)(2,1)S(1)}, bf16[16,16,512]{2,1,0:T(8,128)(2,1)S(1)}, u32[]{:S(2)}, u32[]{:S(2)}) collective-permute-start(bf16[16,16,512]{2,1,0:T(8,128)(2,1)S(1)} %slice.16), channel_id=1, source_target_pairs={{0,2},{1,3},{2,4},{3,5},{4,6},{5,7},{6,0},{7,1},{8,10},{9,11},{10,... | collective-permute-start | bytes 786440 | tf_op jit(solution)/shard_map/ppermute | solution.py:605
  78.7 1.3 copy-start.1
  81.8 5.0 %collective-permute-start.9 = (bf16[2,64,512]{2,1,0:T(8,128)(2,1)S(1)}, bf16[2,64,512]{2,1,0:T(8,128)(2,1)S(1)}, u32[]{:S(2)}, u32[]{:S(2)}) collective-permute-start(bf16[2,64,512]{2,1,0:T(8,128)(2,1)S(1)} %get-tuple-element.39), channel_id=1, source_target_pairs={{0,8},{8,16},{16,24},{24,32},{32,40},{40,48},{48,56},{56,64},{64,7... | collective-permute-start | bytes 393224 | tf_op jit(solution)/shard_map/ppermute | solution.py:663
  89.4 27.9 %all-to-all-start.2 = ((bf16[32,72,128]{2,1,0:T(8,128)(2,1)}), bf16[32,72,128]{2,1,0:T(8,128)(2,1)S(1)}, u32[]{:S(2)}, u32[]{:S(2)}) async-start(bf16[32,72,128]{2,1,0:T(8,128)(2,1)} %attend_first.1), calls=%async_computation.3 | async-start | bytes 1179648 | tf_op jit(solution)/shard_map/all_to_all | solution.py:596
  98.1 14.5 %collective-permute-start.10 = (bf16[256,512]{1,0:T(8,128)(2,1)S(1)}, bf16[256,512]{1,0:T(8,128)(2,1)S(1)}, u32[]{:S(2)}, u32[]{:S(2)}) collective-permute-start(bf16[256,512]{1,0:T(8,128)(2,1)S(1)} %constant_dynamic-slice_fusion), channel_id=1, source_target_pairs={{0,4},{1,5},{2,6},{3,7},{4,0},{5,1},{6,2},{7,3},{8,12},{9,13},{10,... | collective-permute-start | bytes 786440 | tf_op jit(solution)/shard_map/ppermute | solution.py:605
  112.6 0.7 copy-start.17
  113.3 2.1 %collective-permute-start.11 = (bf16[2,32,16,256]{3,2,1,0:T(8,128)(2,1)}, bf16[2,32,16,256]{3,2,1,0:T(8,128)(2,1)S(1)}, u32[]{:S(2)}, u32[]{:S(2)}) collective-permute-start(bf16[2,32,16,256]{3,2,1,0:T(8,128)(2,1)} %bitcast.9), channel_id=1, source_target_pairs={{0,1},{1,0},{2,3},{3,2},{4,5},{5,4},{6,7},{7,6},{8,9},{9,8},{10,11... | collective-permute-start | bytes 1572872 | tf_op jit(solution)/shard_map/ppermute | solution.py:670
  115.4 1.0 copy-start.6
  118.4 21.1 %copy-start.19 = (bf16[512,256]{1,0:T(8,128)(2,1)}, bf16[512,256]{1,0:T(8,128)(2,1)S(1)}, u32[]{:S(2)}) copy-start(bf16[512,256]{1,0:T(8,128)(2,1)S(1)} %combine.1.own_ref) | copy-start | bytes 786436
  118.4 12.4 %collective-permute-start.13 = (bf16[512,256]{1,0:T(8,128)(2,1)S(1)}, bf16[512,256]{1,0:T(8,128)(2,1)S(1)}, u32[]{:S(2)}, u32[]{:S(2)}) collective-permute-start(bf16[512,256]{1,0:T(8,128)(2,1)S(1)} %combine.1.own_ref), channel_id=1, source_target_pairs={{0,6},{1,7},{2,0},{3,1},{4,2},{5,3},{6,4},{7,5},{8,14},{9,15},{10,... | collective-permute-start | bytes 786440 | tf_op jit(solution)/shard_map/ppermute | solution.py:605
  119.8 13.4 %collective-permute-start.12 = (bf16[512,256]{1,0:T(8,128)(2,1)S(1)}, bf16[512,256]{1,0:T(8,128)(2,1)S(1)}, u32[]{:S(2)}, u32[]{:S(2)}) collective-permute-start(bf16[512,256]{1,0:T(8,128)(2,1)S(1)} %combine.1.own_ref), channel_id=1, source_target_pairs={{0,2},{1,3},{2,4},{3,5},{4,6},{5,7},{6,0},{7,1},{8,10},{9,11},{10,... | collective-permute-start | bytes 786440 | tf_op jit(solution)/shard_map/ppermute | solution.py:605
  120.7 28.7 %all-to-all-start.3 = ((bf16[32,2,16,256]{3,2,1,0:T(8,128)(2,1)}), bf16[32,2,16,256]{3,2,1,0:T(8,128)(2,1)S(1)}, u32[]{:S(2)}, u32[]{:S(2)}) async-start(bf16[32,2,16,256]{3,2,1,0:T(8,128)(2,1)} %place_rows.1), calls=%async_computation.4 | async-start | bytes 1048576 | tf_op jit(solution)/shard_map/all_to_all | solution.py:596
  130.8 5.0 %collective-permute-start.15 = (bf16[256,256]{1,0:T(8,128)(2,1)S(1)}, bf16[256,256]{1,0:T(8,128)(2,1)S(1)}, u32[]{:S(2)}, u32[]{:S(2)}) collective-permute-start(bf16[256,256]{1,0:T(8,128)(2,1)S(1)} %slice.19), channel_id=1, source_target_pairs={{0,6},{1,7},{2,0},{3,1},{4,2},{5,3},{6,4},{7,5},{8,14},{9,15},{10,... | collective-permute-start | bytes 393224 | tf_op jit(solution)/shard_map/ppermute | solution.py:605
  133.2 6.3 %copy-start.8 = (bf16[512,256]{1,0:T(8,128)(2,1)}, bf16[512,256]{1,0:T(8,128)(2,1)S(1)}, u32[]{:S(2)}) copy-start(bf16[512,256]{1,0:T(8,128)(2,1)S(1)} %collective-permute-done.12.prev_ref) | copy-start | bytes 786436
  133.3 6.3 %collective-permute-start.14 = (bf16[256,256]{1,0:T(8,128)(2,1)S(1)}, bf16[256,256]{1,0:T(8,128)(2,1)S(1)}, u32[]{:S(2)}, u32[]{:S(2)}) collective-permute-start(bf16[256,256]{1,0:T(8,128)(2,1)S(1)} %slice.18), channel_id=1, source_target_pairs={{0,2},{1,3},{2,4},{3,5},{4,6},{5,7},{6,0},{7,1},{8,10},{9,11},{10,... | collective-permute-start | bytes 393224 | tf_op jit(solution)/shard_map/ppermute | solution.py:605
  139.5 1.2 copy-start.5
  140.7 0.9 copy-start.9
  141.7 0.9 copy-start.14
  142.6 0.9 copy-start.16
  143.6 0.9 copy-start.18
  144.5 0.9 copy-start.20
  146.8 1.0 copy-start.2
  147.8 1.5 collective-permute-start.16
  149.4 1.2 copy-start.3
Sparse Core Ops, SparseCore 0:
  80.2 32.6 reduce-scatter.1

commit v12 on v11

--- a/solution.py
+++ b/solution.py
@@ -236,7 +236,7 @@
         grid_spec=pltpu.PrefetchScalarGridSpec(
             num_scalar_prefetch=1,
             grid=(len(shards) + 1,),
-            in_specs=[pl.BlockSpec(memory_space=pltpu.VMEM)] * 5
+            in_specs=[pl.BlockSpec(x.shape, lambda i, e: (0, 0, 0)) for x in (*shards, *far)]
             + [own_up, own_up, own_down] * 2,
             out_specs=pl.BlockSpec(out, lambda i, e: (0, 0, 0, 0, 0)),
             scratch_shapes=[pltpu.VMEM((4, rows, hidden), F32)],
@@ -273,13 +273,16 @@
     )(rows, taken)
 
 
-def finish_kernel(back_ref, pick_ref, kept_ref, taken_ref, attended_ref, mixed_ref):
-    mixed_ref[...] = dot(pick_ref[...], back_ref[...]).astype(BF16)
+def finish_kernel(back_ref, slot_ref, kept_ref, taken_ref, attended_ref, mixed_ref):
+    length = mixed_ref.shape[0]
+    column = to_col(slot_ref[:1, :].astype(F32)).astype(I32)
+    pick = flag(column == iota((length, back_ref.shape[0]), 1))
+    mixed_ref[...] = dot(pick, back_ref[...]).astype(BF16)
     attended_ref[...] = (kept_ref[...] + taken_ref[...].astype(F32)).astype(BF16)
 
 
-def finish(back, pick, kept, taken):
-    length, width = pick.shape[0], back.shape[1]
+def finish(back, slot, kept, taken):
+    length, width = slot.shape[1], back.shape[1]
     return pl.pallas_call(
         finish_kernel,
         out_shape=[
@@ -289,7 +292,7 @@
         cost_estimate=cost(2 * length * back.shape[0] * width, 1 << 20),
         compiler_params=BIG,
         name="finish",
-    )(back, pick, kept, taken)
+    )(back, slot, kept, taken)
 
 
 def sort_rows_kernel(peers, perms_ref, arrived_ref, rows_ref, last_ref, slot_ref):
@@ -544,9 +547,7 @@
 
 
 def project_kernel(where_ref, own_ref, prev_ref, next_ref, far_a_ref, far_b_ref, *refs):
-    slot_ref, weights, (kept_ref, given_ref, pick_ref) = refs[0], refs[1:-3], refs[-3:]
-    column = to_col(slot_ref[:1, :].astype(F32)).astype(I32)
-    pick_ref[...] = flag(column == iota(pick_ref.shape, 1))
+    weights, (kept_ref, given_ref) = refs[:-2], refs[-2:]
     far = jnp.concatenate([far_a_ref[...], far_b_ref[...]], axis=0)
     total = dot(own_ref[...], weights[0][...]) + dot(prev_ref[...], weights[1][...])
     total = total + dot(next_ref[...], weights[2][...]) + dot(far, weights[3][...])
@@ -560,36 +561,34 @@
             given_ref[...] = total[:, other * half : (other + 1) * half].astype(BF16)
 
 
-def project(where, heads, w_out, others, slot, slots):
+def project(where, heads, w_out, others):
     length, span = heads[0].shape
     columns = others[0].shape[1]
     half = columns // EXP_DEV
     weights = (w_out, *others)
-    shapes = [x.shape for x in (*heads, slot)] + [(span, columns)] + [x.shape for x in others]
+    shapes = [x.shape for x in heads] + [(span, columns)] + [x.shape for x in others]
 
     def first(i, e):
         return (0, 0)
 
     specs = [pl.BlockSpec(shape, first) for shape in shapes]
-    specs[len(heads) + 1] = pl.BlockSpec((span, columns), lambda i, e: (0, e[0]))
+    specs[len(heads)] = pl.BlockSpec((span, columns), lambda i, e: (0, e[0]))
     return pl.pallas_call(
         project_kernel,
         grid_spec=pltpu.PrefetchScalarGridSpec(
             num_scalar_prefetch=1,
             grid=(1,),
             in_specs=specs,
-            out_specs=[pl.BlockSpec((length, half), first)] * 2
-            + [pl.BlockSpec((slot.shape[1], slots), first)],
+            out_specs=[pl.BlockSpec((length, half), first)] * 2,
         ),
         out_shape=[
             jax.ShapeDtypeStruct((length, half), F32),
             jax.ShapeDtypeStruct((length, half), BF16),
-            jax.ShapeDtypeStruct((slot.shape[1], slots), BF16),
         ],
         cost_estimate=cost(55 * 10**8, 3 << 20),
         compiler_params=BIG,
         name="project",
-    )(where, *heads, slot, *weights)
+    )(where, *heads, *weights)
 
 
 def exchange(x, axis):
@@ -650,8 +649,9 @@
     sibling = [lax.ppermute(after(weight, received), "exp", siblings) for weight in own]
     shards, far_shards = spread(received, chips)
     arrived = exchange(outgoing.reshape(peers, rounds * per_peer, outgoing.shape[1]), "seq")
+    far = columns_of(2, *far_shards)
     expert_part = run_experts(where, shards, far_shards, own, sibling)
-    arrived = after(arrived, expert_part)
+    arrived = after(arrived, expert_part, far)
     rows, last, row_slot = sort_rows(order, arrived)
     expert_rows = lax.psum_scatter(
         expert_part,
@@ -665,22 +665,18 @@
     last = after(last, later)
     packed = attend_first(order, earlier, rows, last, row_slot, later, peers)
     got = exchange(packed, "seq")
-    far = columns_of(2, packed)
-    expert_rows = after(expert_rows, packed, far)
+    expert_rows = after(expert_rows, packed)
     taken = lax.ppermute(expert_rows, "exp", siblings)
     expert_rows = place_rows(expert_rows, taken)
     mixed_heads = combine(after(got, expert_rows), slot_token, w_qk.shape[1])
     expert_back = exchange(after(expert_rows, mixed_heads), "seq")
     heads, far_heads = spread(mixed_heads, chips)
-    slots = peers * EXP_DEV * capacity
-    attn_kept, attn_given, token_pick = project(
-        where, (*heads, *far_heads), w_out, (*near, far), token_slot, slots
-    )
+    attn_kept, attn_given = project(where, (*heads, *far_heads), w_out, (*near, far))
     attn_taken = lax.ppermute(attn_given, "exp", siblings)
     expert_back = after(expert_back, attn_taken)
     return finish(
-        expert_back.reshape(slots, width // parts),
-        token_pick,
+        expert_back.reshape(peers * EXP_DEV * capacity, width // parts),
+        token_slot,
         attn_kept,
         attn_taken,
     )

time: 161 us -> 160 us (level)
  waiting for transfers between devices: 42.8 us -> 36.3 us
  starting transfers between devices: 51.7 us -> 54.9 us
  local copies, waits for them, and re-layouts: 23.4 us -> 26.2 us
    ppermute x11, waiting for transfers between devices: 34.9 us -> 13.9 us  [hop(): return lax.ppermute(x, 'exp', pairs)]
    reduce_scatter x1, waiting for transfers between devices: 0.01 us -> 12.4 us  [body(): lax.psum_scatter(expert_part, 'exp', scatter_dimension=0, tiled=False, ax...]
    ppermute x11, starting transfers between devices: 15.2 us -> 18.8 us  [hop(): return lax.ppermute(x, 'exp', pairs)]
    all_to_all x4, waiting for transfers between devices: 3.53 us -> 5.69 us  [exchange(): return lax.all_to_all(x, axis, split_axis=0, concat_axis=0, tiled=True)]
    unnamed x46 -> x48, local copies, waits for them, and re-layouts: 19.6 us -> 19.5 us
  transfers between devices with their start and end apart: 22 -> 22, of which waited for: 10 -> 11; matrix products, arithmetic and copies ran while one was open for 2% -> 4% of each run, Pallas kernels for 14% -> 14%
where the time goes in v12:
time: 160 us; the launch traced here: 159 us
  starting transfers between devices  54.9 us (34%)
  waiting for transfers between devices  36.3 us (23%)
  Pallas kernels  26.7 us (17%)
  local copies, waits for them, and re-layouts  26.2 us (16%)
  between operations  14.4 us (9%)
    all_to_all x4, starting transfers between devices, exchange(): return lax.all_to_all(x, axis, split_axis=0, concat_axis=0, tiled=True)  35 us
    unnamed x48, local copies, waits for them, and re-layouts  19.5 us
    ppermute x11, starting transfers between devices, hop(): return lax.ppermute(x, 'exp', pairs)  18.8 us
    ppermute x11, waiting for transfers between devices, hop(): return lax.ppermute(x, 'exp', pairs)  13.9 us
    reduce_scatter x1, waiting for transfers between devices, body(): lax.psum_scatter(expert_part, 'exp', scatter_dimension=0, tiled=False, ax...  12.4 us
    pallas_call x1, Pallas kernels, run_experts(): pl.pallas_call(experts_kernel, grid_spec=pltpu.PrefetchScalarGridSpec(num...  7.86 us
    all_to_all x4, waiting for transfers between devices, exchange(): return lax.all_to_all(x, axis, split_axis=0, concat_axis=0, tiled=True)  5.69 us
    pallas_call x1, Pallas kernels, pack_rows(): pl.pallas_call(pack_rows_kernel, grid_spec=pltpu.PrefetchScalarGridSpec(n...  4.8 us
  transfers between devices with their start and end apart: 22, of which 11 were waited for; matrix products, arithmetic and copies ran while one was open for 4% of the time, Pallas kernels for 14%

profile of v12, /device:TPU:32, one launch (start us, length us, event | category | flops | bytes accessed | tf_op | source)
XLA Modules:
  0.0 158.6 jit_solution(8299279233381605380)
XLA Ops:
  7.2 1.5 copy-done
  8.8 0.8 constant_dynamic-slice_fusion.3.tokens_ref
  9.6 0.1 pad_add_fusion.where_ref
  9.7 1.0 copy-done.6
  10.7 0.7 copy-done.23
  11.4 1.2 pack_tokens.1
  12.6 0.8 copy-done.5
  13.4 11.2 %all-to-all-start = ((bf16[32,16,512]{2,1,0:T(8,128)(2,1)}), bf16[32,16,512]{2,1,0:T(8,128)(2,1)}, u32[]{:S(2)}, u32[]{:S(2)}) async-start(bf16[32,16,512]{2,1,0:T(8,128)(2,1)} %bitcast.11), calls=%async_computation | async-start | bytes 1048576 | tf_op jit(solution)/shard_map/all_to_all | solution.py:595
  24.7 0.8 constant_dynamic-slice_fusion.1
  25.5 1.6 collective-permute-start
  27.1 1.7 %collective-permute-start.1 = (bf16[256,512]{1,0:T(8,128)(2,1)}, bf16[256,512]{1,0:T(8,128)(2,1)S(1)}, u32[]{:S(2)}, u32[]{:S(2)}) collective-permute-start(bf16[256,512]{1,0:T(8,128)(2,1)} %get-tuple-element.50), channel_id=1, source_target_pairs={{0,6},{1,7},{2,0},{3,1},{4,2},{5,3},{6,4},{7,5},{8,14},{9,15},{10,... | collective-permute-start | bytes 786440 | tf_op jit(solution)/shard_map/ppermute | solution.py:604
  28.8 1.6 %copy-done.9 = bf16[512,2048]{1,0:T(8,128)(2,1)S(1)} copy-done((bf16[512,2048]{1,0:T(8,128)(2,1)S(1)}, bf16[512,2048]{1,0:T(8,128)(2,1)}, u32[]{:S(2)}) %copy-start.9) | copy-done | bytes 2097176
  30.4 1.2 copy-done.10
  31.6 1.2 copy-done.11
  32.8 4.8 %pack_rows.1 = (bf16[1024,512]{1,0:T(8,128)(2,1)}, s32[2,8,512]{2,1,0:T(8,128)S(1)}, s32[2,512]{1,0:T(2,128)S(1)}, s32[2,128]{1,0:T(2,128)S(1)}) custom-call(s32[1]{0:T(128)} %bitcast.4.me_ref, s32[2,16384]{1,0:T(2,128)S(1)} %copy-done.22, bf16[512,2048]{1,0:T(8,128)(2,1)S(1)} %copy-done.9, bf16[2048,256]{1,0:T(8,128)(2,1)S(1)} %copy-done.10, ...), custom_call_target="tpu_custom_call" | custom-call | flops 1610612736 | bytes 6291456 | tf_op jit(solution)/shard_map/pack_rows/pallas_call | solution.py:105
  37.6 0.7 copy-done.12
  38.3 0.7 copy-done.14
  39.0 3.3 %all-to-all-done.refs_0_ = bf16[32,16,512]{2,1,0:T(8,128)(2,1)} async-done(((bf16[32,16,512]{2,1,0:T(8,128)(2,1)}), bf16[32,16,512]{2,1,0:T(8,128)(2,1)}, u32[]{:S(2)}, u32[]{:S(2)}) %all-to-all-start) | async-done | bytes 524320 | tf_op jit(solution)/shard_map/all_to_all | solution.py:595
  42.3 0.5 collective-permute-start.7
  42.8 1.6 collective-permute-start.2
  44.4 1.7 %collective-permute-start.3 = (bf16[32,16,512]{2,1,0:T(8,128)(2,1)}, bf16[32,16,512]{2,1,0:T(8,128)(2,1)}, u32[]{:S(2)}, u32[]{:S(2)}) collective-permute-start(bf16[32,16,512]{2,1,0:T(8,128)(2,1)} %all-to-all-done.refs_0_), channel_id=1, source_target_pairs={{0,6},{1,7},{2,0},{3,1},{4,2},{5,3},{6,4},{7,5},{8,14},{9,15},{10,... | collective-permute-start | bytes 1572872 | tf_op jit(solution)/shard_map/ppermute | solution.py:604
  46.1 6.5 %all-to-all-start.1 = ((bf16[32,32,512]{2,1,0:T(8,128)(2,1)}), bf16[32,32,512]{2,1,0:T(8,128)(2,1)S(1)}, u32[]{:S(2)}, u32[]{:S(2)}) async-start(bf16[32,32,512]{2,1,0:T(8,128)(2,1)} %bitcast.6), calls=%async_computation.2 | async-start | bytes 2097152 | tf_op jit(solution)/shard_map/all_to_all | solution.py:595
  52.6 6.1 %collective-permute-done.2.refs_1_ = bf16[32,16,512]{2,1,0:T(8,128)(2,1)} collective-permute-done((bf16[32,16,512]{2,1,0:T(8,128)(2,1)}, bf16[32,16,512]{2,1,0:T(8,128)(2,1)}, u32[]{:S(2)}, u32[]{:S(2)}) %collective-permute-start.2) | collective-permute-done | bytes 524320 | tf_op jit(solution)/shard_map/ppermute | solution.py:604
  58.7 1.7 %slice.16 = bf16[16,16,512]{2,1,0:T(8,128)(2,1)} slice(bf16[32,16,512]{2,1,0:T(8,128)(2,1)} %collective-permute-done.2.refs_1_), slice={[0:16], [0:16], [0:512]} | slice | bytes 524288 | tf_op jit(solution)/shard_map/slice | solution.py:611
  60.4 0.3 collective-permute-start.4
  60.7 1.7 %slice.17 = bf16[16,16,512]{2,1,0:T(8,128)(2,1)} slice(bf16[32,16,512]{2,1,0:T(8,128)(2,1)} %collective-permute-done.3.refs_2_), slice={[16:32], [0:16], [0:512]} | slice | bytes 524288 | tf_op jit(solution)/shard_map/slice | solution.py:611
  62.4 2.9 %collective-permute-start.5 = (bf16[16,16,512]{2,1,0:T(8,128)(2,1)}, bf16[16,16,512]{2,1,0:T(8,128)(2,1)}, u32[]{:S(2)}, u32[]{:S(2)}) collective-permute-start(bf16[16,16,512]{2,1,0:T(8,128)(2,1)} %slice.17), channel_id=1, source_target_pairs={{0,6},{1,7},{2,0},{3,1},{4,2},{5,3},{6,4},{7,5},{8,14},{9,15},{10,... | collective-permute-start | bytes 786440 | tf_op jit(solution)/shard_map/ppermute | solution.py:604
  65.3 4.5 %collective-permute-done.4.refs_3_ = bf16[16,16,512]{2,1,0:T(8,128)(2,1)S(1)} collective-permute-done((bf16[16,16,512]{2,1,0:T(8,128)(2,1)}, bf16[16,16,512]{2,1,0:T(8,128)(2,1)S(1)}, u32[]{:S(2)}, u32[]{:S(2)}) %collective-permute-start.4) | collective-permute-done | bytes 262176 | tf_op jit(solution)/shard_map/ppermute | solution.py:604
  69.8 0.7 copy-done.18
  70.5 0.3 collective-permute-done.5.refs_4_
  70.9 1.7 %constant_dynamic-slice_fusion = bf16[256,512]{1,0:T(8,128)(2,1)} fusion(bf16[256,2048]{1,0:T(8,128)(2,1)} %refs_0_.1, s32[]{:T(128)S(6)} %select_n.43), kind=kLoop, calls=%fused_computation | loop fusion | bytes 524292 | tf_op jit(solution)/shard_map/dynamic_slice | solution.py:643
  72.6 2.4 %collective-permute-start.9 = (bf16[256,512]{1,0:T(8,128)(2,1)}, bf16[256,512]{1,0:T(8,128)(2,1)S(1)}, u32[]{:S(2)}, u32[]{:S(2)}) collective-permute-start(bf16[256,512]{1,0:T(8,128)(2,1)} %constant_dynamic-slice_fusion), channel_id=1, source_target_pairs={{0,4},{1,5},{2,6},{3,7},{4,0},{5,1},{6,2},{7,3},{8,12},{9,13},{10,... | collective-permute-start | bytes 786440 | tf_op jit(solution)/shard_map/ppermute | solution.py:604
  75.0 0.9 copy-done.19
  75.9 7.9 %experts.1 = bf16[4,2,32,16,256]{4,3,2,1,0:T(8,128)(2,1)S(1)} custom-call(s32[2]{0:T(128)S(1)} %pad_add_fusion.where_ref, bf16[32,16,512]{2,1,0:T(8,128)(2,1)} %all-to-all-done.refs_0_, bf16[32,16,512]{2,1,0:T(8,128)(2,1)} %collective-permute-done.2.refs_1_, bf16[32,16,512]{2,1,0:T(8,128)(2,1)} %collective-permute-done.3.refs_2_, ...), custom_call_target="tpu_custom_call" | custom-call | flops 15000000512 | bytes 10485760 | tf_op jit(solution)/shard_map/experts/pallas_call | solution.py:234
  83.8 1.3 copy-done.1
  85.2 1.7 %sort_rows.1 = (bf16[2,512,512]{2,1,0:T(8,128)(2,1)S(1)}, bf16[2,64,512]{2,1,0:T(8,128)(2,1)S(1)}, s32[2,8,512]{2,1,0:T(8,128)S(1)}) custom-call(s32[2,512]{1,0:T(2,128)S(1)} %get-tuple-element.33.perms_ref, bf16[32,32,512]{2,1,0:T(8,128)(2,1)S(1)} %all-to-all-done.1.arrived_ref), custom_call_target="tpu_custom_call" | custom-call | flops 34359738368 | bytes 4194304 | tf_op jit(solution)/shard_map/sort_rows/pallas_call | solution.py:318
  86.9 0.5 collective-permute-start.10
  87.4 3.9 %attend_later.1.later_ref = bf16[2,512,384]{2,1,0:T(8,128)(2,1)S(1)} custom-call(s32[2,512]{1,0:T(2,128)S(1)} %get-tuple-element.33.perms_ref, bf16[2,512,512]{2,1,0:T(8,128)(2,1)S(1)} %get-tuple-element.38.rows_ref, s32[2,8,512]{2,1,0:T(8,128)S(1)} %get-tuple-element.40.slot_ref), custom_call_target="tpu_custom_call" | custom-call | flops 34359738368 | bytes 4194304 | tf_op jit(solution)/shard_map/attend_later/pallas_call | solution.py:464
  91.3 0.7 collective-permute-done.10.last_ref
  91.9 2.5 %attend_first.1 = bf16[32,72,128]{2,1,0:T(8,128)(2,1)} custom-call(s32[2,512]{1,0:T(2,128)S(1)} %get-tuple-element.33.perms_ref, s32[2,128]{1,0:T(2,128)S(1)} %get-tuple-element.34.earlier_ref, bf16[2,512,512]{2,1,0:T(8,128)(2,1)S(1)} %get-tuple-element.38.rows_ref, bf16[2,64,512]{2,1,0:T(8,128)(2,1)S(1)} %collective-permute-done.10.last_ref, ...), custom_call_target="tpu_custom_call" | custom-call | flops 34359738368 | bytes 4194304 | tf_op jit(solution)/shard_map/attend_first/pallas_call | solution.py:480
  94.4 7.4 %all-to-all-start.2 = ((bf16[32,72,128]{2,1,0:T(8,128)(2,1)}), bf16[32,72,128]{2,1,0:T(8,128)(2,1)S(1)}, u32[]{:S(2)}, u32[]{:S(2)}) async-start(bf16[32,72,128]{2,1,0:T(8,128)(2,1)} %attend_first.1), calls=%async_computation.3 | async-start | bytes 1179648 | tf_op jit(solution)/shard_map/all_to_all | solution.py:595
  101.8 12.4 %reduce-scatter.2.cloned.1.call-done = bf16[1,2,32,16,256]{4,3,2,1,0:T(8,128)(2,1)} async-done(((bf16[4,2,32,16,256]{4,3,2,1,0:T(8,128)(2,1)}), bf16[1,2,32,16,256]{4,3,2,1,0:T(8,128)(2,1)}) %reduce-scatter.2.cloned.1.call-update) | async-done | bytes 524304 | tf_op jit(solution)/shard_map/reduce_scatter | solution.py:656
  114.3 2.1 %collective-permute-done.11.taken_ref = bf16[2,32,16,256]{3,2,1,0:T(8,128)(2,1)S(1)} collective-permute-done((bf16[2,32,16,256]{3,2,1,0:T(8,128)(2,1)}, bf16[2,32,16,256]{3,2,1,0:T(8,128)(2,1)S(1)}, u32[]{:S(2)}, u32[]{:S(2)}) %collective-permute-start.11) | collective-permute-done | bytes 524320 | tf_op jit(solution)/shard_map/ppermute | solution.py:669
  116.4 1.0 copy-done.4
  117.4 0.8 place_rows.1
  118.3 0.2 all-to-all-done.2.got_ref
  118.5 1.1 combine.1.own_ref
  119.6 2.1 %collective-permute-start.12 = (bf16[512,256]{1,0:T(8,128)(2,1)S(1)}, bf16[512,256]{1,0:T(8,128)(2,1)S(1)}, u32[]{:S(2)}, u32[]{:S(2)}) collective-permute-start(bf16[512,256]{1,0:T(8,128)(2,1)S(1)} %combine.1.own_ref), channel_id=1, source_target_pairs={{0,2},{1,3},{2,4},{3,5},{4,6},{5,7},{6,0},{7,1},{8,10},{9,11},{10,... | collective-permute-start | bytes 786440 | tf_op jit(solution)/shard_map/ppermute | solution.py:604
  121.7 1.2 collective-permute-start.13
  122.9 9.9 %all-to-all-start.3 = ((bf16[32,2,16,256]{3,2,1,0:T(8,128)(2,1)}), bf16[32,2,16,256]{3,2,1,0:T(8,128)(2,1)S(1)}, u32[]{:S(2)}, u32[]{:S(2)}) async-start(bf16[32,2,16,256]{3,2,1,0:T(8,128)(2,1)} %place_rows.1), calls=%async_computation.4 | async-start | bytes 1048576 | tf_op jit(solution)/shard_map/all_to_all | solution.py:595
  132.8 0.1 collective-permute-start.14
  132.9 3.3 %collective-permute-start.15 = (bf16[256,256]{1,0:T(8,128)(2,1)S(1)}, bf16[256,256]{1,0:T(8,128)(2,1)S(1)}, u32[]{:S(2)}, u32[]{:S(2)}) collective-permute-start(bf16[256,256]{1,0:T(8,128)(2,1)S(1)} %slice.19), channel_id=1, source_target_pairs={{0,6},{1,7},{2,0},{3,1},{4,2},{5,3},{6,4},{7,5},{8,14},{9,15},{10,... | collective-permute-start | bytes 393224 | tf_op jit(solution)/shard_map/ppermute | solution.py:604
  136.2 2.8 %collective-permute-done.14.far_a_ref = bf16[256,256]{1,0:T(8,128)(2,1)S(1)} collective-permute-done((bf16[256,256]{1,0:T(8,128)(2,1)S(1)}, bf16[256,256]{1,0:T(8,128)(2,1)S(1)}, u32[]{:S(2)}, u32[]{:S(2)}) %collective-permute-start.14) | collective-permute-done | bytes 131104 | tf_op jit(solution)/shard_map/ppermute | solution.py:604
  139.1 1.2 copy-done.3
  140.3 0.9 copy-done.8
  141.3 0.9 copy-done.13
  142.2 0.9 copy-done.15
  143.2 0.9 copy-done.17
  144.1 0.9 copy-done.21
  145.1 1.3 project.1
  146.4 0.1 collective-permute-start.16
  146.5 1.5 collective-permute-done.16.taken_ref
  148.0 2.2 %all-to-all-done.3 = bf16[32,2,16,256]{3,2,1,0:T(8,128)(2,1)S(1)} async-done(((bf16[32,2,16,256]{3,2,1,0:T(8,128)(2,1)}), bf16[32,2,16,256]{3,2,1,0:T(8,128)(2,1)S(1)}, u32[]{:S(2)}, u32[]{:S(2)}) %all-to-all-start.3) | async-done | bytes 524320 | tf_op jit(solution)/shard_map/all_to_all | solution.py:595
  150.2 1.6 finish.1
  (47 shorter events, 0.2 us)
Async XLA Ops:
  7.2 1.6 %copy-start = (bf16[512,2048]{1,0:T(8,128)(2,1)S(1)}, bf16[512,2048]{1,0:T(8,128)(2,1)}, u32[]{:S(2)}) copy-start(bf16[512,2048]{1,0:T(8,128)(2,1)} %param.15) | copy-start | bytes 6291460
  7.2 17.5 %copy-start.2 = (bf16[256,2048]{1,0:T(8,128)(2,1)S(1)}, bf16[256,2048]{1,0:T(8,128)(2,1)}, u32[]{:S(2)}) copy-start(bf16[256,2048]{1,0:T(8,128)(2,1)} %refs_0_.1) | copy-start | bytes 3145732
  9.7 1.0 copy-start.6
  10.7 0.7 copy-start.23
  11.4 17.4 %copy-start.22 = (s32[2,16384]{1,0:T(2,128)S(1)}, s32[2,16384]{1,0:T(2,128)}, u32[]{:S(2)}) copy-start(s32[2,16384]{1,0:T(2,128)} %perms_ref.1) | copy-start | bytes 393220
  12.6 0.8 copy-start.5
  13.4 28.9 %all-to-all-start = ((bf16[32,16,512]{2,1,0:T(8,128)(2,1)}), bf16[32,16,512]{2,1,0:T(8,128)(2,1)}, u32[]{:S(2)}, u32[]{:S(2)}) async-start(bf16[32,16,512]{2,1,0:T(8,128)(2,1)} %bitcast.11), calls=%async_computation | async-start | bytes 1048576 | tf_op jit(solution)/shard_map/all_to_all | solution.py:595
  25.5 12.1 %collective-permute-start = (bf16[256,512]{1,0:T(8,128)(2,1)}, bf16[256,512]{1,0:T(8,128)(2,1)S(1)}, u32[]{:S(2)}, u32[]{:S(2)}) collective-permute-start(bf16[256,512]{1,0:T(8,128)(2,1)} %get-tuple-element.51), channel_id=1, source_target_pairs={{0,2},{1,3},{2,4},{3,5},{4,6},{5,7},{6,0},{7,1},{8,10},{9,11},{10,... | collective-permute-start | bytes 786440 | tf_op jit(solution)/shard_map/ppermute | solution.py:604
  27.1 11.2 %collective-permute-start.1 = (bf16[256,512]{1,0:T(8,128)(2,1)}, bf16[256,512]{1,0:T(8,128)(2,1)S(1)}, u32[]{:S(2)}, u32[]{:S(2)}) collective-permute-start(bf16[256,512]{1,0:T(8,128)(2,1)} %get-tuple-element.50), channel_id=1, source_target_pairs={{0,6},{1,7},{2,0},{3,1},{4,2},{5,3},{6,4},{7,5},{8,14},{9,15},{10,... | collective-permute-start | bytes 786440 | tf_op jit(solution)/shard_map/ppermute | solution.py:604
  28.8 1.6 %copy-start.9 = (bf16[512,2048]{1,0:T(8,128)(2,1)S(1)}, bf16[512,2048]{1,0:T(8,128)(2,1)}, u32[]{:S(2)}) copy-start(bf16[512,2048]{1,0:T(8,128)(2,1)} %x_ref.1) | copy-start | bytes 6291460
  30.3 1.2 copy-start.10
  31.6 1.2 copy-start.11
  37.6 0.7 copy-start.12
  38.3 0.7 copy-start.14
  42.3 32.6 %collective-permute-start.6 = (bf16[2,2048,256]{2,1,0:T(8,128)(2,1)}, bf16[2,2048,256]{2,1,0:T(8,128)(2,1)}, u32[]{:S(2)}, u32[]{:S(2)}) collective-permute-start(bf16[2,2048,256]{2,1,0:T(8,128)(2,1)} %refs_5_.1), channel_id=1, source_target_pairs={{0,1},{1,0},{2,3},{3,2},{4,5},{5,4},{6,7},{7,6},{8,9},{9,8},{10,11... | collective-permute-start | bytes 6291464 | tf_op jit(solution)/shard_map/ppermute | solution.py:649
  42.3 32.6 %collective-permute-start.7 = (bf16[2,2048,256]{2,1,0:T(8,128)(2,1)}, bf16[2,2048,256]{2,1,0:T(8,128)(2,1)}, u32[]{:S(2)}, u32[]{:S(2)}) collective-permute-start(bf16[2,2048,256]{2,1,0:T(8,128)(2,1)} %refs_6_.1), channel_id=1, source_target_pairs={{0,1},{1,0},{2,3},{3,2},{4,5},{5,4},{6,7},{7,6},{8,9},{9,8},{10,11... | collective-permute-start | bytes 6291464 | tf_op jit(solution)/shard_map/ppermute | solution.py:649
  42.8 32.1 %collective-permute-start.8 = (bf16[2,256,2048]{2,1,0:T(8,128)(2,1)}, bf16[2,256,2048]{2,1,0:T(8,128)(2,1)}, u32[]{:S(2)}, u32[]{:S(2)}) collective-permute-start(bf16[2,256,2048]{2,1,0:T(8,128)(2,1)} %refs_7_.1), channel_id=1, source_target_pairs={{0,1},{1,0},{2,3},{3,2},{4,5},{5,4},{6,7},{7,6},{8,9},{9,8},{10,11... | collective-permute-start | bytes 6291464 | tf_op jit(solution)/shard_map/ppermute | solution.py:649
  42.8 15.9 %collective-permute-start.2 = (bf16[32,16,512]{2,1,0:T(8,128)(2,1)}, bf16[32,16,512]{2,1,0:T(8,128)(2,1)}, u32[]{:S(2)}, u32[]{:S(2)}) collective-permute-start(bf16[32,16,512]{2,1,0:T(8,128)(2,1)} %all-to-all-done.refs_0_), channel_id=1, source_target_pairs={{0,2},{1,3},{2,4},{3,5},{4,6},{5,7},{6,0},{7,1},{8,10},{9,11},{10,... | collective-permute-start | bytes 1572872 | tf_op jit(solution)/shard_map/ppermute | solution.py:604
  44.4 16.3 %collective-permute-start.3 = (bf16[32,16,512]{2,1,0:T(8,128)(2,1)}, bf16[32,16,512]{2,1,0:T(8,128)(2,1)}, u32[]{:S(2)}, u32[]{:S(2)}) collective-permute-start(bf16[32,16,512]{2,1,0:T(8,128)(2,1)} %all-to-all-done.refs_0_), channel_id=1, source_target_pairs={{0,6},{1,7},{2,0},{3,1},{4,2},{5,3},{6,4},{7,5},{8,14},{9,15},{10,... | collective-permute-start | bytes 1572872 | tf_op jit(solution)/shard_map/ppermute | solution.py:604
  46.1 39.1 %all-to-all-start.1 = ((bf16[32,32,512]{2,1,0:T(8,128)(2,1)}), bf16[32,32,512]{2,1,0:T(8,128)(2,1)S(1)}, u32[]{:S(2)}, u32[]{:S(2)}) async-start(bf16[32,32,512]{2,1,0:T(8,128)(2,1)} %bitcast.6), calls=%async_computation.2 | async-start | bytes 2097152 | tf_op jit(solution)/shard_map/all_to_all | solution.py:595
  52.5 61.7 %reduce-scatter.2.cloned.1.call-start = ((), (), s32[]{:S(2)}) async-start(), calls=%async_computation.5 | async-start | bytes 2621440 | tf_op jit(solution)/shard_map/reduce_scatter | solution.py:656
  60.4 9.4 %collective-permute-start.4 = (bf16[16,16,512]{2,1,0:T(8,128)(2,1)}, bf16[16,16,512]{2,1,0:T(8,128)(2,1)S(1)}, u32[]{:S(2)}, u32[]{:S(2)}) collective-permute-start(bf16[16,16,512]{2,1,0:T(8,128)(2,1)} %slice.16), channel_id=1, source_target_pairs={{0,2},{1,3},{2,4},{3,5},{4,6},{5,7},{6,0},{7,1},{8,10},{9,11},{10,... | collective-permute-start | bytes 786440 | tf_op jit(solution)/shard_map/ppermute | solution.py:604
  62.4 8.5 %collective-permute-start.5 = (bf16[16,16,512]{2,1,0:T(8,128)(2,1)}, bf16[16,16,512]{2,1,0:T(8,128)(2,1)}, u32[]{:S(2)}, u32[]{:S(2)}) collective-permute-start(bf16[16,16,512]{2,1,0:T(8,128)(2,1)} %slice.17), channel_id=1, source_target_pairs={{0,6},{1,7},{2,0},{3,1},{4,2},{5,3},{6,4},{7,5},{8,14},{9,15},{10,... | collective-permute-start | bytes 786440 | tf_op jit(solution)/shard_map/ppermute | solution.py:604
  69.8 0.7 copy-start.18
  72.6 12.6 %collective-permute-start.9 = (bf16[256,512]{1,0:T(8,128)(2,1)}, bf16[256,512]{1,0:T(8,128)(2,1)S(1)}, u32[]{:S(2)}, u32[]{:S(2)}) collective-permute-start(bf16[256,512]{1,0:T(8,128)(2,1)} %constant_dynamic-slice_fusion), channel_id=1, source_target_pairs={{0,4},{1,5},{2,6},{3,7},{4,0},{5,1},{6,2},{7,3},{8,12},{9,13},{10,... | collective-permute-start | bytes 786440 | tf_op jit(solution)/shard_map/ppermute | solution.py:604
  74.9 1.0 copy-start.19
  83.8 1.3 copy-start.1
  85.1 1.7 %copy-start.16 = (bf16[256,512]{1,0:T(8,128)(2,1)}, bf16[256,512]{1,0:T(8,128)(2,1)S(1)}, u32[]{:S(2)}) copy-start(bf16[256,512]{1,0:T(8,128)(2,1)S(1)} %collective-permute-done.9.refs_3_) | copy-start | bytes 786436
  86.9 5.0 %collective-permute-start.10 = (bf16[2,64,512]{2,1,0:T(8,128)(2,1)S(1)}, bf16[2,64,512]{2,1,0:T(8,128)(2,1)S(1)}, u32[]{:S(2)}, u32[]{:S(2)}) collective-permute-start(bf16[2,64,512]{2,1,0:T(8,128)(2,1)S(1)} %get-tuple-element.39), channel_id=1, source_target_pairs={{0,8},{8,16},{16,24},{24,32},{32,40},{40,48},{48,56},{56,64},{64,7... | collective-permute-start | bytes 393224 | tf_op jit(solution)/shard_map/ppermute | solution.py:663
  94.4 24.1 %all-to-all-start.2 = ((bf16[32,72,128]{2,1,0:T(8,128)(2,1)}), bf16[32,72,128]{2,1,0:T(8,128)(2,1)S(1)}, u32[]{:S(2)}, u32[]{:S(2)}) async-start(bf16[32,72,128]{2,1,0:T(8,128)(2,1)} %attend_first.1), calls=%async_computation.3 | async-start | bytes 1179648 | tf_op jit(solution)/shard_map/all_to_all | solution.py:595
  114.3 2.1 %collective-permute-start.11 = (bf16[2,32,16,256]{3,2,1,0:T(8,128)(2,1)}, bf16[2,32,16,256]{3,2,1,0:T(8,128)(2,1)S(1)}, u32[]{:S(2)}, u32[]{:S(2)}) collective-permute-start(bf16[2,32,16,256]{3,2,1,0:T(8,128)(2,1)} %bitcast.9), channel_id=1, source_target_pairs={{0,1},{1,0},{2,3},{3,2},{4,5},{5,4},{6,7},{7,6},{8,9},{9,8},{10,11... | collective-permute-start | bytes 1572872 | tf_op jit(solution)/shard_map/ppermute | solution.py:669
  116.4 1.0 copy-start.4
  119.6 19.5 %copy-start.20 = (bf16[512,256]{1,0:T(8,128)(2,1)}, bf16[512,256]{1,0:T(8,128)(2,1)S(1)}, u32[]{:S(2)}) copy-start(bf16[512,256]{1,0:T(8,128)(2,1)S(1)} %combine.1.own_ref) | copy-start | bytes 786436
  119.6 13.2 %collective-permute-start.12 = (bf16[512,256]{1,0:T(8,128)(2,1)S(1)}, bf16[512,256]{1,0:T(8,128)(2,1)S(1)}, u32[]{:S(2)}, u32[]{:S(2)}) collective-permute-start(bf16[512,256]{1,0:T(8,128)(2,1)S(1)} %combine.1.own_ref), channel_id=1, source_target_pairs={{0,2},{1,3},{2,4},{3,5},{4,6},{5,7},{6,0},{7,1},{8,10},{9,11},{10,... | collective-permute-start | bytes 786440 | tf_op jit(solution)/shard_map/ppermute | solution.py:604
  121.7 11.2 %collective-permute-start.13 = (bf16[512,256]{1,0:T(8,128)(2,1)S(1)}, bf16[512,256]{1,0:T(8,128)(2,1)S(1)}, u32[]{:S(2)}, u32[]{:S(2)}) collective-permute-start(bf16[512,256]{1,0:T(8,128)(2,1)S(1)} %combine.1.own_ref), channel_id=1, source_target_pairs={{0,6},{1,7},{2,0},{3,1},{4,2},{5,3},{6,4},{7,5},{8,14},{9,15},{10,... | collective-permute-start | bytes 786440 | tf_op jit(solution)/shard_map/ppermute | solution.py:604
  122.9 27.2 %all-to-all-start.3 = ((bf16[32,2,16,256]{3,2,1,0:T(8,128)(2,1)}), bf16[32,2,16,256]{3,2,1,0:T(8,128)(2,1)S(1)}, u32[]{:S(2)}, u32[]{:S(2)}) async-start(bf16[32,2,16,256]{3,2,1,0:T(8,128)(2,1)} %place_rows.1), calls=%async_computation.4 | async-start | bytes 1048576 | tf_op jit(solution)/shard_map/all_to_all | solution.py:595
  132.8 6.3 %collective-permute-start.14 = (bf16[256,256]{1,0:T(8,128)(2,1)S(1)}, bf16[256,256]{1,0:T(8,128)(2,1)S(1)}, u32[]{:S(2)}, u32[]{:S(2)}) collective-permute-start(bf16[256,256]{1,0:T(8,128)(2,1)S(1)} %slice.18), channel_id=1, source_target_pairs={{0,2},{1,3},{2,4},{3,5},{4,6},{5,7},{6,0},{7,1},{8,10},{9,11},{10,... | collective-permute-start | bytes 393224 | tf_op jit(solution)/shard_map/ppermute | solution.py:604
  132.9 6.2 %copy-start.7 = (bf16[512,256]{1,0:T(8,128)(2,1)}, bf16[512,256]{1,0:T(8,128)(2,1)S(1)}, u32[]{:S(2)}) copy-start(bf16[512,256]{1,0:T(8,128)(2,1)S(1)} %collective-permute-done.13.next_ref) | copy-start | bytes 786436
  132.9 6.1 %collective-permute-start.15 = (bf16[256,256]{1,0:T(8,128)(2,1)S(1)}, bf16[256,256]{1,0:T(8,128)(2,1)S(1)}, u32[]{:S(2)}, u32[]{:S(2)}) collective-permute-start(bf16[256,256]{1,0:T(8,128)(2,1)S(1)} %slice.19), channel_id=1, source_target_pairs={{0,6},{1,7},{2,0},{3,1},{4,2},{5,3},{6,4},{7,5},{8,14},{9,15},{10,... | collective-permute-start | bytes 393224 | tf_op jit(solution)/shard_map/ppermute | solution.py:604
  139.1 1.2 copy-start.3
  140.3 0.9 copy-start.8
  141.3 0.9 copy-start.13
  142.2 0.9 copy-start.15
  143.2 0.9 copy-start.17
  144.1 0.9 copy-start.21
  146.4 1.6 %collective-permute-start.16 = (bf16[512,256]{1,0:T(8,128)(2,1)S(1)}, bf16[512,256]{1,0:T(8,128)(2,1)S(1)}, u32[]{:S(2)}, u32[]{:S(2)}) collective-permute-start(bf16[512,256]{1,0:T(8,128)(2,1)S(1)} %get-tuple-element.46), channel_id=1, source_target_pairs={{0,1},{1,0},{2,3},{3,2},{4,5},{5,4},{6,7},{7,6},{8,9},{9,8},{10,11... | collective-permute-start | bytes 786440 | tf_op jit(solution)/shard_map/ppermute | solution.py:675
Sparse Core Ops, SparseCore 0:
  85.3 28.9 reduce-scatter.1

commit v13 on v12

--- a/solution.py
+++ b/solution.py
@@ -14,7 +14,7 @@
 LANES = 128
 F32, BF16, I32 = jnp.float32, jnp.bfloat16, jnp.int32
 LONG = 1 << 35
-BIG = pltpu.CompilerParams(vmem_limit_bytes=48 * 1024 * 1024)
+BIG = pltpu.CompilerParams(vmem_limit_bytes=24 * 1024 * 1024)
 
 
 def dot(a, b):

time: 160 us -> 164 us (1.025)
  local copies, waits for them, and re-layouts: 26.2 us -> 31 us
    unnamed x48 -> x54, local copies, waits for them, and re-layouts: 19.5 us -> 24.3 us
where the time goes in v13:
time: 164 us; the launch traced here: 163 us
  starting transfers between devices  55 us (34%)
  waiting for transfers between devices  36.3 us (22%)
  local copies, waits for them, and re-layouts  31 us (19%)
  Pallas kernels  25.8 us (16%)
  between operations  14.4 us (9%)
    all_to_all x4, starting transfers between devices, exchange(): return lax.all_to_all(x, axis, split_axis=0, concat_axis=0, tiled=True)  35 us
    unnamed x54, local copies, waits for them, and re-layouts  24.3 us
    ppermute x11, starting transfers between devices, hop(): return lax.ppermute(x, 'exp', pairs)  18.8 us
    ppermute x11, waiting for transfers between devices, hop(): return lax.ppermute(x, 'exp', pairs)  13.9 us
    reduce_scatter x1, waiting for transfers between devices, body(): lax.psum_scatter(expert_part, 'exp', scatter_dimension=0, tiled=False, ax...  12.5 us
    pallas_call x1, Pallas kernels, run_experts(): pl.pallas_call(experts_kernel, grid_spec=pltpu.PrefetchScalarGridSpec(num...  7.02 us
    all_to_all x4, waiting for transfers between devices, exchange(): return lax.all_to_all(x, axis, split_axis=0, concat_axis=0, tiled=True)  5.62 us
    pallas_call x1, Pallas kernels, pack_rows(): pl.pallas_call(pack_rows_kernel, grid_spec=pltpu.PrefetchScalarGridSpec(n...  4.8 us
  transfers between devices with their start and end apart: 22, of which 11 were waited for; matrix products, arithmetic and copies ran while one was open for 4% of the time, Pallas kernels for 14%

profile of v13, /device:TPU:32, one launch (start us, length us, event | category | flops | bytes accessed | tf_op | source)
XLA Modules:
  0.0 162.5 jit_solution(3619408928442682699)
XLA Ops:
  7.2 1.5 copy-done
  8.8 0.8 constant_dynamic-slice_fusion.3.tokens_ref
  9.7 1.0 copy-done.6
  10.7 0.7 copy-done.26
  11.4 1.2 pack_tokens.1
  12.6 0.8 copy-done.5
  13.4 11.2 %all-to-all-start = ((bf16[32,16,512]{2,1,0:T(8,128)(2,1)}), bf16[32,16,512]{2,1,0:T(8,128)(2,1)}, u32[]{:S(2)}, u32[]{:S(2)}) async-start(bf16[32,16,512]{2,1,0:T(8,128)(2,1)} %bitcast.11), calls=%async_computation | async-start | bytes 1048576 | tf_op jit(solution)/shard_map/all_to_all | solution.py:595
  24.7 0.8 constant_dynamic-slice_fusion.1
  25.5 1.6 collective-permute-start
  27.1 1.7 %collective-permute-start.1 = (bf16[256,512]{1,0:T(8,128)(2,1)}, bf16[256,512]{1,0:T(8,128)(2,1)S(1)}, u32[]{:S(2)}, u32[]{:S(2)}) collective-permute-start(bf16[256,512]{1,0:T(8,128)(2,1)} %get-tuple-element.50), channel_id=1, source_target_pairs={{0,6},{1,7},{2,0},{3,1},{4,2},{5,3},{6,4},{7,5},{8,14},{9,15},{10,... | collective-permute-start | bytes 786440 | tf_op jit(solution)/shard_map/ppermute | solution.py:604
  28.8 1.6 copy-done.9
  30.4 1.2 copy-done.13
  31.6 1.2 copy-done.14
  32.8 4.8 %pack_rows.1 = (bf16[1024,512]{1,0:T(8,128)(2,1)}, s32[2,8,512]{2,1,0:T(8,128)S(1)}, s32[2,512]{1,0:T(2,128)S(1)}, s32[2,128]{1,0:T(2,128)S(1)}) custom-call(s32[1]{0:T(128)} %bitcast.4.me_ref, s32[2,16384]{1,0:T(2,128)S(1)} %copy-done.25, bf16[512,2048]{1,0:T(8,128)(2,1)S(1)} %copy-done.9, bf16[2048,256]{1,0:T(8,128)(2,1)S(1)} %copy-done.13, ...), custom_call_target="tpu_custom_call" | custom-call | flops 1610612736 | bytes 6291456 | tf_op jit(solution)/shard_map/pack_rows/pallas_call | solution.py:105
  37.6 0.7 copy-done.15
  38.3 0.7 copy-done.17
  39.0 3.3 %all-to-all-done.refs_0_ = bf16[32,16,512]{2,1,0:T(8,128)(2,1)} async-done(((bf16[32,16,512]{2,1,0:T(8,128)(2,1)}), bf16[32,16,512]{2,1,0:T(8,128)(2,1)}, u32[]{:S(2)}, u32[]{:S(2)}) %all-to-all-start) | async-done | bytes 524320 | tf_op jit(solution)/shard_map/all_to_all | solution.py:595
  42.3 0.5 collective-permute-start.7
  42.8 1.6 collective-permute-start.2
  44.4 1.7 %collective-permute-start.3 = (bf16[32,16,512]{2,1,0:T(8,128)(2,1)}, bf16[32,16,512]{2,1,0:T(8,128)(2,1)}, u32[]{:S(2)}, u32[]{:S(2)}) collective-permute-start(bf16[32,16,512]{2,1,0:T(8,128)(2,1)} %all-to-all-done.refs_0_), channel_id=1, source_target_pairs={{0,6},{1,7},{2,0},{3,1},{4,2},{5,3},{6,4},{7,5},{8,14},{9,15},{10,... | collective-permute-start | bytes 1572872 | tf_op jit(solution)/shard_map/ppermute | solution.py:604
  46.1 6.5 %all-to-all-start.1 = ((bf16[32,32,512]{2,1,0:T(8,128)(2,1)}), bf16[32,32,512]{2,1,0:T(8,128)(2,1)S(1)}, u32[]{:S(2)}, u32[]{:S(2)}) async-start(bf16[32,32,512]{2,1,0:T(8,128)(2,1)} %bitcast.6), calls=%async_computation.2 | async-start | bytes 2097152 | tf_op jit(solution)/shard_map/all_to_all | solution.py:595
  52.6 6.1 %collective-permute-done.2.refs_1_ = bf16[32,16,512]{2,1,0:T(8,128)(2,1)} collective-permute-done((bf16[32,16,512]{2,1,0:T(8,128)(2,1)}, bf16[32,16,512]{2,1,0:T(8,128)(2,1)}, u32[]{:S(2)}, u32[]{:S(2)}) %collective-permute-start.2) | collective-permute-done | bytes 524320 | tf_op jit(solution)/shard_map/ppermute | solution.py:604
  58.7 1.7 %slice.16 = bf16[16,16,512]{2,1,0:T(8,128)(2,1)} slice(bf16[32,16,512]{2,1,0:T(8,128)(2,1)} %collective-permute-done.2.refs_1_), slice={[0:16], [0:16], [0:512]} | slice | bytes 524288 | tf_op jit(solution)/shard_map/slice | solution.py:611
  60.4 0.3 collective-permute-start.4
  60.7 1.7 %slice.17 = bf16[16,16,512]{2,1,0:T(8,128)(2,1)} slice(bf16[32,16,512]{2,1,0:T(8,128)(2,1)} %collective-permute-done.3.refs_2_), slice={[16:32], [0:16], [0:512]} | slice | bytes 524288 | tf_op jit(solution)/shard_map/slice | solution.py:611
  62.4 2.9 %collective-permute-start.5 = (bf16[16,16,512]{2,1,0:T(8,128)(2,1)}, bf16[16,16,512]{2,1,0:T(8,128)(2,1)}, u32[]{:S(2)}, u32[]{:S(2)}) collective-permute-start(bf16[16,16,512]{2,1,0:T(8,128)(2,1)} %slice.17), channel_id=1, source_target_pairs={{0,6},{1,7},{2,0},{3,1},{4,2},{5,3},{6,4},{7,5},{8,14},{9,15},{10,... | collective-permute-start | bytes 786440 | tf_op jit(solution)/shard_map/ppermute | solution.py:604
  65.3 4.5 %collective-permute-done.4.refs_3_ = bf16[16,16,512]{2,1,0:T(8,128)(2,1)S(1)} collective-permute-done((bf16[16,16,512]{2,1,0:T(8,128)(2,1)}, bf16[16,16,512]{2,1,0:T(8,128)(2,1)S(1)}, u32[]{:S(2)}, u32[]{:S(2)}) %collective-permute-start.4) | collective-permute-done | bytes 262176 | tf_op jit(solution)/shard_map/ppermute | solution.py:604
  69.8 0.7 copy-done.21
  70.5 0.3 collective-permute-done.5.refs_4_
  70.9 1.7 %constant_dynamic-slice_fusion = bf16[256,512]{1,0:T(8,128)(2,1)} fusion(bf16[256,2048]{1,0:T(8,128)(2,1)} %refs_0_.1, s32[]{:T(128)S(6)} %select_n.43), kind=kLoop, calls=%fused_computation | loop fusion | bytes 524292 | tf_op jit(solution)/shard_map/dynamic_slice | solution.py:643
  72.6 2.4 %collective-permute-start.9 = (bf16[256,512]{1,0:T(8,128)(2,1)}, bf16[256,512]{1,0:T(8,128)(2,1)S(1)}, u32[]{:S(2)}, u32[]{:S(2)}) collective-permute-start(bf16[256,512]{1,0:T(8,128)(2,1)} %constant_dynamic-slice_fusion), channel_id=1, source_target_pairs={{0,4},{1,5},{2,6},{3,7},{4,0},{5,1},{6,2},{7,3},{8,12},{9,13},{10,... | collective-permute-start | bytes 786440 | tf_op jit(solution)/shard_map/ppermute | solution.py:604
  75.0 1.6 copy-done.10
  76.5 1.6 copy-done.11
  78.1 1.6 copy-done.12
  79.7 0.9 copy-done.22
  80.7 7.0 %experts.1 = bf16[4,2,32,16,256]{4,3,2,1,0:T(8,128)(2,1)S(1)} custom-call(s32[2]{0:T(128)S(1)} %pad_add_fusion.where_ref, bf16[32,16,512]{2,1,0:T(8,128)(2,1)} %all-to-all-done.refs_0_, bf16[32,16,512]{2,1,0:T(8,128)(2,1)} %collective-permute-done.2.refs_1_, bf16[32,16,512]{2,1,0:T(8,128)(2,1)} %collective-permute-done.3.refs_2_, ...), custom_call_target="tpu_custom_call" | custom-call | flops 15000000512 | bytes 10485760 | tf_op jit(solution)/shard_map/experts/pallas_call | solution.py:234
  87.7 1.3 copy-done.1
  89.1 1.7 %sort_rows.1 = (bf16[2,512,512]{2,1,0:T(8,128)(2,1)S(1)}, bf16[2,64,512]{2,1,0:T(8,128)(2,1)S(1)}, s32[2,8,512]{2,1,0:T(8,128)S(1)}) custom-call(s32[2,512]{1,0:T(2,128)S(1)} %get-tuple-element.33.perms_ref, bf16[32,32,512]{2,1,0:T(8,128)(2,1)S(1)} %all-to-all-done.1.arrived_ref), custom_call_target="tpu_custom_call" | custom-call | flops 34359738368 | bytes 4194304 | tf_op jit(solution)/shard_map/sort_rows/pallas_call | solution.py:318
  90.8 0.5 collective-permute-start.10
  91.4 3.8 %attend_later.1.later_ref = bf16[2,512,384]{2,1,0:T(8,128)(2,1)S(1)} custom-call(s32[2,512]{1,0:T(2,128)S(1)} %get-tuple-element.33.perms_ref, bf16[2,512,512]{2,1,0:T(8,128)(2,1)S(1)} %get-tuple-element.38.rows_ref, s32[2,8,512]{2,1,0:T(8,128)S(1)} %get-tuple-element.40.slot_ref), custom_call_target="tpu_custom_call" | custom-call | flops 34359738368 | bytes 4194304 | tf_op jit(solution)/shard_map/attend_later/pallas_call | solution.py:464
  95.2 0.7 collective-permute-done.10.last_ref
  95.9 2.5 %attend_first.1 = bf16[32,72,128]{2,1,0:T(8,128)(2,1)} custom-call(s32[2,512]{1,0:T(2,128)S(1)} %get-tuple-element.33.perms_ref, s32[2,128]{1,0:T(2,128)S(1)} %get-tuple-element.34.earlier_ref, bf16[2,512,512]{2,1,0:T(8,128)(2,1)S(1)} %get-tuple-element.38.rows_ref, bf16[2,64,512]{2,1,0:T(8,128)(2,1)S(1)} %collective-permute-done.10.last_ref, ...), custom_call_target="tpu_custom_call" | custom-call | flops 34359738368 | bytes 4194304 | tf_op jit(solution)/shard_map/attend_first/pallas_call | solution.py:480
  98.4 7.4 %all-to-all-start.2 = ((bf16[32,72,128]{2,1,0:T(8,128)(2,1)}), bf16[32,72,128]{2,1,0:T(8,128)(2,1)S(1)}, u32[]{:S(2)}, u32[]{:S(2)}) async-start(bf16[32,72,128]{2,1,0:T(8,128)(2,1)} %attend_first.1), calls=%async_computation.3 | async-start | bytes 1179648 | tf_op jit(solution)/shard_map/all_to_all | solution.py:595
  105.8 12.5 %reduce-scatter.2.cloned.1.call-done = bf16[1,2,32,16,256]{4,3,2,1,0:T(8,128)(2,1)} async-done(((bf16[4,2,32,16,256]{4,3,2,1,0:T(8,128)(2,1)}), bf16[1,2,32,16,256]{4,3,2,1,0:T(8,128)(2,1)}) %reduce-scatter.2.cloned.1.call-update) | async-done | bytes 524304 | tf_op jit(solution)/shard_map/reduce_scatter | solution.py:656
  118.3 2.1 %collective-permute-done.11.taken_ref = bf16[2,32,16,256]{3,2,1,0:T(8,128)(2,1)S(1)} collective-permute-done((bf16[2,32,16,256]{3,2,1,0:T(8,128)(2,1)}, bf16[2,32,16,256]{3,2,1,0:T(8,128)(2,1)S(1)}, u32[]{:S(2)}, u32[]{:S(2)}) %collective-permute-start.11) | collective-permute-done | bytes 524320 | tf_op jit(solution)/shard_map/ppermute | solution.py:669
  120.4 1.0 copy-done.4
  121.4 0.8 place_rows.1
  122.3 0.2 all-to-all-done.2.got_ref
  122.4 1.1 combine.1.own_ref
  123.5 2.1 %collective-permute-start.12 = (bf16[512,256]{1,0:T(8,128)(2,1)S(1)}, bf16[512,256]{1,0:T(8,128)(2,1)S(1)}, u32[]{:S(2)}, u32[]{:S(2)}) collective-permute-start(bf16[512,256]{1,0:T(8,128)(2,1)S(1)} %combine.1.own_ref), channel_id=1, source_target_pairs={{0,2},{1,3},{2,4},{3,5},{4,6},{5,7},{6,0},{7,1},{8,10},{9,11},{10,... | collective-permute-start | bytes 786440 | tf_op jit(solution)/shard_map/ppermute | solution.py:604
  125.7 1.2 collective-permute-start.13
  126.9 9.9 %all-to-all-start.3 = ((bf16[32,2,16,256]{3,2,1,0:T(8,128)(2,1)}), bf16[32,2,16,256]{3,2,1,0:T(8,128)(2,1)S(1)}, u32[]{:S(2)}, u32[]{:S(2)}) async-start(bf16[32,2,16,256]{3,2,1,0:T(8,128)(2,1)} %place_rows.1), calls=%async_computation.4 | async-start | bytes 1048576 | tf_op jit(solution)/shard_map/all_to_all | solution.py:595
  136.9 3.3 %collective-permute-start.15 = (bf16[256,256]{1,0:T(8,128)(2,1)S(1)}, bf16[256,256]{1,0:T(8,128)(2,1)S(1)}, u32[]{:S(2)}, u32[]{:S(2)}) collective-permute-start(bf16[256,256]{1,0:T(8,128)(2,1)S(1)} %slice.19), channel_id=1, source_target_pairs={{0,6},{1,7},{2,0},{3,1},{4,2},{5,3},{6,4},{7,5},{8,14},{9,15},{10,... | collective-permute-start | bytes 393224 | tf_op jit(solution)/shard_map/ppermute | solution.py:604
  140.2 2.8 %collective-permute-done.14.far_a_ref = bf16[256,256]{1,0:T(8,128)(2,1)S(1)} collective-permute-done((bf16[256,256]{1,0:T(8,128)(2,1)S(1)}, bf16[256,256]{1,0:T(8,128)(2,1)S(1)}, u32[]{:S(2)}, u32[]{:S(2)}) %collective-permute-start.14) | collective-permute-done | bytes 131104 | tf_op jit(solution)/shard_map/ppermute | solution.py:604
  143.0 1.2 copy-done.3
  144.3 0.9 copy-done.8
  145.2 0.9 copy-done.16
  146.2 0.9 copy-done.18
  147.1 0.9 copy-done.20
  148.1 0.9 copy-done.24
  149.0 1.3 project.1
  150.4 1.5 collective-permute-done.16.taken_ref
  151.9 2.2 %all-to-all-done.3 = bf16[32,2,16,256]{3,2,1,0:T(8,128)(2,1)S(1)} async-done(((bf16[32,2,16,256]{3,2,1,0:T(8,128)(2,1)}), bf16[32,2,16,256]{3,2,1,0:T(8,128)(2,1)S(1)}, u32[]{:S(2)}, u32[]{:S(2)}) %all-to-all-start.3) | async-done | bytes 524320 | tf_op jit(solution)/shard_map/all_to_all | solution.py:595
  154.1 1.6 finish.1
  (53 shorter events, 0.4 us)
Async XLA Ops:
  7.2 1.6 copy-start
  7.2 17.5 %copy-start.2 = (bf16[256,2048]{1,0:T(8,128)(2,1)S(1)}, bf16[256,2048]{1,0:T(8,128)(2,1)}, u32[]{:S(2)}) copy-start(bf16[256,2048]{1,0:T(8,128)(2,1)} %refs_0_.1) | copy-start | bytes 3145732
  9.7 1.0 copy-start.6
  10.7 0.7 copy-start.26
  11.4 17.4 %copy-start.25 = (s32[2,16384]{1,0:T(2,128)S(1)}, s32[2,16384]{1,0:T(2,128)}, u32[]{:S(2)}) copy-start(s32[2,16384]{1,0:T(2,128)} %perms_ref.1) | copy-start | bytes 393220
  12.6 0.8 copy-start.5
  13.4 28.9 %all-to-all-start = ((bf16[32,16,512]{2,1,0:T(8,128)(2,1)}), bf16[32,16,512]{2,1,0:T(8,128)(2,1)}, u32[]{:S(2)}, u32[]{:S(2)}) async-start(bf16[32,16,512]{2,1,0:T(8,128)(2,1)} %bitcast.11), calls=%async_computation | async-start | bytes 1048576 | tf_op jit(solution)/shard_map/all_to_all | solution.py:595
  25.5 12.1 %collective-permute-start = (bf16[256,512]{1,0:T(8,128)(2,1)}, bf16[256,512]{1,0:T(8,128)(2,1)S(1)}, u32[]{:S(2)}, u32[]{:S(2)}) collective-permute-start(bf16[256,512]{1,0:T(8,128)(2,1)} %get-tuple-element.51), channel_id=1, source_target_pairs={{0,2},{1,3},{2,4},{3,5},{4,6},{5,7},{6,0},{7,1},{8,10},{9,11},{10,... | collective-permute-start | bytes 786440 | tf_op jit(solution)/shard_map/ppermute | solution.py:604
  27.1 11.2 %collective-permute-start.1 = (bf16[256,512]{1,0:T(8,128)(2,1)}, bf16[256,512]{1,0:T(8,128)(2,1)S(1)}, u32[]{:S(2)}, u32[]{:S(2)}) collective-permute-start(bf16[256,512]{1,0:T(8,128)(2,1)} %get-tuple-element.50), channel_id=1, source_target_pairs={{0,6},{1,7},{2,0},{3,1},{4,2},{5,3},{6,4},{7,5},{8,14},{9,15},{10,... | collective-permute-start | bytes 786440 | tf_op jit(solution)/shard_map/ppermute | solution.py:604
  28.8 1.6 copy-start.9
  30.4 1.2 copy-start.13
  31.6 1.2 copy-start.14
  37.6 0.7 copy-start.15
  38.3 0.7 copy-start.17
  42.3 32.6 %collective-permute-start.6 = (bf16[2,2048,256]{2,1,0:T(8,128)(2,1)}, bf16[2,2048,256]{2,1,0:T(8,128)(2,1)}, u32[]{:S(2)}, u32[]{:S(2)}) collective-permute-start(bf16[2,2048,256]{2,1,0:T(8,128)(2,1)} %refs_5_.1), channel_id=1, source_target_pairs={{0,1},{1,0},{2,3},{3,2},{4,5},{5,4},{6,7},{7,6},{8,9},{9,8},{10,11... | collective-permute-start | bytes 6291464 | tf_op jit(solution)/shard_map/ppermute | solution.py:649
  42.3 32.6 %collective-permute-start.7 = (bf16[2,2048,256]{2,1,0:T(8,128)(2,1)}, bf16[2,2048,256]{2,1,0:T(8,128)(2,1)}, u32[]{:S(2)}, u32[]{:S(2)}) collective-permute-start(bf16[2,2048,256]{2,1,0:T(8,128)(2,1)} %refs_6_.1), channel_id=1, source_target_pairs={{0,1},{1,0},{2,3},{3,2},{4,5},{5,4},{6,7},{7,6},{8,9},{9,8},{10,11... | collective-permute-start | bytes 6291464 | tf_op jit(solution)/shard_map/ppermute | solution.py:649
  42.8 32.1 %collective-permute-start.8 = (bf16[2,256,2048]{2,1,0:T(8,128)(2,1)}, bf16[2,256,2048]{2,1,0:T(8,128)(2,1)}, u32[]{:S(2)}, u32[]{:S(2)}) collective-permute-start(bf16[2,256,2048]{2,1,0:T(8,128)(2,1)} %refs_7_.1), channel_id=1, source_target_pairs={{0,1},{1,0},{2,3},{3,2},{4,5},{5,4},{6,7},{7,6},{8,9},{9,8},{10,11... | collective-permute-start | bytes 6291464 | tf_op jit(solution)/shard_map/ppermute | solution.py:649
  42.8 15.9 %collective-permute-start.2 = (bf16[32,16,512]{2,1,0:T(8,128)(2,1)}, bf16[32,16,512]{2,1,0:T(8,128)(2,1)}, u32[]{:S(2)}, u32[]{:S(2)}) collective-permute-start(bf16[32,16,512]{2,1,0:T(8,128)(2,1)} %all-to-all-done.refs_0_), channel_id=1, source_target_pairs={{0,2},{1,3},{2,4},{3,5},{4,6},{5,7},{6,0},{7,1},{8,10},{9,11},{10,... | collective-permute-start | bytes 1572872 | tf_op jit(solution)/shard_map/ppermute | solution.py:604
  44.4 16.3 %collective-permute-start.3 = (bf16[32,16,512]{2,1,0:T(8,128)(2,1)}, bf16[32,16,512]{2,1,0:T(8,128)(2,1)}, u32[]{:S(2)}, u32[]{:S(2)}) collective-permute-start(bf16[32,16,512]{2,1,0:T(8,128)(2,1)} %all-to-all-done.refs_0_), channel_id=1, source_target_pairs={{0,6},{1,7},{2,0},{3,1},{4,2},{5,3},{6,4},{7,5},{8,14},{9,15},{10,... | collective-permute-start | bytes 1572872 | tf_op jit(solution)/shard_map/ppermute | solution.py:604
  46.1 43.0 %all-to-all-start.1 = ((bf16[32,32,512]{2,1,0:T(8,128)(2,1)}), bf16[32,32,512]{2,1,0:T(8,128)(2,1)S(1)}, u32[]{:S(2)}, u32[]{:S(2)}) async-start(bf16[32,32,512]{2,1,0:T(8,128)(2,1)} %bitcast.6), calls=%async_computation.2 | async-start | bytes 2097152 | tf_op jit(solution)/shard_map/all_to_all | solution.py:595
  52.6 65.7 %reduce-scatter.2.cloned.1.call-start = ((), (), s32[]{:S(2)}) async-start(), calls=%async_computation.5 | async-start | bytes 2621440 | tf_op jit(solution)/shard_map/reduce_scatter | solution.py:656
  60.4 9.4 %collective-permute-start.4 = (bf16[16,16,512]{2,1,0:T(8,128)(2,1)}, bf16[16,16,512]{2,1,0:T(8,128)(2,1)S(1)}, u32[]{:S(2)}, u32[]{:S(2)}) collective-permute-start(bf16[16,16,512]{2,1,0:T(8,128)(2,1)} %slice.16), channel_id=1, source_target_pairs={{0,2},{1,3},{2,4},{3,5},{4,6},{5,7},{6,0},{7,1},{8,10},{9,11},{10,... | collective-permute-start | bytes 786440 | tf_op jit(solution)/shard_map/ppermute | solution.py:604
  62.4 8.5 %collective-permute-start.5 = (bf16[16,16,512]{2,1,0:T(8,128)(2,1)}, bf16[16,16,512]{2,1,0:T(8,128)(2,1)}, u32[]{:S(2)}, u32[]{:S(2)}) collective-permute-start(bf16[16,16,512]{2,1,0:T(8,128)(2,1)} %slice.17), channel_id=1, source_target_pairs={{0,6},{1,7},{2,0},{3,1},{4,2},{5,3},{6,4},{7,5},{8,14},{9,15},{10,... | collective-permute-start | bytes 786440 | tf_op jit(solution)/shard_map/ppermute | solution.py:604
  69.8 0.7 copy-start.21
  72.6 16.5 %collective-permute-start.9 = (bf16[256,512]{1,0:T(8,128)(2,1)}, bf16[256,512]{1,0:T(8,128)(2,1)S(1)}, u32[]{:S(2)}, u32[]{:S(2)}) collective-permute-start(bf16[256,512]{1,0:T(8,128)(2,1)} %constant_dynamic-slice_fusion), channel_id=1, source_target_pairs={{0,4},{1,5},{2,6},{3,7},{4,0},{5,1},{6,2},{7,3},{8,12},{9,13},{10,... | collective-permute-start | bytes 786440 | tf_op jit(solution)/shard_map/ppermute | solution.py:604
  74.9 1.6 copy-start.10
  76.5 1.6 copy-start.11
  78.1 1.6 copy-start.12
  79.7 0.9 copy-start.22
  87.7 1.3 copy-start.1
  89.1 1.7 %copy-start.19 = (bf16[256,512]{1,0:T(8,128)(2,1)}, bf16[256,512]{1,0:T(8,128)(2,1)S(1)}, u32[]{:S(2)}) copy-start(bf16[256,512]{1,0:T(8,128)(2,1)S(1)} %collective-permute-done.9.refs_3_) | copy-start | bytes 786436
  90.8 5.0 %collective-permute-start.10 = (bf16[2,64,512]{2,1,0:T(8,128)(2,1)S(1)}, bf16[2,64,512]{2,1,0:T(8,128)(2,1)S(1)}, u32[]{:S(2)}, u32[]{:S(2)}) collective-permute-start(bf16[2,64,512]{2,1,0:T(8,128)(2,1)S(1)} %get-tuple-element.39), channel_id=1, source_target_pairs={{0,8},{8,16},{16,24},{24,32},{32,40},{40,48},{48,56},{56,64},{64,7... | collective-permute-start | bytes 393224 | tf_op jit(solution)/shard_map/ppermute | solution.py:663
  98.4 24.1 %all-to-all-start.2 = ((bf16[32,72,128]{2,1,0:T(8,128)(2,1)}), bf16[32,72,128]{2,1,0:T(8,128)(2,1)S(1)}, u32[]{:S(2)}, u32[]{:S(2)}) async-start(bf16[32,72,128]{2,1,0:T(8,128)(2,1)} %attend_first.1), calls=%async_computation.3 | async-start | bytes 1179648 | tf_op jit(solution)/shard_map/all_to_all | solution.py:595
  118.3 2.1 %collective-permute-start.11 = (bf16[2,32,16,256]{3,2,1,0:T(8,128)(2,1)}, bf16[2,32,16,256]{3,2,1,0:T(8,128)(2,1)S(1)}, u32[]{:S(2)}, u32[]{:S(2)}) collective-permute-start(bf16[2,32,16,256]{3,2,1,0:T(8,128)(2,1)} %bitcast.9), channel_id=1, source_target_pairs={{0,1},{1,0},{2,3},{3,2},{4,5},{5,4},{6,7},{7,6},{8,9},{9,8},{10,11... | collective-permute-start | bytes 1572872 | tf_op jit(solution)/shard_map/ppermute | solution.py:669
  120.4 1.0 copy-start.4
  123.5 19.5 %copy-start.23 = (bf16[512,256]{1,0:T(8,128)(2,1)}, bf16[512,256]{1,0:T(8,128)(2,1)S(1)}, u32[]{:S(2)}) copy-start(bf16[512,256]{1,0:T(8,128)(2,1)S(1)} %combine.1.own_ref) | copy-start | bytes 786436
  123.5 13.2 %collective-permute-start.12 = (bf16[512,256]{1,0:T(8,128)(2,1)S(1)}, bf16[512,256]{1,0:T(8,128)(2,1)S(1)}, u32[]{:S(2)}, u32[]{:S(2)}) collective-permute-start(bf16[512,256]{1,0:T(8,128)(2,1)S(1)} %combine.1.own_ref), channel_id=1, source_target_pairs={{0,2},{1,3},{2,4},{3,5},{4,6},{5,7},{6,0},{7,1},{8,10},{9,11},{10,... | collective-permute-start | bytes 786440 | tf_op jit(solution)/shard_map/ppermute | solution.py:604
  125.7 11.2 %collective-permute-start.13 = (bf16[512,256]{1,0:T(8,128)(2,1)S(1)}, bf16[512,256]{1,0:T(8,128)(2,1)S(1)}, u32[]{:S(2)}, u32[]{:S(2)}) collective-permute-start(bf16[512,256]{1,0:T(8,128)(2,1)S(1)} %combine.1.own_ref), channel_id=1, source_target_pairs={{0,6},{1,7},{2,0},{3,1},{4,2},{5,3},{6,4},{7,5},{8,14},{9,15},{10,... | collective-permute-start | bytes 786440 | tf_op jit(solution)/shard_map/ppermute | solution.py:604
  126.9 27.2 %all-to-all-start.3 = ((bf16[32,2,16,256]{3,2,1,0:T(8,128)(2,1)}), bf16[32,2,16,256]{3,2,1,0:T(8,128)(2,1)S(1)}, u32[]{:S(2)}, u32[]{:S(2)}) async-start(bf16[32,2,16,256]{3,2,1,0:T(8,128)(2,1)} %place_rows.1), calls=%async_computation.4 | async-start | bytes 1048576 | tf_op jit(solution)/shard_map/all_to_all | solution.py:595
  136.8 6.3 %collective-permute-start.14 = (bf16[256,256]{1,0:T(8,128)(2,1)S(1)}, bf16[256,256]{1,0:T(8,128)(2,1)S(1)}, u32[]{:S(2)}, u32[]{:S(2)}) collective-permute-start(bf16[256,256]{1,0:T(8,128)(2,1)S(1)} %slice.18), channel_id=1, source_target_pairs={{0,2},{1,3},{2,4},{3,5},{4,6},{5,7},{6,0},{7,1},{8,10},{9,11},{10,... | collective-permute-start | bytes 393224 | tf_op jit(solution)/shard_map/ppermute | solution.py:604
  136.9 6.2 %copy-start.7 = (bf16[512,256]{1,0:T(8,128)(2,1)}, bf16[512,256]{1,0:T(8,128)(2,1)S(1)}, u32[]{:S(2)}) copy-start(bf16[512,256]{1,0:T(8,128)(2,1)S(1)} %collective-permute-done.13.next_ref) | copy-start | bytes 786436
  136.9 6.1 %collective-permute-start.15 = (bf16[256,256]{1,0:T(8,128)(2,1)S(1)}, bf16[256,256]{1,0:T(8,128)(2,1)S(1)}, u32[]{:S(2)}, u32[]{:S(2)}) collective-permute-start(bf16[256,256]{1,0:T(8,128)(2,1)S(1)} %slice.19), channel_id=1, source_target_pairs={{0,6},{1,7},{2,0},{3,1},{4,2},{5,3},{6,4},{7,5},{8,14},{9,15},{10,... | collective-permute-start | bytes 393224 | tf_op jit(solution)/shard_map/ppermute | solution.py:604
  143.0 1.2 copy-start.3
  144.3 0.9 copy-start.8
  145.2 0.9 copy-start.16
  146.2 0.9 copy-start.18
  147.1 0.9 copy-start.20
  148.1 0.9 copy-start.24
  150.3 1.6 collective-permute-start.16
Sparse Core Ops, SparseCore 0:
  89.2 29.0 reduce-scatter.1

commit v14 on v10

--- a/solution.py
+++ b/solution.py
@@ -15,6 +15,7 @@
 F32, BF16, I32 = jnp.float32, jnp.bfloat16, jnp.int32
 LONG = 1 << 35
 BIG = pltpu.CompilerParams(vmem_limit_bytes=48 * 1024 * 1024)
+ALL = pltpu.CompilerParams(vmem_limit_bytes=60 * 1024 * 1024)
 
 
 def dot(a, b):
@@ -163,7 +164,7 @@
             jax.ShapeDtypeStruct((8, length), I32),
         ],
         cost_estimate=cost(2 * slots * length * part, 2 << 20),
-        compiler_params=BIG,
+        compiler_params=ALL,
         name="pack_tokens",
     )(where, ids, tokens)
 

time: 153 us -> 153 us (level)
  waiting for transfers between devices: 44.3 us -> 42.4 us
  local copies, waits for them, and re-layouts: 12.7 us -> 11 us
  Pallas kernels: 29.7 us -> 31.3 us
    all_to_all x4, waiting for transfers between devices: 13.6 us -> 11.2 us  [exchange(): return lax.all_to_all(x, axis, split_axis=0, concat_axis=0, tiled=True)]
    pallas_call x1, Pallas kernels: 2.21 us -> 3.79 us  [pack_tokens(): pl.pallas_call(functools.partial(pack_tokens_kernel, peers), grid_spec=pl...]
    unnamed x22 -> x28, local copies, waits for them, and re-layouts: 7.71 us -> 6.15 us
where the time goes in v14:
time: 153 us
  starting transfers between devices  52.7 us (34%)
  waiting for transfers between devices  42.4 us (28%)
  Pallas kernels  31.3 us (20%)
  between operations  14.3 us (9%)
  local copies, waits for them, and re-layouts  11 us (7%)
    all_to_all x4, starting transfers between devices, exchange(): return lax.all_to_all(x, axis, split_axis=0, concat_axis=0, tiled=True)  32.6 us
    ppermute x11, starting transfers between devices, hop(): return lax.ppermute(x, 'exp', pairs)  18.9 us
    ppermute x11, waiting for transfers between devices, hop(): return lax.ppermute(x, 'exp', pairs)  15.6 us
    reduce_scatter x1, waiting for transfers between devices, body(): lax.psum_scatter(expert_part, 'exp', scatter_dimension=0, tiled=False, ax...  11.9 us
    all_to_all x4, waiting for transfers between devices, exchange(): return lax.all_to_all(x, axis, split_axis=0, concat_axis=0, tiled=True)  11.2 us
    pallas_call x1, Pallas kernels, run_experts(): pl.pallas_call(experts_kernel, grid_spec=pltpu.PrefetchScalarGridSpec(num...  8.94 us
    unnamed x28, local copies, waits for them, and re-layouts  6.15 us
    pallas_call x1, Pallas kernels, pack_rows(): pl.pallas_call(pack_rows_kernel, grid_spec=pltpu.PrefetchScalarGridSpec(n...  4.82 us
  transfers between devices with their start and end apart: 22, of which 11 were waited for; matrix products, arithmetic and copies ran while one was open for 3% of the time, Pallas kernels for 16%

profile of v14, /device:TPU:32, one launch (start us, length us, event | category | flops | bytes accessed | tf_op | source)
XLA Modules:
  0.0 152.5 jit_solution(15948254256222450861)
XLA Ops:
  7.2 0.7 pad_add_fusion.where_ref
  7.9 3.8 %pack_tokens.1 = (bf16[512,512]{1,0:T(8,128)(2,1)}, s32[8,512]{1,0:T(8,128)}) custom-call(s32[2]{0:T(128)} %pad_add_fusion.where_ref, s32[1,512]{1,0:T(1,128)} %bitcast.14, bf16[512,2048]{1,0:T(8,128)(2,1)} %tokens_ref.1), custom_call_target="tpu_custom_call" | custom-call | flops 268435456 | bytes 2097152 | tf_op jit(solution)/shard_map/pack_tokens/pallas_call | solution.py:147
  11.7 11.2 %all-to-all-start = ((bf16[32,16,512]{2,1,0:T(8,128)(2,1)}), bf16[32,16,512]{2,1,0:T(8,128)(2,1)S(1)}, u32[]{:S(2)}, u32[]{:S(2)}) async-start(bf16[32,16,512]{2,1,0:T(8,128)(2,1)} %bitcast.13), calls=%async_computation | async-start | bytes 1048576 | tf_op jit(solution)/shard_map/all_to_all | solution.py:622
  22.9 0.7 constant_dynamic-slice_fusion.1
  23.7 1.6 %collective-permute-start = (bf16[256,512]{1,0:T(8,128)(2,1)}, bf16[256,512]{1,0:T(8,128)(2,1)S(1)}, u32[]{:S(2)}, u32[]{:S(2)}) collective-permute-start(bf16[256,512]{1,0:T(8,128)(2,1)} %get-tuple-element.47), channel_id=1, source_target_pairs={{0,2},{1,3},{2,4},{3,5},{4,6},{5,7},{6,0},{7,1},{8,10},{9,11},{10,... | collective-permute-start | bytes 786440 | tf_op jit(solution)/shard_map/ppermute | solution.py:631
  25.2 1.7 %collective-permute-start.1 = (bf16[256,512]{1,0:T(8,128)(2,1)S(1)}, bf16[256,512]{1,0:T(8,128)(2,1)S(1)}, u32[]{:S(2)}, u32[]{:S(2)}) collective-permute-start(bf16[256,512]{1,0:T(8,128)(2,1)S(1)} %get-tuple-element.46), channel_id=1, source_target_pairs={{0,6},{1,7},{2,0},{3,1},{4,2},{5,3},{6,4},{7,5},{8,14},{9,15},{10,... | collective-permute-start | bytes 786440 | tf_op jit(solution)/shard_map/ppermute | solution.py:631
  26.9 1.6 %copy-done.4 = bf16[512,2048]{1,0:T(8,128)(2,1)S(1)} copy-done((bf16[512,2048]{1,0:T(8,128)(2,1)S(1)}, bf16[512,2048]{1,0:T(8,128)(2,1)}, u32[]{:S(2)}) %copy-start.4) | copy-done | bytes 2097176
  28.5 1.2 copy-done.6
  29.7 4.8 %pack_rows.1 = (bf16[1024,512]{1,0:T(8,128)(2,1)}, s32[2,8,512]{2,1,0:T(8,128)S(1)}) custom-call(s32[1]{0:T(128)} %bitcast.4.me_ref, s32[2,16384]{1,0:T(2,128)S(1)} %copy-done.11, bf16[512,2048]{1,0:T(8,128)(2,1)S(1)} %copy-done.4, bf16[2048,256]{1,0:T(8,128)(2,1)S(1)} %copy-done.5, bf16[2048,256]{1,0:T(8,128)(2,1)S(1)} %copy-done.6), custom_call_target="tpu_custom_call" | custom-call | flops 1610612736 | bytes 6291456 | tf_op jit(solution)/shard_map/pack_rows/pallas_call | solution.py:91
  34.5 0.6 copy-done.12
  35.1 0.0 collective-permute-done.refs_1_
  35.1 0.0 collective-permute-done.1.refs_2_
  35.2 0.7 copy-done.7
  35.9 4.6 %all-to-all-done.refs_0_ = bf16[32,16,512]{2,1,0:T(8,128)(2,1)S(1)} async-done(((bf16[32,16,512]{2,1,0:T(8,128)(2,1)}), bf16[32,16,512]{2,1,0:T(8,128)(2,1)S(1)}, u32[]{:S(2)}, u32[]{:S(2)}) %all-to-all-start) | async-done | bytes 524320 | tf_op jit(solution)/shard_map/all_to_all | solution.py:622
  40.5 0.0 collective-permute-start.6
  40.5 0.5 collective-permute-start.7
  41.0 0.0 collective-permute-start.8
  41.0 1.6 %collective-permute-start.2 = (bf16[32,16,512]{2,1,0:T(8,128)(2,1)S(1)}, bf16[32,16,512]{2,1,0:T(8,128)(2,1)S(1)}, u32[]{:S(2)}, u32[]{:S(2)}) collective-permute-start(bf16[32,16,512]{2,1,0:T(8,128)(2,1)S(1)} %all-to-all-done.refs_0_), channel_id=1, source_target_pairs={{0,2},{1,3},{2,4},{3,5},{4,6},{5,7},{6,0},{7,1},{8,10},{9,11},{10,... | collective-permute-start | bytes 1572872 | tf_op jit(solution)/shard_map/ppermute | solution.py:631
  42.6 1.7 %collective-permute-start.3 = (bf16[32,16,512]{2,1,0:T(8,128)(2,1)S(1)}, bf16[32,16,512]{2,1,0:T(8,128)(2,1)}, u32[]{:S(2)}, u32[]{:S(2)}) collective-permute-start(bf16[32,16,512]{2,1,0:T(8,128)(2,1)S(1)} %all-to-all-done.refs_0_), channel_id=1, source_target_pairs={{0,6},{1,7},{2,0},{3,1},{4,2},{5,3},{6,4},{7,5},{8,14},{9,15},{10,... | collective-permute-start | bytes 1572872 | tf_op jit(solution)/shard_map/ppermute | solution.py:631
  44.2 5.2 %all-to-all-start.1 = ((bf16[32,32,512]{2,1,0:T(8,128)(2,1)}), bf16[32,32,512]{2,1,0:T(8,128)(2,1)S(1)}, u32[]{:S(2)}, u32[]{:S(2)}) async-start(bf16[32,32,512]{2,1,0:T(8,128)(2,1)} %bitcast.6), calls=%async_computation.2 | async-start | bytes 2097152 | tf_op jit(solution)/shard_map/all_to_all | solution.py:622
  49.4 0.0 reduce-scatter.2.cloned.1.call-start
  49.5 7.1 %collective-permute-done.2.refs_1_ = bf16[32,16,512]{2,1,0:T(8,128)(2,1)S(1)} collective-permute-done((bf16[32,16,512]{2,1,0:T(8,128)(2,1)S(1)}, bf16[32,16,512]{2,1,0:T(8,128)(2,1)S(1)}, u32[]{:S(2)}, u32[]{:S(2)}) %collective-permute-start.2) | collective-permute-done | bytes 524320 | tf_op jit(solution)/shard_map/ppermute | solution.py:631
  56.6 0.7 slice.20
  57.3 0.3 collective-permute-start.4
  57.6 0.0 collective-permute-done.3.refs_2_
  57.6 1.7 %slice.21 = bf16[16,16,512]{2,1,0:T(8,128)(2,1)} slice(bf16[32,16,512]{2,1,0:T(8,128)(2,1)} %collective-permute-done.3.refs_2_), slice={[16:32], [0:16], [0:512]} | slice | bytes 524288 | tf_op jit(solution)/shard_map/slice | solution.py:638
  59.3 2.9 %collective-permute-start.5 = (bf16[16,16,512]{2,1,0:T(8,128)(2,1)}, bf16[16,16,512]{2,1,0:T(8,128)(2,1)}, u32[]{:S(2)}, u32[]{:S(2)}) collective-permute-start(bf16[16,16,512]{2,1,0:T(8,128)(2,1)} %slice.21), channel_id=1, source_target_pairs={{0,6},{1,7},{2,0},{3,1},{4,2},{5,3},{6,4},{7,5},{8,14},{9,15},{10,... | collective-permute-start | bytes 786440 | tf_op jit(solution)/shard_map/ppermute | solution.py:631
  62.2 4.6 %collective-permute-done.4.refs_3_ = bf16[16,16,512]{2,1,0:T(8,128)(2,1)} collective-permute-done((bf16[16,16,512]{2,1,0:T(8,128)(2,1)}, bf16[16,16,512]{2,1,0:T(8,128)(2,1)}, u32[]{:S(2)}, u32[]{:S(2)}) %collective-permute-start.4) | collective-permute-done | bytes 262176 | tf_op jit(solution)/shard_map/ppermute | solution.py:631
  66.9 0.9 collective-permute-done.5.refs_4_
  67.8 0.7 constant_dynamic-slice_fusion
  68.5 2.5 %collective-permute-start.9 = (bf16[256,512]{1,0:T(8,128)(2,1)}, bf16[256,512]{1,0:T(8,128)(2,1)}, u32[]{:S(2)}, u32[]{:S(2)}) collective-permute-start(bf16[256,512]{1,0:T(8,128)(2,1)} %constant_dynamic-slice_fusion), channel_id=1, source_target_pairs={{0,4},{1,5},{2,6},{3,7},{4,0},{5,1},{6,2},{7,3},{8,12},{9,13},{10,... | collective-permute-start | bytes 786440 | tf_op jit(solution)/shard_map/ppermute | solution.py:631
  71.0 8.9 %experts.1 = bf16[4,2,32,16,256]{4,3,2,1,0:T(8,128)(2,1)} custom-call(s32[2]{0:T(128)S(1)} %copy-done.3, bf16[32,16,512]{2,1,0:T(8,128)(2,1)S(1)} %all-to-all-done.refs_0_, bf16[32,16,512]{2,1,0:T(8,128)(2,1)S(1)} %collective-permute-done.2.refs_1_, bf16[32,16,512]{2,1,0:T(8,128)(2,1)} %collective-permute-done.3.refs_2_, ...), custom_call_target="tpu_custom_call" | custom-call | flops 15000000512 | bytes 10485760 | tf_op jit(solution)/shard_map/experts/pallas_call | solution.py:223
  80.0 0.0 reduce-scatter.2.cloned.1.call-update
  80.0 0.0 collective-permute-done.9.refs_3_
  80.0 1.7 %sort_rows.1 = (bf16[2,512,512]{2,1,0:T(8,128)(2,1)S(1)}, bf16[2,64,512]{2,1,0:T(8,128)(2,1)S(1)}, s32[2,8,512]{2,1,0:T(8,128)S(1)}) custom-call(s32[1]{0:T(128)} %bitcast.4.me_ref, s32[2,16384]{1,0:T(2,128)S(1)} %copy-done.11, bf16[32,32,512]{2,1,0:T(8,128)(2,1)S(1)} %all-to-all-done.1.arrived_ref), custom_call_target="tpu_custom_call" | custom-call | flops 34359738368 | bytes 4194304 | tf_op jit(solution)/shard_map/sort_rows/pallas_call | solution.py:307
  81.7 0.5 collective-permute-start.10
  82.3 3.8 %attend_later.1.later_ref = bf16[2,512,384]{2,1,0:T(8,128)(2,1)S(1)} custom-call(s32[1]{0:T(128)} %bitcast.4.me_ref, s32[2,16384]{1,0:T(2,128)S(1)} %copy-done.11, bf16[2,512,512]{2,1,0:T(8,128)(2,1)S(1)} %get-tuple-element.34.rows_ref, s32[2,8,512]{2,1,0:T(8,128)S(1)} %get-tuple-element.36.slot_ref), custom_call_target="tpu_custom_call" | custom-call | flops 34359738368 | bytes 4194304 | tf_op jit(solution)/shard_map/attend_later/pallas_call | solution.py:469
  86.1 0.7 collective-permute-done.10.last_ref
  86.8 2.5 %attend_first.1 = bf16[32,72,128]{2,1,0:T(8,128)(2,1)} custom-call(s32[1]{0:T(128)} %bitcast.4.me_ref, s32[2,16384]{1,0:T(2,128)S(1)} %copy-done.11, s32[2,16384]{1,0:T(2,128)S(1)} %copy-done.11, bf16[2,512,512]{2,1,0:T(8,128)(2,1)S(1)} %get-tuple-element.34.rows_ref, bf16[2,64,512]{2,1,0:T(8,128)(2,1)S(1)} %collective-permute-done.10.last_ref, ...), custom_call_target="tpu_custom_call" | custom-call | flops 34359738368 | bytes 4194304 | tf_op jit(solution)/shard_map/attend_first/pallas_call | solution.py:498
  89.3 6.5 %all-to-all-start.2 = ((bf16[32,72,128]{2,1,0:T(8,128)(2,1)}), bf16[32,72,128]{2,1,0:T(8,128)(2,1)S(1)}, u32[]{:S(2)}, u32[]{:S(2)}) async-start(bf16[32,72,128]{2,1,0:T(8,128)(2,1)} %attend_first.1), calls=%async_computation.3 | async-start | bytes 1179648 | tf_op jit(solution)/shard_map/all_to_all | solution.py:622
  95.8 11.9 %reduce-scatter.2.cloned.1.call-done = bf16[1,2,32,16,256]{4,3,2,1,0:T(8,128)(2,1)} async-done(((bf16[4,2,32,16,256]{4,3,2,1,0:T(8,128)(2,1)}), bf16[1,2,32,16,256]{4,3,2,1,0:T(8,128)(2,1)}) %reduce-scatter.2.cloned.1.call-update) | async-done | bytes 524304 | tf_op jit(solution)/shard_map/reduce_scatter | solution.py:682
  107.7 1.0 slice_bitcast_fusion
  108.7 0.1 collective-permute-start.11
  108.8 1.5 collective-permute-done.11.taken_ref
  110.4 1.0 copy-done
  111.4 0.8 place_rows.1
  112.3 0.3 all-to-all-done.2.got_ref
  112.6 1.1 combine.1.own_ref
  113.7 0.0 copy-start.9
  113.7 2.1 %collective-permute-start.12 = (bf16[512,256]{1,0:T(8,128)(2,1)S(1)}, bf16[512,256]{1,0:T(8,128)(2,1)S(1)}, u32[]{:S(2)}, u32[]{:S(2)}) collective-permute-start(bf16[512,256]{1,0:T(8,128)(2,1)S(1)} %combine.1.own_ref), channel_id=1, source_target_pairs={{0,2},{1,3},{2,4},{3,5},{4,6},{5,7},{6,0},{7,1},{8,10},{9,11},{10,... | collective-permute-start | bytes 786440 | tf_op jit(solution)/shard_map/ppermute | solution.py:631
  115.8 1.2 collective-permute-start.13
  117.0 9.7 %all-to-all-start.3 = ((bf16[32,2,16,256]{3,2,1,0:T(8,128)(2,1)}), bf16[32,2,16,256]{3,2,1,0:T(8,128)(2,1)S(1)}, u32[]{:S(2)}, u32[]{:S(2)}) async-start(bf16[32,2,16,256]{3,2,1,0:T(8,128)(2,1)} %place_rows.1), calls=%async_computation.4 | async-start | bytes 1048576 | tf_op jit(solution)/shard_map/all_to_all | solution.py:622
  126.8 0.0 collective-permute-done.12.prev_ref
  126.8 0.1 collective-permute-start.14
  126.9 0.0 collective-permute-done.13.next_ref
  126.9 3.3 %collective-permute-start.15 = (bf16[256,256]{1,0:T(8,128)(2,1)S(1)}, bf16[256,256]{1,0:T(8,128)(2,1)S(1)}, u32[]{:S(2)}, u32[]{:S(2)}) collective-permute-start(bf16[256,256]{1,0:T(8,128)(2,1)S(1)} %slice.23), channel_id=1, source_target_pairs={{0,6},{1,7},{2,0},{3,1},{4,2},{5,3},{6,4},{7,5},{8,14},{9,15},{10,... | collective-permute-start | bytes 393224 | tf_op jit(solution)/shard_map/ppermute | solution.py:631
  130.2 2.8 %collective-permute-done.14.far_a_ref = bf16[256,256]{1,0:T(8,128)(2,1)S(1)} collective-permute-done((bf16[256,256]{1,0:T(8,128)(2,1)S(1)}, bf16[256,256]{1,0:T(8,128)(2,1)S(1)}, u32[]{:S(2)}, u32[]{:S(2)}) %collective-permute-start.14) | collective-permute-done | bytes 131104 | tf_op jit(solution)/shard_map/ppermute | solution.py:631
  133.1 0.0 copy-start.10
  133.1 0.9 copy-done.10
  134.0 2.3 %project.1 = (f32[512,256]{1,0:T(8,128)S(1)}, bf16[512,256]{1,0:T(8,128)(2,1)S(1)}) custom-call(s32[2]{0:T(128)S(1)} %copy-done.3, bf16[512,256]{1,0:T(8,128)(2,1)S(1)} %copy-done.10, bf16[512,256]{1,0:T(8,128)(2,1)S(1)} %collective-permute-done.12.prev_ref, bf16[512,256]{1,0:T(8,128)(2,1)S(1)} %collective-permute-done.13.next_ref, ...), custom_call_target="tpu_custom_call" | custom-call | flops 5500000256 | bytes 3145728 | tf_op jit(solution)/shard_map/project/pallas_call | solution.py:603
  136.3 0.1 collective-permute-start.16
  136.4 1.5 collective-permute-done.16.taken_ref
  137.9 6.2 %all-to-all-done.3 = bf16[32,2,16,256]{3,2,1,0:T(8,128)(2,1)S(1)} async-done(((bf16[32,2,16,256]{3,2,1,0:T(8,128)(2,1)}), bf16[32,2,16,256]{3,2,1,0:T(8,128)(2,1)S(1)}, u32[]{:S(2)}, u32[]{:S(2)}) %all-to-all-start.3) | async-done | bytes 524320 | tf_op jit(solution)/shard_map/all_to_all | solution.py:622
  144.1 1.6 %finish.1 = (bf16[512,256]{1,0:T(8,128)(2,1)}, bf16[512,256]{1,0:T(8,128)(2,1)}) custom-call(bf16[1024,256]{1,0:T(8,128)(2,1)S(1)} %bitcast.10, s32[8,512]{1,0:T(8,128)S(1)} %copy-done.2, f32[512,256]{1,0:T(8,128)S(1)} %get-tuple-element.45.kept_ref, bf16[512,256]{1,0:T(8,128)(2,1)S(1)} %collective-permute-done.16.taken_ref), custom_call_target="tpu_custom_call" | custom-call | flops 268435456 | bytes 1048576 | tf_op jit(solution)/shard_map/finish/pallas_call | solution.py:275
  (27 shorter events, 0.1 us)
Async XLA Ops:
  7.2 15.7 %copy-start.1 = (bf16[256,2048]{1,0:T(8,128)(2,1)S(1)}, bf16[256,2048]{1,0:T(8,128)(2,1)}, u32[]{:S(2)}) copy-start(bf16[256,2048]{1,0:T(8,128)(2,1)} %refs_0_.1) | copy-start | bytes 3145732
  7.9 19.0 %copy-start.5 = (bf16[2048,256]{1,0:T(8,128)(2,1)S(1)}, bf16[2048,256]{1,0:T(8,128)(2,1)}, u32[]{:S(2)}) copy-start(bf16[2048,256]{1,0:T(8,128)(2,1)} %qk_ref.1) | copy-start | bytes 3145732
  7.9 19.0 %copy-start.11 = (s32[2,16384]{1,0:T(2,128)S(1)}, s32[2,16384]{1,0:T(2,128)}, u32[]{:S(2)}) copy-start(s32[2,16384]{1,0:T(2,128)} %earlier_ref.1) | copy-start | bytes 393220
  11.7 28.8 %all-to-all-start = ((bf16[32,16,512]{2,1,0:T(8,128)(2,1)}), bf16[32,16,512]{2,1,0:T(8,128)(2,1)S(1)}, u32[]{:S(2)}, u32[]{:S(2)}) async-start(bf16[32,16,512]{2,1,0:T(8,128)(2,1)} %bitcast.13), calls=%async_computation | async-start | bytes 1048576 | tf_op jit(solution)/shard_map/all_to_all | solution.py:622
  23.7 11.5 %collective-permute-start = (bf16[256,512]{1,0:T(8,128)(2,1)}, bf16[256,512]{1,0:T(8,128)(2,1)S(1)}, u32[]{:S(2)}, u32[]{:S(2)}) collective-permute-start(bf16[256,512]{1,0:T(8,128)(2,1)} %get-tuple-element.47), channel_id=1, source_target_pairs={{0,2},{1,3},{2,4},{3,5},{4,6},{5,7},{6,0},{7,1},{8,10},{9,11},{10,... | collective-permute-start | bytes 786440 | tf_op jit(solution)/shard_map/ppermute | solution.py:631
  25.2 9.9 %collective-permute-start.1 = (bf16[256,512]{1,0:T(8,128)(2,1)S(1)}, bf16[256,512]{1,0:T(8,128)(2,1)S(1)}, u32[]{:S(2)}, u32[]{:S(2)}) collective-permute-start(bf16[256,512]{1,0:T(8,128)(2,1)S(1)} %get-tuple-element.46), channel_id=1, source_target_pairs={{0,6},{1,7},{2,0},{3,1},{4,2},{5,3},{6,4},{7,5},{8,14},{9,15},{10,... | collective-permute-start | bytes 786440 | tf_op jit(solution)/shard_map/ppermute | solution.py:631
  26.9 1.6 %copy-start.4 = (bf16[512,2048]{1,0:T(8,128)(2,1)S(1)}, bf16[512,2048]{1,0:T(8,128)(2,1)}, u32[]{:S(2)}) copy-start(bf16[512,2048]{1,0:T(8,128)(2,1)} %x_ref.1) | copy-start | bytes 6291460
  28.5 1.2 copy-start.6
  34.5 0.6 copy-start.12
  35.1 35.9 %copy-start.3 = (s32[2]{0:T(128)S(1)}, s32[2]{0:T(128)}, u32[]{:S(2)}) copy-start(s32[2]{0:T(128)} %pad_add_fusion.where_ref) | copy-start | bytes 28
  35.1 0.7 copy-start.7
  40.5 30.5 %collective-permute-start.6 = (bf16[2,2048,256]{2,1,0:T(8,128)(2,1)}, bf16[2,2048,256]{2,1,0:T(8,128)(2,1)}, u32[]{:S(2)}, u32[]{:S(2)}) collective-permute-start(bf16[2,2048,256]{2,1,0:T(8,128)(2,1)} %refs_5_.1), channel_id=1, source_target_pairs={{0,1},{1,0},{2,3},{3,2},{4,5},{5,4},{6,7},{7,6},{8,9},{9,8},{10,11... | collective-permute-start | bytes 6291464 | tf_op jit(solution)/shard_map/ppermute | solution.py:675
  40.5 30.5 %collective-permute-start.7 = (bf16[2,2048,256]{2,1,0:T(8,128)(2,1)}, bf16[2,2048,256]{2,1,0:T(8,128)(2,1)}, u32[]{:S(2)}, u32[]{:S(2)}) collective-permute-start(bf16[2,2048,256]{2,1,0:T(8,128)(2,1)} %refs_6_.1), channel_id=1, source_target_pairs={{0,1},{1,0},{2,3},{3,2},{4,5},{5,4},{6,7},{7,6},{8,9},{9,8},{10,11... | collective-permute-start | bytes 6291464 | tf_op jit(solution)/shard_map/ppermute | solution.py:675
  41.0 30.0 %collective-permute-start.8 = (bf16[2,256,2048]{2,1,0:T(8,128)(2,1)}, bf16[2,256,2048]{2,1,0:T(8,128)(2,1)}, u32[]{:S(2)}, u32[]{:S(2)}) collective-permute-start(bf16[2,256,2048]{2,1,0:T(8,128)(2,1)} %refs_7_.1), channel_id=1, source_target_pairs={{0,1},{1,0},{2,3},{3,2},{4,5},{5,4},{6,7},{7,6},{8,9},{9,8},{10,11... | collective-permute-start | bytes 6291464 | tf_op jit(solution)/shard_map/ppermute | solution.py:675
  41.0 15.6 %collective-permute-start.2 = (bf16[32,16,512]{2,1,0:T(8,128)(2,1)S(1)}, bf16[32,16,512]{2,1,0:T(8,128)(2,1)S(1)}, u32[]{:S(2)}, u32[]{:S(2)}) collective-permute-start(bf16[32,16,512]{2,1,0:T(8,128)(2,1)S(1)} %all-to-all-done.refs_0_), channel_id=1, source_target_pairs={{0,2},{1,3},{2,4},{3,5},{4,6},{5,7},{6,0},{7,1},{8,10},{9,11},{10,... | collective-permute-start | bytes 1572872 | tf_op jit(solution)/shard_map/ppermute | solution.py:631
  42.6 15.1 %collective-permute-start.3 = (bf16[32,16,512]{2,1,0:T(8,128)(2,1)S(1)}, bf16[32,16,512]{2,1,0:T(8,128)(2,1)}, u32[]{:S(2)}, u32[]{:S(2)}) collective-permute-start(bf16[32,16,512]{2,1,0:T(8,128)(2,1)S(1)} %all-to-all-done.refs_0_), channel_id=1, source_target_pairs={{0,6},{1,7},{2,0},{3,1},{4,2},{5,3},{6,4},{7,5},{8,14},{9,15},{10,... | collective-permute-start | bytes 1572872 | tf_op jit(solution)/shard_map/ppermute | solution.py:631
  44.2 35.8 %all-to-all-start.1 = ((bf16[32,32,512]{2,1,0:T(8,128)(2,1)}), bf16[32,32,512]{2,1,0:T(8,128)(2,1)S(1)}, u32[]{:S(2)}, u32[]{:S(2)}) async-start(bf16[32,32,512]{2,1,0:T(8,128)(2,1)} %bitcast.6), calls=%async_computation.2 | async-start | bytes 2097152 | tf_op jit(solution)/shard_map/all_to_all | solution.py:622
  49.4 58.3 %reduce-scatter.2.cloned.1.call-start = ((), (), s32[]{:S(2)}) async-start(), calls=%async_computation.5 | async-start | bytes 2621440 | tf_op jit(solution)/shard_map/reduce_scatter | solution.py:682
  57.3 9.5 %collective-permute-start.4 = (bf16[16,16,512]{2,1,0:T(8,128)(2,1)}, bf16[16,16,512]{2,1,0:T(8,128)(2,1)}, u32[]{:S(2)}, u32[]{:S(2)}) collective-permute-start(bf16[16,16,512]{2,1,0:T(8,128)(2,1)} %slice.20), channel_id=1, source_target_pairs={{0,2},{1,3},{2,4},{3,5},{4,6},{5,7},{6,0},{7,1},{8,10},{9,11},{10,... | collective-permute-start | bytes 786440 | tf_op jit(solution)/shard_map/ppermute | solution.py:631
  59.3 8.5 %collective-permute-start.5 = (bf16[16,16,512]{2,1,0:T(8,128)(2,1)}, bf16[16,16,512]{2,1,0:T(8,128)(2,1)}, u32[]{:S(2)}, u32[]{:S(2)}) collective-permute-start(bf16[16,16,512]{2,1,0:T(8,128)(2,1)} %slice.21), channel_id=1, source_target_pairs={{0,6},{1,7},{2,0},{3,1},{4,2},{5,3},{6,4},{7,5},{8,14},{9,15},{10,... | collective-permute-start | bytes 786440 | tf_op jit(solution)/shard_map/ppermute | solution.py:631
  68.5 11.5 %collective-permute-start.9 = (bf16[256,512]{1,0:T(8,128)(2,1)}, bf16[256,512]{1,0:T(8,128)(2,1)}, u32[]{:S(2)}, u32[]{:S(2)}) collective-permute-start(bf16[256,512]{1,0:T(8,128)(2,1)} %constant_dynamic-slice_fusion), channel_id=1, source_target_pairs={{0,4},{1,5},{2,6},{3,7},{4,0},{5,1},{6,2},{7,3},{8,12},{9,13},{10,... | collective-permute-start | bytes 786440 | tf_op jit(solution)/shard_map/ppermute | solution.py:631
  81.7 5.0 %collective-permute-start.10 = (bf16[2,64,512]{2,1,0:T(8,128)(2,1)S(1)}, bf16[2,64,512]{2,1,0:T(8,128)(2,1)S(1)}, u32[]{:S(2)}, u32[]{:S(2)}) collective-permute-start(bf16[2,64,512]{2,1,0:T(8,128)(2,1)S(1)} %get-tuple-element.35), channel_id=1, source_target_pairs={{0,8},{8,16},{16,24},{24,32},{32,40},{40,48},{48,56},{56,64},{64,7... | collective-permute-start | bytes 393224 | tf_op jit(solution)/shard_map/ppermute | solution.py:689
  89.3 23.3 %copy-start.13 = (s32[2,8,512]{2,1,0:T(8,128)S(1)}, s32[2,8,512]{2,1,0:T(8,128)}, u32[]{:S(2)}) copy-start(s32[2,8,512]{2,1,0:T(8,128)} %copy-done.12) | copy-start | bytes 98308
  89.3 23.3 %all-to-all-start.2 = ((bf16[32,72,128]{2,1,0:T(8,128)(2,1)}), bf16[32,72,128]{2,1,0:T(8,128)(2,1)S(1)}, u32[]{:S(2)}, u32[]{:S(2)}) async-start(bf16[32,72,128]{2,1,0:T(8,128)(2,1)} %attend_first.1), calls=%async_computation.3 | async-start | bytes 1179648 | tf_op jit(solution)/shard_map/all_to_all | solution.py:622
  107.7 25.3 %copy-start.8 = (bf16[256,512]{1,0:T(8,128)(2,1)S(1)}, bf16[256,512]{1,0:T(8,128)(2,1)}, u32[]{:S(2)}) copy-start(bf16[256,512]{1,0:T(8,128)(2,1)} %copy-done.7) | copy-start | bytes 786436
  108.7 1.6 %collective-permute-start.11 = (bf16[32,16,256]{2,1,0:T(8,128)(2,1)S(1)}, bf16[32,16,256]{2,1,0:T(8,128)(2,1)S(1)}, u32[]{:S(2)}, u32[]{:S(2)}) collective-permute-start(bf16[32,16,256]{2,1,0:T(8,128)(2,1)S(1)} %slice_bitcast_fusion), channel_id=1, source_target_pairs={{0,1},{1,0},{2,3},{3,2},{4,5},{5,4},{6,7},{7,6},{8,9},{9,8},{10,11... | collective-permute-start | bytes 786440 | tf_op jit(solution)/shard_map/ppermute | solution.py:695
  110.4 1.0 copy-start
  113.7 19.3 %copy-start.9 = (bf16[512,256]{1,0:T(8,128)(2,1)}, bf16[512,256]{1,0:T(8,128)(2,1)S(1)}, u32[]{:S(2)}) copy-start(bf16[512,256]{1,0:T(8,128)(2,1)S(1)} %combine.1.own_ref) | copy-start | bytes 786436
  113.7 13.0 %collective-permute-start.12 = (bf16[512,256]{1,0:T(8,128)(2,1)S(1)}, bf16[512,256]{1,0:T(8,128)(2,1)S(1)}, u32[]{:S(2)}, u32[]{:S(2)}) collective-permute-start(bf16[512,256]{1,0:T(8,128)(2,1)S(1)} %combine.1.own_ref), channel_id=1, source_target_pairs={{0,2},{1,3},{2,4},{3,5},{4,6},{5,7},{6,0},{7,1},{8,10},{9,11},{10,... | collective-permute-start | bytes 786440 | tf_op jit(solution)/shard_map/ppermute | solution.py:631
  115.8 11.0 %collective-permute-start.13 = (bf16[512,256]{1,0:T(8,128)(2,1)S(1)}, bf16[512,256]{1,0:T(8,128)(2,1)S(1)}, u32[]{:S(2)}, u32[]{:S(2)}) collective-permute-start(bf16[512,256]{1,0:T(8,128)(2,1)S(1)} %combine.1.own_ref), channel_id=1, source_target_pairs={{0,6},{1,7},{2,0},{3,1},{4,2},{5,3},{6,4},{7,5},{8,14},{9,15},{10,... | collective-permute-start | bytes 786440 | tf_op jit(solution)/shard_map/ppermute | solution.py:631
  117.0 27.1 %all-to-all-start.3 = ((bf16[32,2,16,256]{3,2,1,0:T(8,128)(2,1)}), bf16[32,2,16,256]{3,2,1,0:T(8,128)(2,1)S(1)}, u32[]{:S(2)}, u32[]{:S(2)}) async-start(bf16[32,2,16,256]{3,2,1,0:T(8,128)(2,1)} %place_rows.1), calls=%async_computation.4 | async-start | bytes 1048576 | tf_op jit(solution)/shard_map/all_to_all | solution.py:622
  126.8 6.3 %collective-permute-start.14 = (bf16[256,256]{1,0:T(8,128)(2,1)S(1)}, bf16[256,256]{1,0:T(8,128)(2,1)S(1)}, u32[]{:S(2)}, u32[]{:S(2)}) collective-permute-start(bf16[256,256]{1,0:T(8,128)(2,1)S(1)} %slice.22), channel_id=1, source_target_pairs={{0,2},{1,3},{2,4},{3,5},{4,6},{5,7},{6,0},{7,1},{8,10},{9,11},{10,... | collective-permute-start | bytes 393224 | tf_op jit(solution)/shard_map/ppermute | solution.py:631
  126.9 17.2 %copy-start.2 = (s32[8,512]{1,0:T(8,128)S(1)}, s32[8,512]{1,0:T(8,128)}, u32[]{:S(2)}) copy-start(s32[8,512]{1,0:T(8,128)} %get-tuple-element.44.slot_ref) | copy-start | bytes 49156
  126.9 6.1 %collective-permute-start.15 = (bf16[256,256]{1,0:T(8,128)(2,1)S(1)}, bf16[256,256]{1,0:T(8,128)(2,1)S(1)}, u32[]{:S(2)}, u32[]{:S(2)}) collective-permute-start(bf16[256,256]{1,0:T(8,128)(2,1)S(1)} %slice.23), channel_id=1, source_target_pairs={{0,6},{1,7},{2,0},{3,1},{4,2},{5,3},{6,4},{7,5},{8,14},{9,15},{10,... | collective-permute-start | bytes 393224 | tf_op jit(solution)/shard_map/ppermute | solution.py:631
  133.1 1.0 copy-start.10
  136.3 1.6 %collective-permute-start.16 = (bf16[512,256]{1,0:T(8,128)(2,1)S(1)}, bf16[512,256]{1,0:T(8,128)(2,1)S(1)}, u32[]{:S(2)}, u32[]{:S(2)}) collective-permute-start(bf16[512,256]{1,0:T(8,128)(2,1)S(1)} %get-tuple-element.42), channel_id=1, source_target_pairs={{0,1},{1,0},{2,3},{3,2},{4,5},{5,4},{6,7},{7,6},{8,9},{9,8},{10,11... | collective-permute-start | bytes 786440 | tf_op jit(solution)/shard_map/ppermute | solution.py:701
Sparse Core Ops, SparseCore 0:
  80.1 27.5 reduce-scatter.1

commit v15 on v10

--- a/solution.py
+++ b/solution.py
@@ -693,7 +693,7 @@
     expert_rows = after(expert_rows, packed)
     taken = lax.ppermute(expert_rows[1], "exp", siblings)
     expert_rows = place_rows(expert_rows, taken)
-    mixed_heads = combine(after(got, expert_rows), slot_token, w_qk.shape[1])
+    mixed_heads = combine(got, slot_token, w_qk.shape[1])
     expert_back = exchange(after(expert_rows, mixed_heads), "seq")
     heads, far_heads = spread(mixed_heads, chips)
     attn_kept, attn_given = project(where, (*heads, *far_heads), w_out, (*near, far))

time: 153 us -> 152 us (level)
  starting transfers between devices: 51.4 us -> 48.5 us
    all_to_all x4, starting transfers between devices: 31.2 us -> 28.4 us  [exchange(): return lax.all_to_all(x, axis, split_axis=0, concat_axis=0, tiled=True)]
    all_to_all x4, waiting for transfers between devices: 13.6 us -> 15.8 us  [exchange(): return lax.all_to_all(x, axis, split_axis=0, concat_axis=0, tiled=True)]
    unnamed x22 -> x26, local copies, waits for them, and re-layouts: 7.71 us -> 7.63 us
  transfers between devices with their start and end apart: 22 -> 22, of which waited for: 11 -> 10; matrix products, arithmetic and copies ran while one was open for 3% -> 4% of each run, Pallas kernels for 16% -> 17%
where the time goes in v15:
time: 152 us; the launch traced here: 151 us
  starting transfers between devices  48.5 us (32%)
  waiting for transfers between devices  45 us (30%)
  Pallas kernels  29.8 us (20%)
  between operations  14.3 us (9%)
  local copies, waits for them, and re-layouts  13.3 us (9%)
    all_to_all x4, starting transfers between devices, exchange(): return lax.all_to_all(x, axis, split_axis=0, concat_axis=0, tiled=True)  28.4 us
    ppermute x11, starting transfers between devices, hop(): return lax.ppermute(x, 'exp', pairs)  18.9 us
    ppermute x11, waiting for transfers between devices, hop(): return lax.ppermute(x, 'exp', pairs)  15.9 us
    all_to_all x4, waiting for transfers between devices, exchange(): return lax.all_to_all(x, axis, split_axis=0, concat_axis=0, tiled=True)  15.8 us
    reduce_scatter x1, waiting for transfers between devices, body(): lax.psum_scatter(expert_part, 'exp', scatter_dimension=0, tiled=False, ax...  11 us
    pallas_call x1, Pallas kernels, run_experts(): pl.pallas_call(experts_kernel, grid_spec=pltpu.PrefetchScalarGridSpec(num...  8.95 us
    unnamed x26, local copies, waits for them, and re-layouts  7.63 us
    pallas_call x1, Pallas kernels, pack_rows(): pl.pallas_call(pack_rows_kernel, grid_spec=pltpu.PrefetchScalarGridSpec(n...  4.8 us
  transfers between devices with their start and end apart: 22, of which 10 were waited for; matrix products, arithmetic and copies ran while one was open for 4% of the time, Pallas kernels for 17%

profile of v15, /device:TPU:32, one launch (start us, length us, event | category | flops | bytes accessed | tf_op | source)
XLA Modules:
  0.0 150.9 jit_solution(15883266152966673482)
XLA Ops:
  7.2 0.1 pad_add_fusion.where_ref
  7.3 1.6 %copy-done = bf16[512,2048]{1,0:T(8,128)(2,1)S(1)} copy-done((bf16[512,2048]{1,0:T(8,128)(2,1)S(1)}, bf16[512,2048]{1,0:T(8,128)(2,1)}, u32[]{:S(2)}) %copy-start) | copy-done | bytes 2097176
  8.9 0.7 copy-done.3
  9.5 2.2 %pack_tokens.1 = (bf16[512,512]{1,0:T(8,128)(2,1)}, s32[8,512]{1,0:T(8,128)S(1)}) custom-call(s32[2]{0:T(128)S(1)} %pad_add_fusion.where_ref, s32[1,512]{1,0:T(1,128)S(1)} %bitcast.13, bf16[512,2048]{1,0:T(8,128)(2,1)S(1)} %copy-done), custom_call_target="tpu_custom_call" | custom-call | flops 268435456 | bytes 2097152 | tf_op jit(solution)/shard_map/pack_tokens/pallas_call | solution.py:146
  11.8 11.2 %all-to-all-start = ((bf16[32,16,512]{2,1,0:T(8,128)(2,1)}), bf16[32,16,512]{2,1,0:T(8,128)(2,1)S(1)}, u32[]{:S(2)}, u32[]{:S(2)}) async-start(bf16[32,16,512]{2,1,0:T(8,128)(2,1)} %bitcast.3), calls=%async_computation | async-start | bytes 1048576 | tf_op jit(solution)/shard_map/all_to_all | solution.py:621
  23.0 0.8 constant_dynamic-slice_fusion.1
  23.9 1.6 %collective-permute-start = (bf16[256,512]{1,0:T(8,128)(2,1)}, bf16[256,512]{1,0:T(8,128)(2,1)S(1)}, u32[]{:S(2)}, u32[]{:S(2)}) collective-permute-start(bf16[256,512]{1,0:T(8,128)(2,1)} %get-tuple-element.45), channel_id=1, source_target_pairs={{0,2},{1,3},{2,4},{3,5},{4,6},{5,7},{6,0},{7,1},{8,10},{9,11},{10,... | collective-permute-start | bytes 786440 | tf_op jit(solution)/shard_map/ppermute | solution.py:630
  25.4 1.7 %collective-permute-start.1 = (bf16[256,512]{1,0:T(8,128)(2,1)}, bf16[256,512]{1,0:T(8,128)(2,1)S(1)}, u32[]{:S(2)}, u32[]{:S(2)}) collective-permute-start(bf16[256,512]{1,0:T(8,128)(2,1)} %get-tuple-element.44), channel_id=1, source_target_pairs={{0,6},{1,7},{2,0},{3,1},{4,2},{5,3},{6,4},{7,5},{8,14},{9,15},{10,... | collective-permute-start | bytes 786440 | tf_op jit(solution)/shard_map/ppermute | solution.py:630
  27.1 1.6 %copy-done.4 = bf16[512,2048]{1,0:T(8,128)(2,1)S(1)} copy-done((bf16[512,2048]{1,0:T(8,128)(2,1)S(1)}, bf16[512,2048]{1,0:T(8,128)(2,1)}, u32[]{:S(2)}) %copy-start.4) | copy-done | bytes 2097176
  28.7 1.2 copy-done.6
  29.9 4.8 %pack_rows.1 = (bf16[1024,512]{1,0:T(8,128)(2,1)}, s32[2,8,512]{2,1,0:T(8,128)S(1)}) custom-call(s32[1]{0:T(128)} %bitcast.4.me_ref, s32[2,16384]{1,0:T(2,128)S(1)} %copy-done.11, bf16[512,2048]{1,0:T(8,128)(2,1)S(1)} %copy-done.4, bf16[2048,256]{1,0:T(8,128)(2,1)S(1)} %copy-done.5, bf16[2048,256]{1,0:T(8,128)(2,1)S(1)} %copy-done.6), custom_call_target="tpu_custom_call" | custom-call | flops 1610612736 | bytes 6291456 | tf_op jit(solution)/shard_map/pack_rows/pallas_call | solution.py:90
  34.7 0.0 collective-permute-done.1.refs_2_
  34.7 0.7 copy-done.7
  35.4 5.2 %all-to-all-done.refs_0_ = bf16[32,16,512]{2,1,0:T(8,128)(2,1)S(1)} async-done(((bf16[32,16,512]{2,1,0:T(8,128)(2,1)}), bf16[32,16,512]{2,1,0:T(8,128)(2,1)S(1)}, u32[]{:S(2)}, u32[]{:S(2)}) %all-to-all-start) | async-done | bytes 524320 | tf_op jit(solution)/shard_map/all_to_all | solution.py:621
  40.6 0.0 collective-permute-start.6
  40.6 0.5 collective-permute-start.7
  41.1 0.0 collective-permute-start.8
  41.1 1.6 %collective-permute-start.2 = (bf16[32,16,512]{2,1,0:T(8,128)(2,1)S(1)}, bf16[32,16,512]{2,1,0:T(8,128)(2,1)S(1)}, u32[]{:S(2)}, u32[]{:S(2)}) collective-permute-start(bf16[32,16,512]{2,1,0:T(8,128)(2,1)S(1)} %all-to-all-done.refs_0_), channel_id=1, source_target_pairs={{0,2},{1,3},{2,4},{3,5},{4,6},{5,7},{6,0},{7,1},{8,10},{9,11},{10,... | collective-permute-start | bytes 1572872 | tf_op jit(solution)/shard_map/ppermute | solution.py:630
  42.7 1.7 %collective-permute-start.3 = (bf16[32,16,512]{2,1,0:T(8,128)(2,1)S(1)}, bf16[32,16,512]{2,1,0:T(8,128)(2,1)}, u32[]{:S(2)}, u32[]{:S(2)}) collective-permute-start(bf16[32,16,512]{2,1,0:T(8,128)(2,1)S(1)} %all-to-all-done.refs_0_), channel_id=1, source_target_pairs={{0,6},{1,7},{2,0},{3,1},{4,2},{5,3},{6,4},{7,5},{8,14},{9,15},{10,... | collective-permute-start | bytes 1572872 | tf_op jit(solution)/shard_map/ppermute | solution.py:630
  44.3 4.9 %all-to-all-start.1 = ((bf16[32,32,512]{2,1,0:T(8,128)(2,1)}), bf16[32,32,512]{2,1,0:T(8,128)(2,1)S(1)}, u32[]{:S(2)}, u32[]{:S(2)}) async-start(bf16[32,32,512]{2,1,0:T(8,128)(2,1)} %bitcast.6), calls=%async_computation.2 | async-start | bytes 2097152 | tf_op jit(solution)/shard_map/all_to_all | solution.py:621
  49.2 0.0 reduce-scatter.2.cloned.1.call-start
  49.3 7.5 %collective-permute-done.2.refs_1_ = bf16[32,16,512]{2,1,0:T(8,128)(2,1)S(1)} collective-permute-done((bf16[32,16,512]{2,1,0:T(8,128)(2,1)S(1)}, bf16[32,16,512]{2,1,0:T(8,128)(2,1)S(1)}, u32[]{:S(2)}, u32[]{:S(2)}) %collective-permute-start.2) | collective-permute-done | bytes 524320 | tf_op jit(solution)/shard_map/ppermute | solution.py:630
  56.7 0.7 slice.20
  57.4 0.3 collective-permute-start.4
  57.7 1.7 %slice.21 = bf16[16,16,512]{2,1,0:T(8,128)(2,1)} slice(bf16[32,16,512]{2,1,0:T(8,128)(2,1)} %collective-permute-done.3.refs_2_), slice={[16:32], [0:16], [0:512]} | slice | bytes 524288 | tf_op jit(solution)/shard_map/slice | solution.py:637
  59.4 2.9 %collective-permute-start.5 = (bf16[16,16,512]{2,1,0:T(8,128)(2,1)}, bf16[16,16,512]{2,1,0:T(8,128)(2,1)}, u32[]{:S(2)}, u32[]{:S(2)}) collective-permute-start(bf16[16,16,512]{2,1,0:T(8,128)(2,1)} %slice.21), channel_id=1, source_target_pairs={{0,6},{1,7},{2,0},{3,1},{4,2},{5,3},{6,4},{7,5},{8,14},{9,15},{10,... | collective-permute-start | bytes 786440 | tf_op jit(solution)/shard_map/ppermute | solution.py:630
  62.3 4.6 %collective-permute-done.4.refs_3_ = bf16[16,16,512]{2,1,0:T(8,128)(2,1)} collective-permute-done((bf16[16,16,512]{2,1,0:T(8,128)(2,1)}, bf16[16,16,512]{2,1,0:T(8,128)(2,1)}, u32[]{:S(2)}, u32[]{:S(2)}) %collective-permute-start.4) | collective-permute-done | bytes 262176 | tf_op jit(solution)/shard_map/ppermute | solution.py:630
  67.0 0.9 collective-permute-done.5.refs_4_
  67.9 0.7 constant_dynamic-slice_fusion
  68.6 2.5 %collective-permute-start.9 = (bf16[256,512]{1,0:T(8,128)(2,1)}, bf16[256,512]{1,0:T(8,128)(2,1)}, u32[]{:S(2)}, u32[]{:S(2)}) collective-permute-start(bf16[256,512]{1,0:T(8,128)(2,1)} %constant_dynamic-slice_fusion), channel_id=1, source_target_pairs={{0,4},{1,5},{2,6},{3,7},{4,0},{5,1},{6,2},{7,3},{8,12},{9,13},{10,... | collective-permute-start | bytes 786440 | tf_op jit(solution)/shard_map/ppermute | solution.py:630
  71.1 0.0 collective-permute-done.6.refs_8_
  71.1 9.0 %experts.1 = bf16[4,2,32,16,256]{4,3,2,1,0:T(8,128)(2,1)} custom-call(s32[2]{0:T(128)S(1)} %pad_add_fusion.where_ref, bf16[32,16,512]{2,1,0:T(8,128)(2,1)S(1)} %all-to-all-done.refs_0_, bf16[32,16,512]{2,1,0:T(8,128)(2,1)S(1)} %collective-permute-done.2.refs_1_, bf16[32,16,512]{2,1,0:T(8,128)(2,1)} %collective-permute-done.3.refs_2_, ...), custom_call_target="tpu_custom_call" | custom-call | flops 15000000512 | bytes 10485760 | tf_op jit(solution)/shard_map/experts/pallas_call | solution.py:222
  80.1 0.0 reduce-scatter.2.cloned.1.call-update
  80.1 0.0 collective-permute-done.9.refs_3_
  80.1 0.9 copy-done.12
  81.0 1.7 %sort_rows.1 = (bf16[2,512,512]{2,1,0:T(8,128)(2,1)S(1)}, bf16[2,64,512]{2,1,0:T(8,128)(2,1)S(1)}, s32[2,8,512]{2,1,0:T(8,128)S(1)}) custom-call(s32[1]{0:T(128)} %bitcast.4.me_ref, s32[2,16384]{1,0:T(2,128)S(1)} %copy-done.12, bf16[32,32,512]{2,1,0:T(8,128)(2,1)S(1)} %all-to-all-done.1.arrived_ref), custom_call_target="tpu_custom_call" | custom-call | flops 34359738368 | bytes 4194304 | tf_op jit(solution)/shard_map/sort_rows/pallas_call | solution.py:306
  82.7 0.5 collective-permute-start.10
  83.2 3.8 %attend_later.1.later_ref = bf16[2,512,384]{2,1,0:T(8,128)(2,1)S(1)} custom-call(s32[1]{0:T(128)} %bitcast.4.me_ref, s32[2,16384]{1,0:T(2,128)S(1)} %copy-done.12, bf16[2,512,512]{2,1,0:T(8,128)(2,1)S(1)} %get-tuple-element.33.rows_ref, s32[2,8,512]{2,1,0:T(8,128)S(1)} %get-tuple-element.35.slot_ref), custom_call_target="tpu_custom_call" | custom-call | flops 34359738368 | bytes 4194304 | tf_op jit(solution)/shard_map/attend_later/pallas_call | solution.py:468
  87.1 0.7 collective-permute-done.10.last_ref
  87.8 2.5 %attend_first.1 = bf16[32,72,128]{2,1,0:T(8,128)(2,1)} custom-call(s32[1]{0:T(128)} %bitcast.4.me_ref, s32[2,16384]{1,0:T(2,128)S(1)} %copy-done.12, s32[2,16384]{1,0:T(2,128)S(1)} %copy-done.12, bf16[2,512,512]{2,1,0:T(8,128)(2,1)S(1)} %get-tuple-element.33.rows_ref, bf16[2,64,512]{2,1,0:T(8,128)(2,1)S(1)} %collective-permute-done.10.last_ref, ...), custom_call_target="tpu_custom_call" | custom-call | flops 34359738368 | bytes 4194304 | tf_op jit(solution)/shard_map/attend_first/pallas_call | solution.py:497
  90.3 6.3 %all-to-all-start.2 = ((bf16[32,72,128]{2,1,0:T(8,128)(2,1)}), bf16[32,72,128]{2,1,0:T(8,128)(2,1)S(1)}, u32[]{:S(2)}, u32[]{:S(2)}) async-start(bf16[32,72,128]{2,1,0:T(8,128)(2,1)} %attend_first.1), calls=%async_computation.3 | async-start | bytes 1179648 | tf_op jit(solution)/shard_map/all_to_all | solution.py:621
  96.6 11.0 %reduce-scatter.2.cloned.1.call-done = bf16[1,2,32,16,256]{4,3,2,1,0:T(8,128)(2,1)} async-done(((bf16[4,2,32,16,256]{4,3,2,1,0:T(8,128)(2,1)}), bf16[1,2,32,16,256]{4,3,2,1,0:T(8,128)(2,1)}) %reduce-scatter.2.cloned.1.call-update) | async-done | bytes 524304 | tf_op jit(solution)/shard_map/reduce_scatter | solution.py:681
  107.7 1.7 %slice_bitcast_fusion = bf16[32,16,256]{2,1,0:T(8,128)(2,1)} fusion(bf16[2,32,16,256]{3,2,1,0:T(8,128)(2,1)} %bitcast.11), kind=kLoop, calls=%fused_computation | loop fusion | bytes 524288 | tf_op jit(solution)/shard_map/squeeze | solution.py:694
  109.4 0.0 collective-permute-start.11
  109.4 4.1 %all-to-all-done.2.got_ref = bf16[32,72,128]{2,1,0:T(8,128)(2,1)S(1)} async-done(((bf16[32,72,128]{2,1,0:T(8,128)(2,1)}), bf16[32,72,128]{2,1,0:T(8,128)(2,1)S(1)}, u32[]{:S(2)}, u32[]{:S(2)}) %all-to-all-start.2) | async-done | bytes 589856 | tf_op jit(solution)/shard_map/all_to_all | solution.py:621
  113.5 1.1 combine.1.own_ref
  114.5 0.0 copy-start.9
  114.5 2.1 %collective-permute-start.12 = (bf16[512,256]{1,0:T(8,128)(2,1)S(1)}, bf16[512,256]{1,0:T(8,128)(2,1)S(1)}, u32[]{:S(2)}, u32[]{:S(2)}) collective-permute-start(bf16[512,256]{1,0:T(8,128)(2,1)S(1)} %combine.1.own_ref), channel_id=1, source_target_pairs={{0,2},{1,3},{2,4},{3,5},{4,6},{5,7},{6,0},{7,1},{8,10},{9,11},{10,... | collective-permute-start | bytes 786440 | tf_op jit(solution)/shard_map/ppermute | solution.py:630
  116.7 1.2 collective-permute-start.13
  117.9 0.0 collective-permute-done.11.taken_ref
  117.9 0.8 place_rows.1
  118.7 6.0 %all-to-all-start.3 = ((bf16[32,2,16,256]{3,2,1,0:T(8,128)(2,1)}), bf16[32,2,16,256]{3,2,1,0:T(8,128)(2,1)S(1)}, u32[]{:S(2)}, u32[]{:S(2)}) async-start(bf16[32,2,16,256]{3,2,1,0:T(8,128)(2,1)} %place_rows.1), calls=%async_computation.4 | async-start | bytes 1048576 | tf_op jit(solution)/shard_map/all_to_all | solution.py:621
  124.7 0.0 collective-permute-done.12.prev_ref
  124.8 0.1 collective-permute-start.14
  124.9 0.0 collective-permute-done.13.next_ref
  124.9 3.3 %collective-permute-start.15 = (bf16[256,256]{1,0:T(8,128)(2,1)S(1)}, bf16[256,256]{1,0:T(8,128)(2,1)S(1)}, u32[]{:S(2)}, u32[]{:S(2)}) collective-permute-start(bf16[256,256]{1,0:T(8,128)(2,1)S(1)} %slice.23), channel_id=1, source_target_pairs={{0,6},{1,7},{2,0},{3,1},{4,2},{5,3},{6,4},{7,5},{8,14},{9,15},{10,... | collective-permute-start | bytes 393224 | tf_op jit(solution)/shard_map/ppermute | solution.py:630
  128.2 2.8 %collective-permute-done.14.far_a_ref = bf16[256,256]{1,0:T(8,128)(2,1)S(1)} collective-permute-done((bf16[256,256]{1,0:T(8,128)(2,1)S(1)}, bf16[256,256]{1,0:T(8,128)(2,1)S(1)}, u32[]{:S(2)}, u32[]{:S(2)}) %collective-permute-start.14) | collective-permute-done | bytes 131104 | tf_op jit(solution)/shard_map/ppermute | solution.py:630
  131.0 0.0 copy-start.10
  131.0 0.9 copy-done.10
  132.0 2.3 %project.1 = (f32[512,256]{1,0:T(8,128)S(1)}, bf16[512,256]{1,0:T(8,128)(2,1)S(1)}) custom-call(s32[2]{0:T(128)S(1)} %pad_add_fusion.where_ref, bf16[512,256]{1,0:T(8,128)(2,1)S(1)} %copy-done.10, bf16[512,256]{1,0:T(8,128)(2,1)S(1)} %collective-permute-done.12.prev_ref, bf16[512,256]{1,0:T(8,128)(2,1)S(1)} %collective-permute-done.13.next_ref, ...), custom_call_target="tpu_custom_call" | custom-call | flops 5500000256 | bytes 3145728 | tf_op jit(solution)/shard_map/project/pallas_call | solution.py:602
  134.2 0.1 collective-permute-start.16
  134.3 1.5 %collective-permute-done.16.taken_ref = bf16[512,256]{1,0:T(8,128)(2,1)S(1)} collective-permute-done((bf16[512,256]{1,0:T(8,128)(2,1)S(1)}, bf16[512,256]{1,0:T(8,128)(2,1)S(1)}, u32[]{:S(2)}, u32[]{:S(2)}) %collective-permute-start.16) | collective-permute-done | bytes 262176 | tf_op jit(solution)/shard_map/ppermute | solution.py:700
  135.9 6.6 %all-to-all-done.3 = bf16[32,2,16,256]{3,2,1,0:T(8,128)(2,1)S(1)} async-done(((bf16[32,2,16,256]{3,2,1,0:T(8,128)(2,1)}), bf16[32,2,16,256]{3,2,1,0:T(8,128)(2,1)S(1)}, u32[]{:S(2)}, u32[]{:S(2)}) %all-to-all-start.3) | async-done | bytes 524320 | tf_op jit(solution)/shard_map/all_to_all | solution.py:621
  142.5 1.6 %finish.1 = (bf16[512,256]{1,0:T(8,128)(2,1)}, bf16[512,256]{1,0:T(8,128)(2,1)}) custom-call(bf16[1024,256]{1,0:T(8,128)(2,1)S(1)} %bitcast.10, s32[8,512]{1,0:T(8,128)S(1)} %get-tuple-element.42.slot_ref, f32[512,256]{1,0:T(8,128)S(1)} %get-tuple-element.43.kept_ref, bf16[512,256]{1,0:T(8,128)(2,1)S(1)} %collective-permute-done.16.taken_ref), custom_call_target="tpu_custom_call" | custom-call | flops 268435456 | bytes 1048576 | tf_op jit(solution)/shard_map/finish/pallas_call | solution.py:274
  (25 shorter events, 0.1 us)
Async XLA Ops:
  7.3 1.6 %copy-start = (bf16[512,2048]{1,0:T(8,128)(2,1)S(1)}, bf16[512,2048]{1,0:T(8,128)(2,1)}, u32[]{:S(2)}) copy-start(bf16[512,2048]{1,0:T(8,128)(2,1)} %tokens_ref.1) | copy-start | bytes 6291460
  8.9 0.7 copy-start.3
  9.5 13.5 %copy-start.2 = (bf16[256,2048]{1,0:T(8,128)(2,1)S(1)}, bf16[256,2048]{1,0:T(8,128)(2,1)}, u32[]{:S(2)}) copy-start(bf16[256,2048]{1,0:T(8,128)(2,1)} %refs_0_.1) | copy-start | bytes 3145732
  9.5 17.6 %copy-start.5 = (bf16[2048,256]{1,0:T(8,128)(2,1)S(1)}, bf16[2048,256]{1,0:T(8,128)(2,1)}, u32[]{:S(2)}) copy-start(bf16[2048,256]{1,0:T(8,128)(2,1)} %qk_ref.1) | copy-start | bytes 3145732
  9.5 17.6 %copy-start.11 = (s32[2,16384]{1,0:T(2,128)S(1)}, s32[2,16384]{1,0:T(2,128)}, u32[]{:S(2)}) copy-start(s32[2,16384]{1,0:T(2,128)} %earlier_ref.1) | copy-start | bytes 393220
  11.8 28.8 %all-to-all-start = ((bf16[32,16,512]{2,1,0:T(8,128)(2,1)}), bf16[32,16,512]{2,1,0:T(8,128)(2,1)S(1)}, u32[]{:S(2)}, u32[]{:S(2)}) async-start(bf16[32,16,512]{2,1,0:T(8,128)(2,1)} %bitcast.3), calls=%async_computation | async-start | bytes 1048576 | tf_op jit(solution)/shard_map/all_to_all | solution.py:621
  23.9 10.9 %collective-permute-start = (bf16[256,512]{1,0:T(8,128)(2,1)}, bf16[256,512]{1,0:T(8,128)(2,1)S(1)}, u32[]{:S(2)}, u32[]{:S(2)}) collective-permute-start(bf16[256,512]{1,0:T(8,128)(2,1)} %get-tuple-element.45), channel_id=1, source_target_pairs={{0,2},{1,3},{2,4},{3,5},{4,6},{5,7},{6,0},{7,1},{8,10},{9,11},{10,... | collective-permute-start | bytes 786440 | tf_op jit(solution)/shard_map/ppermute | solution.py:630
  25.4 9.3 %collective-permute-start.1 = (bf16[256,512]{1,0:T(8,128)(2,1)}, bf16[256,512]{1,0:T(8,128)(2,1)S(1)}, u32[]{:S(2)}, u32[]{:S(2)}) collective-permute-start(bf16[256,512]{1,0:T(8,128)(2,1)} %get-tuple-element.44), channel_id=1, source_target_pairs={{0,6},{1,7},{2,0},{3,1},{4,2},{5,3},{6,4},{7,5},{8,14},{9,15},{10,... | collective-permute-start | bytes 786440 | tf_op jit(solution)/shard_map/ppermute | solution.py:630
  27.1 1.6 %copy-start.4 = (bf16[512,2048]{1,0:T(8,128)(2,1)S(1)}, bf16[512,2048]{1,0:T(8,128)(2,1)}, u32[]{:S(2)}) copy-start(bf16[512,2048]{1,0:T(8,128)(2,1)} %x_ref.1) | copy-start | bytes 6291460
  28.7 1.2 copy-start.6
  34.7 0.7 copy-start.7
  40.6 30.5 %collective-permute-start.6 = (bf16[2,2048,256]{2,1,0:T(8,128)(2,1)}, bf16[2,2048,256]{2,1,0:T(8,128)(2,1)}, u32[]{:S(2)}, u32[]{:S(2)}) collective-permute-start(bf16[2,2048,256]{2,1,0:T(8,128)(2,1)} %refs_5_.1), channel_id=1, source_target_pairs={{0,1},{1,0},{2,3},{3,2},{4,5},{5,4},{6,7},{7,6},{8,9},{9,8},{10,11... | collective-permute-start | bytes 6291464 | tf_op jit(solution)/shard_map/ppermute | solution.py:674
  40.6 30.5 %collective-permute-start.7 = (bf16[2,2048,256]{2,1,0:T(8,128)(2,1)}, bf16[2,2048,256]{2,1,0:T(8,128)(2,1)}, u32[]{:S(2)}, u32[]{:S(2)}) collective-permute-start(bf16[2,2048,256]{2,1,0:T(8,128)(2,1)} %refs_6_.1), channel_id=1, source_target_pairs={{0,1},{1,0},{2,3},{3,2},{4,5},{5,4},{6,7},{7,6},{8,9},{9,8},{10,11... | collective-permute-start | bytes 6291464 | tf_op jit(solution)/shard_map/ppermute | solution.py:674
  41.1 30.0 %collective-permute-start.8 = (bf16[2,256,2048]{2,1,0:T(8,128)(2,1)}, bf16[2,256,2048]{2,1,0:T(8,128)(2,1)}, u32[]{:S(2)}, u32[]{:S(2)}) collective-permute-start(bf16[2,256,2048]{2,1,0:T(8,128)(2,1)} %refs_7_.1), channel_id=1, source_target_pairs={{0,1},{1,0},{2,3},{3,2},{4,5},{5,4},{6,7},{7,6},{8,9},{9,8},{10,11... | collective-permute-start | bytes 6291464 | tf_op jit(solution)/shard_map/ppermute | solution.py:674
  41.1 15.6 %collective-permute-start.2 = (bf16[32,16,512]{2,1,0:T(8,128)(2,1)S(1)}, bf16[32,16,512]{2,1,0:T(8,128)(2,1)S(1)}, u32[]{:S(2)}, u32[]{:S(2)}) collective-permute-start(bf16[32,16,512]{2,1,0:T(8,128)(2,1)S(1)} %all-to-all-done.refs_0_), channel_id=1, source_target_pairs={{0,2},{1,3},{2,4},{3,5},{4,6},{5,7},{6,0},{7,1},{8,10},{9,11},{10,... | collective-permute-start | bytes 1572872 | tf_op jit(solution)/shard_map/ppermute | solution.py:630
  42.7 15.1 %collective-permute-start.3 = (bf16[32,16,512]{2,1,0:T(8,128)(2,1)S(1)}, bf16[32,16,512]{2,1,0:T(8,128)(2,1)}, u32[]{:S(2)}, u32[]{:S(2)}) collective-permute-start(bf16[32,16,512]{2,1,0:T(8,128)(2,1)S(1)} %all-to-all-done.refs_0_), channel_id=1, source_target_pairs={{0,6},{1,7},{2,0},{3,1},{4,2},{5,3},{6,4},{7,5},{8,14},{9,15},{10,... | collective-permute-start | bytes 1572872 | tf_op jit(solution)/shard_map/ppermute | solution.py:630
  44.3 35.8 %all-to-all-start.1 = ((bf16[32,32,512]{2,1,0:T(8,128)(2,1)}), bf16[32,32,512]{2,1,0:T(8,128)(2,1)S(1)}, u32[]{:S(2)}, u32[]{:S(2)}) async-start(bf16[32,32,512]{2,1,0:T(8,128)(2,1)} %bitcast.6), calls=%async_computation.2 | async-start | bytes 2097152 | tf_op jit(solution)/shard_map/all_to_all | solution.py:621
  49.2 58.4 %reduce-scatter.2.cloned.1.call-start = ((), (), s32[]{:S(2)}) async-start(), calls=%async_computation.5 | async-start | bytes 2621440 | tf_op jit(solution)/shard_map/reduce_scatter | solution.py:681
  57.4 9.5 %collective-permute-start.4 = (bf16[16,16,512]{2,1,0:T(8,128)(2,1)}, bf16[16,16,512]{2,1,0:T(8,128)(2,1)}, u32[]{:S(2)}, u32[]{:S(2)}) collective-permute-start(bf16[16,16,512]{2,1,0:T(8,128)(2,1)} %slice.20), channel_id=1, source_target_pairs={{0,2},{1,3},{2,4},{3,5},{4,6},{5,7},{6,0},{7,1},{8,10},{9,11},{10,... | collective-permute-start | bytes 786440 | tf_op jit(solution)/shard_map/ppermute | solution.py:630
  59.4 8.5 %collective-permute-start.5 = (bf16[16,16,512]{2,1,0:T(8,128)(2,1)}, bf16[16,16,512]{2,1,0:T(8,128)(2,1)}, u32[]{:S(2)}, u32[]{:S(2)}) collective-permute-start(bf16[16,16,512]{2,1,0:T(8,128)(2,1)} %slice.21), channel_id=1, source_target_pairs={{0,6},{1,7},{2,0},{3,1},{4,2},{5,3},{6,4},{7,5},{8,14},{9,15},{10,... | collective-permute-start | bytes 786440 | tf_op jit(solution)/shard_map/ppermute | solution.py:630
  68.6 11.5 %collective-permute-start.9 = (bf16[256,512]{1,0:T(8,128)(2,1)}, bf16[256,512]{1,0:T(8,128)(2,1)}, u32[]{:S(2)}, u32[]{:S(2)}) collective-permute-start(bf16[256,512]{1,0:T(8,128)(2,1)} %constant_dynamic-slice_fusion), channel_id=1, source_target_pairs={{0,4},{1,5},{2,6},{3,7},{4,0},{5,1},{6,2},{7,3},{8,12},{9,13},{10,... | collective-permute-start | bytes 786440 | tf_op jit(solution)/shard_map/ppermute | solution.py:630
  80.1 0.9 copy-start.12
  82.7 5.0 %collective-permute-start.10 = (bf16[2,64,512]{2,1,0:T(8,128)(2,1)S(1)}, bf16[2,64,512]{2,1,0:T(8,128)(2,1)S(1)}, u32[]{:S(2)}, u32[]{:S(2)}) collective-permute-start(bf16[2,64,512]{2,1,0:T(8,128)(2,1)S(1)} %get-tuple-element.34), channel_id=1, source_target_pairs={{0,8},{8,16},{16,24},{24,32},{32,40},{40,48},{48,56},{56,64},{64,7... | collective-permute-start | bytes 393224 | tf_op jit(solution)/shard_map/ppermute | solution.py:688
  90.3 23.2 %all-to-all-start.2 = ((bf16[32,72,128]{2,1,0:T(8,128)(2,1)}), bf16[32,72,128]{2,1,0:T(8,128)(2,1)S(1)}, u32[]{:S(2)}, u32[]{:S(2)}) async-start(bf16[32,72,128]{2,1,0:T(8,128)(2,1)} %attend_first.1), calls=%async_computation.3 | async-start | bytes 1179648 | tf_op jit(solution)/shard_map/all_to_all | solution.py:621
  107.7 10.2 %copy-start.1 = (bf16[1,2,32,16,256]{4,3,2,1,0:T(8,128)(2,1)S(1)}, bf16[1,2,32,16,256]{4,3,2,1,0:T(8,128)(2,1)}, u32[]{:S(2)}) copy-start(bf16[1,2,32,16,256]{4,3,2,1,0:T(8,128)(2,1)} %reduce-scatter.2.cloned.1.call-done) | copy-start | bytes 1572868
  109.4 8.5 %collective-permute-start.11 = (bf16[32,16,256]{2,1,0:T(8,128)(2,1)}, bf16[32,16,256]{2,1,0:T(8,128)(2,1)S(1)}, u32[]{:S(2)}, u32[]{:S(2)}) collective-permute-start(bf16[32,16,256]{2,1,0:T(8,128)(2,1)} %slice_bitcast_fusion), channel_id=1, source_target_pairs={{0,1},{1,0},{2,3},{3,2},{4,5},{5,4},{6,7},{7,6},{8,9},{9,8},{10,11... | collective-permute-start | bytes 786440 | tf_op jit(solution)/shard_map/ppermute | solution.py:694
  113.5 17.6 %copy-start.8 = (bf16[256,512]{1,0:T(8,128)(2,1)S(1)}, bf16[256,512]{1,0:T(8,128)(2,1)}, u32[]{:S(2)}) copy-start(bf16[256,512]{1,0:T(8,128)(2,1)} %copy-done.7) | copy-start | bytes 786436
  114.5 16.5 %copy-start.9 = (bf16[512,256]{1,0:T(8,128)(2,1)}, bf16[512,256]{1,0:T(8,128)(2,1)S(1)}, u32[]{:S(2)}) copy-start(bf16[512,256]{1,0:T(8,128)(2,1)S(1)} %combine.1.own_ref) | copy-start | bytes 786436
  114.5 10.2 %collective-permute-start.12 = (bf16[512,256]{1,0:T(8,128)(2,1)S(1)}, bf16[512,256]{1,0:T(8,128)(2,1)S(1)}, u32[]{:S(2)}, u32[]{:S(2)}) collective-permute-start(bf16[512,256]{1,0:T(8,128)(2,1)S(1)} %combine.1.own_ref), channel_id=1, source_target_pairs={{0,2},{1,3},{2,4},{3,5},{4,6},{5,7},{6,0},{7,1},{8,10},{9,11},{10,... | collective-permute-start | bytes 786440 | tf_op jit(solution)/shard_map/ppermute | solution.py:630
  116.7 8.2 %collective-permute-start.13 = (bf16[512,256]{1,0:T(8,128)(2,1)S(1)}, bf16[512,256]{1,0:T(8,128)(2,1)S(1)}, u32[]{:S(2)}, u32[]{:S(2)}) collective-permute-start(bf16[512,256]{1,0:T(8,128)(2,1)S(1)} %combine.1.own_ref), channel_id=1, source_target_pairs={{0,6},{1,7},{2,0},{3,1},{4,2},{5,3},{6,4},{7,5},{8,14},{9,15},{10,... | collective-permute-start | bytes 786440 | tf_op jit(solution)/shard_map/ppermute | solution.py:630
  118.7 23.8 %all-to-all-start.3 = ((bf16[32,2,16,256]{3,2,1,0:T(8,128)(2,1)}), bf16[32,2,16,256]{3,2,1,0:T(8,128)(2,1)S(1)}, u32[]{:S(2)}, u32[]{:S(2)}) async-start(bf16[32,2,16,256]{3,2,1,0:T(8,128)(2,1)} %place_rows.1), calls=%async_computation.4 | async-start | bytes 1048576 | tf_op jit(solution)/shard_map/all_to_all | solution.py:621
  124.8 6.3 %collective-permute-start.14 = (bf16[256,256]{1,0:T(8,128)(2,1)S(1)}, bf16[256,256]{1,0:T(8,128)(2,1)S(1)}, u32[]{:S(2)}, u32[]{:S(2)}) collective-permute-start(bf16[256,256]{1,0:T(8,128)(2,1)S(1)} %slice.22), channel_id=1, source_target_pairs={{0,2},{1,3},{2,4},{3,5},{4,6},{5,7},{6,0},{7,1},{8,10},{9,11},{10,... | collective-permute-start | bytes 393224 | tf_op jit(solution)/shard_map/ppermute | solution.py:630
  124.9 6.1 %collective-permute-start.15 = (bf16[256,256]{1,0:T(8,128)(2,1)S(1)}, bf16[256,256]{1,0:T(8,128)(2,1)S(1)}, u32[]{:S(2)}, u32[]{:S(2)}) collective-permute-start(bf16[256,256]{1,0:T(8,128)(2,1)S(1)} %slice.23), channel_id=1, source_target_pairs={{0,6},{1,7},{2,0},{3,1},{4,2},{5,3},{6,4},{7,5},{8,14},{9,15},{10,... | collective-permute-start | bytes 393224 | tf_op jit(solution)/shard_map/ppermute | solution.py:630
  131.0 1.0 copy-start.10
  134.2 1.6 %collective-permute-start.16 = (bf16[512,256]{1,0:T(8,128)(2,1)S(1)}, bf16[512,256]{1,0:T(8,128)(2,1)S(1)}, u32[]{:S(2)}, u32[]{:S(2)}) collective-permute-start(bf16[512,256]{1,0:T(8,128)(2,1)S(1)} %get-tuple-element.40), channel_id=1, source_target_pairs={{0,1},{1,0},{2,3},{3,2},{4,5},{5,4},{6,7},{7,6},{8,9},{9,8},{10,11... | collective-permute-start | bytes 786440 | tf_op jit(solution)/shard_map/ppermute | solution.py:700
Sparse Core Ops, SparseCore 0:
  80.2 27.3 reduce-scatter.1
